TPU v7x, 32 devices: a whole 2x2x4 slice. The times are simulated.
32 devices in a mesh: row: 8 (over y, x, core), col: 4 (over z).
Axes of the slice: x: 2, y: 2, z: 4, core: 2. Of those that a mesh axis runs over, the one named last changes fastest.
Arguments:
- rhs_rows: float32 [16384, 256], P(('row', 'col')), may hold values from -6 to 6
- dest_row: int32 [16384], P(('row', 'col')), may hold values from 0 to 16383, as said below
- diag_inverse: bfloat16 [4, 32, 128, 128], P(None, ('row', 'col')), may hold values from -1 to 1.5, as said below
- lower_blocks: bfloat16 [3, 8, 4, 128, 4, 8, 128], P(None, 'row', None, None, 'col'), may hold values from -0.09375 to 0.09375
- block_mask: int32 [3, 8, 4, 4, 8], P(None, 'row', None, 'col'), may hold values 0 or 1
Outputs:
- solution: bfloat16 [4, 32, 128, 256], P(None, ('row', 'col'))
Inputs may be any that keep to these rules, and one draw needn't show every extreme that they name: dest_row is a permutation of the rows. In each aligned block of 512 entries, exactly 16 entries g have (g // 128) % 32 equal to q, for every supernode index q. `diag_inverse`: every block is lower triangular with positive diagonal entries.
All inputs are finite; a program needn't handle non-finite values. No bound on the sum of `block_mask` on one device may be relied on, other than what follows from the above.
Results may differ from a plain program's by a relative error of at most 0.029.
Values may be sent and summed in bfloat16 or wider, within the bound.
No kernel may reach another device: no remote copies, remote signals or barrier semaphores. Data moves between devices by JAX's collectives and lax.ppermute only.
A program may use at most 128 MiB of HBM per device.

v0:
```python
import jax
import jax.numpy as jnp
from jax import lax
from jax.sharding import PartitionSpec as P

B = 128
NLEV = 4


def per_device(rhs_rows, dest_row, diag_inverse, lower_blocks, block_mask):
    col_count = lax.axis_size("col")
    row_count = lax.axis_size("row")
    supernodes = row_count * col_count
    local_rows = rhs_rows.shape[0]
    column_total = rhs_rows.shape[1]
    group_rows = local_rows // supernodes
    owner_idx = dest_row // B % supernodes
    position = dest_row // (supernodes * B) * B + dest_row % B
    sort_order = jnp.argsort(owner_idx, stable=True)
    sending = rhs_rows[sort_order]
    places = position[sort_order]
    arrived, arrived_pos = (
        lax.all_to_all(
            sending.reshape(supernodes, group_rows, column_total).astype(jnp.bfloat16),
            ("row", "col"),
            split_axis=0,
            concat_axis=0,
            tiled=True,
        ).astype(jnp.float32),
        lax.all_to_all(
            places.reshape(supernodes, group_rows),
            ("row", "col"),
            split_axis=0,
            concat_axis=0,
            tiled=True,
        ),
    )
    ordered = (
        jnp.zeros_like(rhs_rows)
        .at[arrived_pos.reshape(local_rows)]
        .set(arrived.reshape(local_rows, column_total))
    )
    ordered = ordered.reshape(NLEV, B, column_total)
    diag_inv = diag_inverse[:, 0]
    masked = []
    for level_idx in range(NLEV - 1):
        block_tile = lower_blocks[level_idx, 0, :, :, 0]
        tile_mask = block_mask[level_idx, 0, :, 0, :].astype(jnp.bfloat16)
        masked.append(
            (block_tile * tile_mask[:, None, :, None]).reshape(col_count * B, row_count * B)
        )
    column_count = ordered.shape[2]
    solved = []
    for level_idx in range(NLEV):
        if level_idx == 0:
            residual = ordered[0].astype(jnp.bfloat16)
        else:
            level_tile = masked[level_idx - 1]

            def add_piece(running, shard_piece, first_row, level_tile=level_tile):
                return jnp.dot(level_tile, shard_piece, preferred_element_type=jnp.float32)

            start_sum = jnp.zeros((col_count * B, column_count), jnp.float32)
            partial_sum = add_piece(
                start_sum,
                lax.all_gather(solved[level_idx - 1], "row", axis=0, tiled=True),
                jnp.int32(0),
            )
            coupled = lax.psum_scatter(
                partial_sum.astype(jnp.bfloat16), "col", scatter_dimension=0, tiled=True
            ).astype(jnp.float32)
            residual = (ordered[level_idx] - coupled).astype(jnp.bfloat16)
        solved.append(
            jnp.dot(diag_inv[level_idx], residual, preferred_element_type=jnp.float32).astype(
                jnp.bfloat16
            )
        )
    solution = [None] * NLEV
    for level_idx in range(NLEV - 1, -1, -1):
        if level_idx == NLEV - 1:
            residual = solved[level_idx]
        else:
            upper_blocks = lax.all_gather(solution[level_idx + 1], "col", axis=0, tiled=True)
            level_tile = masked[level_idx]

            def column_term(first_row, row_span, level_tile=level_tile, upper_blocks=upper_blocks):
                return lax.dot_general(
                    level_tile,
                    upper_blocks,
                    (((0,), (0,)), ((), ())),
                    preferred_element_type=jnp.float32,
                )

            back_coupled = lax.psum_scatter(
                column_term(jnp.int32(0), B * lax.axis_size("row")).astype(jnp.bfloat16),
                "row",
                scatter_dimension=0,
                tiled=True,
            ).astype(jnp.float32)
            residual = (solved[level_idx].astype(jnp.float32) - back_coupled).astype(jnp.bfloat16)
        product = lax.dot_general(
            diag_inv[level_idx],
            residual,
            (((0,), (0,)), ((), ())),
            preferred_element_type=jnp.float32,
        )
        solution[level_idx] = product.astype(jnp.bfloat16)
    results = jnp.stack(solution)
    return results[:, None]


def solution(mesh):
    in_specs = (
        P(("row", "col"), None),
        P(("row", "col")),
        P(None, ("row", "col"), None, None),
        P(None, "row", None, None, "col", None, None),
        P(None, "row", None, "col", None),
    )
    out_specs = P(None, ("row", "col"), None, None)
    return jax.shard_map(
        per_device, mesh=mesh, in_specs=in_specs, out_specs=out_specs, check_vma=False
    )
```

profile of v0, /device:TPU:0, one launch (start us, length us, event | category | flops | bytes accessed | tf_op | source)
XLA Modules:
  0.0 295.9 jit_solution(598830287623475489)
XLA Ops:
  6.5 0.8 add_select_fusion
  7.3 3.8 %sort.17 = (s32[512]{0:T(512)}, s32[512]{0:T(512)S(1)}) sort(s32[512]{0:T(512)S(1)} %get-tuple-element.13, s32[512]{0:T(512)S(1)} %iota.4), dimensions={0}, to_apply=%region_0.1 | sort | flops 4608 | bytes 8192 | tf_op jit(solution)/shard_map/jit(argsort)/sort | solution.py:19
  11.1 3.5 %gather_fusion = s32[512]{0:T(512)S(1)} fusion(s32[512]{0:T(512)S(1)} %get-tuple-element.14, s32[1024]{0:T(1024)S(1)} %pad_clamp_fusion), kind=kCustom, calls=%fused_computation | custom fusion | bytes 6144 | tf_op jit(solution)/shard_map/gather | solution.py:21
  14.6 0.7 all_to_all.9
  15.3 7.3 %all-to-all-start = ((s32[32,1,16]{2,1,0:T(1,128)}), s32[32,1,16]{2,1,0:T(1,128)S(1)}, u32[]{:S(2)}, u32[]{:S(2)}) async-start(s32[32,1,16]{2,1,0:T(1,128)} %bitcast), calls=%async_computation | async-start | bytes 32768 | tf_op jit(solution)/shard_map/all_to_all | solution.py:30
  22.6 0.7 convert.10
  23.3 2.2 gather_fusion.1
  25.5 4.2 %all-to-all-done = s32[32,1,16]{2,1,0:T(1,128)S(1)} async-done(((s32[32,1,16]{2,1,0:T(1,128)}), s32[32,1,16]{2,1,0:T(1,128)S(1)}, u32[]{:S(2)}, u32[]{:S(2)}) %all-to-all-start) | async-done | bytes 2080 | tf_op jit(solution)/shard_map/all_to_all | solution.py:30
  29.7 2.6 all-to-all-start.1
  32.4 3.4 %fusion.35 = (bf16[1,1,4,128,1,8,128]{6,5,4,3,2,1,0:T(8,128)(2,1)}, bf16[1,1,4,128,1,8,128]{6,5,4,3,2,1,0:T(8,128)(2,1)S(1)}, bf16[1,1,4,128,1,8,128]{6,5,4,3,2,1,0:T(8,128)(2,1)}) fusion(bf16[3,1,4,128,1,8,128]{6,5,4,3,2,1,0:T(8,128)(2,1)} %param.8), kind=kLoop, calls=%fused_computation.75 | loop fusion | bytes 6291456 | tf_op jit(solution)/shard_map/slice | solution.py:47
  35.8 0.5 broadcast.59
  36.3 0.6 reduce.3
  36.9 0.1 reshape.89
  37.0 5.5 %all-to-all-done.1 = bf16[32,16,256]{2,1,0:T(8,128)(2,1)S(1)} async-done(((bf16[32,16,256]{2,1,0:T(8,128)(2,1)}), bf16[32,16,256]{2,1,0:T(8,128)(2,1)S(1)}, u32[]{:S(2)}, u32[]{:S(2)}) %all-to-all-start.1) | async-done | bytes 262176 | tf_op jit(solution)/shard_map/all_to_all | solution.py:23
  42.5 2.4 scatter_custom_fusion
  44.9 0.2 fusion
  45.1 9.5 %all_gather.18 = bf16[1024,256]{0,1:T(8,128)(2,1)S(1)} all-gather(bf16[128,256]{0,1:T(8,128)(2,1)S(1)} %fusion), channel_id=1, replica_groups=mesh['row'=8,'col'=4] {'row'}, dimensions={0}, use_global_device_ids=true | all-gather | bytes 589824 | tf_op jit(solution)/shard_map/all_gather | solution.py:66
  54.7 0.2 mul.41
  54.9 1.2 convolution_convert_fusion.5
  56.2 18.3 %reduce-scatter.13.cloned.1.call-done = bf16[128,256]{1,0:T(8,128)(2,1)} async-done(((bf16[512,256]{1,0:T(8,128)(2,1)}), bf16[128,256]{1,0:T(8,128)(2,1)}) %reduce-scatter.13.cloned.1.call-update) | async-done | bytes 65552 | tf_op jit(solution)/shard_map/reduce_scatter | solution.py:69
  74.5 1.0 fusion.1
  75.5 10.0 %all_gather.19 = bf16[1024,256]{0,1:T(8,128)(2,1)S(1)} all-gather(bf16[128,256]{0,1:T(8,128)(2,1)S(1)} %fusion.1), channel_id=1, replica_groups=mesh['row'=8,'col'=4] {'row'}, dimensions={0}, use_global_device_ids=true | all-gather | bytes 589824 | tf_op jit(solution)/shard_map/all_gather | solution.py:66
  85.5 0.2 mul.44
  85.7 2.4 convolution_convert_fusion.4
  88.2 17.1 %reduce-scatter.15.cloned.1.call-done = bf16[128,256]{1,0:T(8,128)(2,1)} async-done(((bf16[512,256]{1,0:T(8,128)(2,1)}), bf16[128,256]{1,0:T(8,128)(2,1)}) %reduce-scatter.15.cloned.1.call-update) | async-done | bytes 65552 | tf_op jit(solution)/shard_map/reduce_scatter | solution.py:69
  105.3 1.0 fusion.2
  106.3 10.0 %all_gather.20 = bf16[1024,256]{0,1:T(8,128)(2,1)S(1)} all-gather(bf16[128,256]{0,1:T(8,128)(2,1)S(1)} %fusion.2), channel_id=1, replica_groups=mesh['row'=8,'col'=4] {'row'}, dimensions={0}, use_global_device_ids=true | all-gather | bytes 589824 | tf_op jit(solution)/shard_map/all_gather | solution.py:66
  116.3 0.2 mul.47
  116.5 1.0 copy-done.1
  117.5 2.4 convolution_convert_fusion.3
  119.9 17.1 %reduce-scatter.17.cloned.1.call-done = bf16[128,256]{1,0:T(8,128)(2,1)} async-done(((bf16[512,256]{1,0:T(8,128)(2,1)}), bf16[128,256]{1,0:T(8,128)(2,1)}) %reduce-scatter.17.cloned.1.call-update) | async-done | bytes 65552 | tf_op jit(solution)/shard_map/reduce_scatter | solution.py:69
  137.0 1.2 convolution_convert_fusion.9
  138.2 12.8 %all_gather.21 = bf16[512,256]{0,1:T(8,128)(2,1)S(1)} all-gather(bf16[128,256]{0,1:T(8,128)(2,1)S(1)} %bitcast.111), channel_id=1, replica_groups=mesh['row'=8,'col'=4] {'col'}, dimensions={0}, use_global_device_ids=true | all-gather | bytes 327680 | tf_op jit(solution)/shard_map/all_gather | solution.py:83
  151.0 2.9 convolution_convert_fusion.2
  154.0 32.7 %reduce-scatter.19.cloned.1.call-done = bf16[128,256]{1,0:T(8,128)(2,1)} async-done(((bf16[1024,256]{1,0:T(8,128)(2,1)}), bf16[128,256]{1,0:T(8,128)(2,1)}) %reduce-scatter.19.cloned.1.call-update) | async-done | bytes 65552
  186.7 0.9 copy.14
  187.6 0.2 convolution_convert_fusion.8
  187.8 12.8 %all_gather.22 = bf16[512,256]{0,1:T(8,128)(2,1)S(1)} all-gather(bf16[128,256]{0,1:T(8,128)(2,1)S(1)} %bitcast.113), channel_id=1, replica_groups=mesh['row'=8,'col'=4] {'col'}, dimensions={0}, use_global_device_ids=true | all-gather | bytes 327680 | tf_op jit(solution)/shard_map/all_gather | solution.py:83
  200.6 2.6 convolution_convert_fusion.1
  203.3 33.6 %reduce-scatter.21.cloned.1.call-done = bf16[128,256]{1,0:T(8,128)(2,1)} async-done(((bf16[1024,256]{1,0:T(8,128)(2,1)}), bf16[128,256]{1,0:T(8,128)(2,1)}) %reduce-scatter.21.cloned.1.call-update) | async-done | bytes 65552
  236.9 0.9 copy.16
  237.8 0.1 convolution_convert_fusion.7
  238.0 12.8 %all_gather.23 = bf16[512,256]{0,1:T(8,128)(2,1)S(1)} all-gather(bf16[128,256]{0,1:T(8,128)(2,1)S(1)} %bitcast.115), channel_id=1, replica_groups=mesh['row'=8,'col'=4] {'col'}, dimensions={0}, use_global_device_ids=true | all-gather | bytes 327680 | tf_op jit(solution)/shard_map/all_gather | solution.py:83
  250.8 2.6 convolution_convert_fusion
  253.4 33.6 %reduce-scatter.23.cloned.1.call-done = bf16[128,256]{1,0:T(8,128)(2,1)} async-done(((bf16[1024,256]{1,0:T(8,128)(2,1)}), bf16[128,256]{1,0:T(8,128)(2,1)}) %reduce-scatter.23.cloned.1.call-update) | async-done | bytes 65552
  287.1 0.9 copy.18
  288.0 0.2 fusion.3
  288.2 0.8 copy.12
  (27 shorter events, 0.4 us)
Async XLA Ops:
  6.5 16.8 %copy-start = (f32[512,256]{1,0:T(8,128)S(1)}, f32[512,256]{1,0:T(8,128)}, u32[]{:S(2)}) copy-start(f32[512,256]{1,0:T(8,128)} %param.5) | copy-start | bytes 1572868
  15.3 14.5 %all-to-all-start = ((s32[32,1,16]{2,1,0:T(1,128)}), s32[32,1,16]{2,1,0:T(1,128)S(1)}, u32[]{:S(2)}, u32[]{:S(2)}) async-start(s32[32,1,16]{2,1,0:T(1,128)} %bitcast), calls=%async_computation | async-start | bytes 32768 | tf_op jit(solution)/shard_map/all_to_all | solution.py:30
  29.7 12.8 %all-to-all-start.1 = ((bf16[32,16,256]{2,1,0:T(8,128)(2,1)}), bf16[32,16,256]{2,1,0:T(8,128)(2,1)S(1)}, u32[]{:S(2)}, u32[]{:S(2)}) async-start(bf16[32,16,256]{2,1,0:T(8,128)(2,1)} %bitcast.2), calls=%async_computation.1 | async-start | bytes 524288 | tf_op jit(solution)/shard_map/all_to_all | solution.py:23
  32.3 12.6 %copy-start.3 = (bf16[4,1,128,128]{3,2,1,0:T(8,128)(2,1)S(1)}, bf16[4,1,128,128]{3,2,1,0:T(8,128)(2,1)}, u32[]{:S(2)}) copy-start(bf16[4,1,128,128]{3,2,1,0:T(8,128)(2,1)} %param.7) | copy-start | bytes 393220
  32.3 42.1 %reduce-scatter.13.cloned.1.call-start = ((), (), s32[]{:S(2)}) async-start(), calls=%async_computation.8 | async-start | bytes 327680 | tf_op jit(solution)/shard_map/reduce_scatter | solution.py:69
  35.8 20.3 %copy-start.2 = (bf16[1,1,4,128,1,8,128]{6,5,4,3,2,1,0:T(8,128)(2,1)}, bf16[1,1,4,128,1,8,128]{6,5,4,3,2,1,0:T(8,128)(2,1)S(1)}, u32[]{:S(2)}) copy-start(bf16[1,1,4,128,1,8,128]{6,5,4,3,2,1,0:T(8,128)(2,1)S(1)} %get-tuple-element.8) | copy-start | bytes 3145732
  56.1 49.1 %reduce-scatter.15.cloned.1.call-start = ((), (), s32[]{:S(2)}) async-start(), calls=%async_computation.9 | async-start | bytes 327680 | tf_op jit(solution)/shard_map/reduce_scatter | solution.py:69
  88.1 48.9 %reduce-scatter.17.cloned.1.call-start = ((), (), s32[]{:S(2)}) async-start(), calls=%async_computation.10 | async-start | bytes 327680 | tf_op jit(solution)/shard_map/reduce_scatter | solution.py:69
  116.5 1.0 copy-start.1
  119.9 66.8 %reduce-scatter.19.cloned.1.call-start = ((), (), s32[]{:S(2)}) async-start(), calls=%async_computation.11 | async-start | bytes 589824
  153.9 82.9 %reduce-scatter.21.cloned.1.call-start = ((), (), s32[]{:S(2)}) async-start(), calls=%async_computation.12 | async-start | bytes 589824
  203.2 83.8 %reduce-scatter.23.cloned.1.call-start = ((), (), s32[]{:S(2)}) async-start(), calls=%async_computation.13 | async-start | bytes 589824
Sparse Core Ops, SparseCore 0:
  56.2 18.1 reduce-scatter.12
  88.2 16.9 reduce-scatter.14
  120.0 16.9 reduce-scatter.16
  154.0 32.5 reduce-scatter.18
  203.4 33.4 reduce-scatter.20
  253.6 33.4 reduce-scatter.22
where the time goes:
time: 297 us; the launch traced here: 296 us
  waiting for transfers between devices  162 us (55%)
  blocking collectives  67.9 us (23%)
  matrix products  18 us (6%)
  local copies, waits for them, and re-layouts  15.7 us (5%)
  between operations  13.7 us (5%)
  starting transfers between devices  10.1 us (3%)
  other arithmetic  8.27 us (3%)
    unnamed x9, waiting for transfers between devices  100 us
    reduce_scatter x3, waiting for transfers between devices, per_device(): lax.psum_scatter(partial_sum.astype(jnp.bfloat16), 'col', scatter_dimensi...  52.5 us
    all_gather x3, blocking collectives, per_device(): lax.all_gather(solution[level_idx + 1], 'col', axis=0, tiled=True)  38.4 us
    all_gather x3, blocking collectives, per_device(): lax.all_gather(solved[level_idx - 1], 'row', axis=0, tiled=True)  29.5 us
    dot_general x3, matrix products, column_term(): lax.dot_general(level_tile, upper_blocks, (((0,), (0,)), ((), ())), prefe...  8.14 us
    all_to_all x1, starting transfers between devices, per_device(): lax.all_to_all(places.reshape(supernodes, group_rows), ('row', 'col'), sp...  7.3 us
    dot_general x3, matrix products, add_piece(): return jnp.dot(level_tile, shard_piece, preferred_element_type=jnp.float32)  6.04 us
  transfers between devices with their start and end apart: 8, of which 8 were waited for; matrix products, arithmetic and copies ran while one was open for 3% of the time, Pallas kernels for 0%

commit v1 on v0

v1 whole, which is shorter than its diff:
```python
import functools

import jax
import jax.numpy as jnp
from jax import lax
from jax.experimental import pallas as pl
from jax.experimental.pallas import tpu as pltpu
from jax.sharding import PartitionSpec as P

B = 128
NLEV = 4
LANES = 128
F32 = jnp.float32
BF16 = jnp.bfloat16


def swap(value, axis, distance):
    count = lax.axis_size(axis)
    return lax.ppermute(value, axis, [(i, i ^ distance) for i in range(count)])


def call(body, out_shape, args, scratch=(), flops=0):
    moved = sum(a.size * a.dtype.itemsize for a in args)
    in_specs = [
        pl.BlockSpec(memory_space=pltpu.SMEM if i == 0 else pltpu.VMEM) for i in range(len(args))
    ]
    several = isinstance(out_shape, (list, tuple))
    out_specs = (
        [pl.BlockSpec(memory_space=pltpu.VMEM) for _ in out_shape]
        if several
        else pl.BlockSpec(memory_space=pltpu.VMEM)
    )
    return pl.pallas_call(
        body,
        out_shape=out_shape,
        in_specs=in_specs,
        out_specs=out_specs,
        scratch_shapes=list(scratch),
        compiler_params=pltpu.CompilerParams(vmem_limit_bytes=40 * 1024 * 1024),
        cost_estimate=pl.CostEstimate(flops=flops, bytes_accessed=moved, transcendentals=0),
    )(*args)


def aligned(start, size, step):
    return pl.ds(pl.multiple_of(start * step, step), size)


def pack_body(supernodes, chunk_rows, total_rows, idx_ref, rhs_ref, dest_ref, out_ref):
    local_rows = rhs_ref.shape[0]
    pairs = supernodes // 2
    shards_per_line = LANES // chunk_rows
    me = idx_ref[2]
    dest = dest_ref[...]
    supernode = (dest // B) % supernodes
    level = dest // (supernodes * B)
    within = dest % B
    pair = supernode // 2
    place_high = (level * 2 + supernode % 2).astype(F32)
    place_low = within.astype(F32)
    pair_iota = lax.broadcasted_iota(jnp.int32, (pairs, local_rows), 0)
    member = pair_iota == pair
    member_f = jnp.where(member, 1.0, 0.0)
    before = (
        lax.broadcasted_iota(jnp.int32, (local_rows, local_rows), 0)
        < lax.broadcasted_iota(jnp.int32, (local_rows, local_rows), 1)
    )
    counts = jnp.dot(
        member_f.astype(BF16), jnp.where(before, 1.0, 0.0).astype(BF16), preferred_element_type=F32
    )
    rank = jnp.sum(member_f * counts, axis=0, keepdims=True).astype(jnp.int32)
    slot = pair * chunk_rows + rank
    chosen = lax.broadcasted_iota(jnp.int32, (local_rows, local_rows), 0) == slot
    sorted_rows = jnp.dot(
        jnp.where(chosen, 1.0, 0.0).astype(BF16),
        rhs_ref[...].astype(BF16),
        preferred_element_type=F32,
    )
    tail = total_rows - chunk_rows
    tail_iota = lax.broadcasted_iota(jnp.int32, (pairs * tail, local_rows), 0)
    tail_pair = tail_iota // tail
    tail_row = tail_iota % tail
    tail_value = jnp.where(tail_row == 0, place_high, jnp.where(tail_row == 1, place_low, 0.0))
    tail_value = jnp.where(tail_pair == pair, tail_value, 0.0).astype(BF16)
    lane = rank + (me % shards_per_line) * chunk_rows
    lane_hot = lax.broadcasted_iota(jnp.int32, (LANES, local_rows), 0) == lane
    tails = lax.dot_general(
        tail_value,
        jnp.where(lane_hot, 1.0, 0.0).astype(BF16),
        (((1,), (1,)), ((), ())),
        preferred_element_type=F32,
    )
    half = rhs_ref.shape[1] // 2
    for g in range(pairs):
        rows = sorted_rows[g * chunk_rows : (g + 1) * chunk_rows]
        ending = tails[g * tail : (g + 1) * tail]
        for h in range(2):
            chunk = jnp.concatenate([rows[:, h * half : (h + 1) * half], ending], axis=0)
            out_ref[2 * g + h] = chunk.astype(BF16)


def place_rows(arrived_ref, first_place, place_count, chunk_rows):
    shards = arrived_ref.shape[0]
    shards_per_line = LANES // chunk_rows
    hots = []
    place = lax.broadcasted_iota(jnp.int32, (place_count, LANES), 0) + first_place
    for first in range(0, shards, shards_per_line):
        ending = jnp.zeros((8, LANES), F32)
        for s in range(first, first + shards_per_line):
            ending = ending + arrived_ref[s, chunk_rows:, :].astype(F32)[:8]
        where_to = (ending[0:1] * B + ending[1:2]).astype(jnp.int32)
        hots.append(jnp.where(place == where_to, 1.0, 0.0).astype(BF16))
    hot = jnp.concatenate(hots, axis=1)
    rows = jnp.concatenate(
        [arrived_ref[s].astype(F32)[:chunk_rows] for s in range(shards)], axis=0
    ).astype(BF16)
    return jnp.dot(hot, rows, preferred_element_type=F32)


def first_body(chunk_rows, idx_ref, arrived_ref, own_ref, par_ref, out_ref, residual):
    residual[...] = place_rows(arrived_ref, 0, 2 * B, chunk_rows).astype(BF16)
    apply_diag(idx_ref[1] % 2, residual, own_ref, par_ref, out_ref)


def apply_diag(parity, residual, own_ref, par_ref, out_ref):
    mine, other = aligned(parity, B, B), aligned(1 - parity, B, B)
    out_ref[mine, :] = jnp.dot(
        own_ref[...], residual[mine, :], preferred_element_type=F32
    ).astype(BF16)
    out_ref[other, :] = jnp.dot(
        par_ref[...], residual[other, :], preferred_element_type=F32
    ).astype(BF16)


def rest_body(chunk_rows, idx_ref, arrived_ref, out_ref):
    out_ref[...] = place_rows(arrived_ref, 2 * B, out_ref.shape[0], chunk_rows).astype(BF16)


def down_body(idx_ref, own_ref, par_ref, *refs, rows, pairs):
    pieces, outs, gathered = refs[:rows], refs[rows : rows + pairs], refs[rows + pairs]
    row, col = idx_ref[0], idx_ref[1]
    parity, pair = col % 2, col // 2
    for kk, piece in enumerate(pieces):
        at = aligned(row ^ kk, B, B)
        gathered[parity, at, :] = piece[0:B]
        gathered[1 - parity, at, :] = piece[B : 2 * B]
    for m in list(range(1, pairs)) + [0]:
        at = aligned(pair ^ m, 2 * B, 2 * B)
        total = jnp.dot(own_ref[at, :], gathered[0], preferred_element_type=F32)
        total = total + jnp.dot(par_ref[at, :], gathered[1], preferred_element_type=F32)
        outs[m][...] = total.astype(outs[m].dtype)


def residual_body(idx_ref, rhs_ref, own_ref, par_ref, kept_ref, *refs, last):
    if last:
        arrived, outs, residual, solved = refs[:-3], refs[-3], refs[-2], refs[-1]
    else:
        arrived, solved, residual = refs[:-2], refs[-2], refs[-1]
    coupled = kept_ref[...]
    for ref in arrived:
        coupled = coupled + ref[...].astype(F32)
    residual[...] = (rhs_ref[...].astype(F32) - coupled).astype(BF16)
    parity = idx_ref[1] % 2
    apply_diag(parity, residual, own_ref, par_ref, solved)
    if last:
        for at, factor in ((parity, own_ref), (1 - parity, par_ref)):
            product = lax.dot_general(
                solved[aligned(at, B, B), :],
                factor[...],
                (((0,), (0,)), ((), ())),
                preferred_element_type=F32,
            )
            outs[:, aligned(at, B, B)] = product.astype(BF16)


def up_body(idx_ref, own_ref, par_ref, *refs, rows, pairs):
    pieces, odd_ref, even_ref = refs[:pairs], refs[pairs], refs[pairs + 1]
    gathered, product = refs[pairs + 2], refs[pairs + 3]
    row, col = idx_ref[0], idx_ref[1]
    parity, pair = col % 2, col // 2
    for m, piece in enumerate(pieces):
        gathered[:, aligned(pair ^ m, 2 * B, 2 * B)] = piece[...]
    product[parity] = jnp.dot(gathered[...], own_ref[...], preferred_element_type=F32)
    product[1 - parity] = jnp.dot(gathered[...], par_ref[...], preferred_element_type=F32)
    for kk in range(rows):
        out = odd_ref if kk % 2 else even_ref
        at = aligned(row ^ kk, B, B)
        for cc in range(2):
            out[kk // 2, :, cc * B : (cc + 1) * B] = product[cc, :, at].astype(out.dtype)


def add_body(idx_ref, even_ref, sibling_ref, *outs):
    for k, out in enumerate(outs):
        out[...] = (even_ref[k] + sibling_ref[k].astype(F32)).astype(out.dtype)


def final_body(idx_ref, solved_ref, own_ref, par_ref, kept_ref, *refs):
    arrived, outs, residual = refs[:-2], refs[-2], refs[-1]
    back = kept_ref[...]
    for ref in arrived:
        back = back + ref[...].astype(F32)
    residual[...] = (solved_ref[...].astype(F32) - back).astype(BF16)
    parity = idx_ref[1] % 2
    for at, factor in ((parity, own_ref), (1 - parity, par_ref)):
        lanes = aligned(at, B, B)
        outs[:, lanes] = jnp.dot(
            residual[:, lanes], factor[...], preferred_element_type=F32
        ).astype(BF16)


def per_device(rhs_rows, dest_row, diag_inverse, lower_blocks, block_mask):
    rows = lax.axis_size("row")
    cols = lax.axis_size("col")
    pairs = cols // 2
    supernodes = rows * cols
    local_rows = rhs_rows.shape[0]
    half = rhs_rows.shape[1] // 2
    chunk_rows = 2 * (local_rows // supernodes)
    total_rows = (chunk_rows + 2 + 15) // 16 * 16
    row, col = lax.axis_index("row"), lax.axis_index("col")
    parity = col % 2
    idx = jnp.stack([row, col, row * cols + col]).astype(jnp.int32)

    def shape(dims, dtype=BF16):
        return jax.ShapeDtypeStruct(dims, dtype)

    diag_own = diag_inverse[:, 0]
    diag_par = swap(diag_own, "col", 1)
    own, par = [], []
    for level in range(NLEV - 1):
        tile = lower_blocks[level, 0, :, :, 0]
        mask = block_mask[level, 0, :, 0, :].astype(BF16)
        masked = (tile * mask[:, None, :, None]).reshape(cols * B, rows * B)
        own.append(masked)
        par.append(swap(masked, "col", 1))

    sending = call(
        functools.partial(pack_body, supernodes, chunk_rows, total_rows),
        shape((supernodes, total_rows, half)),
        (idx, rhs_rows, dest_row.reshape(1, local_rows)),
        flops=2 * local_rows * local_rows * 2 * half,
    )
    arrived = lax.all_to_all(sending, ("row", "col"), split_axis=0, concat_axis=0, tiled=True)
    block = (2 * B, half)
    block_t = (half, 2 * B)
    solved = [
        call(
            functools.partial(first_body, chunk_rows),
            shape(block),
            (idx, arrived, diag_own[0], diag_par[0]),
            [pltpu.VMEM(block, BF16)],
        )
    ]
    rest = call(
        functools.partial(rest_body, chunk_rows),
        shape(((NLEV - 1) * 2 * B, half)),
        (idx, arrived),
    )
    upper = None
    for level in range(1, NLEV):
        pieces = [None] * rows
        pieces[0] = solved[-1]
        for kk in range(2, rows, 2):
            pieces[kk] = swap(solved[-1], "row", kk)
        for kk in range(0, rows, 2):
            pieces[kk + 1] = swap(pieces[kk], "row", 1)
        partial_sums = call(
            functools.partial(down_body, rows=rows, pairs=pairs),
            [shape(block, F32 if m == 0 else BF16) for m in range(pairs)],
            (idx, own[level - 1], par[level - 1], *pieces),
            [pltpu.VMEM((2, rows * B, half), BF16)],
            flops=4 * rows * cols * B * B * half,
        )
        passed = [swap(partial_sums[m], "col", 2 * m) for m in range(1, pairs)]
        last = level == NLEV - 1
        result = call(
            functools.partial(residual_body, last=last),
            shape(block_t if last else block),
            (
                idx,
                rest[(level - 1) * 2 * B : level * 2 * B],
                diag_own[level],
                diag_par[level],
                partial_sums[0],
                *passed,
            ),
            [pltpu.VMEM(block, BF16)] * (2 if last else 1),
        )
        if last:
            upper = result
        else:
            solved.append(result)

    solution = [None] * NLEV
    solution[NLEV - 1] = upper
    for level in range(NLEV - 2, -1, -1):
        pieces = [upper] + [swap(upper, "col", 2 * m) for m in range(1, pairs)]
        odd, even = call(
            functools.partial(up_body, rows=rows, pairs=pairs),
            [shape((rows // 2, *block_t)), shape((rows // 2, *block_t), F32)],
            (idx, own[level], par[level], *pieces),
            [pltpu.VMEM((half, cols * B), BF16), pltpu.VMEM((2, half, rows * B), F32)],
            flops=4 * rows * cols * B * B * half,
        )
        sibling = swap(odd, "row", 1)
        sums = call(
            add_body,
            [shape(block_t, F32 if k == 0 else BF16) for k in range(rows // 2)],
            (idx, even, sibling),
        )
        passed = [swap(sums[k], "row", 2 * k) for k in range(1, rows // 2)]
        upper = call(
            final_body,
            shape(block_t),
            (idx, solved[level].T, diag_own[level], diag_par[level], sums[0], *passed),
            [pltpu.VMEM(block_t, BF16)],
        )
        solution[level] = upper

    results = []
    for level in range(NLEV):
        both = solution[level]
        mine = lax.dynamic_slice_in_dim(both, parity * B, B, axis=1).T
        theirs = lax.dynamic_slice_in_dim(both, (1 - parity) * B, B, axis=1).T
        got = swap(theirs, "col", 1)
        results.append(
            jnp.where(
                parity == 0,
                jnp.concatenate([mine, got], axis=1),
                jnp.concatenate([got, mine], axis=1),
            )
        )
    return jnp.stack(results)[:, None]


def solution(mesh):
    in_specs = (
        P(("row", "col"), None),
        P(("row", "col")),
        P(None, ("row", "col"), None, None),
        P(None, "row", None, None, "col", None, None),
        P(None, "row", None, "col", None),
    )
    out_specs = P(None, ("row", "col"), None, None)
    return jax.shard_map(
        per_device, mesh=mesh, in_specs=in_specs, out_specs=out_specs, check_vma=False
    )
```

time: 297 us -> 187 us (0.63)
  waiting for transfers between devices: 162 us -> 90.7 us
  blocking collectives: 67.9 us -> 0 us
  starting transfers between devices: 10.1 us -> 63.3 us
  Pallas kernels: 0 us -> 21.7 us
  matrix products: 18 us -> 0 us
  between operations: 13.7 us -> 0.43 us
  local copies, waits for them, and re-layouts: 15.7 us -> 8.56 us
  other arithmetic: 8.27 us -> 1.6 us
    unnamed x9 -> x0, waiting for transfers between devices: 100 us -> none
    ppermute x0 -> x47, waiting for transfers between devices: none -> 90.7 us  [swap(): return lax.ppermute(value, axis, [(i, i ^ distance) for i in range(count)])]
    all_gather x6 -> x0, blocking collectives: 67.9 us -> none  [the longest x3 38.4 us: per_device(): lax.all_gather(solution[level_idx + 1], 'col', axis=0, tiled=True)]
    ppermute x0 -> x47, starting transfers between devices: none -> 56 us  [swap(): return lax.ppermute(value, axis, [(i, i ^ distance) for i in range(count)])]
    reduce_scatter x3 -> x0, waiting for transfers between devices: 52.5 us -> none  [per_device(): lax.psum_scatter(partial_sum.astype(jnp.bfloat16), 'col', scatter_dimensi...]
    pallas_call x0 -> x18, Pallas kernels: none -> 21.7 us  [call(): pl.pallas_call(body, out_shape=out_shape, in_specs=in_specs, out_specs=ou...]
    dot_general x13 -> x0, matrix products: 18 us -> none  [the longest x3 8.14 us: column_term(): lax.dot_general(level_tile, upper_blocks, (((0,), (0,)), ((), ())), prefe...]
    all_to_all x2 -> x1, waiting for transfers between devices: 9.76 us -> 0.01 us  [per_device(): lax.all_to_all(sending, ('row', 'col'), split_axis=0, concat_axis=0, tile...]
  transfers between devices with their start and end apart: 8 -> 48, of which waited for: 8 -> 30; matrix products, arithmetic and copies ran while one was open for 3% -> 3% of each run, Pallas kernels for 0% -> 5%
where the time goes in v1:
time: 187 us; the launch traced here: 186 us
  waiting for transfers between devices  90.7 us (49%)
  starting transfers between devices  63.3 us (34%)
  Pallas kernels  21.7 us (12%)
  local copies, waits for them, and re-layouts  8.56 us (5%)
    ppermute x47, waiting for transfers between devices, swap(): return lax.ppermute(value, axis, [(i, i ^ distance) for i in range(count)])  90.7 us
    ppermute x47, starting transfers between devices, swap(): return lax.ppermute(value, axis, [(i, i ^ distance) for i in range(count)])  56 us
    pallas_call x18, Pallas kernels, call(): pl.pallas_call(body, out_shape=out_shape, in_specs=in_specs, out_specs=ou...  21.7 us
    all_to_all x1, starting transfers between devices, per_device(): lax.all_to_all(sending, ('row', 'col'), split_axis=0, concat_axis=0, tile...  7.3 us
  transfers between devices with their start and end apart: 48, of which 30 were waited for; matrix products, arithmetic and copies ran while one was open for 3% of the time, Pallas kernels for 5%

profile of v1, /device:TPU:0, one launch (start us, length us, event | category | flops | bytes accessed | tf_op | source)
XLA Modules:
  0.0 186.3 jit_solution(16778445066821256183)
XLA Ops:
  1.8 1.9 %shard_map.55 = bf16[32,48,128]{2,1,0:T(8,128)(2,1)} custom-call(s32[3]{0:T(128)S(1)} %pad_add_fusion.idx_ref, f32[512,256]{1,0:T(8,128)S(1)} %copy-done.2, s32[1,512]{1,0:T(1,128)S(1)} %bitcast.88), custom_call_target="tpu_custom_call" | custom-call | flops 134217728 | bytes 526348 | tf_op jit(solution)/shard_map/pallas_call | solution.py:33
  3.7 7.3 %all-to-all-start = ((bf16[32,48,128]{2,1,0:T(8,128)(2,1)}), bf16[32,48,128]{2,1,0:T(8,128)(2,1)S(1)}, u32[]{:S(2)}, u32[]{:S(2)}) async-start(bf16[32,48,128]{2,1,0:T(8,128)(2,1)} %shard_map.55), calls=%async_computation | async-start | bytes 786432 | tf_op jit(solution)/shard_map/all_to_all | solution.py:242
  11.0 1.8 collective-permute-start
  13.5 2.1 %fusion = (bf16[1,1,4,128,1,8,128]{6,5,4,3,2,1,0:T(8,128)(2,1)S(1)}, bf16[1,1,4,128,1,8,128]{6,5,4,3,2,1,0:T(8,128)(2,1)S(1)}, bf16[1,1,4,128,1,8,128]{6,5,4,3,2,1,0:T(8,128)(2,1)S(1)}) fusion(bf16[3,1,4,128,1,8,128]{6,5,4,3,2,1,0:T(8,128)(2,1)} %param.8), kind=kLoop, calls=%fused_computation.28 | loop fusion | bytes 6291456 | tf_op jit(solution)/shard_map/slice | solution.py:230
  16.9 1.8 collective-permute-start.10
  20.1 3.3 %collective-permute-done = bf16[4,128,128]{2,1,0:T(8,128)(2,1)S(1)} collective-permute-done((bf16[4,128,128]{2,1,0:T(8,128)(2,1)}, bf16[4,128,128]{2,1,0:T(8,128)(2,1)S(1)}, u32[]{:S(2)}, u32[]{:S(2)}) %collective-permute-start) | collective-permute-done | bytes 131104 | tf_op jit(solution)/shard_map/ppermute | solution.py:19
  26.7 1.5 collective-permute-start.3
  29.7 1.5 collective-permute-done.3.refs_2_
  31.2 2.4 %collective-permute-start.7 = (bf16[256,128]{1,0:T(8,128)(2,1)S(1)}, bf16[256,128]{1,0:T(8,128)(2,1)S(1)}, u32[]{:S(2)}, u32[]{:S(2)}) collective-permute-start(bf16[256,128]{1,0:T(8,128)(2,1)S(1)} %shard_map.56.refs_0_), channel_id=1, source_target_pairs={{0,24},{4,28},{8,16},{12,20},{16,8},{20,12},{24,0},{28,4},{1,25},{... | collective-permute-start | bytes 196616 | tf_op jit(solution)/shard_map/ppermute | solution.py:19
  33.6 2.8 %collective-permute-done.7.refs_6_ = bf16[256,128]{1,0:T(8,128)(2,1)S(1)} collective-permute-done((bf16[256,128]{1,0:T(8,128)(2,1)S(1)}, bf16[256,128]{1,0:T(8,128)(2,1)S(1)}, u32[]{:S(2)}, u32[]{:S(2)}) %collective-permute-start.7) | collective-permute-done | bytes 65568 | tf_op jit(solution)/shard_map/ppermute | solution.py:19
  38.1 7.9 %collective-permute-done.1.par_ref = bf16[512,1024]{1,0:T(8,128)(2,1)} collective-permute-done((bf16[512,1024]{1,0:T(8,128)(2,1)S(1)}, bf16[512,1024]{1,0:T(8,128)(2,1)}, u32[]{:S(2)}, u32[]{:S(2)}) %collective-permute-start.1) | collective-permute-done | bytes 1048608 | tf_op jit(solution)/shard_map/ppermute | solution.py:19
  46.0 2.0 %shard_map.58 = (f32[256,128]{1,0:T(8,128)S(1)}, bf16[256,128]{1,0:T(8,128)(2,1)S(1)}) custom-call(s32[3]{0:T(128)S(1)} %pad_add_fusion.idx_ref, bf16[512,1024]{1,0:T(8,128)(2,1)S(1)} %bitcast_multiply_fusion.2.own_ref, bf16[512,1024]{1,0:T(8,128)(2,1)} %collective-permute-done.1.par_ref, bf16[256,128]{1,0:T(8,128)(2,1)S(1)} %shard_map.56.refs_0_, ...), custom_call_target="tpu_custom_call" | custom-call | flops 268435456 | bytes 2621452 | tf_op jit(solution)/shard_map/pallas_call | solution.py:33
  48.0 2.5 %collective-permute-start.9 = (bf16[256,128]{1,0:T(8,128)(2,1)S(1)}, bf16[256,128]{1,0:T(8,128)(2,1)S(1)}, u32[]{:S(2)}, u32[]{:S(2)}) collective-permute-start(bf16[256,128]{1,0:T(8,128)(2,1)S(1)} %get-tuple-element.30), channel_id=1, source_target_pairs={{0,2},{1,3},{2,0},{3,1},{4,6},{5,7},{6,4},{7,5},{8,10},{9,11},{10,... | collective-permute-start | bytes 196616 | tf_op jit(solution)/shard_map/ppermute | solution.py:19
  50.5 39.1 %collective-permute-done.9.refs_0_ = bf16[256,128]{1,0:T(8,128)(2,1)S(1)} collective-permute-done((bf16[256,128]{1,0:T(8,128)(2,1)S(1)}, bf16[256,128]{1,0:T(8,128)(2,1)S(1)}, u32[]{:S(2)}, u32[]{:S(2)}) %collective-permute-start.9) | collective-permute-done | bytes 65568 | tf_op jit(solution)/shard_map/ppermute | solution.py:19
  90.4 1.7 collective-permute-start.12
  92.1 1.5 collective-permute-start.14
  94.7 2.4 %collective-permute-done.14.refs_4_ = bf16[256,128]{1,0:T(8,128)(2,1)S(1)} collective-permute-done((bf16[256,128]{1,0:T(8,128)(2,1)S(1)}, bf16[256,128]{1,0:T(8,128)(2,1)S(1)}, u32[]{:S(2)}, u32[]{:S(2)}) %collective-permute-start.14) | collective-permute-done | bytes 65568 | tf_op jit(solution)/shard_map/ppermute | solution.py:19
  97.1 1.7 collective-permute-done.16.refs_6_
  100.0 2.0 %shard_map.60 = (f32[256,128]{1,0:T(8,128)S(1)}, bf16[256,128]{1,0:T(8,128)(2,1)S(1)}) custom-call(s32[3]{0:T(128)S(1)} %pad_add_fusion.idx_ref, bf16[512,1024]{1,0:T(8,128)(2,1)S(1)} %bitcast_multiply_fusion.1.own_ref, bf16[512,1024]{1,0:T(8,128)(2,1)} %collective-permute-done.10.par_ref, bf16[256,128]{1,0:T(8,128)(2,1)S(1)} %shard_map.59.refs_0_, ...), custom_call_target="tpu_custom_call" | custom-call | flops 268435456 | bytes 2621452 | tf_op jit(solution)/shard_map/pallas_call | solution.py:33
  102.0 3.4 %collective-permute-start.18 = (bf16[256,128]{1,0:T(8,128)(2,1)S(1)}, bf16[256,128]{1,0:T(8,128)(2,1)S(1)}, u32[]{:S(2)}, u32[]{:S(2)}) collective-permute-start(bf16[256,128]{1,0:T(8,128)(2,1)S(1)} %get-tuple-element.32), channel_id=1, source_target_pairs={{0,2},{1,3},{2,0},{3,1},{4,6},{5,7},{6,4},{7,5},{8,10},{9,11},{10,... | collective-permute-start | bytes 196616 | tf_op jit(solution)/shard_map/ppermute | solution.py:19
  105.4 2.4 %collective-permute-done.18.refs_0_ = bf16[256,128]{1,0:T(8,128)(2,1)S(1)} collective-permute-done((bf16[256,128]{1,0:T(8,128)(2,1)S(1)}, bf16[256,128]{1,0:T(8,128)(2,1)S(1)}, u32[]{:S(2)}, u32[]{:S(2)}) %collective-permute-start.18) | collective-permute-done | bytes 65568 | tf_op jit(solution)/shard_map/ppermute | solution.py:19
  109.6 2.6 %collective-permute-start.25 = (bf16[256,128]{1,0:T(8,128)(2,1)S(1)}, bf16[256,128]{1,0:T(8,128)(2,1)S(1)}, u32[]{:S(2)}, u32[]{:S(2)}) collective-permute-start(bf16[256,128]{1,0:T(8,128)(2,1)S(1)} %shard_map.61.refs_0_), channel_id=1, source_target_pairs={{0,24},{4,28},{8,16},{12,20},{16,8},{20,12},{24,0},{28,4},{1,25},{... | collective-permute-start | bytes 196616 | tf_op jit(solution)/shard_map/ppermute | solution.py:19
  116.0 2.0 %shard_map.62 = (f32[256,128]{1,0:T(8,128)S(1)}, bf16[256,128]{1,0:T(8,128)(2,1)S(1)}) custom-call(s32[3]{0:T(128)S(1)} %pad_add_fusion.idx_ref, bf16[512,1024]{1,0:T(8,128)(2,1)S(1)} %bitcast_multiply_fusion.own_ref, bf16[512,1024]{1,0:T(8,128)(2,1)} %collective-permute-done.19.par_ref, bf16[256,128]{1,0:T(8,128)(2,1)S(1)} %shard_map.61.refs_0_, ...), custom_call_target="tpu_custom_call" | custom-call | flops 268435456 | bytes 2621452 | tf_op jit(solution)/shard_map/pallas_call | solution.py:33
  118.0 2.8 %collective-permute-start.27 = (bf16[256,128]{1,0:T(8,128)(2,1)S(1)}, bf16[256,128]{1,0:T(8,128)(2,1)S(1)}, u32[]{:S(2)}, u32[]{:S(2)}) collective-permute-start(bf16[256,128]{1,0:T(8,128)(2,1)S(1)} %get-tuple-element.34), channel_id=1, source_target_pairs={{0,2},{1,3},{2,0},{3,1},{4,6},{5,7},{6,4},{7,5},{8,10},{9,11},{10,... | collective-permute-start | bytes 196616 | tf_op jit(solution)/shard_map/ppermute | solution.py:19
  120.8 2.4 %collective-permute-done.27.refs_0_ = bf16[256,128]{1,0:T(8,128)(2,1)S(1)} collective-permute-done((bf16[256,128]{1,0:T(8,128)(2,1)S(1)}, bf16[256,128]{1,0:T(8,128)(2,1)S(1)}, u32[]{:S(2)}, u32[]{:S(2)}) %collective-permute-start.27) | collective-permute-done | bytes 65568 | tf_op jit(solution)/shard_map/ppermute | solution.py:19
  124.1 2.8 %collective-permute-start.28 = (bf16[128,256]{1,0:T(8,128)(2,1)S(1)}, bf16[128,256]{1,0:T(8,128)(2,1)S(1)}, u32[]{:S(2)}, u32[]{:S(2)}) collective-permute-start(bf16[128,256]{1,0:T(8,128)(2,1)S(1)} %shard_map.63.refs_0_), channel_id=1, source_target_pairs={{0,2},{1,3},{2,0},{3,1},{4,6},{5,7},{6,4},{7,5},{8,10},{9,11},{10,... | collective-permute-start | bytes 196616 | tf_op jit(solution)/shard_map/ppermute | solution.py:19
  127.0 2.4 %collective-permute-done.28.refs_1_ = bf16[128,256]{1,0:T(8,128)(2,1)S(1)} collective-permute-done((bf16[128,256]{1,0:T(8,128)(2,1)S(1)}, bf16[128,256]{1,0:T(8,128)(2,1)S(1)}, u32[]{:S(2)}, u32[]{:S(2)}) %collective-permute-start.28) | collective-permute-done | bytes 65568 | tf_op jit(solution)/shard_map/ppermute | solution.py:19
  129.4 1.8 shard_map.64
  131.3 1.5 collective-permute-done.29.sibling_ref
  133.4 1.7 collective-permute-start.30
  137.7 1.7 collective-permute-done.31.refs_1_
  139.4 2.4 %collective-permute-done.32.refs_2_ = bf16[128,256]{1,0:T(8,128)(2,1)S(1)} collective-permute-done((bf16[128,256]{1,0:T(8,128)(2,1)S(1)}, bf16[128,256]{1,0:T(8,128)(2,1)S(1)}, u32[]{:S(2)}, u32[]{:S(2)}) %collective-permute-start.32) | collective-permute-done | bytes 65568 | tf_op jit(solution)/shard_map/ppermute | solution.py:19
  142.5 2.9 %collective-permute-start.33 = (bf16[128,256]{1,0:T(8,128)(2,1)S(1)}, bf16[128,256]{1,0:T(8,128)(2,1)S(1)}, u32[]{:S(2)}, u32[]{:S(2)}) collective-permute-start(bf16[128,256]{1,0:T(8,128)(2,1)S(1)} %shard_map.66.refs_0_), channel_id=1, source_target_pairs={{0,2},{1,3},{2,0},{3,1},{4,6},{5,7},{6,4},{7,5},{8,10},{9,11},{10,... | collective-permute-start | bytes 196616 | tf_op jit(solution)/shard_map/ppermute | solution.py:19
  145.4 2.3 %collective-permute-done.33.refs_1_ = bf16[128,256]{1,0:T(8,128)(2,1)S(1)} collective-permute-done((bf16[128,256]{1,0:T(8,128)(2,1)S(1)}, bf16[128,256]{1,0:T(8,128)(2,1)S(1)}, u32[]{:S(2)}, u32[]{:S(2)}) %collective-permute-start.33) | collective-permute-done | bytes 65568 | tf_op jit(solution)/shard_map/ppermute | solution.py:19
  147.7 1.8 shard_map.67
  149.7 1.5 collective-permute-done.34.sibling_ref
  152.8 2.5 %collective-permute-start.37 = (bf16[128,256]{1,0:T(8,128)(2,1)S(1)}, bf16[128,256]{1,0:T(8,128)(2,1)S(1)}, u32[]{:S(2)}, u32[]{:S(2)}) collective-permute-start(bf16[128,256]{1,0:T(8,128)(2,1)S(1)} %get-tuple-element.46), channel_id=1, source_target_pairs={{0,24},{4,28},{8,16},{12,20},{16,8},{20,12},{24,0},{28,4},{1,25},{... | collective-permute-start | bytes 196616 | tf_op jit(solution)/shard_map/ppermute | solution.py:19
  158.7 2.9 %collective-permute-start.38 = (bf16[128,256]{1,0:T(8,128)(2,1)S(1)}, bf16[128,256]{1,0:T(8,128)(2,1)S(1)}, u32[]{:S(2)}, u32[]{:S(2)}) collective-permute-start(bf16[128,256]{1,0:T(8,128)(2,1)S(1)} %shard_map.69.refs_0_), channel_id=1, source_target_pairs={{0,2},{1,3},{2,0},{3,1},{4,6},{5,7},{6,4},{7,5},{8,10},{9,11},{10,... | collective-permute-start | bytes 196616 | tf_op jit(solution)/shard_map/ppermute | solution.py:19
  161.7 2.8 %collective-permute-start.46 = (bf16[128,128]{0,1:T(8,128)(2,1)S(1)}, bf16[128,128]{0,1:T(8,128)(2,1)S(1)}, u32[]{:S(2)}, u32[]{:S(2)}) collective-permute-start(bf16[128,128]{0,1:T(8,128)(2,1)S(1)} %get-tuple-element.74), channel_id=1, source_target_pairs={{0,1},{1,0},{2,3},{3,2},{4,5},{5,4},{6,7},{7,6},{8,9},{9,8},{10,11... | collective-permute-start | bytes 98312 | tf_op jit(solution)/shard_map/ppermute | solution.py:19
  164.5 1.8 shard_map.70
  166.4 3.4 %collective-permute-start.45 = (bf16[128,128]{0,1:T(8,128)(2,1)S(1)}, bf16[128,128]{0,1:T(8,128)(2,1)S(1)}, u32[]{:S(2)}, u32[]{:S(2)}) collective-permute-start(bf16[128,128]{0,1:T(8,128)(2,1)S(1)} %get-tuple-element.72), channel_id=1, source_target_pairs={{0,1},{1,0},{2,3},{3,2},{4,5},{5,4},{6,7},{7,6},{8,9},{9,8},{10,11... | collective-permute-start | bytes 98312 | tf_op jit(solution)/shard_map/ppermute | solution.py:19
  169.8 1.9 %collective-permute-done.45 = bf16[128,128]{0,1:T(8,128)(2,1)S(1)} collective-permute-done((bf16[128,128]{0,1:T(8,128)(2,1)S(1)}, bf16[128,128]{0,1:T(8,128)(2,1)S(1)}, u32[]{:S(2)}, u32[]{:S(2)}) %collective-permute-start.45) | collective-permute-done | bytes 32800 | tf_op jit(solution)/shard_map/ppermute | solution.py:19
  172.4 1.6 collective-permute-start.40
  174.0 1.5 collective-permute-start.41
  176.0 1.9 %collective-permute-start.44 = (bf16[128,128]{0,1:T(8,128)(2,1)S(1)}, bf16[128,128]{0,1:T(8,128)(2,1)S(1)}, u32[]{:S(2)}, u32[]{:S(2)}) collective-permute-start(bf16[128,128]{0,1:T(8,128)(2,1)S(1)} %get-tuple-element.70), channel_id=1, source_target_pairs={{0,1},{1,0},{2,3},{3,2},{4,5},{5,4},{6,7},{7,6},{8,9},{9,8},{10,11... | collective-permute-start | bytes 98312 | tf_op jit(solution)/shard_map/ppermute | solution.py:19
  178.2 2.4 %collective-permute-done.42.refs_2_ = bf16[128,256]{1,0:T(8,128)(2,1)S(1)} collective-permute-done((bf16[128,256]{1,0:T(8,128)(2,1)S(1)}, bf16[128,256]{1,0:T(8,128)(2,1)S(1)}, u32[]{:S(2)}, u32[]{:S(2)}) %collective-permute-start.42) | collective-permute-done | bytes 65568 | tf_op jit(solution)/shard_map/ppermute | solution.py:19
  181.4 2.0 %collective-permute-start.43 = (bf16[128,128]{0,1:T(8,128)(2,1)S(1)}, bf16[128,128]{0,1:T(8,128)(2,1)S(1)}, u32[]{:S(2)}, u32[]{:S(2)}) collective-permute-start(bf16[128,128]{0,1:T(8,128)(2,1)S(1)} %get-tuple-element.68), channel_id=1, source_target_pairs={{0,1},{1,0},{2,3},{3,2},{4,5},{5,4},{6,7},{7,6},{8,9},{9,8},{10,11... | collective-permute-start | bytes 98312 | tf_op jit(solution)/shard_map/ppermute | solution.py:19
  183.4 1.9 %collective-permute-done.43 = bf16[128,128]{0,1:T(8,128)(2,1)S(1)} collective-permute-done((bf16[128,128]{0,1:T(8,128)(2,1)S(1)}, bf16[128,128]{0,1:T(8,128)(2,1)S(1)}, u32[]{:S(2)}, u32[]{:S(2)}) %collective-permute-start.43) | collective-permute-done | bytes 32800 | tf_op jit(solution)/shard_map/ppermute | solution.py:19
  (128 shorter events, 33.4 us)
Async XLA Ops:
  3.7 20.5 %all-to-all-start = ((bf16[32,48,128]{2,1,0:T(8,128)(2,1)}), bf16[32,48,128]{2,1,0:T(8,128)(2,1)S(1)}, u32[]{:S(2)}, u32[]{:S(2)}) async-start(bf16[32,48,128]{2,1,0:T(8,128)(2,1)} %shard_map.55), calls=%async_computation | async-start | bytes 786432 | tf_op jit(solution)/shard_map/all_to_all | solution.py:242
  11.0 12.5 %collective-permute-start = (bf16[4,128,128]{2,1,0:T(8,128)(2,1)}, bf16[4,128,128]{2,1,0:T(8,128)(2,1)S(1)}, u32[]{:S(2)}, u32[]{:S(2)}) collective-permute-start(bf16[4,128,128]{2,1,0:T(8,128)(2,1)} %bitcast.95), channel_id=1, source_target_pairs={{0,1},{1,0},{2,3},{3,2},{4,5},{5,4},{6,7},{7,6},{8,9},{9,8},{10,11... | collective-permute-start | bytes 393224 | tf_op jit(solution)/shard_map/ppermute | solution.py:19
  16.1 30.0 %collective-permute-start.1 = (bf16[512,1024]{1,0:T(8,128)(2,1)S(1)}, bf16[512,1024]{1,0:T(8,128)(2,1)}, u32[]{:S(2)}, u32[]{:S(2)}) collective-permute-start(bf16[512,1024]{1,0:T(8,128)(2,1)S(1)} %bitcast_multiply_fusion.2.own_ref), channel_id=1, source_target_pairs={{0,1},{1,0},{2,3},{3,2},{4,5},{5,4},{6,7},{7,6},{8,9},{9,8},{10,11... | collective-permute-start | bytes 3145736 | tf_op jit(solution)/shard_map/ppermute | solution.py:19
  16.9 77.1 %collective-permute-start.10 = (bf16[512,1024]{1,0:T(8,128)(2,1)S(1)}, bf16[512,1024]{1,0:T(8,128)(2,1)}, u32[]{:S(2)}, u32[]{:S(2)}) collective-permute-start(bf16[512,1024]{1,0:T(8,128)(2,1)S(1)} %bitcast_multiply_fusion.1.own_ref), channel_id=1, source_target_pairs={{0,1},{1,0},{2,3},{3,2},{4,5},{5,4},{6,7},{7,6},{8,9},{9,8},{10,11... | collective-permute-start | bytes 3145736 | tf_op jit(solution)/shard_map/ppermute | solution.py:19
  19.2 95.6 %collective-permute-start.19 = (bf16[512,1024]{1,0:T(8,128)(2,1)S(1)}, bf16[512,1024]{1,0:T(8,128)(2,1)}, u32[]{:S(2)}, u32[]{:S(2)}) collective-permute-start(bf16[512,1024]{1,0:T(8,128)(2,1)S(1)} %bitcast_multiply_fusion.own_ref), channel_id=1, source_target_pairs={{0,1},{1,0},{2,3},{3,2},{4,5},{5,4},{6,7},{7,6},{8,9},{9,8},{10,11... | collective-permute-start | bytes 3145736 | tf_op jit(solution)/shard_map/ppermute | solution.py:19
  26.7 1.6 collective-permute-start.2
  26.7 4.5 %collective-permute-start.3 = (bf16[256,128]{1,0:T(8,128)(2,1)S(1)}, bf16[256,128]{1,0:T(8,128)(2,1)S(1)}, u32[]{:S(2)}, u32[]{:S(2)}) collective-permute-start(bf16[256,128]{1,0:T(8,128)(2,1)S(1)} %shard_map.56.refs_0_), channel_id=1, source_target_pairs={{0,8},{4,12},{8,0},{12,4},{16,24},{20,28},{24,16},{28,20},{1,9},{5... | collective-permute-start | bytes 196616 | tf_op jit(solution)/shard_map/ppermute | solution.py:19
  28.3 5.3 %collective-permute-start.5 = (bf16[256,128]{1,0:T(8,128)(2,1)S(1)}, bf16[256,128]{1,0:T(8,128)(2,1)S(1)}, u32[]{:S(2)}, u32[]{:S(2)}) collective-permute-start(bf16[256,128]{1,0:T(8,128)(2,1)S(1)} %shard_map.56.refs_0_), channel_id=1, source_target_pairs={{0,16},{4,20},{8,24},{12,28},{16,0},{20,4},{24,8},{28,12},{1,17},{... | collective-permute-start | bytes 196616 | tf_op jit(solution)/shard_map/ppermute | solution.py:19
  31.2 5.2 %collective-permute-start.7 = (bf16[256,128]{1,0:T(8,128)(2,1)S(1)}, bf16[256,128]{1,0:T(8,128)(2,1)S(1)}, u32[]{:S(2)}, u32[]{:S(2)}) collective-permute-start(bf16[256,128]{1,0:T(8,128)(2,1)S(1)} %shard_map.56.refs_0_), channel_id=1, source_target_pairs={{0,24},{4,28},{8,16},{12,20},{16,8},{20,12},{24,0},{28,4},{1,25},{... | collective-permute-start | bytes 196616 | tf_op jit(solution)/shard_map/ppermute | solution.py:19
  33.6 2.8 %collective-permute-start.4 = (bf16[256,128]{1,0:T(8,128)(2,1)S(1)}, bf16[256,128]{1,0:T(8,128)(2,1)S(1)}, u32[]{:S(2)}, u32[]{:S(2)}) collective-permute-start(bf16[256,128]{1,0:T(8,128)(2,1)S(1)} %collective-permute-done.3.refs_2_), channel_id=1, source_target_pairs={{0,4},{4,0},{8,12},{12,8},{16,20},{20,16},{24,28},{28,24},{1,5},{5... | collective-permute-start | bytes 196616 | tf_op jit(solution)/shard_map/ppermute | solution.py:19
  36.4 1.7 collective-permute-start.6
  36.4 1.7 collective-permute-start.8
  48.0 41.6 %collective-permute-start.9 = (bf16[256,128]{1,0:T(8,128)(2,1)S(1)}, bf16[256,128]{1,0:T(8,128)(2,1)S(1)}, u32[]{:S(2)}, u32[]{:S(2)}) collective-permute-start(bf16[256,128]{1,0:T(8,128)(2,1)S(1)} %get-tuple-element.30), channel_id=1, source_target_pairs={{0,2},{1,3},{2,0},{3,1},{4,6},{5,7},{6,4},{7,5},{8,10},{9,11},{10,... | collective-permute-start | bytes 196616 | tf_op jit(solution)/shard_map/ppermute | solution.py:19
  90.4 4.3 %collective-permute-start.12 = (bf16[256,128]{1,0:T(8,128)(2,1)S(1)}, bf16[256,128]{1,0:T(8,128)(2,1)S(1)}, u32[]{:S(2)}, u32[]{:S(2)}) collective-permute-start(bf16[256,128]{1,0:T(8,128)(2,1)S(1)} %shard_map.59.refs_0_), channel_id=1, source_target_pairs={{0,8},{4,12},{8,0},{12,4},{16,24},{20,28},{24,16},{28,20},{1,9},{5... | collective-permute-start | bytes 196616 | tf_op jit(solution)/shard_map/ppermute | solution.py:19
  92.1 5.0 %collective-permute-start.14 = (bf16[256,128]{1,0:T(8,128)(2,1)S(1)}, bf16[256,128]{1,0:T(8,128)(2,1)S(1)}, u32[]{:S(2)}, u32[]{:S(2)}) collective-permute-start(bf16[256,128]{1,0:T(8,128)(2,1)S(1)} %shard_map.59.refs_0_), channel_id=1, source_target_pairs={{0,16},{4,20},{8,24},{12,28},{16,0},{20,4},{24,8},{28,12},{1,17},{... | collective-permute-start | bytes 196616 | tf_op jit(solution)/shard_map/ppermute | solution.py:19
  93.6 5.2 %collective-permute-start.16 = (bf16[256,128]{1,0:T(8,128)(2,1)S(1)}, bf16[256,128]{1,0:T(8,128)(2,1)S(1)}, u32[]{:S(2)}, u32[]{:S(2)}) collective-permute-start(bf16[256,128]{1,0:T(8,128)(2,1)S(1)} %shard_map.59.refs_0_), channel_id=1, source_target_pairs={{0,24},{4,28},{8,16},{12,20},{16,8},{20,12},{24,0},{28,4},{1,25},{... | collective-permute-start | bytes 196616 | tf_op jit(solution)/shard_map/ppermute | solution.py:19
  93.9 4.8 %collective-permute-start.11 = (bf16[256,128]{1,0:T(8,128)(2,1)S(1)}, bf16[256,128]{1,0:T(8,128)(2,1)S(1)}, u32[]{:S(2)}, u32[]{:S(2)}) collective-permute-start(bf16[256,128]{1,0:T(8,128)(2,1)S(1)} %shard_map.59.refs_0_), channel_id=1, source_target_pairs={{0,4},{4,0},{8,12},{12,8},{16,20},{20,16},{24,28},{28,24},{1,5},{5... | collective-permute-start | bytes 196616 | tf_op jit(solution)/shard_map/ppermute | solution.py:19
  94.7 4.0 %collective-permute-start.13 = (bf16[256,128]{1,0:T(8,128)(2,1)S(1)}, bf16[256,128]{1,0:T(8,128)(2,1)S(1)}, u32[]{:S(2)}, u32[]{:S(2)}) collective-permute-start(bf16[256,128]{1,0:T(8,128)(2,1)S(1)} %collective-permute-done.12.refs_2_), channel_id=1, source_target_pairs={{0,4},{4,0},{8,12},{12,8},{16,20},{20,16},{24,28},{28,24},{1,5},{5... | collective-permute-start | bytes 196616 | tf_op jit(solution)/shard_map/ppermute | solution.py:19
  97.1 1.7 collective-permute-start.15
  98.7 1.3 collective-permute-start.17
  102.0 5.9 %collective-permute-start.18 = (bf16[256,128]{1,0:T(8,128)(2,1)S(1)}, bf16[256,128]{1,0:T(8,128)(2,1)S(1)}, u32[]{:S(2)}, u32[]{:S(2)}) collective-permute-start(bf16[256,128]{1,0:T(8,128)(2,1)S(1)} %get-tuple-element.32), channel_id=1, source_target_pairs={{0,2},{1,3},{2,0},{3,1},{4,6},{5,7},{6,4},{7,5},{8,10},{9,11},{10,... | collective-permute-start | bytes 196616 | tf_op jit(solution)/shard_map/ppermute | solution.py:19
  108.6 4.9 %collective-permute-start.21 = (bf16[256,128]{1,0:T(8,128)(2,1)S(1)}, bf16[256,128]{1,0:T(8,128)(2,1)S(1)}, u32[]{:S(2)}, u32[]{:S(2)}) collective-permute-start(bf16[256,128]{1,0:T(8,128)(2,1)S(1)} %shard_map.61.refs_0_), channel_id=1, source_target_pairs={{0,8},{4,12},{8,0},{12,4},{16,24},{20,28},{24,16},{28,20},{1,9},{5... | collective-permute-start | bytes 196616 | tf_op jit(solution)/shard_map/ppermute | solution.py:19
  109.2 4.6 %collective-permute-start.23 = (bf16[256,128]{1,0:T(8,128)(2,1)S(1)}, bf16[256,128]{1,0:T(8,128)(2,1)S(1)}, u32[]{:S(2)}, u32[]{:S(2)}) collective-permute-start(bf16[256,128]{1,0:T(8,128)(2,1)S(1)} %shard_map.61.refs_0_), channel_id=1, source_target_pairs={{0,16},{4,20},{8,24},{12,28},{16,0},{20,4},{24,8},{28,12},{1,17},{... | collective-permute-start | bytes 196616 | tf_op jit(solution)/shard_map/ppermute | solution.py:19
  109.6 5.2 %collective-permute-start.25 = (bf16[256,128]{1,0:T(8,128)(2,1)S(1)}, bf16[256,128]{1,0:T(8,128)(2,1)S(1)}, u32[]{:S(2)}, u32[]{:S(2)}) collective-permute-start(bf16[256,128]{1,0:T(8,128)(2,1)S(1)} %shard_map.61.refs_0_), channel_id=1, source_target_pairs={{0,24},{4,28},{8,16},{12,20},{16,8},{20,12},{24,0},{28,4},{1,25},{... | collective-permute-start | bytes 196616 | tf_op jit(solution)/shard_map/ppermute | solution.py:19
  112.1 2.6 %collective-permute-start.20 = (bf16[256,128]{1,0:T(8,128)(2,1)S(1)}, bf16[256,128]{1,0:T(8,128)(2,1)S(1)}, u32[]{:S(2)}, u32[]{:S(2)}) collective-permute-start(bf16[256,128]{1,0:T(8,128)(2,1)S(1)} %shard_map.61.refs_0_), channel_id=1, source_target_pairs={{0,4},{4,0},{8,12},{12,8},{16,20},{20,16},{24,28},{28,24},{1,5},{5... | collective-permute-start | bytes 196616 | tf_op jit(solution)/shard_map/ppermute | solution.py:19
  113.5 1.3 collective-permute-start.22
  113.8 1.3 collective-permute-start.24
  114.7 1.3 collective-permute-start.26
  118.0 5.2 %collective-permute-start.27 = (bf16[256,128]{1,0:T(8,128)(2,1)S(1)}, bf16[256,128]{1,0:T(8,128)(2,1)S(1)}, u32[]{:S(2)}, u32[]{:S(2)}) collective-permute-start(bf16[256,128]{1,0:T(8,128)(2,1)S(1)} %get-tuple-element.34), channel_id=1, source_target_pairs={{0,2},{1,3},{2,0},{3,1},{4,6},{5,7},{6,4},{7,5},{8,10},{9,11},{10,... | collective-permute-start | bytes 196616 | tf_op jit(solution)/shard_map/ppermute | solution.py:19
  124.1 5.2 %collective-permute-start.28 = (bf16[128,256]{1,0:T(8,128)(2,1)S(1)}, bf16[128,256]{1,0:T(8,128)(2,1)S(1)}, u32[]{:S(2)}, u32[]{:S(2)}) collective-permute-start(bf16[128,256]{1,0:T(8,128)(2,1)S(1)} %shard_map.63.refs_0_), channel_id=1, source_target_pairs={{0,2},{1,3},{2,0},{3,1},{4,6},{5,7},{6,4},{7,5},{8,10},{9,11},{10,... | collective-permute-start | bytes 196616 | tf_op jit(solution)/shard_map/ppermute | solution.py:19
  131.2 1.6 collective-permute-start.29
  133.4 4.3 %collective-permute-start.30 = (bf16[128,256]{1,0:T(8,128)(2,1)S(1)}, bf16[128,256]{1,0:T(8,128)(2,1)S(1)}, u32[]{:S(2)}, u32[]{:S(2)}) collective-permute-start(bf16[128,256]{1,0:T(8,128)(2,1)S(1)} %get-tuple-element.38), channel_id=1, source_target_pairs={{0,8},{4,12},{8,0},{12,4},{16,24},{20,28},{24,16},{28,20},{1,9},{5... | collective-permute-start | bytes 196616 | tf_op jit(solution)/shard_map/ppermute | solution.py:19
  135.1 4.3 %collective-permute-start.31 = (bf16[128,256]{1,0:T(8,128)(2,1)S(1)}, bf16[128,256]{1,0:T(8,128)(2,1)S(1)}, u32[]{:S(2)}, u32[]{:S(2)}) collective-permute-start(bf16[128,256]{1,0:T(8,128)(2,1)S(1)} %get-tuple-element.39), channel_id=1, source_target_pairs={{0,16},{4,20},{8,24},{12,28},{16,0},{20,4},{24,8},{28,12},{1,17},{... | collective-permute-start | bytes 196616 | tf_op jit(solution)/shard_map/ppermute | solution.py:19
  136.6 5.2 %collective-permute-start.32 = (bf16[128,256]{1,0:T(8,128)(2,1)S(1)}, bf16[128,256]{1,0:T(8,128)(2,1)S(1)}, u32[]{:S(2)}, u32[]{:S(2)}) collective-permute-start(bf16[128,256]{1,0:T(8,128)(2,1)S(1)} %get-tuple-element.40), channel_id=1, source_target_pairs={{0,24},{4,28},{8,16},{12,20},{16,8},{20,12},{24,0},{28,4},{1,25},{... | collective-permute-start | bytes 196616 | tf_op jit(solution)/shard_map/ppermute | solution.py:19
  142.5 5.2 %collective-permute-start.33 = (bf16[128,256]{1,0:T(8,128)(2,1)S(1)}, bf16[128,256]{1,0:T(8,128)(2,1)S(1)}, u32[]{:S(2)}, u32[]{:S(2)}) collective-permute-start(bf16[128,256]{1,0:T(8,128)(2,1)S(1)} %shard_map.66.refs_0_), channel_id=1, source_target_pairs={{0,2},{1,3},{2,0},{3,1},{4,6},{5,7},{6,4},{7,5},{8,10},{9,11},{10,... | collective-permute-start | bytes 196616 | tf_op jit(solution)/shard_map/ppermute | solution.py:19
  149.6 1.6 collective-permute-start.34
  151.8 4.5 %collective-permute-start.35 = (bf16[128,256]{1,0:T(8,128)(2,1)S(1)}, bf16[128,256]{1,0:T(8,128)(2,1)S(1)}, u32[]{:S(2)}, u32[]{:S(2)}) collective-permute-start(bf16[128,256]{1,0:T(8,128)(2,1)S(1)} %get-tuple-element.44), channel_id=1, source_target_pairs={{0,8},{4,12},{8,0},{12,4},{16,24},{20,28},{24,16},{28,20},{1,9},{5... | collective-permute-start | bytes 196616 | tf_op jit(solution)/shard_map/ppermute | solution.py:19
  152.4 5.0 %collective-permute-start.36 = (bf16[128,256]{1,0:T(8,128)(2,1)S(1)}, bf16[128,256]{1,0:T(8,128)(2,1)S(1)}, u32[]{:S(2)}, u32[]{:S(2)}) collective-permute-start(bf16[128,256]{1,0:T(8,128)(2,1)S(1)} %get-tuple-element.45), channel_id=1, source_target_pairs={{0,16},{4,20},{8,24},{12,28},{16,0},{20,4},{24,8},{28,12},{1,17},{... | collective-permute-start | bytes 196616 | tf_op jit(solution)/shard_map/ppermute | solution.py:19
  152.8 5.2 %collective-permute-start.37 = (bf16[128,256]{1,0:T(8,128)(2,1)S(1)}, bf16[128,256]{1,0:T(8,128)(2,1)S(1)}, u32[]{:S(2)}, u32[]{:S(2)}) collective-permute-start(bf16[128,256]{1,0:T(8,128)(2,1)S(1)} %get-tuple-element.46), channel_id=1, source_target_pairs={{0,24},{4,28},{8,16},{12,20},{16,8},{20,12},{24,0},{28,4},{1,25},{... | collective-permute-start | bytes 196616 | tf_op jit(solution)/shard_map/ppermute | solution.py:19
  158.7 5.7 %collective-permute-start.38 = (bf16[128,256]{1,0:T(8,128)(2,1)S(1)}, bf16[128,256]{1,0:T(8,128)(2,1)S(1)}, u32[]{:S(2)}, u32[]{:S(2)}) collective-permute-start(bf16[128,256]{1,0:T(8,128)(2,1)S(1)} %shard_map.69.refs_0_), channel_id=1, source_target_pairs={{0,2},{1,3},{2,0},{3,1},{4,6},{5,7},{6,4},{7,5},{8,10},{9,11},{10,... | collective-permute-start | bytes 196616 | tf_op jit(solution)/shard_map/ppermute | solution.py:19
  161.7 8.1 %collective-permute-start.46 = (bf16[128,128]{0,1:T(8,128)(2,1)S(1)}, bf16[128,128]{0,1:T(8,128)(2,1)S(1)}, u32[]{:S(2)}, u32[]{:S(2)}) collective-permute-start(bf16[128,128]{0,1:T(8,128)(2,1)S(1)} %get-tuple-element.74), channel_id=1, source_target_pairs={{0,1},{1,0},{2,3},{3,2},{4,5},{5,4},{6,7},{7,6},{8,9},{9,8},{10,11... | collective-permute-start | bytes 98312 | tf_op jit(solution)/shard_map/ppermute | solution.py:19
  166.3 5.5 %collective-permute-start.39 = (bf16[4,128,256]{2,1,0:T(8,128)(2,1)S(1)}, bf16[4,128,256]{2,1,0:T(8,128)(2,1)S(1)}, u32[]{:S(2)}, u32[]{:S(2)}) collective-permute-start(bf16[4,128,256]{2,1,0:T(8,128)(2,1)S(1)} %get-tuple-element.48), channel_id=1, source_target_pairs={{0,4},{4,0},{8,12},{12,8},{16,20},{20,16},{24,28},{28,24},{1,5},{5... | collective-permute-start | bytes 786440 | tf_op jit(solution)/shard_map/ppermute | solution.py:19
  166.4 5.4 %collective-permute-start.45 = (bf16[128,128]{0,1:T(8,128)(2,1)S(1)}, bf16[128,128]{0,1:T(8,128)(2,1)S(1)}, u32[]{:S(2)}, u32[]{:S(2)}) collective-permute-start(bf16[128,128]{0,1:T(8,128)(2,1)S(1)} %get-tuple-element.72), channel_id=1, source_target_pairs={{0,1},{1,0},{2,3},{3,2},{4,5},{5,4},{6,7},{7,6},{8,9},{9,8},{10,11... | collective-permute-start | bytes 98312 | tf_op jit(solution)/shard_map/ppermute | solution.py:19
  172.4 5.5 %collective-permute-start.40 = (bf16[128,256]{1,0:T(8,128)(2,1)S(1)}, bf16[128,256]{1,0:T(8,128)(2,1)S(1)}, u32[]{:S(2)}, u32[]{:S(2)}) collective-permute-start(bf16[128,256]{1,0:T(8,128)(2,1)S(1)} %get-tuple-element.50), channel_id=1, source_target_pairs={{0,8},{4,12},{8,0},{12,4},{16,24},{20,28},{24,16},{28,20},{1,9},{5... | collective-permute-start | bytes 196616 | tf_op jit(solution)/shard_map/ppermute | solution.py:19
  174.0 4.3 %collective-permute-start.41 = (bf16[128,256]{1,0:T(8,128)(2,1)S(1)}, bf16[128,256]{1,0:T(8,128)(2,1)S(1)}, u32[]{:S(2)}, u32[]{:S(2)}) collective-permute-start(bf16[128,256]{1,0:T(8,128)(2,1)S(1)} %get-tuple-element.51), channel_id=1, source_target_pairs={{0,16},{4,20},{8,24},{12,28},{16,0},{20,4},{24,8},{28,12},{1,17},{... | collective-permute-start | bytes 196616 | tf_op jit(solution)/shard_map/ppermute | solution.py:19
  175.4 5.2 %collective-permute-start.42 = (bf16[128,256]{1,0:T(8,128)(2,1)S(1)}, bf16[128,256]{1,0:T(8,128)(2,1)S(1)}, u32[]{:S(2)}, u32[]{:S(2)}) collective-permute-start(bf16[128,256]{1,0:T(8,128)(2,1)S(1)} %get-tuple-element.52), channel_id=1, source_target_pairs={{0,24},{4,28},{8,16},{12,20},{16,8},{20,12},{24,0},{28,4},{1,25},{... | collective-permute-start | bytes 196616 | tf_op jit(solution)/shard_map/ppermute | solution.py:19
  176.0 7.4 %collective-permute-start.44 = (bf16[128,128]{0,1:T(8,128)(2,1)S(1)}, bf16[128,128]{0,1:T(8,128)(2,1)S(1)}, u32[]{:S(2)}, u32[]{:S(2)}) collective-permute-start(bf16[128,128]{0,1:T(8,128)(2,1)S(1)} %get-tuple-element.70), channel_id=1, source_target_pairs={{0,1},{1,0},{2,3},{3,2},{4,5},{5,4},{6,7},{7,6},{8,9},{9,8},{10,11... | collective-permute-start | bytes 98312 | tf_op jit(solution)/shard_map/ppermute | solution.py:19
  181.4 4.0 %collective-permute-start.43 = (bf16[128,128]{0,1:T(8,128)(2,1)S(1)}, bf16[128,128]{0,1:T(8,128)(2,1)S(1)}, u32[]{:S(2)}, u32[]{:S(2)}) collective-permute-start(bf16[128,128]{0,1:T(8,128)(2,1)S(1)} %get-tuple-element.68), channel_id=1, source_target_pairs={{0,1},{1,0},{2,3},{3,2},{4,5},{5,4},{6,7},{7,6},{8,9},{9,8},{10,11... | collective-permute-start | bytes 98312 | tf_op jit(solution)/shard_map/ppermute | solution.py:19
  (17 other events, 609.0 us)

commit v2 on v1

v2 whole, which is shorter than its diff:
```python
import functools

import jax
import jax.numpy as jnp
from jax import lax
from jax.experimental import pallas as pl
from jax.experimental.pallas import tpu as pltpu
from jax.sharding import PartitionSpec as P

B = 128
NLEV = 4
LANES = 128
F32 = jnp.float32
BF16 = jnp.bfloat16


def swap(value, axis, distance):
    count = lax.axis_size(axis)
    return lax.ppermute(value, axis, [(i, i ^ distance) for i in range(count)])


def call(body, out_shape, args, scratch=(), flops=0):
    moved = sum(a.size * a.dtype.itemsize for a in args)
    in_specs = [
        pl.BlockSpec(memory_space=pltpu.SMEM if i == 0 else pltpu.VMEM) for i in range(len(args))
    ]
    several = isinstance(out_shape, (list, tuple))
    out_specs = (
        [pl.BlockSpec(memory_space=pltpu.VMEM) for _ in out_shape]
        if several
        else pl.BlockSpec(memory_space=pltpu.VMEM)
    )
    return pl.pallas_call(
        body,
        out_shape=out_shape,
        in_specs=in_specs,
        out_specs=out_specs,
        scratch_shapes=list(scratch),
        compiler_params=pltpu.CompilerParams(vmem_limit_bytes=40 * 1024 * 1024),
        cost_estimate=pl.CostEstimate(flops=flops, bytes_accessed=moved, transcendentals=0),
    )(*args)


def aligned(start, size, step):
    return pl.ds(pl.multiple_of(start * step, step), size)


def pack_body(rows, cols, chunk_rows, total_rows, idx_ref, rhs_ref, dest_ref, out_ref):
    local_rows = rhs_ref.shape[0]
    supernodes = rows * cols
    pairs = supernodes // 2
    shards_per_line = LANES // chunk_rows
    me = idx_ref[2]
    dest = dest_ref[...]
    supernode = (dest // B) % supernodes
    level = dest // (supernodes * B)
    within = dest % B
    owner_row = supernode // cols
    pair = owner_row // 2 * cols + supernode % cols
    place_high = (level * 2 + owner_row % 2).astype(F32)
    place_low = within.astype(F32)
    pair_iota = lax.broadcasted_iota(jnp.int32, (pairs, local_rows), 0)
    member = pair_iota == pair
    member_f = jnp.where(member, 1.0, 0.0)
    before = (
        lax.broadcasted_iota(jnp.int32, (local_rows, local_rows), 0)
        < lax.broadcasted_iota(jnp.int32, (local_rows, local_rows), 1)
    )
    counts = jnp.dot(
        member_f.astype(BF16), jnp.where(before, 1.0, 0.0).astype(BF16), preferred_element_type=F32
    )
    rank = jnp.sum(member_f * counts, axis=0, keepdims=True).astype(jnp.int32)
    slot = pair * chunk_rows + rank
    chosen = lax.broadcasted_iota(jnp.int32, (local_rows, local_rows), 0) == slot
    sorted_rows = jnp.dot(
        jnp.where(chosen, 1.0, 0.0).astype(BF16),
        rhs_ref[...].astype(BF16),
        preferred_element_type=F32,
    )
    tail = total_rows - chunk_rows
    tail_iota = lax.broadcasted_iota(jnp.int32, (pairs * tail, local_rows), 0)
    tail_pair = tail_iota // tail
    tail_row = tail_iota % tail
    tail_value = jnp.where(tail_row == 0, place_high, jnp.where(tail_row == 1, place_low, 0.0))
    tail_value = jnp.where(tail_pair == pair, tail_value, 0.0).astype(BF16)
    lane = rank + (me % shards_per_line) * chunk_rows
    lane_hot = lax.broadcasted_iota(jnp.int32, (LANES, local_rows), 0) == lane
    tails = lax.dot_general(
        tail_value,
        jnp.where(lane_hot, 1.0, 0.0).astype(BF16),
        (((1,), (1,)), ((), ())),
        preferred_element_type=F32,
    )
    half = rhs_ref.shape[1] // 2
    for g in range(pairs):
        chosen_rows = sorted_rows[g * chunk_rows : (g + 1) * chunk_rows]
        ending = tails[g * tail : (g + 1) * tail]
        for h in range(2):
            side = chosen_rows[:, h * half : (h + 1) * half]
            chunk = jnp.concatenate([side, ending], axis=0)
            out_ref[(2 * (g // cols) + h) * cols + g % cols] = chunk.astype(BF16)


def place_rows(arrived_ref, first_place, place_count, chunk_rows):
    shards = arrived_ref.shape[0]
    shards_per_line = LANES // chunk_rows
    hots = []
    place = lax.broadcasted_iota(jnp.int32, (place_count, LANES), 0) + first_place
    for first in range(0, shards, shards_per_line):
        ending = jnp.zeros((8, LANES), F32)
        for s in range(first, first + shards_per_line):
            ending = ending + arrived_ref[s, chunk_rows:, :].astype(F32)[:8]
        where_to = (ending[0:1] * B + ending[1:2]).astype(jnp.int32)
        hots.append(jnp.where(place == where_to, 1.0, 0.0).astype(BF16))
    hot = jnp.concatenate(hots, axis=1)
    rows = jnp.concatenate(
        [arrived_ref[s].astype(F32)[:chunk_rows] for s in range(shards)], axis=0
    ).astype(BF16)
    return lax.dot_general(
        rows, hot, (((0,), (1,)), ((), ())), preferred_element_type=F32
    ).astype(BF16)


def times(left, right):
    return jnp.dot(left, right, preferred_element_type=F32)


def times_t(left, right):
    return lax.dot_general(left, right, (((1,), (1,)), ((), ())), preferred_element_type=F32)


def apply_diag(product, parity, residual, own_ref, par_ref, out_ref):
    for at, factor in ((parity, own_ref), (1 - parity, par_ref)):
        lanes = aligned(at, B, B)
        out_ref[:, lanes] = product(residual[:, lanes], factor[...]).astype(BF16)


def first_body(chunk_rows, idx_ref, arrived_ref, own_ref, par_ref, out_ref, residual):
    residual[...] = place_rows(arrived_ref, 0, 2 * B, chunk_rows)
    apply_diag(times_t, idx_ref[0] % 2, residual, own_ref, par_ref, out_ref)


def rest_body(chunk_rows, idx_ref, arrived_ref, *outs):
    placed = place_rows(arrived_ref, 2 * B, len(outs) * 2 * B, chunk_rows)
    for k, out in enumerate(outs):
        out[...] = placed[:, k * 2 * B : (k + 1) * 2 * B]


def down_body(idx_ref, own_ref, par_ref, *refs, groups, cols):
    pieces, outs = refs[:groups], refs[groups : groups + cols]
    gathered, product = refs[groups + cols :]
    row, col = idx_ref[0], idx_ref[1]
    parity, group = row % 2, row // 2
    for m, piece in enumerate(pieces):
        gathered[:, aligned(group ^ m, 2 * B, 2 * B)] = piece[...]
    product[parity] = times_t(gathered[...], own_ref[...])
    product[1 - parity] = times_t(gathered[...], par_ref[...])
    for m, out in enumerate(outs):
        at = aligned(col ^ m, B, B)
        for rr in range(2):
            out[:, rr * B : (rr + 1) * B] = product[rr, :, at].astype(out.dtype)


def residual_body(idx_ref, rhs_ref, own_ref, par_ref, kept_ref, *refs, last):
    if last:
        arrived, outs, residual, solved = refs[:-3], refs[-3], refs[-2], refs[-1]
    else:
        arrived, solved, residual = refs[:-2], refs[-2], refs[-1]
    coupled = kept_ref[...]
    for ref in arrived:
        coupled = coupled + ref[...].astype(F32)
    residual[...] = (rhs_ref[...].astype(F32) - coupled).astype(BF16)
    parity = idx_ref[0] % 2
    apply_diag(times_t, parity, residual, own_ref, par_ref, solved)
    if last:
        apply_diag(times, parity, solved, own_ref, par_ref, outs)


def up_body(idx_ref, own_ref, par_ref, *refs, groups, cols):
    pieces, outs = refs[:cols], refs[cols : cols + groups]
    gathered, product = refs[cols + groups :]
    row, col = idx_ref[0], idx_ref[1]
    parity, group = row % 2, row // 2
    for m, piece in enumerate(pieces):
        for rr in range(2):
            gathered[rr, :, aligned(col ^ m, B, B)] = piece[:, rr * B : (rr + 1) * B]
    product[...] = times(gathered[parity], own_ref[...]) + times(
        gathered[1 - parity], par_ref[...]
    )
    for m, out in enumerate(outs):
        out[...] = product[:, aligned(group ^ m, 2 * B, 2 * B)].astype(out.dtype)


def final_body(idx_ref, solved_ref, own_ref, par_ref, kept_ref, *refs):
    arrived, outs, residual = refs[:-2], refs[-2], refs[-1]
    back = kept_ref[...]
    for ref in arrived:
        back = back + ref[...].astype(F32)
    residual[...] = (solved_ref[...].astype(F32) - back).astype(BF16)
    apply_diag(times, idx_ref[0] % 2, residual, own_ref, par_ref, outs)


def per_device(rhs_rows, dest_row, diag_inverse, lower_blocks, block_mask):
    rows = lax.axis_size("row")
    cols = lax.axis_size("col")
    groups = rows // 2
    supernodes = rows * cols
    local_rows = rhs_rows.shape[0]
    half = rhs_rows.shape[1] // 2
    chunk_rows = 2 * (local_rows // supernodes)
    total_rows = (chunk_rows + 2 + 15) // 16 * 16
    row, col = lax.axis_index("row"), lax.axis_index("col")
    parity = row % 2
    idx = jnp.stack([row, col, row * cols + col]).astype(jnp.int32)

    def shape(dims, dtype=BF16):
        return jax.ShapeDtypeStruct(dims, dtype)

    diag_own = diag_inverse[:, 0]
    diag_par = swap(diag_own, "row", 1)
    own, par = [], []
    for level in range(NLEV - 1):
        tile = lower_blocks[level, 0, :, :, 0]
        mask = block_mask[level, 0, :, 0, :].astype(BF16)
        masked = (tile * mask[:, None, :, None]).reshape(cols * B, rows * B)
        own.append(masked)
        par.append(swap(masked, "row", 1))

    sending = call(
        functools.partial(pack_body, rows, cols, chunk_rows, total_rows),
        shape((supernodes, total_rows, half)),
        (idx, rhs_rows, dest_row.reshape(1, local_rows)),
        flops=2 * local_rows * local_rows * 2 * half,
    )
    arrived = lax.all_to_all(sending, ("row", "col"), split_axis=0, concat_axis=0, tiled=True)
    block = (half, 2 * B)
    solved = [
        call(
            functools.partial(first_body, chunk_rows),
            shape(block),
            (idx, arrived, diag_own[0], diag_par[0]),
            [pltpu.VMEM(block, BF16)],
        )
    ]
    rest = call(
        functools.partial(rest_body, chunk_rows),
        [shape(block) for _ in range(NLEV - 1)],
        (idx, arrived),
    )
    upper = None
    for level in range(1, NLEV):
        pieces = [solved[-1]] + [swap(solved[-1], "row", 2 * m) for m in range(1, groups)]
        sums = call(
            functools.partial(down_body, groups=groups, cols=cols),
            [shape(block, F32 if m == 0 else BF16) for m in range(cols)],
            (idx, own[level - 1], par[level - 1], *pieces),
            [pltpu.VMEM((half, rows * B), BF16), pltpu.VMEM((2, half, cols * B), F32)],
            flops=4 * rows * cols * B * B * half,
        )
        passed = [swap(sums[m], "col", m) for m in range(1, cols)]
        last = level == NLEV - 1
        result = call(
            functools.partial(residual_body, last=last),
            shape(block),
            (idx, rest[level - 1], diag_own[level], diag_par[level], sums[0], *passed),
            [pltpu.VMEM(block, BF16)] * (2 if last else 1),
        )
        if last:
            upper = result
        else:
            solved.append(result)

    solution = [None] * NLEV
    solution[NLEV - 1] = upper
    for level in range(NLEV - 2, -1, -1):
        pieces = [upper] + [swap(upper, "col", m) for m in range(1, cols)]
        sums = call(
            functools.partial(up_body, groups=groups, cols=cols),
            [shape(block, F32 if m == 0 else BF16) for m in range(groups)],
            (idx, own[level], par[level], *pieces),
            [pltpu.VMEM((2, half, cols * B), BF16), pltpu.VMEM((half, rows * B), F32)],
            flops=4 * rows * cols * B * B * half,
        )
        passed = [swap(sums[m], "row", 2 * m) for m in range(1, groups)]
        upper = call(
            final_body,
            shape(block),
            (idx, solved[level], diag_own[level], diag_par[level], sums[0], *passed),
            [pltpu.VMEM(block, BF16)],
        )
        solution[level] = upper

    results = []
    for level in range(NLEV):
        both = solution[level]
        mine = lax.dynamic_slice_in_dim(both, parity * B, B, axis=1).T
        theirs = lax.dynamic_slice_in_dim(both, (1 - parity) * B, B, axis=1).T
        got = swap(theirs, "row", 1)
        results.append(
            jnp.where(
                parity == 0,
                jnp.concatenate([mine, got], axis=1),
                jnp.concatenate([got, mine], axis=1),
            )
        )
    return jnp.stack(results)[:, None]


def solution(mesh):
    in_specs = (
        P(("row", "col"), None),
        P(("row", "col")),
        P(None, ("row", "col"), None, None),
        P(None, "row", None, None, "col", None, None),
        P(None, "row", None, "col", None),
    )
    out_specs = P(None, ("row", "col"), None, None)
    return jax.shard_map(
        per_device, mesh=mesh, in_specs=in_specs, out_specs=out_specs, check_vma=False
    )
```

time: 187 us -> 143 us (0.76)
  waiting for transfers between devices: 90.7 us -> 55.1 us
  starting transfers between devices: 63.3 us -> 57.4 us
    ppermute x47 -> x44, waiting for transfers between devices: 90.7 us -> 51.1 us  [swap(): return lax.ppermute(value, axis, [(i, i ^ distance) for i in range(count)])]
    ppermute x47 -> x44, starting transfers between devices: 56 us -> 50.1 us  [swap(): return lax.ppermute(value, axis, [(i, i ^ distance) for i in range(count)])]
    all_to_all x1, waiting for transfers between devices: 0.01 us -> 3.97 us  [per_device(): lax.all_to_all(sending, ('row', 'col'), split_axis=0, concat_axis=0, tile...]
    pallas_call x18 -> x15, Pallas kernels: 21.7 us -> 20.3 us  [call(): pl.pallas_call(body, out_shape=out_shape, in_specs=in_specs, out_specs=ou...]
  transfers between devices with their start and end apart: 48 -> 45, of which waited for: 30 -> 33; matrix products, arithmetic and copies ran while one was open for 3% -> 3% of each run, Pallas kernels for 5% -> 8%
where the time goes in v2:
time: 143 us; the launch traced here: 142 us
  starting transfers between devices  57.4 us (40%)
  waiting for transfers between devices  55.1 us (39%)
  Pallas kernels  20.3 us (14%)
  local copies, waits for them, and re-layouts  8.2 us (6%)
    ppermute x44, waiting for transfers between devices, swap(): return lax.ppermute(value, axis, [(i, i ^ distance) for i in range(count)])  51.1 us
    ppermute x44, starting transfers between devices, swap(): return lax.ppermute(value, axis, [(i, i ^ distance) for i in range(count)])  50.1 us
    pallas_call x15, Pallas kernels, call(): pl.pallas_call(body, out_shape=out_shape, in_specs=in_specs, out_specs=ou...  20.3 us
    all_to_all x1, starting transfers between devices, per_device(): lax.all_to_all(sending, ('row', 'col'), split_axis=0, concat_axis=0, tile...  7.3 us
    all_to_all x1, waiting for transfers between devices, per_device(): lax.all_to_all(sending, ('row', 'col'), split_axis=0, concat_axis=0, tile...  3.97 us
    unnamed x42, local copies, waits for them, and re-layouts  3.32 us
  transfers between devices with their start and end apart: 45, of which 33 were waited for; matrix products, arithmetic and copies ran while one was open for 3% of the time, Pallas kernels for 8%

profile of v2, /device:TPU:0, one launch (start us, length us, event | category | flops | bytes accessed | tf_op | source)
XLA Modules:
  0.0 142.3 jit_solution(6084012360978448938)
XLA Ops:
  1.8 1.9 %shard_map.55 = bf16[32,48,128]{2,1,0:T(8,128)(2,1)} custom-call(s32[3]{0:T(128)S(1)} %pad_add_fusion.idx_ref, f32[512,256]{1,0:T(8,128)S(1)} %copy-done.2, s32[1,512]{1,0:T(1,128)S(1)} %bitcast.82), custom_call_target="tpu_custom_call" | custom-call | flops 134217728 | bytes 526348 | tf_op jit(solution)/shard_map/pallas_call | solution.py:33
  3.7 7.3 %all-to-all-start = ((bf16[32,48,128]{2,1,0:T(8,128)(2,1)}), bf16[32,48,128]{2,1,0:T(8,128)(2,1)S(1)}, u32[]{:S(2)}, u32[]{:S(2)}) async-start(bf16[32,48,128]{2,1,0:T(8,128)(2,1)} %shard_map.55), calls=%async_computation | async-start | bytes 786432 | tf_op jit(solution)/shard_map/all_to_all | solution.py:235
  11.0 2.1 %fusion = (bf16[1,1,4,128,1,8,128]{6,5,4,3,2,1,0:T(8,128)(2,1)S(1)}, bf16[1,1,4,128,1,8,128]{6,5,4,3,2,1,0:T(8,128)(2,1)S(1)}, bf16[1,1,4,128,1,8,128]{6,5,4,3,2,1,0:T(8,128)(2,1)S(1)}) fusion(bf16[3,1,4,128,1,8,128]{6,5,4,3,2,1,0:T(8,128)(2,1)} %param.8), kind=kLoop, calls=%fused_computation.28 | loop fusion | bytes 6291456 | tf_op jit(solution)/shard_map/slice | solution.py:223
  16.4 1.8 %collective-permute-done = bf16[4,128,128]{2,1,0:T(8,128)(2,1)S(1)} collective-permute-done((bf16[4,128,128]{2,1,0:T(8,128)(2,1)S(1)}, bf16[4,128,128]{2,1,0:T(8,128)(2,1)S(1)}, u32[]{:S(2)}, u32[]{:S(2)}) %collective-permute-start) | collective-permute-done | bytes 131104 | tf_op jit(solution)/shard_map/ppermute | solution.py:19
  18.9 4.0 %all-to-all-done.arrived_ref = bf16[32,48,128]{2,1,0:T(8,128)(2,1)S(1)} async-done(((bf16[32,48,128]{2,1,0:T(8,128)(2,1)}), bf16[32,48,128]{2,1,0:T(8,128)(2,1)S(1)}, u32[]{:S(2)}, u32[]{:S(2)}) %all-to-all-start) | async-done | bytes 393248 | tf_op jit(solution)/shard_map/all_to_all | solution.py:235
  25.4 1.5 %collective-permute-start.2 = (bf16[128,256]{1,0:T(8,128)(2,1)S(1)}, bf16[128,256]{1,0:T(8,128)(2,1)S(1)}, u32[]{:S(2)}, u32[]{:S(2)}) collective-permute-start(bf16[128,256]{1,0:T(8,128)(2,1)S(1)} %shard_map.56.refs_0_.solved_ref), channel_id=1, source_target_pairs={{0,8},{4,12},{8,0},{12,4},{16,24},{20,28},{24,16},{28,20},{1,9},{5... | collective-permute-start | bytes 196616 | tf_op jit(solution)/shard_map/ppermute | solution.py:19
  28.1 2.2 %collective-permute-done.2.refs_1_ = bf16[128,256]{1,0:T(8,128)(2,1)S(1)} collective-permute-done((bf16[128,256]{1,0:T(8,128)(2,1)S(1)}, bf16[128,256]{1,0:T(8,128)(2,1)S(1)}, u32[]{:S(2)}, u32[]{:S(2)}) %collective-permute-start.2) | collective-permute-done | bytes 65568 | tf_op jit(solution)/shard_map/ppermute | solution.py:19
  30.2 1.7 %collective-permute-start.4 = (bf16[128,256]{1,0:T(8,128)(2,1)S(1)}, bf16[128,256]{1,0:T(8,128)(2,1)S(1)}, u32[]{:S(2)}, u32[]{:S(2)}) collective-permute-start(bf16[128,256]{1,0:T(8,128)(2,1)S(1)} %shard_map.56.refs_0_.solved_ref), channel_id=1, source_target_pairs={{0,24},{4,28},{8,16},{12,20},{16,8},{20,12},{24,0},{28,4},{1,25},{... | collective-permute-start | bytes 196616 | tf_op jit(solution)/shard_map/ppermute | solution.py:19
  31.9 3.5 %collective-permute-done.4.refs_3_ = bf16[128,256]{1,0:T(8,128)(2,1)S(1)} collective-permute-done((bf16[128,256]{1,0:T(8,128)(2,1)S(1)}, bf16[128,256]{1,0:T(8,128)(2,1)S(1)}, u32[]{:S(2)}, u32[]{:S(2)}) %collective-permute-start.4) | collective-permute-done | bytes 65568 | tf_op jit(solution)/shard_map/ppermute | solution.py:19
  35.4 2.1 %shard_map.58 = (f32[128,256]{1,0:T(8,128)S(1)}, bf16[128,256]{1,0:T(8,128)(2,1)S(1)}, bf16[128,256]{1,0:T(8,128)(2,1)S(1)}, bf16[128,256]{1,0:T(8,128)(2,1)S(1)}) custom-call(s32[3]{0:T(128)S(1)} %pad_add_fusion.idx_ref, bf16[512,1024]{1,0:T(8,128)(2,1)S(1)} %bitcast_multiply_fusion.2.own_ref, bf16[512,1024]{1,0:T(8,128)(2,1)} %collective-permute-done.1.par_ref, ...), custom_call_target="tpu_custom_call" | custom-call | flops 268435456 | bytes 2359308 | tf_op jit(solution)/shard_map/pallas_call | solution.py:33
  37.6 1.9 %collective-permute-start.5 = (bf16[128,256]{1,0:T(8,128)(2,1)S(1)}, bf16[128,256]{1,0:T(8,128)(2,1)S(1)}, u32[]{:S(2)}, u32[]{:S(2)}) collective-permute-start(bf16[128,256]{1,0:T(8,128)(2,1)S(1)} %get-tuple-element.34), channel_id=1, source_target_pairs={{0,1},{1,0},{2,3},{3,2},{4,5},{5,4},{6,7},{7,6},{8,9},{9,8},{10,11... | collective-permute-start | bytes 196616 | tf_op jit(solution)/shard_map/ppermute | solution.py:19
  40.3 1.7 %collective-permute-start.7 = (bf16[128,256]{1,0:T(8,128)(2,1)S(1)}, bf16[128,256]{1,0:T(8,128)(2,1)S(1)}, u32[]{:S(2)}, u32[]{:S(2)}) collective-permute-start(bf16[128,256]{1,0:T(8,128)(2,1)S(1)} %get-tuple-element.36), channel_id=1, source_target_pairs={{0,3},{1,2},{2,1},{3,0},{4,7},{5,6},{6,5},{7,4},{8,11},{9,10},{10,... | collective-permute-start | bytes 196616 | tf_op jit(solution)/shard_map/ppermute | solution.py:19
  43.3 1.7 %collective-permute-done.6.refs_1_ = bf16[128,256]{1,0:T(8,128)(2,1)S(1)} collective-permute-done((bf16[128,256]{1,0:T(8,128)(2,1)S(1)}, bf16[128,256]{1,0:T(8,128)(2,1)S(1)}, u32[]{:S(2)}, u32[]{:S(2)}) %collective-permute-start.6) | collective-permute-done | bytes 65568 | tf_op jit(solution)/shard_map/ppermute | solution.py:19
  45.0 1.4 collective-permute-done.7.refs_2_
  47.1 1.5 %collective-permute-start.10 = (bf16[128,256]{1,0:T(8,128)(2,1)S(1)}, bf16[128,256]{1,0:T(8,128)(2,1)S(1)}, u32[]{:S(2)}, u32[]{:S(2)}) collective-permute-start(bf16[128,256]{1,0:T(8,128)(2,1)S(1)} %shard_map.59.refs_0_.solved_ref), channel_id=1, source_target_pairs={{0,16},{4,20},{8,24},{12,28},{16,0},{20,4},{24,8},{28,12},{1,17},{... | collective-permute-start | bytes 196616 | tf_op jit(solution)/shard_map/ppermute | solution.py:19
  48.6 1.5 %collective-permute-start.11 = (bf16[128,256]{1,0:T(8,128)(2,1)S(1)}, bf16[128,256]{1,0:T(8,128)(2,1)S(1)}, u32[]{:S(2)}, u32[]{:S(2)}) collective-permute-start(bf16[128,256]{1,0:T(8,128)(2,1)S(1)} %shard_map.59.refs_0_.solved_ref), channel_id=1, source_target_pairs={{0,24},{4,28},{8,16},{12,20},{16,8},{20,12},{24,0},{28,4},{1,25},{... | collective-permute-start | bytes 196616 | tf_op jit(solution)/shard_map/ppermute | solution.py:19
  51.4 2.4 %collective-permute-done.11.refs_3_ = bf16[128,256]{1,0:T(8,128)(2,1)S(1)} collective-permute-done((bf16[128,256]{1,0:T(8,128)(2,1)S(1)}, bf16[128,256]{1,0:T(8,128)(2,1)S(1)}, u32[]{:S(2)}, u32[]{:S(2)}) %collective-permute-start.11) | collective-permute-done | bytes 65568 | tf_op jit(solution)/shard_map/ppermute | solution.py:19
  54.4 2.1 %shard_map.60 = (f32[128,256]{1,0:T(8,128)S(1)}, bf16[128,256]{1,0:T(8,128)(2,1)S(1)}, bf16[128,256]{1,0:T(8,128)(2,1)S(1)}, bf16[128,256]{1,0:T(8,128)(2,1)S(1)}) custom-call(s32[3]{0:T(128)S(1)} %pad_add_fusion.idx_ref, bf16[512,1024]{1,0:T(8,128)(2,1)S(1)} %bitcast_multiply_fusion.1.own_ref, bf16[512,1024]{1,0:T(8,128)(2,1)} %collective-permute-done.8.par_ref, ...), custom_call_target="tpu_custom_call" | custom-call | flops 268435456 | bytes 2359308 | tf_op jit(solution)/shard_map/pallas_call | solution.py:33
  56.6 2.5 %collective-permute-start.13 = (bf16[128,256]{1,0:T(8,128)(2,1)S(1)}, bf16[128,256]{1,0:T(8,128)(2,1)S(1)}, u32[]{:S(2)}, u32[]{:S(2)}) collective-permute-start(bf16[128,256]{1,0:T(8,128)(2,1)S(1)} %get-tuple-element.40), channel_id=1, source_target_pairs={{0,2},{1,3},{2,0},{3,1},{4,6},{5,7},{6,4},{7,5},{8,10},{9,11},{10,... | collective-permute-start | bytes 196616 | tf_op jit(solution)/shard_map/ppermute | solution.py:19
  59.1 1.9 %collective-permute-start.14 = (bf16[128,256]{1,0:T(8,128)(2,1)S(1)}, bf16[128,256]{1,0:T(8,128)(2,1)S(1)}, u32[]{:S(2)}, u32[]{:S(2)}) collective-permute-start(bf16[128,256]{1,0:T(8,128)(2,1)S(1)} %get-tuple-element.41), channel_id=1, source_target_pairs={{0,3},{1,2},{2,1},{3,0},{4,7},{5,6},{6,5},{7,4},{8,11},{9,10},{10,... | collective-permute-start | bytes 196616 | tf_op jit(solution)/shard_map/ppermute | solution.py:19
  61.8 3.3 %collective-permute-done.14.refs_2_ = bf16[128,256]{1,0:T(8,128)(2,1)S(1)} collective-permute-done((bf16[128,256]{1,0:T(8,128)(2,1)S(1)}, bf16[128,256]{1,0:T(8,128)(2,1)S(1)}, u32[]{:S(2)}, u32[]{:S(2)}) %collective-permute-start.14) | collective-permute-done | bytes 65568 | tf_op jit(solution)/shard_map/ppermute | solution.py:19
  66.6 1.3 collective-permute-start.17
  68.0 1.4 %collective-permute-start.18 = (bf16[128,256]{1,0:T(8,128)(2,1)S(1)}, bf16[128,256]{1,0:T(8,128)(2,1)S(1)}, u32[]{:S(2)}, u32[]{:S(2)}) collective-permute-start(bf16[128,256]{1,0:T(8,128)(2,1)S(1)} %shard_map.61.refs_0_.solved_ref), channel_id=1, source_target_pairs={{0,24},{4,28},{8,16},{12,20},{16,8},{20,12},{24,0},{28,4},{1,25},{... | collective-permute-start | bytes 196616 | tf_op jit(solution)/shard_map/ppermute | solution.py:19
  70.9 2.2 %collective-permute-done.18.refs_3_ = bf16[128,256]{1,0:T(8,128)(2,1)S(1)} collective-permute-done((bf16[128,256]{1,0:T(8,128)(2,1)S(1)}, bf16[128,256]{1,0:T(8,128)(2,1)S(1)}, u32[]{:S(2)}, u32[]{:S(2)}) %collective-permute-start.18) | collective-permute-done | bytes 65568 | tf_op jit(solution)/shard_map/ppermute | solution.py:19
  73.1 2.1 %shard_map.62 = (f32[128,256]{1,0:T(8,128)S(1)}, bf16[128,256]{1,0:T(8,128)(2,1)S(1)}, bf16[128,256]{1,0:T(8,128)(2,1)S(1)}, bf16[128,256]{1,0:T(8,128)(2,1)S(1)}) custom-call(s32[3]{0:T(128)S(1)} %pad_add_fusion.idx_ref, bf16[512,1024]{1,0:T(8,128)(2,1)S(1)} %bitcast_multiply_fusion.own_ref, bf16[512,1024]{1,0:T(8,128)(2,1)} %collective-permute-done.15.par_ref, ...), custom_call_target="tpu_custom_call" | custom-call | flops 268435456 | bytes 2359308 | tf_op jit(solution)/shard_map/pallas_call | solution.py:33
  75.4 2.4 %collective-permute-start.20 = (bf16[128,256]{1,0:T(8,128)(2,1)S(1)}, bf16[128,256]{1,0:T(8,128)(2,1)S(1)}, u32[]{:S(2)}, u32[]{:S(2)}) collective-permute-start(bf16[128,256]{1,0:T(8,128)(2,1)S(1)} %get-tuple-element.45), channel_id=1, source_target_pairs={{0,2},{1,3},{2,0},{3,1},{4,6},{5,7},{6,4},{7,5},{8,10},{9,11},{10,... | collective-permute-start | bytes 196616 | tf_op jit(solution)/shard_map/ppermute | solution.py:19
  77.8 1.9 %collective-permute-start.21 = (bf16[128,256]{1,0:T(8,128)(2,1)S(1)}, bf16[128,256]{1,0:T(8,128)(2,1)S(1)}, u32[]{:S(2)}, u32[]{:S(2)}) collective-permute-start(bf16[128,256]{1,0:T(8,128)(2,1)S(1)} %get-tuple-element.46), channel_id=1, source_target_pairs={{0,3},{1,2},{2,1},{3,0},{4,7},{5,6},{6,5},{7,4},{8,11},{9,10},{10,... | collective-permute-start | bytes 196616 | tf_op jit(solution)/shard_map/ppermute | solution.py:19
  80.3 3.7 %collective-permute-done.20.refs_1_ = bf16[128,256]{1,0:T(8,128)(2,1)S(1)} collective-permute-done((bf16[128,256]{1,0:T(8,128)(2,1)S(1)}, bf16[128,256]{1,0:T(8,128)(2,1)S(1)}, u32[]{:S(2)}, u32[]{:S(2)}) %collective-permute-start.20) | collective-permute-done | bytes 65568 | tf_op jit(solution)/shard_map/ppermute | solution.py:19
  84.9 1.3 collective-permute-start.22
  86.2 1.2 collective-permute-start.23
  87.4 1.9 %collective-permute-start.24 = (bf16[128,256]{1,0:T(8,128)(2,1)S(1)}, bf16[128,256]{1,0:T(8,128)(2,1)}, u32[]{:S(2)}, u32[]{:S(2)}) collective-permute-start(bf16[128,256]{1,0:T(8,128)(2,1)S(1)} %shard_map.63.refs_0_), channel_id=1, source_target_pairs={{0,3},{1,2},{2,1},{3,0},{4,7},{5,6},{6,5},{7,4},{8,11},{9,10},{10,... | collective-permute-start | bytes 196616 | tf_op jit(solution)/shard_map/ppermute | solution.py:19
  89.3 2.8 %collective-permute-done.23.refs_2_ = bf16[128,256]{1,0:T(8,128)(2,1)} collective-permute-done((bf16[128,256]{1,0:T(8,128)(2,1)S(1)}, bf16[128,256]{1,0:T(8,128)(2,1)}, u32[]{:S(2)}, u32[]{:S(2)}) %collective-permute-start.23) | collective-permute-done | bytes 65568 | tf_op jit(solution)/shard_map/ppermute | solution.py:19
  92.2 1.4 %collective-permute-done.24.refs_3_ = bf16[128,256]{1,0:T(8,128)(2,1)} collective-permute-done((bf16[128,256]{1,0:T(8,128)(2,1)S(1)}, bf16[128,256]{1,0:T(8,128)(2,1)}, u32[]{:S(2)}, u32[]{:S(2)}) %collective-permute-start.24) | collective-permute-done | bytes 65568 | tf_op jit(solution)/shard_map/ppermute | solution.py:19
  93.6 1.8 %shard_map.64 = (f32[128,256]{1,0:T(8,128)S(1)}, bf16[128,256]{1,0:T(8,128)(2,1)S(1)}, bf16[128,256]{1,0:T(8,128)(2,1)S(1)}, bf16[128,256]{1,0:T(8,128)(2,1)S(1)}) custom-call(s32[3]{0:T(128)S(1)} %pad_add_fusion.idx_ref, bf16[512,1024]{1,0:T(8,128)(2,1)S(1)} %bitcast_multiply_fusion.own_ref, bf16[512,1024]{1,0:T(8,128)(2,1)} %collective-permute-done.15.par_ref, ...), custom_call_target="tpu_custom_call" | custom-call | flops 268435456 | bytes 2359308 | tf_op jit(solution)/shard_map/pallas_call | solution.py:33
  97.5 1.5 %collective-permute-start.27 = (bf16[128,256]{1,0:T(8,128)(2,1)S(1)}, bf16[128,256]{1,0:T(8,128)(2,1)S(1)}, u32[]{:S(2)}, u32[]{:S(2)}) collective-permute-start(bf16[128,256]{1,0:T(8,128)(2,1)S(1)} %get-tuple-element.50), channel_id=1, source_target_pairs={{0,24},{4,28},{8,16},{12,20},{16,8},{20,12},{24,0},{28,4},{1,25},{... | collective-permute-start | bytes 196616 | tf_op jit(solution)/shard_map/ppermute | solution.py:19
  100.5 2.1 %collective-permute-done.27.refs_2_ = bf16[128,256]{1,0:T(8,128)(2,1)S(1)} collective-permute-done((bf16[128,256]{1,0:T(8,128)(2,1)S(1)}, bf16[128,256]{1,0:T(8,128)(2,1)S(1)}, u32[]{:S(2)}, u32[]{:S(2)}) %collective-permute-start.27) | collective-permute-done | bytes 65568 | tf_op jit(solution)/shard_map/ppermute | solution.py:19
  103.5 2.4 %collective-permute-start.29 = (bf16[128,256]{1,0:T(8,128)(2,1)S(1)}, bf16[128,256]{1,0:T(8,128)(2,1)S(1)}, u32[]{:S(2)}, u32[]{:S(2)}) collective-permute-start(bf16[128,256]{1,0:T(8,128)(2,1)S(1)} %shard_map.65.refs_0_), channel_id=1, source_target_pairs={{0,2},{1,3},{2,0},{3,1},{4,6},{5,7},{6,4},{7,5},{8,10},{9,11},{10,... | collective-permute-start | bytes 196616 | tf_op jit(solution)/shard_map/ppermute | solution.py:19
  105.9 2.0 %collective-permute-start.30 = (bf16[128,256]{1,0:T(8,128)(2,1)S(1)}, bf16[128,256]{1,0:T(8,128)(2,1)S(1)}, u32[]{:S(2)}, u32[]{:S(2)}) collective-permute-start(bf16[128,256]{1,0:T(8,128)(2,1)S(1)} %shard_map.65.refs_0_), channel_id=1, source_target_pairs={{0,3},{1,2},{2,1},{3,0},{4,7},{5,6},{6,5},{7,4},{8,11},{9,10},{10,... | collective-permute-start | bytes 196616 | tf_op jit(solution)/shard_map/ppermute | solution.py:19
  108.8 3.2 %collective-permute-done.30.refs_3_ = bf16[128,256]{1,0:T(8,128)(2,1)S(1)} collective-permute-done((bf16[128,256]{1,0:T(8,128)(2,1)S(1)}, bf16[128,256]{1,0:T(8,128)(2,1)S(1)}, u32[]{:S(2)}, u32[]{:S(2)}) %collective-permute-start.30) | collective-permute-done | bytes 65568 | tf_op jit(solution)/shard_map/ppermute | solution.py:19
  111.9 1.7 %shard_map.66 = (f32[128,256]{1,0:T(8,128)S(1)}, bf16[128,256]{1,0:T(8,128)(2,1)S(1)}, bf16[128,256]{1,0:T(8,128)(2,1)S(1)}, bf16[128,256]{1,0:T(8,128)(2,1)S(1)}) custom-call(s32[3]{0:T(128)S(1)} %pad_add_fusion.idx_ref, bf16[512,1024]{1,0:T(8,128)(2,1)S(1)} %bitcast_multiply_fusion.1.own_ref, bf16[512,1024]{1,0:T(8,128)(2,1)} %collective-permute-done.8.par_ref, ...), custom_call_target="tpu_custom_call" | custom-call | flops 268435456 | bytes 2359308 | tf_op jit(solution)/shard_map/pallas_call | solution.py:33
  115.8 1.4 %collective-permute-start.33 = (bf16[128,256]{1,0:T(8,128)(2,1)S(1)}, bf16[128,256]{1,0:T(8,128)(2,1)S(1)}, u32[]{:S(2)}, u32[]{:S(2)}) collective-permute-start(bf16[128,256]{1,0:T(8,128)(2,1)S(1)} %get-tuple-element.54), channel_id=1, source_target_pairs={{0,24},{4,28},{8,16},{12,20},{16,8},{20,12},{24,0},{28,4},{1,25},{... | collective-permute-start | bytes 196616 | tf_op jit(solution)/shard_map/ppermute | solution.py:19
  118.9 2.1 %collective-permute-done.33.refs_2_ = bf16[128,256]{1,0:T(8,128)(2,1)S(1)} collective-permute-done((bf16[128,256]{1,0:T(8,128)(2,1)S(1)}, bf16[128,256]{1,0:T(8,128)(2,1)S(1)}, u32[]{:S(2)}, u32[]{:S(2)}) %collective-permute-start.33) | collective-permute-done | bytes 65568 | tf_op jit(solution)/shard_map/ppermute | solution.py:19
  121.8 2.5 %collective-permute-start.35 = (bf16[128,256]{1,0:T(8,128)(2,1)S(1)}, bf16[128,256]{1,0:T(8,128)(2,1)S(1)}, u32[]{:S(2)}, u32[]{:S(2)}) collective-permute-start(bf16[128,256]{1,0:T(8,128)(2,1)S(1)} %shard_map.67.refs_0_), channel_id=1, source_target_pairs={{0,2},{1,3},{2,0},{3,1},{4,6},{5,7},{6,4},{7,5},{8,10},{9,11},{10,... | collective-permute-start | bytes 196616 | tf_op jit(solution)/shard_map/ppermute | solution.py:19
  124.3 1.9 %collective-permute-start.36 = (bf16[128,256]{1,0:T(8,128)(2,1)S(1)}, bf16[128,256]{1,0:T(8,128)(2,1)S(1)}, u32[]{:S(2)}, u32[]{:S(2)}) collective-permute-start(bf16[128,256]{1,0:T(8,128)(2,1)S(1)} %shard_map.67.refs_0_), channel_id=1, source_target_pairs={{0,3},{1,2},{2,1},{3,0},{4,7},{5,6},{6,5},{7,4},{8,11},{9,10},{10,... | collective-permute-start | bytes 196616 | tf_op jit(solution)/shard_map/ppermute | solution.py:19
  127.0 3.3 %collective-permute-done.36.refs_3_ = bf16[128,256]{1,0:T(8,128)(2,1)S(1)} collective-permute-done((bf16[128,256]{1,0:T(8,128)(2,1)S(1)}, bf16[128,256]{1,0:T(8,128)(2,1)S(1)}, u32[]{:S(2)}, u32[]{:S(2)}) %collective-permute-start.36) | collective-permute-done | bytes 65568 | tf_op jit(solution)/shard_map/ppermute | solution.py:19
  130.3 1.8 %shard_map.68 = (f32[128,256]{1,0:T(8,128)S(1)}, bf16[128,256]{1,0:T(8,128)(2,1)S(1)}, bf16[128,256]{1,0:T(8,128)(2,1)S(1)}, bf16[128,256]{1,0:T(8,128)(2,1)S(1)}) custom-call(s32[3]{0:T(128)S(1)} %pad_add_fusion.idx_ref, bf16[512,1024]{1,0:T(8,128)(2,1)S(1)} %bitcast_multiply_fusion.2.own_ref, bf16[512,1024]{1,0:T(8,128)(2,1)} %collective-permute-done.1.par_ref, ...), custom_call_target="tpu_custom_call" | custom-call | flops 268435456 | bytes 2359308 | tf_op jit(solution)/shard_map/pallas_call | solution.py:33
  134.2 1.5 %collective-permute-start.39 = (bf16[128,256]{1,0:T(8,128)(2,1)S(1)}, bf16[128,256]{1,0:T(8,128)(2,1)S(1)}, u32[]{:S(2)}, u32[]{:S(2)}) collective-permute-start(bf16[128,256]{1,0:T(8,128)(2,1)S(1)} %get-tuple-element.58), channel_id=1, source_target_pairs={{0,24},{4,28},{8,16},{12,20},{16,8},{20,12},{24,0},{28,4},{1,25},{... | collective-permute-start | bytes 196616 | tf_op jit(solution)/shard_map/ppermute | solution.py:19
  137.2 2.1 %collective-permute-done.39.refs_2_ = bf16[128,256]{1,0:T(8,128)(2,1)S(1)} collective-permute-done((bf16[128,256]{1,0:T(8,128)(2,1)S(1)}, bf16[128,256]{1,0:T(8,128)(2,1)S(1)}, u32[]{:S(2)}, u32[]{:S(2)}) %collective-permute-start.39) | collective-permute-done | bytes 65568 | tf_op jit(solution)/shard_map/ppermute | solution.py:19
  (121 shorter events, 36.8 us)
Async XLA Ops:
  3.7 19.1 %all-to-all-start = ((bf16[32,48,128]{2,1,0:T(8,128)(2,1)}), bf16[32,48,128]{2,1,0:T(8,128)(2,1)S(1)}, u32[]{:S(2)}, u32[]{:S(2)}) async-start(bf16[32,48,128]{2,1,0:T(8,128)(2,1)} %shard_map.55), calls=%async_computation | async-start | bytes 786432 | tf_op jit(solution)/shard_map/all_to_all | solution.py:235
  13.6 21.8 %collective-permute-start.1 = (bf16[512,1024]{1,0:T(8,128)(2,1)S(1)}, bf16[512,1024]{1,0:T(8,128)(2,1)}, u32[]{:S(2)}, u32[]{:S(2)}) collective-permute-start(bf16[512,1024]{1,0:T(8,128)(2,1)S(1)} %bitcast_multiply_fusion.2.own_ref), channel_id=1, source_target_pairs={{0,4},{4,0},{8,12},{12,8},{16,20},{20,16},{24,28},{28,24},{1,5},{5... | collective-permute-start | bytes 3145736 | tf_op jit(solution)/shard_map/ppermute | solution.py:19
  14.4 36.3 %collective-permute-start.8 = (bf16[512,1024]{1,0:T(8,128)(2,1)S(1)}, bf16[512,1024]{1,0:T(8,128)(2,1)}, u32[]{:S(2)}, u32[]{:S(2)}) collective-permute-start(bf16[512,1024]{1,0:T(8,128)(2,1)S(1)} %bitcast_multiply_fusion.1.own_ref), channel_id=1, source_target_pairs={{0,4},{4,0},{8,12},{12,8},{16,20},{20,16},{24,28},{28,24},{1,5},{5... | collective-permute-start | bytes 3145736 | tf_op jit(solution)/shard_map/ppermute | solution.py:19
  15.2 54.2 %collective-permute-start.15 = (bf16[512,1024]{1,0:T(8,128)(2,1)S(1)}, bf16[512,1024]{1,0:T(8,128)(2,1)}, u32[]{:S(2)}, u32[]{:S(2)}) collective-permute-start(bf16[512,1024]{1,0:T(8,128)(2,1)S(1)} %bitcast_multiply_fusion.own_ref), channel_id=1, source_target_pairs={{0,4},{4,0},{8,12},{12,8},{16,20},{20,16},{24,28},{28,24},{1,5},{5... | collective-permute-start | bytes 3145736 | tf_op jit(solution)/shard_map/ppermute | solution.py:19
  15.5 2.7 %collective-permute-start = (bf16[4,128,128]{2,1,0:T(8,128)(2,1)S(1)}, bf16[4,128,128]{2,1,0:T(8,128)(2,1)S(1)}, u32[]{:S(2)}, u32[]{:S(2)}) collective-permute-start(bf16[4,128,128]{2,1,0:T(8,128)(2,1)S(1)} %bitcast.89), channel_id=1, source_target_pairs={{0,4},{4,0},{8,12},{12,8},{16,20},{20,16},{24,28},{28,24},{1,5},{5... | collective-permute-start | bytes 393224 | tf_op jit(solution)/shard_map/ppermute | solution.py:19
  25.4 4.8 %collective-permute-start.2 = (bf16[128,256]{1,0:T(8,128)(2,1)S(1)}, bf16[128,256]{1,0:T(8,128)(2,1)S(1)}, u32[]{:S(2)}, u32[]{:S(2)}) collective-permute-start(bf16[128,256]{1,0:T(8,128)(2,1)S(1)} %shard_map.56.refs_0_.solved_ref), channel_id=1, source_target_pairs={{0,8},{4,12},{8,0},{12,4},{16,24},{20,28},{24,16},{28,20},{1,9},{5... | collective-permute-start | bytes 196616 | tf_op jit(solution)/shard_map/ppermute | solution.py:19
  27.0 5.0 %collective-permute-start.3 = (bf16[128,256]{1,0:T(8,128)(2,1)S(1)}, bf16[128,256]{1,0:T(8,128)(2,1)S(1)}, u32[]{:S(2)}, u32[]{:S(2)}) collective-permute-start(bf16[128,256]{1,0:T(8,128)(2,1)S(1)} %shard_map.56.refs_0_.solved_ref), channel_id=1, source_target_pairs={{0,16},{4,20},{8,24},{12,28},{16,0},{20,4},{24,8},{28,12},{1,17},{... | collective-permute-start | bytes 196616 | tf_op jit(solution)/shard_map/ppermute | solution.py:19
  30.2 5.2 %collective-permute-start.4 = (bf16[128,256]{1,0:T(8,128)(2,1)S(1)}, bf16[128,256]{1,0:T(8,128)(2,1)S(1)}, u32[]{:S(2)}, u32[]{:S(2)}) collective-permute-start(bf16[128,256]{1,0:T(8,128)(2,1)S(1)} %shard_map.56.refs_0_.solved_ref), channel_id=1, source_target_pairs={{0,24},{4,28},{8,16},{12,20},{16,8},{20,12},{24,0},{28,4},{1,25},{... | collective-permute-start | bytes 196616 | tf_op jit(solution)/shard_map/ppermute | solution.py:19
  37.6 46.4 %copy-start.15 = (bf16[128,128]{1,0:T(8,128)(2,1)S(1)}, bf16[128,128]{1,0:T(8,128)(2,1)}, u32[]{:S(2)}) copy-start(bf16[128,128]{1,0:T(8,128)(2,1)} %get-tuple-element.68.own_ref) | copy-start | bytes 98308
  37.6 46.4 %copy-start.16 = (bf16[128,128]{1,0:T(8,128)(2,1)S(1)}, bf16[128,128]{1,0:T(8,128)(2,1)}, u32[]{:S(2)}) copy-start(bf16[128,128]{1,0:T(8,128)(2,1)} %get-tuple-element.63.par_ref) | copy-start | bytes 98308
  37.6 5.7 %collective-permute-start.5 = (bf16[128,256]{1,0:T(8,128)(2,1)S(1)}, bf16[128,256]{1,0:T(8,128)(2,1)S(1)}, u32[]{:S(2)}, u32[]{:S(2)}) collective-permute-start(bf16[128,256]{1,0:T(8,128)(2,1)S(1)} %get-tuple-element.34), channel_id=1, source_target_pairs={{0,1},{1,0},{2,3},{3,2},{4,5},{5,4},{6,7},{7,6},{8,9},{9,8},{10,11... | collective-permute-start | bytes 196616 | tf_op jit(solution)/shard_map/ppermute | solution.py:19
  39.4 5.5 %collective-permute-start.6 = (bf16[128,256]{1,0:T(8,128)(2,1)S(1)}, bf16[128,256]{1,0:T(8,128)(2,1)S(1)}, u32[]{:S(2)}, u32[]{:S(2)}) collective-permute-start(bf16[128,256]{1,0:T(8,128)(2,1)S(1)} %get-tuple-element.35), channel_id=1, source_target_pairs={{0,2},{1,3},{2,0},{3,1},{4,6},{5,7},{6,4},{7,5},{8,10},{9,11},{10,... | collective-permute-start | bytes 196616 | tf_op jit(solution)/shard_map/ppermute | solution.py:19
  40.3 6.1 %collective-permute-start.7 = (bf16[128,256]{1,0:T(8,128)(2,1)S(1)}, bf16[128,256]{1,0:T(8,128)(2,1)S(1)}, u32[]{:S(2)}, u32[]{:S(2)}) collective-permute-start(bf16[128,256]{1,0:T(8,128)(2,1)S(1)} %get-tuple-element.36), channel_id=1, source_target_pairs={{0,3},{1,2},{2,1},{3,0},{4,7},{5,6},{6,5},{7,4},{8,11},{9,10},{10,... | collective-permute-start | bytes 196616 | tf_op jit(solution)/shard_map/ppermute | solution.py:19
  47.1 4.3 %collective-permute-start.10 = (bf16[128,256]{1,0:T(8,128)(2,1)S(1)}, bf16[128,256]{1,0:T(8,128)(2,1)S(1)}, u32[]{:S(2)}, u32[]{:S(2)}) collective-permute-start(bf16[128,256]{1,0:T(8,128)(2,1)S(1)} %shard_map.59.refs_0_.solved_ref), channel_id=1, source_target_pairs={{0,16},{4,20},{8,24},{12,28},{16,0},{20,4},{24,8},{28,12},{1,17},{... | collective-permute-start | bytes 196616 | tf_op jit(solution)/shard_map/ppermute | solution.py:19
  48.6 5.2 %collective-permute-start.11 = (bf16[128,256]{1,0:T(8,128)(2,1)S(1)}, bf16[128,256]{1,0:T(8,128)(2,1)S(1)}, u32[]{:S(2)}, u32[]{:S(2)}) collective-permute-start(bf16[128,256]{1,0:T(8,128)(2,1)S(1)} %shard_map.59.refs_0_.solved_ref), channel_id=1, source_target_pairs={{0,24},{4,28},{8,16},{12,20},{16,8},{20,12},{24,0},{28,4},{1,25},{... | collective-permute-start | bytes 196616 | tf_op jit(solution)/shard_map/ppermute | solution.py:19
  50.1 4.3 %collective-permute-start.9 = (bf16[128,256]{1,0:T(8,128)(2,1)S(1)}, bf16[128,256]{1,0:T(8,128)(2,1)S(1)}, u32[]{:S(2)}, u32[]{:S(2)}) collective-permute-start(bf16[128,256]{1,0:T(8,128)(2,1)S(1)} %shard_map.59.refs_0_.solved_ref), channel_id=1, source_target_pairs={{0,8},{4,12},{8,0},{12,4},{16,24},{20,28},{24,16},{28,20},{1,9},{5... | collective-permute-start | bytes 196616 | tf_op jit(solution)/shard_map/ppermute | solution.py:19
  56.5 46.1 %copy-start.12 = (bf16[128,128]{1,0:T(8,128)(2,1)S(1)}, bf16[128,128]{1,0:T(8,128)(2,1)}, u32[]{:S(2)}) copy-start(bf16[128,128]{1,0:T(8,128)(2,1)} %get-tuple-element.69.own_ref) | copy-start | bytes 98308
  56.5 4.5 %collective-permute-start.12 = (bf16[128,256]{1,0:T(8,128)(2,1)S(1)}, bf16[128,256]{1,0:T(8,128)(2,1)S(1)}, u32[]{:S(2)}, u32[]{:S(2)}) collective-permute-start(bf16[128,256]{1,0:T(8,128)(2,1)S(1)} %get-tuple-element.39), channel_id=1, source_target_pairs={{0,1},{1,0},{2,3},{3,2},{4,5},{5,4},{6,7},{7,6},{8,9},{9,8},{10,11... | collective-permute-start | bytes 196616 | tf_op jit(solution)/shard_map/ppermute | solution.py:19
  56.6 5.2 %collective-permute-start.13 = (bf16[128,256]{1,0:T(8,128)(2,1)S(1)}, bf16[128,256]{1,0:T(8,128)(2,1)S(1)}, u32[]{:S(2)}, u32[]{:S(2)}) collective-permute-start(bf16[128,256]{1,0:T(8,128)(2,1)S(1)} %get-tuple-element.40), channel_id=1, source_target_pairs={{0,2},{1,3},{2,0},{3,1},{4,6},{5,7},{6,4},{7,5},{8,10},{9,11},{10,... | collective-permute-start | bytes 196616 | tf_op jit(solution)/shard_map/ppermute | solution.py:19
  59.1 6.1 %collective-permute-start.14 = (bf16[128,256]{1,0:T(8,128)(2,1)S(1)}, bf16[128,256]{1,0:T(8,128)(2,1)S(1)}, u32[]{:S(2)}, u32[]{:S(2)}) collective-permute-start(bf16[128,256]{1,0:T(8,128)(2,1)S(1)} %get-tuple-element.41), channel_id=1, source_target_pairs={{0,3},{1,2},{2,1},{3,0},{4,7},{5,6},{6,5},{7,4},{8,11},{9,10},{10,... | collective-permute-start | bytes 196616 | tf_op jit(solution)/shard_map/ppermute | solution.py:19
  65.9 4.3 %collective-permute-start.16 = (bf16[128,256]{1,0:T(8,128)(2,1)S(1)}, bf16[128,256]{1,0:T(8,128)(2,1)S(1)}, u32[]{:S(2)}, u32[]{:S(2)}) collective-permute-start(bf16[128,256]{1,0:T(8,128)(2,1)S(1)} %shard_map.61.refs_0_.solved_ref), channel_id=1, source_target_pairs={{0,8},{4,12},{8,0},{12,4},{16,24},{20,28},{24,16},{28,20},{1,9},{5... | collective-permute-start | bytes 196616 | tf_op jit(solution)/shard_map/ppermute | solution.py:19
  66.6 4.3 %collective-permute-start.17 = (bf16[128,256]{1,0:T(8,128)(2,1)S(1)}, bf16[128,256]{1,0:T(8,128)(2,1)S(1)}, u32[]{:S(2)}, u32[]{:S(2)}) collective-permute-start(bf16[128,256]{1,0:T(8,128)(2,1)S(1)} %shard_map.61.refs_0_.solved_ref), channel_id=1, source_target_pairs={{0,16},{4,20},{8,24},{12,28},{16,0},{20,4},{24,8},{28,12},{1,17},{... | collective-permute-start | bytes 196616 | tf_op jit(solution)/shard_map/ppermute | solution.py:19
  68.0 5.2 %collective-permute-start.18 = (bf16[128,256]{1,0:T(8,128)(2,1)S(1)}, bf16[128,256]{1,0:T(8,128)(2,1)S(1)}, u32[]{:S(2)}, u32[]{:S(2)}) collective-permute-start(bf16[128,256]{1,0:T(8,128)(2,1)S(1)} %shard_map.61.refs_0_.solved_ref), channel_id=1, source_target_pairs={{0,24},{4,28},{8,16},{12,20},{16,8},{20,12},{24,0},{28,4},{1,25},{... | collective-permute-start | bytes 196616 | tf_op jit(solution)/shard_map/ppermute | solution.py:19
  75.3 5.0 %collective-permute-start.19 = (bf16[128,256]{1,0:T(8,128)(2,1)S(1)}, bf16[128,256]{1,0:T(8,128)(2,1)S(1)}, u32[]{:S(2)}, u32[]{:S(2)}) collective-permute-start(bf16[128,256]{1,0:T(8,128)(2,1)S(1)} %get-tuple-element.44), channel_id=1, source_target_pairs={{0,1},{1,0},{2,3},{3,2},{4,5},{5,4},{6,7},{7,6},{8,9},{9,8},{10,11... | collective-permute-start | bytes 196616 | tf_op jit(solution)/shard_map/ppermute | solution.py:19
  75.4 8.6 %collective-permute-start.20 = (bf16[128,256]{1,0:T(8,128)(2,1)S(1)}, bf16[128,256]{1,0:T(8,128)(2,1)S(1)}, u32[]{:S(2)}, u32[]{:S(2)}) collective-permute-start(bf16[128,256]{1,0:T(8,128)(2,1)S(1)} %get-tuple-element.45), channel_id=1, source_target_pairs={{0,2},{1,3},{2,0},{3,1},{4,6},{5,7},{6,4},{7,5},{8,10},{9,11},{10,... | collective-permute-start | bytes 196616 | tf_op jit(solution)/shard_map/ppermute | solution.py:19
  77.8 6.2 %collective-permute-start.21 = (bf16[128,256]{1,0:T(8,128)(2,1)S(1)}, bf16[128,256]{1,0:T(8,128)(2,1)S(1)}, u32[]{:S(2)}, u32[]{:S(2)}) collective-permute-start(bf16[128,256]{1,0:T(8,128)(2,1)S(1)} %get-tuple-element.46), channel_id=1, source_target_pairs={{0,3},{1,2},{2,1},{3,0},{4,7},{5,6},{6,5},{7,4},{8,11},{9,10},{10,... | collective-permute-start | bytes 196616 | tf_op jit(solution)/shard_map/ppermute | solution.py:19
  84.9 4.5 %collective-permute-start.22 = (bf16[128,256]{1,0:T(8,128)(2,1)S(1)}, bf16[128,256]{1,0:T(8,128)(2,1)S(1)}, u32[]{:S(2)}, u32[]{:S(2)}) collective-permute-start(bf16[128,256]{1,0:T(8,128)(2,1)S(1)} %shard_map.63.refs_0_), channel_id=1, source_target_pairs={{0,1},{1,0},{2,3},{3,2},{4,5},{5,4},{6,7},{7,6},{8,9},{9,8},{10,11... | collective-permute-start | bytes 196616 | tf_op jit(solution)/shard_map/ppermute | solution.py:19
  86.2 6.0 %collective-permute-start.23 = (bf16[128,256]{1,0:T(8,128)(2,1)S(1)}, bf16[128,256]{1,0:T(8,128)(2,1)}, u32[]{:S(2)}, u32[]{:S(2)}) collective-permute-start(bf16[128,256]{1,0:T(8,128)(2,1)S(1)} %shard_map.63.refs_0_), channel_id=1, source_target_pairs={{0,2},{1,3},{2,0},{3,1},{4,6},{5,7},{6,4},{7,5},{8,10},{9,11},{10,... | collective-permute-start | bytes 196616 | tf_op jit(solution)/shard_map/ppermute | solution.py:19
  87.4 6.2 %collective-permute-start.24 = (bf16[128,256]{1,0:T(8,128)(2,1)S(1)}, bf16[128,256]{1,0:T(8,128)(2,1)}, u32[]{:S(2)}, u32[]{:S(2)}) collective-permute-start(bf16[128,256]{1,0:T(8,128)(2,1)S(1)} %shard_map.63.refs_0_), channel_id=1, source_target_pairs={{0,3},{1,2},{2,1},{3,0},{4,7},{5,6},{6,5},{7,4},{8,11},{9,10},{10,... | collective-permute-start | bytes 196616 | tf_op jit(solution)/shard_map/ppermute | solution.py:19
  95.4 4.3 %collective-permute-start.25 = (bf16[128,256]{1,0:T(8,128)(2,1)S(1)}, bf16[128,256]{1,0:T(8,128)(2,1)S(1)}, u32[]{:S(2)}, u32[]{:S(2)}) collective-permute-start(bf16[128,256]{1,0:T(8,128)(2,1)S(1)} %get-tuple-element.48), channel_id=1, source_target_pairs={{0,8},{4,12},{8,0},{12,4},{16,24},{20,28},{24,16},{28,20},{1,9},{5... | collective-permute-start | bytes 196616 | tf_op jit(solution)/shard_map/ppermute | solution.py:19
  96.3 4.3 %collective-permute-start.26 = (bf16[128,256]{1,0:T(8,128)(2,1)S(1)}, bf16[128,256]{1,0:T(8,128)(2,1)S(1)}, u32[]{:S(2)}, u32[]{:S(2)}) collective-permute-start(bf16[128,256]{1,0:T(8,128)(2,1)S(1)} %get-tuple-element.49), channel_id=1, source_target_pairs={{0,16},{4,20},{8,24},{12,28},{16,0},{20,4},{24,8},{28,12},{1,17},{... | collective-permute-start | bytes 196616 | tf_op jit(solution)/shard_map/ppermute | solution.py:19
  97.5 5.2 %collective-permute-start.27 = (bf16[128,256]{1,0:T(8,128)(2,1)S(1)}, bf16[128,256]{1,0:T(8,128)(2,1)S(1)}, u32[]{:S(2)}, u32[]{:S(2)}) collective-permute-start(bf16[128,256]{1,0:T(8,128)(2,1)S(1)} %get-tuple-element.50), channel_id=1, source_target_pairs={{0,24},{4,28},{8,16},{12,20},{16,8},{20,12},{24,0},{28,4},{1,25},{... | collective-permute-start | bytes 196616 | tf_op jit(solution)/shard_map/ppermute | solution.py:19
  98.9 18.3 %collective-permute-start.43 = (bf16[128,128]{0,1:T(8,128)(2,1)S(1)}, bf16[128,128]{0,1:T(8,128)(2,1)S(1)}, u32[]{:S(2)}, u32[]{:S(2)}) collective-permute-start(bf16[128,128]{0,1:T(8,128)(2,1)S(1)} %get-tuple-element.77), channel_id=1, source_target_pairs={{0,4},{4,0},{8,12},{12,8},{16,20},{20,16},{24,28},{28,24},{1,5},{5... | collective-permute-start | bytes 98312 | tf_op jit(solution)/shard_map/ppermute | solution.py:19
  103.4 4.7 %collective-permute-start.28 = (bf16[128,256]{1,0:T(8,128)(2,1)S(1)}, bf16[128,256]{1,0:T(8,128)(2,1)S(1)}, u32[]{:S(2)}, u32[]{:S(2)}) collective-permute-start(bf16[128,256]{1,0:T(8,128)(2,1)S(1)} %shard_map.65.refs_0_), channel_id=1, source_target_pairs={{0,1},{1,0},{2,3},{3,2},{4,5},{5,4},{6,7},{7,6},{8,9},{9,8},{10,11... | collective-permute-start | bytes 196616 | tf_op jit(solution)/shard_map/ppermute | solution.py:19
  103.5 5.3 %collective-permute-start.29 = (bf16[128,256]{1,0:T(8,128)(2,1)S(1)}, bf16[128,256]{1,0:T(8,128)(2,1)S(1)}, u32[]{:S(2)}, u32[]{:S(2)}) collective-permute-start(bf16[128,256]{1,0:T(8,128)(2,1)S(1)} %shard_map.65.refs_0_), channel_id=1, source_target_pairs={{0,2},{1,3},{2,0},{3,1},{4,6},{5,7},{6,4},{7,5},{8,10},{9,11},{10,... | collective-permute-start | bytes 196616 | tf_op jit(solution)/shard_map/ppermute | solution.py:19
  105.9 6.1 %collective-permute-start.30 = (bf16[128,256]{1,0:T(8,128)(2,1)S(1)}, bf16[128,256]{1,0:T(8,128)(2,1)S(1)}, u32[]{:S(2)}, u32[]{:S(2)}) collective-permute-start(bf16[128,256]{1,0:T(8,128)(2,1)S(1)} %shard_map.65.refs_0_), channel_id=1, source_target_pairs={{0,3},{1,2},{2,1},{3,0},{4,7},{5,6},{6,5},{7,4},{8,11},{9,10},{10,... | collective-permute-start | bytes 196616 | tf_op jit(solution)/shard_map/ppermute | solution.py:19
  107.8 18.3 %collective-permute-start.42 = (bf16[128,128]{0,1:T(8,128)(2,1)S(1)}, bf16[128,128]{0,1:T(8,128)(2,1)S(1)}, u32[]{:S(2)}, u32[]{:S(2)}) collective-permute-start(bf16[128,128]{0,1:T(8,128)(2,1)S(1)} %get-tuple-element.75), channel_id=1, source_target_pairs={{0,4},{4,0},{8,12},{12,8},{16,20},{20,16},{24,28},{28,24},{1,5},{5... | collective-permute-start | bytes 98312 | tf_op jit(solution)/shard_map/ppermute | solution.py:19
  113.7 4.3 %collective-permute-start.31 = (bf16[128,256]{1,0:T(8,128)(2,1)S(1)}, bf16[128,256]{1,0:T(8,128)(2,1)S(1)}, u32[]{:S(2)}, u32[]{:S(2)}) collective-permute-start(bf16[128,256]{1,0:T(8,128)(2,1)S(1)} %get-tuple-element.52), channel_id=1, source_target_pairs={{0,8},{4,12},{8,0},{12,4},{16,24},{20,28},{24,16},{28,20},{1,9},{5... | collective-permute-start | bytes 196616 | tf_op jit(solution)/shard_map/ppermute | solution.py:19
  114.6 4.3 %collective-permute-start.32 = (bf16[128,256]{1,0:T(8,128)(2,1)S(1)}, bf16[128,256]{1,0:T(8,128)(2,1)S(1)}, u32[]{:S(2)}, u32[]{:S(2)}) collective-permute-start(bf16[128,256]{1,0:T(8,128)(2,1)S(1)} %get-tuple-element.53), channel_id=1, source_target_pairs={{0,16},{4,20},{8,24},{12,28},{16,0},{20,4},{24,8},{28,12},{1,17},{... | collective-permute-start | bytes 196616 | tf_op jit(solution)/shard_map/ppermute | solution.py:19
  115.8 5.2 %collective-permute-start.33 = (bf16[128,256]{1,0:T(8,128)(2,1)S(1)}, bf16[128,256]{1,0:T(8,128)(2,1)S(1)}, u32[]{:S(2)}, u32[]{:S(2)}) collective-permute-start(bf16[128,256]{1,0:T(8,128)(2,1)S(1)} %get-tuple-element.54), channel_id=1, source_target_pairs={{0,24},{4,28},{8,16},{12,20},{16,8},{20,12},{24,0},{28,4},{1,25},{... | collective-permute-start | bytes 196616 | tf_op jit(solution)/shard_map/ppermute | solution.py:19
  121.7 4.5 %collective-permute-start.34 = (bf16[128,256]{1,0:T(8,128)(2,1)S(1)}, bf16[128,256]{1,0:T(8,128)(2,1)S(1)}, u32[]{:S(2)}, u32[]{:S(2)}) collective-permute-start(bf16[128,256]{1,0:T(8,128)(2,1)S(1)} %shard_map.67.refs_0_), channel_id=1, source_target_pairs={{0,1},{1,0},{2,3},{3,2},{4,5},{5,4},{6,7},{7,6},{8,9},{9,8},{10,11... | collective-permute-start | bytes 196616 | tf_op jit(solution)/shard_map/ppermute | solution.py:19
  121.8 5.2 %collective-permute-start.35 = (bf16[128,256]{1,0:T(8,128)(2,1)S(1)}, bf16[128,256]{1,0:T(8,128)(2,1)S(1)}, u32[]{:S(2)}, u32[]{:S(2)}) collective-permute-start(bf16[128,256]{1,0:T(8,128)(2,1)S(1)} %shard_map.67.refs_0_), channel_id=1, source_target_pairs={{0,2},{1,3},{2,0},{3,1},{4,6},{5,7},{6,4},{7,5},{8,10},{9,11},{10,... | collective-permute-start | bytes 196616 | tf_op jit(solution)/shard_map/ppermute | solution.py:19
  124.3 6.1 %collective-permute-start.36 = (bf16[128,256]{1,0:T(8,128)(2,1)S(1)}, bf16[128,256]{1,0:T(8,128)(2,1)S(1)}, u32[]{:S(2)}, u32[]{:S(2)}) collective-permute-start(bf16[128,256]{1,0:T(8,128)(2,1)S(1)} %shard_map.67.refs_0_), channel_id=1, source_target_pairs={{0,3},{1,2},{2,1},{3,0},{4,7},{5,6},{6,5},{7,4},{8,11},{9,10},{10,... | collective-permute-start | bytes 196616 | tf_op jit(solution)/shard_map/ppermute | solution.py:19
  132.1 4.3 %collective-permute-start.37 = (bf16[128,256]{1,0:T(8,128)(2,1)S(1)}, bf16[128,256]{1,0:T(8,128)(2,1)S(1)}, u32[]{:S(2)}, u32[]{:S(2)}) collective-permute-start(bf16[128,256]{1,0:T(8,128)(2,1)S(1)} %get-tuple-element.56), channel_id=1, source_target_pairs={{0,8},{4,12},{8,0},{12,4},{16,24},{20,28},{24,16},{28,20},{1,9},{5... | collective-permute-start | bytes 196616 | tf_op jit(solution)/shard_map/ppermute | solution.py:19
  133.0 4.3 %collective-permute-start.38 = (bf16[128,256]{1,0:T(8,128)(2,1)S(1)}, bf16[128,256]{1,0:T(8,128)(2,1)S(1)}, u32[]{:S(2)}, u32[]{:S(2)}) collective-permute-start(bf16[128,256]{1,0:T(8,128)(2,1)S(1)} %get-tuple-element.57), channel_id=1, source_target_pairs={{0,16},{4,20},{8,24},{12,28},{16,0},{20,4},{24,8},{28,12},{1,17},{... | collective-permute-start | bytes 196616 | tf_op jit(solution)/shard_map/ppermute | solution.py:19
  134.2 5.2 %collective-permute-start.39 = (bf16[128,256]{1,0:T(8,128)(2,1)S(1)}, bf16[128,256]{1,0:T(8,128)(2,1)S(1)}, u32[]{:S(2)}, u32[]{:S(2)}) collective-permute-start(bf16[128,256]{1,0:T(8,128)(2,1)S(1)} %get-tuple-element.58), channel_id=1, source_target_pairs={{0,24},{4,28},{8,16},{12,20},{16,8},{20,12},{24,0},{28,4},{1,25},{... | collective-permute-start | bytes 196616 | tf_op jit(solution)/shard_map/ppermute | solution.py:19
  135.7 4.5 %collective-permute-start.41 = (bf16[128,128]{0,1:T(8,128)(2,1)S(1)}, bf16[128,128]{0,1:T(8,128)(2,1)S(1)}, u32[]{:S(2)}, u32[]{:S(2)}) collective-permute-start(bf16[128,128]{0,1:T(8,128)(2,1)S(1)} %get-tuple-element.73), channel_id=1, source_target_pairs={{0,4},{4,0},{8,12},{12,8},{16,20},{20,16},{24,28},{28,24},{1,5},{5... | collective-permute-start | bytes 98312 | tf_op jit(solution)/shard_map/ppermute | solution.py:19
  140.1 1.3 collective-permute-start.40
  (17 other events, 397.8 us)

commit v3 on v2

--- a/solution.py
+++ b/solution.py
@@ -10,6 +10,7 @@
 B = 128
 NLEV = 4
 LANES = 128
+VMEM_BYTES = 16 * 1024 * 1024
 F32 = jnp.float32
 BF16 = jnp.bfloat16
 
@@ -21,9 +22,7 @@
 
 def call(body, out_shape, args, scratch=(), flops=0):
     moved = sum(a.size * a.dtype.itemsize for a in args)
-    in_specs = [
-        pl.BlockSpec(memory_space=pltpu.SMEM if i == 0 else pltpu.VMEM) for i in range(len(args))
-    ]
+    in_specs = [pl.BlockSpec(memory_space=pltpu.VMEM) for _ in args]
     several = isinstance(out_shape, (list, tuple))
     out_specs = (
         [pl.BlockSpec(memory_space=pltpu.VMEM) for _ in out_shape]
@@ -36,7 +35,7 @@
         in_specs=in_specs,
         out_specs=out_specs,
         scratch_shapes=list(scratch),
-        compiler_params=pltpu.CompilerParams(vmem_limit_bytes=40 * 1024 * 1024),
+        compiler_params=pltpu.CompilerParams(vmem_limit_bytes=VMEM_BYTES),
         cost_estimate=pl.CostEstimate(flops=flops, bytes_accessed=moved, transcendentals=0),
     )(*args)
 
@@ -45,12 +44,39 @@
     return pl.ds(pl.multiple_of(start * step, step), size)
 
 
-def pack_body(rows, cols, chunk_rows, total_rows, idx_ref, rhs_ref, dest_ref, out_ref):
+def fetch_body(own_ref, par_ref, after_ref, own_out, par_out, sems):
+    half = own_ref.shape[0] // 2
+    copies = []
+    for k, (source, target) in enumerate(((own_ref, own_out), (par_ref, par_out))):
+        for h in range(2):
+            at = pl.ds(h * half, half)
+            copies.append(pltpu.make_async_copy(source.at[at], target.at[at], sems.at[2 * k + h]))
+    for copy in copies:
+        copy.start()
+    for copy in copies:
+        copy.wait()
+
+
+def fetch(own, par, after):
+    return pl.pallas_call(
+        fetch_body,
+        out_shape=[pltpu.VMEM(own.shape, own.dtype), pltpu.VMEM(par.shape, par.dtype)],
+        in_specs=[pl.BlockSpec(memory_space=pl.ANY)] * 3,
+        out_specs=[pl.BlockSpec(memory_space=pltpu.VMEM)] * 2,
+        scratch_shapes=[pltpu.SemaphoreType.DMA((4,))],
+        compiler_params=pltpu.CompilerParams(vmem_limit_bytes=VMEM_BYTES),
+        cost_estimate=pl.CostEstimate(
+            flops=0, bytes_accessed=4 * own.size * own.dtype.itemsize, transcendentals=0
+        ),
+    )(own, par, after)
+
+
+def pack_body(rows, cols, chunk_rows, total_rows, rhs_ref, dest_ref, out_ref):
     local_rows = rhs_ref.shape[0]
     supernodes = rows * cols
     pairs = supernodes // 2
     shards_per_line = LANES // chunk_rows
-    me = idx_ref[2]
+    me = lax.axis_index("row") * cols + lax.axis_index("col")
     dest = dest_ref[...]
     supernode = (dest // B) % supernodes
     level = dest // (supernodes * B)
@@ -129,27 +155,28 @@
     return lax.dot_general(left, right, (((1,), (1,)), ((), ())), preferred_element_type=F32)
 
 
-def apply_diag(product, parity, residual, own_ref, par_ref, out_ref):
+def apply_diag(product, level, residual, own_ref, par_ref, out_ref):
+    parity = lax.axis_index("row") % 2
     for at, factor in ((parity, own_ref), (1 - parity, par_ref)):
         lanes = aligned(at, B, B)
-        out_ref[:, lanes] = product(residual[:, lanes], factor[...]).astype(BF16)
-
-
-def first_body(chunk_rows, idx_ref, arrived_ref, own_ref, par_ref, out_ref, residual):
+        out_ref[:, lanes] = product(residual[:, lanes], factor[level]).astype(BF16)
+
+
+def first_body(chunk_rows, arrived_ref, own_ref, par_ref, out_ref, residual):
     residual[...] = place_rows(arrived_ref, 0, 2 * B, chunk_rows)
-    apply_diag(times_t, idx_ref[0] % 2, residual, own_ref, par_ref, out_ref)
-
-
-def rest_body(chunk_rows, idx_ref, arrived_ref, *outs):
+    apply_diag(times_t, 0, residual, own_ref, par_ref, out_ref)
+
+
+def rest_body(chunk_rows, arrived_ref, *outs):
     placed = place_rows(arrived_ref, 2 * B, len(outs) * 2 * B, chunk_rows)
     for k, out in enumerate(outs):
         out[...] = placed[:, k * 2 * B : (k + 1) * 2 * B]
 
 
-def down_body(idx_ref, own_ref, par_ref, *refs, groups, cols):
+def down_body(own_ref, par_ref, *refs, groups, cols):
     pieces, outs = refs[:groups], refs[groups : groups + cols]
     gathered, product = refs[groups + cols :]
-    row, col = idx_ref[0], idx_ref[1]
+    row, col = lax.axis_index("row"), lax.axis_index("col")
     parity, group = row % 2, row // 2
     for m, piece in enumerate(pieces):
         gathered[:, aligned(group ^ m, 2 * B, 2 * B)] = piece[...]
@@ -161,7 +188,8 @@
             out[:, rr * B : (rr + 1) * B] = product[rr, :, at].astype(out.dtype)
 
 
-def residual_body(idx_ref, rhs_ref, own_ref, par_ref, kept_ref, *refs, last):
+def residual_body(rhs_ref, own_ref, par_ref, kept_ref, *refs, level):
+    last = level == NLEV - 1
     if last:
         arrived, outs, residual, solved = refs[:-3], refs[-3], refs[-2], refs[-1]
     else:
@@ -170,16 +198,15 @@
     for ref in arrived:
         coupled = coupled + ref[...].astype(F32)
     residual[...] = (rhs_ref[...].astype(F32) - coupled).astype(BF16)
-    parity = idx_ref[0] % 2
-    apply_diag(times_t, parity, residual, own_ref, par_ref, solved)
+    apply_diag(times_t, level, residual, own_ref, par_ref, solved)
     if last:
-        apply_diag(times, parity, solved, own_ref, par_ref, outs)
-
-
-def up_body(idx_ref, own_ref, par_ref, *refs, groups, cols):
+        apply_diag(times, level, solved, own_ref, par_ref, outs)
+
+
+def up_body(own_ref, par_ref, *refs, groups, cols):
     pieces, outs = refs[:cols], refs[cols : cols + groups]
     gathered, product = refs[cols + groups :]
-    row, col = idx_ref[0], idx_ref[1]
+    row, col = lax.axis_index("row"), lax.axis_index("col")
     parity, group = row % 2, row // 2
     for m, piece in enumerate(pieces):
         for rr in range(2):
@@ -191,13 +218,13 @@
         out[...] = product[:, aligned(group ^ m, 2 * B, 2 * B)].astype(out.dtype)
 
 
-def final_body(idx_ref, solved_ref, own_ref, par_ref, kept_ref, *refs):
+def final_body(solved_ref, own_ref, par_ref, kept_ref, *refs, level):
     arrived, outs, residual = refs[:-2], refs[-2], refs[-1]
     back = kept_ref[...]
     for ref in arrived:
         back = back + ref[...].astype(F32)
     residual[...] = (solved_ref[...].astype(F32) - back).astype(BF16)
-    apply_diag(times, idx_ref[0] % 2, residual, own_ref, par_ref, outs)
+    apply_diag(times, level, residual, own_ref, par_ref, outs)
 
 
 def per_device(rhs_rows, dest_row, diag_inverse, lower_blocks, block_mask):
@@ -209,9 +236,7 @@
     half = rhs_rows.shape[1] // 2
     chunk_rows = 2 * (local_rows // supernodes)
     total_rows = (chunk_rows + 2 + 15) // 16 * 16
-    row, col = lax.axis_index("row"), lax.axis_index("col")
-    parity = row % 2
-    idx = jnp.stack([row, col, row * cols + col]).astype(jnp.int32)
+    parity = lax.axis_index("row") % 2
 
     def shape(dims, dtype=BF16):
         return jax.ShapeDtypeStruct(dims, dtype)
@@ -229,7 +254,7 @@
     sending = call(
         functools.partial(pack_body, rows, cols, chunk_rows, total_rows),
         shape((supernodes, total_rows, half)),
-        (idx, rhs_rows, dest_row.reshape(1, local_rows)),
+        (rhs_rows, dest_row.reshape(1, local_rows)),
         flops=2 * local_rows * local_rows * 2 * half,
     )
     arrived = lax.all_to_all(sending, ("row", "col"), split_axis=0, concat_axis=0, tiled=True)
@@ -238,14 +263,14 @@
         call(
             functools.partial(first_body, chunk_rows),
             shape(block),
-            (idx, arrived, diag_own[0], diag_par[0]),
+            (arrived, diag_own, diag_par),
             [pltpu.VMEM(block, BF16)],
         )
     ]
     rest = call(
         functools.partial(rest_body, chunk_rows),
         [shape(block) for _ in range(NLEV - 1)],
-        (idx, arrived),
+        (arrived,),
     )
     upper = None
     for level in range(1, NLEV):
@@ -253,16 +278,16 @@
         sums = call(
             functools.partial(down_body, groups=groups, cols=cols),
             [shape(block, F32 if m == 0 else BF16) for m in range(cols)],
-            (idx, own[level - 1], par[level - 1], *pieces),
+            (*fetch(own[level - 1], par[level - 1], solved[-1]), *pieces),
             [pltpu.VMEM((half, rows * B), BF16), pltpu.VMEM((2, half, cols * B), F32)],
             flops=4 * rows * cols * B * B * half,
         )
         passed = [swap(sums[m], "col", m) for m in range(1, cols)]
         last = level == NLEV - 1
         result = call(
-            functools.partial(residual_body, last=last),
+            functools.partial(residual_body, level=level),
             shape(block),
-            (idx, rest[level - 1], diag_own[level], diag_par[level], sums[0], *passed),
+            (rest[level - 1], diag_own, diag_par, sums[0], *passed),
             [pltpu.VMEM(block, BF16)] * (2 if last else 1),
         )
         if last:
@@ -277,15 +302,15 @@
         sums = call(
             functools.partial(up_body, groups=groups, cols=cols),
             [shape(block, F32 if m == 0 else BF16) for m in range(groups)],
-            (idx, own[level], par[level], *pieces),
+            (*fetch(own[level], par[level], upper), *pieces),
             [pltpu.VMEM((2, half, cols * B), BF16), pltpu.VMEM((half, rows * B), F32)],
             flops=4 * rows * cols * B * B * half,
         )
         passed = [swap(sums[m], "row", 2 * m) for m in range(1, groups)]
         upper = call(
-            final_body,
+            functools.partial(final_body, level=level),
             shape(block),
-            (idx, solved[level], diag_own[level], diag_par[level], sums[0], *passed),
+            (solved[level], diag_own, diag_par, sums[0], *passed),
             [pltpu.VMEM(block, BF16)],
         )
         solution[level] = upper

time: 143 us -> 129 us (0.902)
  waiting for transfers between devices: 55.1 us -> 46.1 us
  local copies, waits for them, and re-layouts: 8.2 us -> 5.33 us
  Pallas kernels: 20.3 us -> 18.7 us
    pallas_call x15, Pallas kernels: 20.3 us -> 10.9 us  [call(): pl.pallas_call(body, out_shape=out_shape, in_specs=in_specs, out_specs=ou...]
    ppermute x44, waiting for transfers between devices: 51.1 us -> 42.1 us  [swap(): return lax.ppermute(value, axis, [(i, i ^ distance) for i in range(count)])]
    pallas_call x0 -> x6, Pallas kernels: none -> 7.83 us  [fetch(): pl.pallas_call(fetch_body, out_shape=[pltpu.VMEM(own.shape, own.dtype), p...]
    unnamed x42 -> x16, local copies, waits for them, and re-layouts: 3.32 us -> 1.75 us
  transfers between devices with their start and end apart: 45 -> 45, of which waited for: 33 -> 29; matrix products, arithmetic and copies ran while one was open for 3% -> 3% of each run, Pallas kernels for 8% -> 11%
where the time goes in v3:
time: 129 us
  starting transfers between devices  56.7 us (44%)
  waiting for transfers between devices  46.1 us (36%)
  Pallas kernels  18.7 us (14%)
  local copies, waits for them, and re-layouts  5.33 us (4%)
  other arithmetic  1.53 us (1%)
    ppermute x44, starting transfers between devices, swap(): return lax.ppermute(value, axis, [(i, i ^ distance) for i in range(count)])  49.3 us
    ppermute x44, waiting for transfers between devices, swap(): return lax.ppermute(value, axis, [(i, i ^ distance) for i in range(count)])  42.1 us
    pallas_call x15, Pallas kernels, call(): pl.pallas_call(body, out_shape=out_shape, in_specs=in_specs, out_specs=ou...  10.9 us
    pallas_call x6, Pallas kernels, fetch(): pl.pallas_call(fetch_body, out_shape=[pltpu.VMEM(own.shape, own.dtype), p...  7.83 us
    all_to_all x1, starting transfers between devices, per_device(): lax.all_to_all(sending, ('row', 'col'), split_axis=0, concat_axis=0, tile...  7.41 us
    all_to_all x1, waiting for transfers between devices, per_device(): lax.all_to_all(sending, ('row', 'col'), split_axis=0, concat_axis=0, tile...  3.96 us
  transfers between devices with their start and end apart: 45, of which 29 were waited for; matrix products, arithmetic and copies ran while one was open for 3% of the time, Pallas kernels for 11%

profile of v3, /device:TPU:0, one launch (start us, length us, event | category | flops | bytes accessed | tf_op | source)
XLA Modules:
  0.0 128.8 jit_solution(2501608853118597085)
XLA Ops:
  1.7 1.4 %shard_map.55 = bf16[32,48,128]{2,1,0:T(8,128)(2,1)} custom-call(f32[512,256]{1,0:T(8,128)S(1)} %copy-done.5, s32[1,512]{1,0:T(1,128)S(1)} %bitcast.71), custom_call_target="tpu_custom_call" | custom-call | flops 134217728 | bytes 526336 | tf_op jit(solution)/shard_map/pallas_call | solution.py:32
  3.1 7.4 %all-to-all-start = ((bf16[32,48,128]{2,1,0:T(8,128)(2,1)}), bf16[32,48,128]{2,1,0:T(8,128)(2,1)}, u32[]{:S(2)}, u32[]{:S(2)}) async-start(bf16[32,48,128]{2,1,0:T(8,128)(2,1)} %shard_map.55), calls=%async_computation | async-start | bytes 786432 | tf_op jit(solution)/shard_map/all_to_all | solution.py:260
  11.2 2.1 %fusion = (bf16[1,1,4,128,1,8,128]{6,5,4,3,2,1,0:T(8,128)(2,1)S(1)}, bf16[1,1,4,128,1,8,128]{6,5,4,3,2,1,0:T(8,128)(2,1)S(1)}, bf16[1,1,4,128,1,8,128]{6,5,4,3,2,1,0:T(8,128)(2,1)S(1)}) fusion(bf16[3,1,4,128,1,8,128]{6,5,4,3,2,1,0:T(8,128)(2,1)} %param.8), kind=kLoop, calls=%fused_computation.19 | loop fusion | bytes 6291456 | tf_op jit(solution)/shard_map/slice | solution.py:248
  15.9 2.4 %collective-permute-done.par_ref = bf16[4,128,128]{2,1,0:T(8,128)(2,1)S(1)} collective-permute-done((bf16[4,128,128]{2,1,0:T(8,128)(2,1)S(1)}, bf16[4,128,128]{2,1,0:T(8,128)(2,1)S(1)}, u32[]{:S(2)}, u32[]{:S(2)}) %collective-permute-start) | collective-permute-done | bytes 131104 | tf_op jit(solution)/shard_map/ppermute | solution.py:20
  18.4 4.0 %all-to-all-done.arrived_ref = bf16[32,48,128]{2,1,0:T(8,128)(2,1)} async-done(((bf16[32,48,128]{2,1,0:T(8,128)(2,1)}), bf16[32,48,128]{2,1,0:T(8,128)(2,1)}, u32[]{:S(2)}, u32[]{:S(2)}) %all-to-all-start) | async-done | bytes 393248 | tf_op jit(solution)/shard_map/all_to_all | solution.py:260
  22.3 1.5 %shard_map.56.after_ref.refs_0_.solved_ref = bf16[128,256]{1,0:T(8,128)(2,1)S(1)} custom-call(bf16[32,48,128]{2,1,0:T(8,128)(2,1)} %all-to-all-done.arrived_ref, bf16[4,128,128]{2,1,0:T(8,128)(2,1)S(1)} %bitcast.64, bf16[4,128,128]{2,1,0:T(8,128)(2,1)S(1)} %collective-permute-done.par_ref), custom_call_target="tpu_custom_call" | custom-call | bytes 655360 | tf_op jit(solution)/shard_map/pallas_call | solution.py:32
  23.8 1.5 %collective-permute-start.2 = (bf16[128,256]{1,0:T(8,128)(2,1)S(1)}, bf16[128,256]{1,0:T(8,128)(2,1)S(1)}, u32[]{:S(2)}, u32[]{:S(2)}) collective-permute-start(bf16[128,256]{1,0:T(8,128)(2,1)S(1)} %shard_map.56.after_ref.refs_0_.solved_ref), channel_id=1, source_target_pairs={{0,8},{4,12},{8,0},{12,4},{16,24},{20,28},{24,16},{28,20},{1,9},{5... | collective-permute-start | bytes 196616 | tf_op jit(solution)/shard_map/ppermute | solution.py:20
  27.4 1.3 %shard_map.58 = (bf16[512,1024]{1,0:T(8,128)(2,1)S(1)}, bf16[512,1024]{1,0:T(8,128)(2,1)S(1)}) custom-call(bf16[512,1024]{1,0:T(8,128)(2,1)S(1)} %bitcast_multiply_fusion.2.own_ref, bf16[512,1024]{1,0:T(8,128)(2,1)} %collective-permute-done.1.par_ref, bf16[128,256]{1,0:T(8,128)(2,1)S(1)} %shard_map.56.after_ref.refs_0_.solved_ref), custom_call_target="tpu_custom_call" | custom-call | bytes 4194304 | tf_op jit(solution)/shard_map/pallas_call | solution.py:61
  28.7 2.0 %collective-permute-done.3.refs_2_ = bf16[128,256]{1,0:T(8,128)(2,1)S(1)} collective-permute-done((bf16[128,256]{1,0:T(8,128)(2,1)S(1)}, bf16[128,256]{1,0:T(8,128)(2,1)S(1)}, u32[]{:S(2)}, u32[]{:S(2)}) %collective-permute-start.3) | collective-permute-done | bytes 65568 | tf_op jit(solution)/shard_map/ppermute | solution.py:20
  33.7 1.5 %collective-permute-start.6 = (bf16[128,256]{1,0:T(8,128)(2,1)S(1)}, bf16[128,256]{1,0:T(8,128)(2,1)S(1)}, u32[]{:S(2)}, u32[]{:S(2)}) collective-permute-start(bf16[128,256]{1,0:T(8,128)(2,1)S(1)} %get-tuple-element.49), channel_id=1, source_target_pairs={{0,2},{1,3},{2,0},{3,1},{4,6},{5,7},{6,4},{7,5},{8,10},{9,11},{10,... | collective-permute-start | bytes 196616 | tf_op jit(solution)/shard_map/ppermute | solution.py:20
  35.1 1.9 %collective-permute-start.7 = (bf16[128,256]{1,0:T(8,128)(2,1)S(1)}, bf16[128,256]{1,0:T(8,128)(2,1)S(1)}, u32[]{:S(2)}, u32[]{:S(2)}) collective-permute-start(bf16[128,256]{1,0:T(8,128)(2,1)S(1)} %get-tuple-element.50), channel_id=1, source_target_pairs={{0,3},{1,2},{2,1},{3,0},{4,7},{5,6},{6,5},{7,4},{8,11},{9,10},{10,... | collective-permute-start | bytes 196616 | tf_op jit(solution)/shard_map/ppermute | solution.py:20
  37.0 1.7 %shard_map.57 = (bf16[128,256]{1,0:T(8,128)(2,1)S(1)}, bf16[128,256]{1,0:T(8,128)(2,1)S(1)}, bf16[128,256]{1,0:T(8,128)(2,1)S(1)}) custom-call(bf16[32,48,128]{2,1,0:T(8,128)(2,1)} %all-to-all-done.arrived_ref), custom_call_target="tpu_custom_call" | custom-call | bytes 393216 | tf_op jit(solution)/shard_map/pallas_call | solution.py:32
  39.6 1.6 %collective-permute-done.7.refs_2_ = bf16[128,256]{1,0:T(8,128)(2,1)S(1)} collective-permute-done((bf16[128,256]{1,0:T(8,128)(2,1)S(1)}, bf16[128,256]{1,0:T(8,128)(2,1)S(1)}, u32[]{:S(2)}, u32[]{:S(2)}) %collective-permute-start.7) | collective-permute-done | bytes 65568 | tf_op jit(solution)/shard_map/ppermute | solution.py:20
  41.4 1.7 %collective-permute-start.9 = (bf16[128,256]{1,0:T(8,128)(2,1)S(1)}, bf16[128,256]{1,0:T(8,128)(2,1)S(1)}, u32[]{:S(2)}, u32[]{:S(2)}) collective-permute-start(bf16[128,256]{1,0:T(8,128)(2,1)S(1)} %shard_map.60.after_ref.refs_0_.solved_ref), channel_id=1, source_target_pairs={{0,8},{4,12},{8,0},{12,4},{16,24},{20,28},{24,16},{28,20},{1,9},{5... | collective-permute-start | bytes 196616 | tf_op jit(solution)/shard_map/ppermute | solution.py:20
  44.9 1.3 %shard_map.61 = (bf16[512,1024]{1,0:T(8,128)(2,1)S(1)}, bf16[512,1024]{1,0:T(8,128)(2,1)S(1)}) custom-call(bf16[512,1024]{1,0:T(8,128)(2,1)S(1)} %bitcast_multiply_fusion.1.own_ref, bf16[512,1024]{1,0:T(8,128)(2,1)} %collective-permute-done.8.par_ref, bf16[128,256]{1,0:T(8,128)(2,1)S(1)} %shard_map.60.after_ref.refs_0_.solved_ref), custom_call_target="tpu_custom_call" | custom-call | bytes 4194304 | tf_op jit(solution)/shard_map/pallas_call | solution.py:61
  47.4 1.5 %collective-permute-done.11.refs_3_ = bf16[128,256]{1,0:T(8,128)(2,1)S(1)} collective-permute-done((bf16[128,256]{1,0:T(8,128)(2,1)S(1)}, bf16[128,256]{1,0:T(8,128)(2,1)S(1)}, u32[]{:S(2)}, u32[]{:S(2)}) %collective-permute-start.11) | collective-permute-done | bytes 65568 | tf_op jit(solution)/shard_map/ppermute | solution.py:20
  50.6 1.4 %collective-permute-start.13 = (bf16[128,256]{1,0:T(8,128)(2,1)S(1)}, bf16[128,256]{1,0:T(8,128)(2,1)S(1)}, u32[]{:S(2)}, u32[]{:S(2)}) collective-permute-start(bf16[128,256]{1,0:T(8,128)(2,1)S(1)} %get-tuple-element.56), channel_id=1, source_target_pairs={{0,2},{1,3},{2,0},{3,1},{4,6},{5,7},{6,4},{7,5},{8,10},{9,11},{10,... | collective-permute-start | bytes 196616 | tf_op jit(solution)/shard_map/ppermute | solution.py:20
  51.9 2.3 %collective-permute-start.14 = (bf16[128,256]{1,0:T(8,128)(2,1)S(1)}, bf16[128,256]{1,0:T(8,128)(2,1)S(1)}, u32[]{:S(2)}, u32[]{:S(2)}) collective-permute-start(bf16[128,256]{1,0:T(8,128)(2,1)S(1)} %get-tuple-element.57), channel_id=1, source_target_pairs={{0,3},{1,2},{2,1},{3,0},{4,7},{5,6},{6,5},{7,4},{8,11},{9,10},{10,... | collective-permute-start | bytes 196616 | tf_op jit(solution)/shard_map/ppermute | solution.py:20
  54.2 1.5 %collective-permute-done.13.refs_1_ = bf16[128,256]{1,0:T(8,128)(2,1)S(1)} collective-permute-done((bf16[128,256]{1,0:T(8,128)(2,1)S(1)}, bf16[128,256]{1,0:T(8,128)(2,1)S(1)}, u32[]{:S(2)}, u32[]{:S(2)}) %collective-permute-start.13) | collective-permute-done | bytes 65568 | tf_op jit(solution)/shard_map/ppermute | solution.py:20
  55.7 2.3 %collective-permute-done.14.refs_2_ = bf16[128,256]{1,0:T(8,128)(2,1)S(1)} collective-permute-done((bf16[128,256]{1,0:T(8,128)(2,1)S(1)}, bf16[128,256]{1,0:T(8,128)(2,1)S(1)}, u32[]{:S(2)}, u32[]{:S(2)}) %collective-permute-start.14) | collective-permute-done | bytes 65568 | tf_op jit(solution)/shard_map/ppermute | solution.py:20
  58.2 1.3 %collective-permute-start.16 = (bf16[128,256]{1,0:T(8,128)(2,1)S(1)}, bf16[128,256]{1,0:T(8,128)(2,1)S(1)}, u32[]{:S(2)}, u32[]{:S(2)}) collective-permute-start(bf16[128,256]{1,0:T(8,128)(2,1)S(1)} %shard_map.63.after_ref.refs_0_.solved_ref), channel_id=1, source_target_pairs={{0,8},{4,12},{8,0},{12,4},{16,24},{20,28},{24,16},{28,20},{1,9},{5... | collective-permute-start | bytes 196616 | tf_op jit(solution)/shard_map/ppermute | solution.py:20
  61.7 1.3 %shard_map.64 = (bf16[512,1024]{1,0:T(8,128)(2,1)S(1)}, bf16[512,1024]{1,0:T(8,128)(2,1)S(1)}) custom-call(bf16[512,1024]{1,0:T(8,128)(2,1)S(1)} %bitcast_multiply_fusion.own_ref, bf16[512,1024]{1,0:T(8,128)(2,1)} %collective-permute-done.15.par_ref, bf16[128,256]{1,0:T(8,128)(2,1)S(1)} %shard_map.63.after_ref.refs_0_.solved_ref), custom_call_target="tpu_custom_call" | custom-call | bytes 4194304 | tf_op jit(solution)/shard_map/pallas_call | solution.py:61
  63.8 1.8 %collective-permute-done.18.refs_3_ = bf16[128,256]{1,0:T(8,128)(2,1)S(1)} collective-permute-done((bf16[128,256]{1,0:T(8,128)(2,1)S(1)}, bf16[128,256]{1,0:T(8,128)(2,1)S(1)}, u32[]{:S(2)}, u32[]{:S(2)}) %collective-permute-start.18) | collective-permute-done | bytes 65568 | tf_op jit(solution)/shard_map/ppermute | solution.py:20
  66.6 2.5 %collective-permute-start.20 = (bf16[128,256]{1,0:T(8,128)(2,1)S(1)}, bf16[128,256]{1,0:T(8,128)(2,1)S(1)}, u32[]{:S(2)}, u32[]{:S(2)}) collective-permute-start(bf16[128,256]{1,0:T(8,128)(2,1)S(1)} %get-tuple-element.63), channel_id=1, source_target_pairs={{0,2},{1,3},{2,0},{3,1},{4,6},{5,7},{6,4},{7,5},{8,10},{9,11},{10,... | collective-permute-start | bytes 196616 | tf_op jit(solution)/shard_map/ppermute | solution.py:20
  69.1 1.9 %collective-permute-start.21 = (bf16[128,256]{1,0:T(8,128)(2,1)S(1)}, bf16[128,256]{1,0:T(8,128)(2,1)S(1)}, u32[]{:S(2)}, u32[]{:S(2)}) collective-permute-start(bf16[128,256]{1,0:T(8,128)(2,1)S(1)} %get-tuple-element.64), channel_id=1, source_target_pairs={{0,3},{1,2},{2,1},{3,0},{4,7},{5,6},{6,5},{7,4},{8,11},{9,10},{10,... | collective-permute-start | bytes 196616 | tf_op jit(solution)/shard_map/ppermute | solution.py:20
  71.6 2.7 %collective-permute-done.20.refs_1_ = bf16[128,256]{1,0:T(8,128)(2,1)S(1)} collective-permute-done((bf16[128,256]{1,0:T(8,128)(2,1)S(1)}, bf16[128,256]{1,0:T(8,128)(2,1)S(1)}, u32[]{:S(2)}, u32[]{:S(2)}) %collective-permute-start.20) | collective-permute-done | bytes 65568 | tf_op jit(solution)/shard_map/ppermute | solution.py:20
  76.7 1.4 %collective-permute-start.23 = (bf16[128,256]{1,0:T(8,128)(2,1)S(1)}, bf16[128,256]{1,0:T(8,128)(2,1)}, u32[]{:S(2)}, u32[]{:S(2)}) collective-permute-start(bf16[128,256]{1,0:T(8,128)(2,1)S(1)} %shard_map.66.after_ref.refs_0_), channel_id=1, source_target_pairs={{0,2},{1,3},{2,0},{3,1},{4,6},{5,7},{6,4},{7,5},{8,10},{9,11},{10,... | collective-permute-start | bytes 196616 | tf_op jit(solution)/shard_map/ppermute | solution.py:20
  78.1 1.9 %collective-permute-start.24 = (bf16[128,256]{1,0:T(8,128)(2,1)S(1)}, bf16[128,256]{1,0:T(8,128)(2,1)}, u32[]{:S(2)}, u32[]{:S(2)}) collective-permute-start(bf16[128,256]{1,0:T(8,128)(2,1)S(1)} %shard_map.66.after_ref.refs_0_), channel_id=1, source_target_pairs={{0,3},{1,2},{2,1},{3,0},{4,7},{5,6},{6,5},{7,4},{8,11},{9,10},{10,... | collective-permute-start | bytes 196616 | tf_op jit(solution)/shard_map/ppermute | solution.py:20
  81.3 1.3 %collective-permute-done.23.refs_2_ = bf16[128,256]{1,0:T(8,128)(2,1)} collective-permute-done((bf16[128,256]{1,0:T(8,128)(2,1)S(1)}, bf16[128,256]{1,0:T(8,128)(2,1)}, u32[]{:S(2)}, u32[]{:S(2)}) %collective-permute-start.23) | collective-permute-done | bytes 65568 | tf_op jit(solution)/shard_map/ppermute | solution.py:20
  82.6 1.6 %collective-permute-done.24.refs_3_ = bf16[128,256]{1,0:T(8,128)(2,1)} collective-permute-done((bf16[128,256]{1,0:T(8,128)(2,1)S(1)}, bf16[128,256]{1,0:T(8,128)(2,1)}, u32[]{:S(2)}, u32[]{:S(2)}) %collective-permute-start.24) | collective-permute-done | bytes 65568 | tf_op jit(solution)/shard_map/ppermute | solution.py:20
  84.2 1.4 %shard_map.68 = (f32[128,256]{1,0:T(8,128)S(1)}, bf16[128,256]{1,0:T(8,128)(2,1)S(1)}, bf16[128,256]{1,0:T(8,128)(2,1)S(1)}, bf16[128,256]{1,0:T(8,128)(2,1)S(1)}) custom-call(bf16[512,1024]{1,0:T(8,128)(2,1)S(1)} %get-tuple-element.65.own_ref, bf16[512,1024]{1,0:T(8,128)(2,1)S(1)} %get-tuple-element.66.par_ref, ...), custom_call_target="tpu_custom_call" | custom-call | flops 268435456 | bytes 2359296 | tf_op jit(solution)/shard_map/pallas_call | solution.py:32
  85.7 1.5 %collective-permute-start.25 = (bf16[128,256]{1,0:T(8,128)(2,1)S(1)}, bf16[128,256]{1,0:T(8,128)(2,1)S(1)}, u32[]{:S(2)}, u32[]{:S(2)}) collective-permute-start(bf16[128,256]{1,0:T(8,128)(2,1)S(1)} %get-tuple-element.68), channel_id=1, source_target_pairs={{0,8},{4,12},{8,0},{12,4},{16,24},{20,28},{24,16},{28,20},{1,9},{5... | collective-permute-start | bytes 196616 | tf_op jit(solution)/shard_map/ppermute | solution.py:20
  90.0 1.4 %collective-permute-done.26.refs_1_ = bf16[128,256]{1,0:T(8,128)(2,1)S(1)} collective-permute-done((bf16[128,256]{1,0:T(8,128)(2,1)S(1)}, bf16[128,256]{1,0:T(8,128)(2,1)S(1)}, u32[]{:S(2)}, u32[]{:S(2)}) %collective-permute-start.26) | collective-permute-done | bytes 65568 | tf_op jit(solution)/shard_map/ppermute | solution.py:20
  91.4 1.8 %collective-permute-done.27.refs_2_ = bf16[128,256]{1,0:T(8,128)(2,1)S(1)} collective-permute-done((bf16[128,256]{1,0:T(8,128)(2,1)S(1)}, bf16[128,256]{1,0:T(8,128)(2,1)S(1)}, u32[]{:S(2)}, u32[]{:S(2)}) %collective-permute-start.27) | collective-permute-done | bytes 65568 | tf_op jit(solution)/shard_map/ppermute | solution.py:20
  93.5 2.4 %collective-permute-start.29 = (bf16[128,256]{1,0:T(8,128)(2,1)S(1)}, bf16[128,256]{1,0:T(8,128)(2,1)S(1)}, u32[]{:S(2)}, u32[]{:S(2)}) collective-permute-start(bf16[128,256]{1,0:T(8,128)(2,1)S(1)} %shard_map.69.after_ref.refs_0_), channel_id=1, source_target_pairs={{0,2},{1,3},{2,0},{3,1},{4,6},{5,7},{6,4},{7,5},{8,10},{9,11},{10,... | collective-permute-start | bytes 196616 | tf_op jit(solution)/shard_map/ppermute | solution.py:20
  95.9 1.9 %collective-permute-start.30 = (bf16[128,256]{1,0:T(8,128)(2,1)S(1)}, bf16[128,256]{1,0:T(8,128)(2,1)S(1)}, u32[]{:S(2)}, u32[]{:S(2)}) collective-permute-start(bf16[128,256]{1,0:T(8,128)(2,1)S(1)} %shard_map.69.after_ref.refs_0_), channel_id=1, source_target_pairs={{0,3},{1,2},{2,1},{3,0},{4,7},{5,6},{6,5},{7,4},{8,11},{9,10},{10,... | collective-permute-start | bytes 196616 | tf_op jit(solution)/shard_map/ppermute | solution.py:20
  97.9 1.3 %shard_map.70 = (bf16[512,1024]{1,0:T(8,128)(2,1)S(1)}, bf16[512,1024]{1,0:T(8,128)(2,1)S(1)}) custom-call(bf16[512,1024]{1,0:T(8,128)(2,1)S(1)} %bitcast_multiply_fusion.1.own_ref, bf16[512,1024]{1,0:T(8,128)(2,1)} %collective-permute-done.8.par_ref, bf16[128,256]{1,0:T(8,128)(2,1)S(1)} %shard_map.69.after_ref.refs_0_), custom_call_target="tpu_custom_call" | custom-call | bytes 4194304 | tf_op jit(solution)/shard_map/pallas_call | solution.py:61
  99.2 2.8 %collective-permute-done.30.refs_3_ = bf16[128,256]{1,0:T(8,128)(2,1)S(1)} collective-permute-done((bf16[128,256]{1,0:T(8,128)(2,1)S(1)}, bf16[128,256]{1,0:T(8,128)(2,1)S(1)}, u32[]{:S(2)}, u32[]{:S(2)}) %collective-permute-start.30) | collective-permute-done | bytes 65568 | tf_op jit(solution)/shard_map/ppermute | solution.py:20
  102.5 1.4 %collective-permute-start.31 = (bf16[128,256]{1,0:T(8,128)(2,1)S(1)}, bf16[128,256]{1,0:T(8,128)(2,1)S(1)}, u32[]{:S(2)}, u32[]{:S(2)}) collective-permute-start(bf16[128,256]{1,0:T(8,128)(2,1)S(1)} %get-tuple-element.74), channel_id=1, source_target_pairs={{0,8},{4,12},{8,0},{12,4},{16,24},{20,28},{24,16},{28,20},{1,9},{5... | collective-permute-start | bytes 196616 | tf_op jit(solution)/shard_map/ppermute | solution.py:20
  104.3 1.7 %collective-permute-start.33 = (bf16[128,256]{1,0:T(8,128)(2,1)S(1)}, bf16[128,256]{1,0:T(8,128)(2,1)S(1)}, u32[]{:S(2)}, u32[]{:S(2)}) collective-permute-start(bf16[128,256]{1,0:T(8,128)(2,1)S(1)} %get-tuple-element.76), channel_id=1, source_target_pairs={{0,24},{4,28},{8,16},{12,20},{16,8},{20,12},{24,0},{28,4},{1,25},{... | collective-permute-start | bytes 196616 | tf_op jit(solution)/shard_map/ppermute | solution.py:20
  106.9 1.3 %collective-permute-done.32.refs_1_ = bf16[128,256]{1,0:T(8,128)(2,1)S(1)} collective-permute-done((bf16[128,256]{1,0:T(8,128)(2,1)S(1)}, bf16[128,256]{1,0:T(8,128)(2,1)S(1)}, u32[]{:S(2)}, u32[]{:S(2)}) %collective-permute-start.32) | collective-permute-done | bytes 65568 | tf_op jit(solution)/shard_map/ppermute | solution.py:20
  109.8 2.5 %collective-permute-start.35 = (bf16[128,256]{1,0:T(8,128)(2,1)S(1)}, bf16[128,256]{1,0:T(8,128)(2,1)S(1)}, u32[]{:S(2)}, u32[]{:S(2)}) collective-permute-start(bf16[128,256]{1,0:T(8,128)(2,1)S(1)} %shard_map.72.after_ref.refs_0_), channel_id=1, source_target_pairs={{0,2},{1,3},{2,0},{3,1},{4,6},{5,7},{6,4},{7,5},{8,10},{9,11},{10,... | collective-permute-start | bytes 196616 | tf_op jit(solution)/shard_map/ppermute | solution.py:20
  112.2 1.9 %collective-permute-start.36 = (bf16[128,256]{1,0:T(8,128)(2,1)S(1)}, bf16[128,256]{1,0:T(8,128)(2,1)S(1)}, u32[]{:S(2)}, u32[]{:S(2)}) collective-permute-start(bf16[128,256]{1,0:T(8,128)(2,1)S(1)} %shard_map.72.after_ref.refs_0_), channel_id=1, source_target_pairs={{0,3},{1,2},{2,1},{3,0},{4,7},{5,6},{6,5},{7,4},{8,11},{9,10},{10,... | collective-permute-start | bytes 196616 | tf_op jit(solution)/shard_map/ppermute | solution.py:20
  114.2 1.3 %shard_map.73 = (bf16[512,1024]{1,0:T(8,128)(2,1)S(1)}, bf16[512,1024]{1,0:T(8,128)(2,1)S(1)}) custom-call(bf16[512,1024]{1,0:T(8,128)(2,1)S(1)} %bitcast_multiply_fusion.2.own_ref, bf16[512,1024]{1,0:T(8,128)(2,1)} %collective-permute-done.1.par_ref, bf16[128,256]{1,0:T(8,128)(2,1)S(1)} %shard_map.72.after_ref.refs_0_), custom_call_target="tpu_custom_call" | custom-call | bytes 4194304 | tf_op jit(solution)/shard_map/pallas_call | solution.py:61
  115.5 2.8 %collective-permute-done.36.refs_3_ = bf16[128,256]{1,0:T(8,128)(2,1)S(1)} collective-permute-done((bf16[128,256]{1,0:T(8,128)(2,1)S(1)}, bf16[128,256]{1,0:T(8,128)(2,1)S(1)}, u32[]{:S(2)}, u32[]{:S(2)}) %collective-permute-start.36) | collective-permute-done | bytes 65568 | tf_op jit(solution)/shard_map/ppermute | solution.py:20
  118.8 1.5 %collective-permute-start.37 = (bf16[128,256]{1,0:T(8,128)(2,1)S(1)}, bf16[128,256]{1,0:T(8,128)(2,1)S(1)}, u32[]{:S(2)}, u32[]{:S(2)}) collective-permute-start(bf16[128,256]{1,0:T(8,128)(2,1)S(1)} %get-tuple-element.80), channel_id=1, source_target_pairs={{0,8},{4,12},{8,0},{12,4},{16,24},{20,28},{24,16},{28,20},{1,9},{5... | collective-permute-start | bytes 196616 | tf_op jit(solution)/shard_map/ppermute | solution.py:20
  123.1 1.4 %collective-permute-done.38.refs_1_ = bf16[128,256]{1,0:T(8,128)(2,1)S(1)} collective-permute-done((bf16[128,256]{1,0:T(8,128)(2,1)S(1)}, bf16[128,256]{1,0:T(8,128)(2,1)S(1)}, u32[]{:S(2)}, u32[]{:S(2)}) %collective-permute-start.38) | collective-permute-done | bytes 65568 | tf_op jit(solution)/shard_map/ppermute | solution.py:20
  124.6 1.8 %collective-permute-done.39.refs_2_ = bf16[128,256]{1,0:T(8,128)(2,1)S(1)} collective-permute-done((bf16[128,256]{1,0:T(8,128)(2,1)S(1)}, bf16[128,256]{1,0:T(8,128)(2,1)S(1)}, u32[]{:S(2)}, u32[]{:S(2)}) %collective-permute-start.39) | collective-permute-done | bytes 65568 | tf_op jit(solution)/shard_map/ppermute | solution.py:20
  (98 shorter events, 36.1 us)
Async XLA Ops:
  3.1 19.2 %all-to-all-start = ((bf16[32,48,128]{2,1,0:T(8,128)(2,1)}), bf16[32,48,128]{2,1,0:T(8,128)(2,1)}, u32[]{:S(2)}, u32[]{:S(2)}) async-start(bf16[32,48,128]{2,1,0:T(8,128)(2,1)} %shard_map.55), calls=%async_computation | async-start | bytes 786432 | tf_op jit(solution)/shard_map/all_to_all | solution.py:260
  13.8 12.7 %collective-permute-start.1 = (bf16[512,1024]{1,0:T(8,128)(2,1)S(1)}, bf16[512,1024]{1,0:T(8,128)(2,1)}, u32[]{:S(2)}, u32[]{:S(2)}) collective-permute-start(bf16[512,1024]{1,0:T(8,128)(2,1)S(1)} %bitcast_multiply_fusion.2.own_ref), channel_id=1, source_target_pairs={{0,4},{4,0},{8,12},{12,8},{16,20},{20,16},{24,28},{28,24},{1,5},{5... | collective-permute-start | bytes 3145736 | tf_op jit(solution)/shard_map/ppermute | solution.py:20
  14.5 30.5 %collective-permute-start.8 = (bf16[512,1024]{1,0:T(8,128)(2,1)S(1)}, bf16[512,1024]{1,0:T(8,128)(2,1)}, u32[]{:S(2)}, u32[]{:S(2)}) collective-permute-start(bf16[512,1024]{1,0:T(8,128)(2,1)S(1)} %bitcast_multiply_fusion.1.own_ref), channel_id=1, source_target_pairs={{0,4},{4,0},{8,12},{12,8},{16,20},{20,16},{24,28},{28,24},{1,5},{5... | collective-permute-start | bytes 3145736 | tf_op jit(solution)/shard_map/ppermute | solution.py:20
  15.3 46.4 %collective-permute-start.15 = (bf16[512,1024]{1,0:T(8,128)(2,1)S(1)}, bf16[512,1024]{1,0:T(8,128)(2,1)}, u32[]{:S(2)}, u32[]{:S(2)}) collective-permute-start(bf16[512,1024]{1,0:T(8,128)(2,1)S(1)} %bitcast_multiply_fusion.own_ref), channel_id=1, source_target_pairs={{0,4},{4,0},{8,12},{12,8},{16,20},{20,16},{24,28},{28,24},{1,5},{5... | collective-permute-start | bytes 3145736 | tf_op jit(solution)/shard_map/ppermute | solution.py:20
  15.6 2.8 %collective-permute-start = (bf16[4,128,128]{2,1,0:T(8,128)(2,1)S(1)}, bf16[4,128,128]{2,1,0:T(8,128)(2,1)S(1)}, u32[]{:S(2)}, u32[]{:S(2)}) collective-permute-start(bf16[4,128,128]{2,1,0:T(8,128)(2,1)S(1)} %bitcast.63), channel_id=1, source_target_pairs={{0,4},{4,0},{8,12},{12,8},{16,20},{20,16},{24,28},{28,24},{1,5},{5... | collective-permute-start | bytes 393224 | tf_op jit(solution)/shard_map/ppermute | solution.py:20
  23.8 4.9 %collective-permute-start.2 = (bf16[128,256]{1,0:T(8,128)(2,1)S(1)}, bf16[128,256]{1,0:T(8,128)(2,1)S(1)}, u32[]{:S(2)}, u32[]{:S(2)}) collective-permute-start(bf16[128,256]{1,0:T(8,128)(2,1)S(1)} %shard_map.56.after_ref.refs_0_.solved_ref), channel_id=1, source_target_pairs={{0,8},{4,12},{8,0},{12,4},{16,24},{20,28},{24,16},{28,20},{1,9},{5... | collective-permute-start | bytes 196616 | tf_op jit(solution)/shard_map/ppermute | solution.py:20
  25.3 5.4 %collective-permute-start.3 = (bf16[128,256]{1,0:T(8,128)(2,1)S(1)}, bf16[128,256]{1,0:T(8,128)(2,1)S(1)}, u32[]{:S(2)}, u32[]{:S(2)}) collective-permute-start(bf16[128,256]{1,0:T(8,128)(2,1)S(1)} %shard_map.56.after_ref.refs_0_.solved_ref), channel_id=1, source_target_pairs={{0,16},{4,20},{8,24},{12,28},{16,0},{20,4},{24,8},{28,12},{1,17},{... | collective-permute-start | bytes 196616 | tf_op jit(solution)/shard_map/ppermute | solution.py:20
  26.5 5.2 %collective-permute-start.4 = (bf16[128,256]{1,0:T(8,128)(2,1)S(1)}, bf16[128,256]{1,0:T(8,128)(2,1)S(1)}, u32[]{:S(2)}, u32[]{:S(2)}) collective-permute-start(bf16[128,256]{1,0:T(8,128)(2,1)S(1)} %shard_map.56.after_ref.refs_0_.solved_ref), channel_id=1, source_target_pairs={{0,24},{4,28},{8,16},{12,20},{16,8},{20,12},{24,0},{28,4},{1,25},{... | collective-permute-start | bytes 196616 | tf_op jit(solution)/shard_map/ppermute | solution.py:20
  32.5 6.1 %collective-permute-start.5 = (bf16[128,256]{1,0:T(8,128)(2,1)S(1)}, bf16[128,256]{1,0:T(8,128)(2,1)S(1)}, u32[]{:S(2)}, u32[]{:S(2)}) collective-permute-start(bf16[128,256]{1,0:T(8,128)(2,1)S(1)} %get-tuple-element.48), channel_id=1, source_target_pairs={{0,1},{1,0},{2,3},{3,2},{4,5},{5,4},{6,7},{7,6},{8,9},{9,8},{10,11... | collective-permute-start | bytes 196616 | tf_op jit(solution)/shard_map/ppermute | solution.py:20
  33.7 6.0 %collective-permute-start.6 = (bf16[128,256]{1,0:T(8,128)(2,1)S(1)}, bf16[128,256]{1,0:T(8,128)(2,1)S(1)}, u32[]{:S(2)}, u32[]{:S(2)}) collective-permute-start(bf16[128,256]{1,0:T(8,128)(2,1)S(1)} %get-tuple-element.49), channel_id=1, source_target_pairs={{0,2},{1,3},{2,0},{3,1},{4,6},{5,7},{6,4},{7,5},{8,10},{9,11},{10,... | collective-permute-start | bytes 196616 | tf_op jit(solution)/shard_map/ppermute | solution.py:20
  35.1 6.1 %collective-permute-start.7 = (bf16[128,256]{1,0:T(8,128)(2,1)S(1)}, bf16[128,256]{1,0:T(8,128)(2,1)S(1)}, u32[]{:S(2)}, u32[]{:S(2)}) collective-permute-start(bf16[128,256]{1,0:T(8,128)(2,1)S(1)} %get-tuple-element.50), channel_id=1, source_target_pairs={{0,3},{1,2},{2,1},{3,0},{4,7},{5,6},{6,5},{7,4},{8,11},{9,10},{10,... | collective-permute-start | bytes 196616 | tf_op jit(solution)/shard_map/ppermute | solution.py:20
  41.4 21.7 %copy-start.1 = (bf16[128,256]{1,0:T(8,128)(2,1)}, bf16[128,256]{1,0:T(8,128)(2,1)S(1)}, u32[]{:S(2)}) copy-start(bf16[128,256]{1,0:T(8,128)(2,1)S(1)} %shard_map.60.after_ref.refs_0_.solved_ref) | copy-start | bytes 196612
  41.4 4.9 %collective-permute-start.9 = (bf16[128,256]{1,0:T(8,128)(2,1)S(1)}, bf16[128,256]{1,0:T(8,128)(2,1)S(1)}, u32[]{:S(2)}, u32[]{:S(2)}) collective-permute-start(bf16[128,256]{1,0:T(8,128)(2,1)S(1)} %shard_map.60.after_ref.refs_0_.solved_ref), channel_id=1, source_target_pairs={{0,8},{4,12},{8,0},{12,4},{16,24},{20,28},{24,16},{28,20},{1,9},{5... | collective-permute-start | bytes 196616 | tf_op jit(solution)/shard_map/ppermute | solution.py:20
  43.1 4.3 %collective-permute-start.10 = (bf16[128,256]{1,0:T(8,128)(2,1)S(1)}, bf16[128,256]{1,0:T(8,128)(2,1)S(1)}, u32[]{:S(2)}, u32[]{:S(2)}) collective-permute-start(bf16[128,256]{1,0:T(8,128)(2,1)S(1)} %shard_map.60.after_ref.refs_0_.solved_ref), channel_id=1, source_target_pairs={{0,16},{4,20},{8,24},{12,28},{16,0},{20,4},{24,8},{28,12},{1,17},{... | collective-permute-start | bytes 196616 | tf_op jit(solution)/shard_map/ppermute | solution.py:20
  43.7 5.2 %collective-permute-start.11 = (bf16[128,256]{1,0:T(8,128)(2,1)S(1)}, bf16[128,256]{1,0:T(8,128)(2,1)S(1)}, u32[]{:S(2)}, u32[]{:S(2)}) collective-permute-start(bf16[128,256]{1,0:T(8,128)(2,1)S(1)} %shard_map.60.after_ref.refs_0_.solved_ref), channel_id=1, source_target_pairs={{0,24},{4,28},{8,16},{12,20},{16,8},{20,12},{24,0},{28,4},{1,25},{... | collective-permute-start | bytes 196616 | tf_op jit(solution)/shard_map/ppermute | solution.py:20
  49.7 4.5 %collective-permute-start.12 = (bf16[128,256]{1,0:T(8,128)(2,1)S(1)}, bf16[128,256]{1,0:T(8,128)(2,1)S(1)}, u32[]{:S(2)}, u32[]{:S(2)}) collective-permute-start(bf16[128,256]{1,0:T(8,128)(2,1)S(1)} %get-tuple-element.55), channel_id=1, source_target_pairs={{0,1},{1,0},{2,3},{3,2},{4,5},{5,4},{6,7},{7,6},{8,9},{9,8},{10,11... | collective-permute-start | bytes 196616 | tf_op jit(solution)/shard_map/ppermute | solution.py:20
  50.6 5.2 %collective-permute-start.13 = (bf16[128,256]{1,0:T(8,128)(2,1)S(1)}, bf16[128,256]{1,0:T(8,128)(2,1)S(1)}, u32[]{:S(2)}, u32[]{:S(2)}) collective-permute-start(bf16[128,256]{1,0:T(8,128)(2,1)S(1)} %get-tuple-element.56), channel_id=1, source_target_pairs={{0,2},{1,3},{2,0},{3,1},{4,6},{5,7},{6,4},{7,5},{8,10},{9,11},{10,... | collective-permute-start | bytes 196616 | tf_op jit(solution)/shard_map/ppermute | solution.py:20
  51.9 6.1 %collective-permute-start.14 = (bf16[128,256]{1,0:T(8,128)(2,1)S(1)}, bf16[128,256]{1,0:T(8,128)(2,1)S(1)}, u32[]{:S(2)}, u32[]{:S(2)}) collective-permute-start(bf16[128,256]{1,0:T(8,128)(2,1)S(1)} %get-tuple-element.57), channel_id=1, source_target_pairs={{0,3},{1,2},{2,1},{3,0},{4,7},{5,6},{6,5},{7,4},{8,11},{9,10},{10,... | collective-permute-start | bytes 196616 | tf_op jit(solution)/shard_map/ppermute | solution.py:20
  58.2 18.5 %copy-start.3 = (bf16[128,256]{1,0:T(8,128)(2,1)}, bf16[128,256]{1,0:T(8,128)(2,1)S(1)}, u32[]{:S(2)}) copy-start(bf16[128,256]{1,0:T(8,128)(2,1)S(1)} %shard_map.63.after_ref.refs_0_.solved_ref) | copy-start | bytes 196612
  58.2 4.9 %collective-permute-start.16 = (bf16[128,256]{1,0:T(8,128)(2,1)S(1)}, bf16[128,256]{1,0:T(8,128)(2,1)S(1)}, u32[]{:S(2)}, u32[]{:S(2)}) collective-permute-start(bf16[128,256]{1,0:T(8,128)(2,1)S(1)} %shard_map.63.after_ref.refs_0_.solved_ref), channel_id=1, source_target_pairs={{0,8},{4,12},{8,0},{12,4},{16,24},{20,28},{24,16},{28,20},{1,9},{5... | collective-permute-start | bytes 196616 | tf_op jit(solution)/shard_map/ppermute | solution.py:20
  59.5 4.3 %collective-permute-start.17 = (bf16[128,256]{1,0:T(8,128)(2,1)S(1)}, bf16[128,256]{1,0:T(8,128)(2,1)S(1)}, u32[]{:S(2)}, u32[]{:S(2)}) collective-permute-start(bf16[128,256]{1,0:T(8,128)(2,1)S(1)} %shard_map.63.after_ref.refs_0_.solved_ref), channel_id=1, source_target_pairs={{0,16},{4,20},{8,24},{12,28},{16,0},{20,4},{24,8},{28,12},{1,17},{... | collective-permute-start | bytes 196616 | tf_op jit(solution)/shard_map/ppermute | solution.py:20
  60.5 5.2 %collective-permute-start.18 = (bf16[128,256]{1,0:T(8,128)(2,1)S(1)}, bf16[128,256]{1,0:T(8,128)(2,1)S(1)}, u32[]{:S(2)}, u32[]{:S(2)}) collective-permute-start(bf16[128,256]{1,0:T(8,128)(2,1)S(1)} %shard_map.63.after_ref.refs_0_.solved_ref), channel_id=1, source_target_pairs={{0,24},{4,28},{8,16},{12,20},{16,8},{20,12},{24,0},{28,4},{1,25},{... | collective-permute-start | bytes 196616 | tf_op jit(solution)/shard_map/ppermute | solution.py:20
  66.5 5.0 %collective-permute-start.19 = (bf16[128,256]{1,0:T(8,128)(2,1)S(1)}, bf16[128,256]{1,0:T(8,128)(2,1)S(1)}, u32[]{:S(2)}, u32[]{:S(2)}) collective-permute-start(bf16[128,256]{1,0:T(8,128)(2,1)S(1)} %get-tuple-element.62), channel_id=1, source_target_pairs={{0,1},{1,0},{2,3},{3,2},{4,5},{5,4},{6,7},{7,6},{8,9},{9,8},{10,11... | collective-permute-start | bytes 196616 | tf_op jit(solution)/shard_map/ppermute | solution.py:20
  66.6 7.7 %collective-permute-start.20 = (bf16[128,256]{1,0:T(8,128)(2,1)S(1)}, bf16[128,256]{1,0:T(8,128)(2,1)S(1)}, u32[]{:S(2)}, u32[]{:S(2)}) collective-permute-start(bf16[128,256]{1,0:T(8,128)(2,1)S(1)} %get-tuple-element.63), channel_id=1, source_target_pairs={{0,2},{1,3},{2,0},{3,1},{4,6},{5,7},{6,4},{7,5},{8,10},{9,11},{10,... | collective-permute-start | bytes 196616 | tf_op jit(solution)/shard_map/ppermute | solution.py:20
  69.1 6.1 %collective-permute-start.21 = (bf16[128,256]{1,0:T(8,128)(2,1)S(1)}, bf16[128,256]{1,0:T(8,128)(2,1)S(1)}, u32[]{:S(2)}, u32[]{:S(2)}) collective-permute-start(bf16[128,256]{1,0:T(8,128)(2,1)S(1)} %get-tuple-element.64), channel_id=1, source_target_pairs={{0,3},{1,2},{2,1},{3,0},{4,7},{5,6},{6,5},{7,4},{8,11},{9,10},{10,... | collective-permute-start | bytes 196616 | tf_op jit(solution)/shard_map/ppermute | solution.py:20
  75.5 5.8 %collective-permute-start.22 = (bf16[128,256]{1,0:T(8,128)(2,1)S(1)}, bf16[128,256]{1,0:T(8,128)(2,1)}, u32[]{:S(2)}, u32[]{:S(2)}) collective-permute-start(bf16[128,256]{1,0:T(8,128)(2,1)S(1)} %shard_map.66.after_ref.refs_0_), channel_id=1, source_target_pairs={{0,1},{1,0},{2,3},{3,2},{4,5},{5,4},{6,7},{7,6},{8,9},{9,8},{10,11... | collective-permute-start | bytes 196616 | tf_op jit(solution)/shard_map/ppermute | solution.py:20
  76.7 6.0 %collective-permute-start.23 = (bf16[128,256]{1,0:T(8,128)(2,1)S(1)}, bf16[128,256]{1,0:T(8,128)(2,1)}, u32[]{:S(2)}, u32[]{:S(2)}) collective-permute-start(bf16[128,256]{1,0:T(8,128)(2,1)S(1)} %shard_map.66.after_ref.refs_0_), channel_id=1, source_target_pairs={{0,2},{1,3},{2,0},{3,1},{4,6},{5,7},{6,4},{7,5},{8,10},{9,11},{10,... | collective-permute-start | bytes 196616 | tf_op jit(solution)/shard_map/ppermute | solution.py:20
  78.1 6.2 %collective-permute-start.24 = (bf16[128,256]{1,0:T(8,128)(2,1)S(1)}, bf16[128,256]{1,0:T(8,128)(2,1)}, u32[]{:S(2)}, u32[]{:S(2)}) collective-permute-start(bf16[128,256]{1,0:T(8,128)(2,1)S(1)} %shard_map.66.after_ref.refs_0_), channel_id=1, source_target_pairs={{0,3},{1,2},{2,1},{3,0},{4,7},{5,6},{6,5},{7,4},{8,11},{9,10},{10,... | collective-permute-start | bytes 196616 | tf_op jit(solution)/shard_map/ppermute | solution.py:20
  85.6 23.8 %copy-start.2 = (bf16[128,256]{1,0:T(8,128)(2,1)S(1)}, bf16[128,256]{1,0:T(8,128)(2,1)}, u32[]{:S(2)}) copy-start(bf16[128,256]{1,0:T(8,128)(2,1)} %copy-done.1) | copy-start | bytes 196612
  85.7 4.3 %collective-permute-start.25 = (bf16[128,256]{1,0:T(8,128)(2,1)S(1)}, bf16[128,256]{1,0:T(8,128)(2,1)S(1)}, u32[]{:S(2)}, u32[]{:S(2)}) collective-permute-start(bf16[128,256]{1,0:T(8,128)(2,1)S(1)} %get-tuple-element.68), channel_id=1, source_target_pairs={{0,8},{4,12},{8,0},{12,4},{16,24},{20,28},{24,16},{28,20},{1,9},{5... | collective-permute-start | bytes 196616 | tf_op jit(solution)/shard_map/ppermute | solution.py:20
  87.1 4.3 %collective-permute-start.26 = (bf16[128,256]{1,0:T(8,128)(2,1)S(1)}, bf16[128,256]{1,0:T(8,128)(2,1)S(1)}, u32[]{:S(2)}, u32[]{:S(2)}) collective-permute-start(bf16[128,256]{1,0:T(8,128)(2,1)S(1)} %get-tuple-element.69), channel_id=1, source_target_pairs={{0,16},{4,20},{8,24},{12,28},{16,0},{20,4},{24,8},{28,12},{1,17},{... | collective-permute-start | bytes 196616 | tf_op jit(solution)/shard_map/ppermute | solution.py:20
  88.1 5.2 %collective-permute-start.27 = (bf16[128,256]{1,0:T(8,128)(2,1)S(1)}, bf16[128,256]{1,0:T(8,128)(2,1)S(1)}, u32[]{:S(2)}, u32[]{:S(2)}) collective-permute-start(bf16[128,256]{1,0:T(8,128)(2,1)S(1)} %get-tuple-element.70), channel_id=1, source_target_pairs={{0,24},{4,28},{8,16},{12,20},{16,8},{20,12},{24,0},{28,4},{1,25},{... | collective-permute-start | bytes 196616 | tf_op jit(solution)/shard_map/ppermute | solution.py:20
  89.2 16.9 %collective-permute-start.43 = (bf16[128,128]{0,1:T(8,128)(2,1)S(1)}, bf16[128,128]{0,1:T(8,128)(2,1)S(1)}, u32[]{:S(2)}, u32[]{:S(2)}) collective-permute-start(bf16[128,128]{0,1:T(8,128)(2,1)S(1)} %get-tuple-element.93), channel_id=1, source_target_pairs={{0,4},{4,0},{8,12},{12,8},{16,20},{20,16},{24,28},{28,24},{1,5},{5... | collective-permute-start | bytes 98312 | tf_op jit(solution)/shard_map/ppermute | solution.py:20
  93.4 5.8 %collective-permute-start.28 = (bf16[128,256]{1,0:T(8,128)(2,1)S(1)}, bf16[128,256]{1,0:T(8,128)(2,1)S(1)}, u32[]{:S(2)}, u32[]{:S(2)}) collective-permute-start(bf16[128,256]{1,0:T(8,128)(2,1)S(1)} %shard_map.69.after_ref.refs_0_), channel_id=1, source_target_pairs={{0,1},{1,0},{2,3},{3,2},{4,5},{5,4},{6,7},{7,6},{8,9},{9,8},{10,11... | collective-permute-start | bytes 196616 | tf_op jit(solution)/shard_map/ppermute | solution.py:20
  93.5 5.7 %collective-permute-start.29 = (bf16[128,256]{1,0:T(8,128)(2,1)S(1)}, bf16[128,256]{1,0:T(8,128)(2,1)S(1)}, u32[]{:S(2)}, u32[]{:S(2)}) collective-permute-start(bf16[128,256]{1,0:T(8,128)(2,1)S(1)} %shard_map.69.after_ref.refs_0_), channel_id=1, source_target_pairs={{0,2},{1,3},{2,0},{3,1},{4,6},{5,7},{6,4},{7,5},{8,10},{9,11},{10,... | collective-permute-start | bytes 196616 | tf_op jit(solution)/shard_map/ppermute | solution.py:20
  95.9 6.1 %collective-permute-start.30 = (bf16[128,256]{1,0:T(8,128)(2,1)S(1)}, bf16[128,256]{1,0:T(8,128)(2,1)S(1)}, u32[]{:S(2)}, u32[]{:S(2)}) collective-permute-start(bf16[128,256]{1,0:T(8,128)(2,1)S(1)} %shard_map.69.after_ref.refs_0_), channel_id=1, source_target_pairs={{0,3},{1,2},{2,1},{3,0},{4,7},{5,6},{6,5},{7,4},{8,11},{9,10},{10,... | collective-permute-start | bytes 196616 | tf_op jit(solution)/shard_map/ppermute | solution.py:20
  97.9 16.3 %collective-permute-start.42 = (bf16[128,128]{0,1:T(8,128)(2,1)S(1)}, bf16[128,128]{0,1:T(8,128)(2,1)S(1)}, u32[]{:S(2)}, u32[]{:S(2)}) collective-permute-start(bf16[128,128]{0,1:T(8,128)(2,1)S(1)} %get-tuple-element.91), channel_id=1, source_target_pairs={{0,4},{4,0},{8,12},{12,8},{16,20},{20,16},{24,28},{28,24},{1,5},{5... | collective-permute-start | bytes 98312 | tf_op jit(solution)/shard_map/ppermute | solution.py:20
  102.5 4.3 %collective-permute-start.31 = (bf16[128,256]{1,0:T(8,128)(2,1)S(1)}, bf16[128,256]{1,0:T(8,128)(2,1)S(1)}, u32[]{:S(2)}, u32[]{:S(2)}) collective-permute-start(bf16[128,256]{1,0:T(8,128)(2,1)S(1)} %get-tuple-element.74), channel_id=1, source_target_pairs={{0,8},{4,12},{8,0},{12,4},{16,24},{20,28},{24,16},{28,20},{1,9},{5... | collective-permute-start | bytes 196616 | tf_op jit(solution)/shard_map/ppermute | solution.py:20
  103.9 4.3 %collective-permute-start.32 = (bf16[128,256]{1,0:T(8,128)(2,1)S(1)}, bf16[128,256]{1,0:T(8,128)(2,1)S(1)}, u32[]{:S(2)}, u32[]{:S(2)}) collective-permute-start(bf16[128,256]{1,0:T(8,128)(2,1)S(1)} %get-tuple-element.75), channel_id=1, source_target_pairs={{0,16},{4,20},{8,24},{12,28},{16,0},{20,4},{24,8},{28,12},{1,17},{... | collective-permute-start | bytes 196616 | tf_op jit(solution)/shard_map/ppermute | solution.py:20
  104.3 5.2 %collective-permute-start.33 = (bf16[128,256]{1,0:T(8,128)(2,1)S(1)}, bf16[128,256]{1,0:T(8,128)(2,1)S(1)}, u32[]{:S(2)}, u32[]{:S(2)}) collective-permute-start(bf16[128,256]{1,0:T(8,128)(2,1)S(1)} %get-tuple-element.76), channel_id=1, source_target_pairs={{0,24},{4,28},{8,16},{12,20},{16,8},{20,12},{24,0},{28,4},{1,25},{... | collective-permute-start | bytes 196616 | tf_op jit(solution)/shard_map/ppermute | solution.py:20
  109.7 5.8 %collective-permute-start.34 = (bf16[128,256]{1,0:T(8,128)(2,1)S(1)}, bf16[128,256]{1,0:T(8,128)(2,1)S(1)}, u32[]{:S(2)}, u32[]{:S(2)}) collective-permute-start(bf16[128,256]{1,0:T(8,128)(2,1)S(1)} %shard_map.72.after_ref.refs_0_), channel_id=1, source_target_pairs={{0,1},{1,0},{2,3},{3,2},{4,5},{5,4},{6,7},{7,6},{8,9},{9,8},{10,11... | collective-permute-start | bytes 196616 | tf_op jit(solution)/shard_map/ppermute | solution.py:20
  109.8 5.7 %collective-permute-start.35 = (bf16[128,256]{1,0:T(8,128)(2,1)S(1)}, bf16[128,256]{1,0:T(8,128)(2,1)S(1)}, u32[]{:S(2)}, u32[]{:S(2)}) collective-permute-start(bf16[128,256]{1,0:T(8,128)(2,1)S(1)} %shard_map.72.after_ref.refs_0_), channel_id=1, source_target_pairs={{0,2},{1,3},{2,0},{3,1},{4,6},{5,7},{6,4},{7,5},{8,10},{9,11},{10,... | collective-permute-start | bytes 196616 | tf_op jit(solution)/shard_map/ppermute | solution.py:20
  112.2 6.1 %collective-permute-start.36 = (bf16[128,256]{1,0:T(8,128)(2,1)S(1)}, bf16[128,256]{1,0:T(8,128)(2,1)S(1)}, u32[]{:S(2)}, u32[]{:S(2)}) collective-permute-start(bf16[128,256]{1,0:T(8,128)(2,1)S(1)} %shard_map.72.after_ref.refs_0_), channel_id=1, source_target_pairs={{0,3},{1,2},{2,1},{3,0},{4,7},{5,6},{6,5},{7,4},{8,11},{9,10},{10,... | collective-permute-start | bytes 196616 | tf_op jit(solution)/shard_map/ppermute | solution.py:20
  118.8 4.3 %collective-permute-start.37 = (bf16[128,256]{1,0:T(8,128)(2,1)S(1)}, bf16[128,256]{1,0:T(8,128)(2,1)S(1)}, u32[]{:S(2)}, u32[]{:S(2)}) collective-permute-start(bf16[128,256]{1,0:T(8,128)(2,1)S(1)} %get-tuple-element.80), channel_id=1, source_target_pairs={{0,8},{4,12},{8,0},{12,4},{16,24},{20,28},{24,16},{28,20},{1,9},{5... | collective-permute-start | bytes 196616 | tf_op jit(solution)/shard_map/ppermute | solution.py:20
  120.3 4.3 %collective-permute-start.38 = (bf16[128,256]{1,0:T(8,128)(2,1)S(1)}, bf16[128,256]{1,0:T(8,128)(2,1)S(1)}, u32[]{:S(2)}, u32[]{:S(2)}) collective-permute-start(bf16[128,256]{1,0:T(8,128)(2,1)S(1)} %get-tuple-element.81), channel_id=1, source_target_pairs={{0,16},{4,20},{8,24},{12,28},{16,0},{20,4},{24,8},{28,12},{1,17},{... | collective-permute-start | bytes 196616 | tf_op jit(solution)/shard_map/ppermute | solution.py:20
  121.2 5.2 %collective-permute-start.39 = (bf16[128,256]{1,0:T(8,128)(2,1)S(1)}, bf16[128,256]{1,0:T(8,128)(2,1)S(1)}, u32[]{:S(2)}, u32[]{:S(2)}) collective-permute-start(bf16[128,256]{1,0:T(8,128)(2,1)S(1)} %get-tuple-element.82), channel_id=1, source_target_pairs={{0,24},{4,28},{8,16},{12,20},{16,8},{20,12},{24,0},{28,4},{1,25},{... | collective-permute-start | bytes 196616 | tf_op jit(solution)/shard_map/ppermute | solution.py:20
  122.4 4.3 %collective-permute-start.41 = (bf16[128,128]{0,1:T(8,128)(2,1)S(1)}, bf16[128,128]{0,1:T(8,128)(2,1)S(1)}, u32[]{:S(2)}, u32[]{:S(2)}) collective-permute-start(bf16[128,128]{0,1:T(8,128)(2,1)S(1)} %get-tuple-element.89), channel_id=1, source_target_pairs={{0,4},{4,0},{8,12},{12,8},{16,20},{20,16},{24,28},{28,24},{1,5},{5... | collective-permute-start | bytes 98312 | tf_op jit(solution)/shard_map/ppermute | solution.py:20
  126.6 1.3 collective-permute-start.40
  (4 other events, 16.3 us)

commit v4 on v3

--- a/solution.py
+++ b/solution.py
@@ -20,9 +20,9 @@
     return lax.ppermute(value, axis, [(i, i ^ distance) for i in range(count)])
 
 
-def call(body, out_shape, args, scratch=(), flops=0):
+def call(body, out_shape, args, scratch=(), flops=0, space=pltpu.VMEM):
     moved = sum(a.size * a.dtype.itemsize for a in args)
-    in_specs = [pl.BlockSpec(memory_space=pltpu.VMEM) for _ in args]
+    in_specs = [pl.BlockSpec(memory_space=space) for _ in args]
     several = isinstance(out_shape, (list, tuple))
     out_specs = (
         [pl.BlockSpec(memory_space=pltpu.VMEM) for _ in out_shape]
@@ -71,7 +71,9 @@
     )(own, par, after)
 
 
-def pack_body(rows, cols, chunk_rows, total_rows, rhs_ref, dest_ref, out_ref):
+def pack_body(
+    rows, cols, chunk_rows, total_rows, rhs_ref, dest_ref, out_ref
+):
     local_rows = rhs_ref.shape[0]
     supernodes = rows * cols
     pairs = supernodes // 2
@@ -98,11 +100,6 @@
     rank = jnp.sum(member_f * counts, axis=0, keepdims=True).astype(jnp.int32)
     slot = pair * chunk_rows + rank
     chosen = lax.broadcasted_iota(jnp.int32, (local_rows, local_rows), 0) == slot
-    sorted_rows = jnp.dot(
-        jnp.where(chosen, 1.0, 0.0).astype(BF16),
-        rhs_ref[...].astype(BF16),
-        preferred_element_type=F32,
-    )
     tail = total_rows - chunk_rows
     tail_iota = lax.broadcasted_iota(jnp.int32, (pairs * tail, local_rows), 0)
     tail_pair = tail_iota // tail
@@ -115,6 +112,11 @@
         tail_value,
         jnp.where(lane_hot, 1.0, 0.0).astype(BF16),
         (((1,), (1,)), ((), ())),
+        preferred_element_type=F32,
+    )
+    sorted_rows = jnp.dot(
+        jnp.where(chosen, 1.0, 0.0).astype(BF16),
+        rhs_ref[...].astype(BF16),
         preferred_element_type=F32,
     )
     half = rhs_ref.shape[1] // 2
@@ -188,10 +190,23 @@
             out[:, rr * B : (rr + 1) * B] = product[rr, :, at].astype(out.dtype)
 
 
+def split_off(block_ref, theirs_ref):
+    theirs_ref[...] = block_ref[:, aligned(1 - lax.axis_index("row") % 2, B, B)]
+
+
+def finish_body(*refs):
+    blocks, others, out_ref = refs[:NLEV], refs[NLEV : 2 * NLEV], refs[2 * NLEV]
+    parity = lax.axis_index("row") % 2
+    mine, other = aligned(parity, B, B), aligned(1 - parity, B, B)
+    for level in range(NLEV):
+        out_ref[level, 0, :, mine] = blocks[level][:, mine].T
+        out_ref[level, 0, :, other] = others[level][...].T
+
+
 def residual_body(rhs_ref, own_ref, par_ref, kept_ref, *refs, level):
     last = level == NLEV - 1
     if last:
-        arrived, outs, residual, solved = refs[:-3], refs[-3], refs[-2], refs[-1]
+        arrived, outs, theirs, residual, solved = refs[:-4], *refs[-4:]
     else:
         arrived, solved, residual = refs[:-2], refs[-2], refs[-1]
     coupled = kept_ref[...]
@@ -201,6 +216,7 @@
     apply_diag(times_t, level, residual, own_ref, par_ref, solved)
     if last:
         apply_diag(times, level, solved, own_ref, par_ref, outs)
+        split_off(outs, theirs)
 
 
 def up_body(own_ref, par_ref, *refs, groups, cols):
@@ -219,12 +235,13 @@
 
 
 def final_body(solved_ref, own_ref, par_ref, kept_ref, *refs, level):
-    arrived, outs, residual = refs[:-2], refs[-2], refs[-1]
+    arrived, outs, theirs, residual = refs[:-3], *refs[-3:]
     back = kept_ref[...]
     for ref in arrived:
         back = back + ref[...].astype(F32)
     residual[...] = (solved_ref[...].astype(F32) - back).astype(BF16)
     apply_diag(times, level, residual, own_ref, par_ref, outs)
+    split_off(outs, theirs)
 
 
 def per_device(rhs_rows, dest_row, diag_inverse, lower_blocks, block_mask):
@@ -235,21 +252,19 @@
     local_rows = rhs_rows.shape[0]
     half = rhs_rows.shape[1] // 2
     chunk_rows = 2 * (local_rows // supernodes)
-    total_rows = (chunk_rows + 2 + 15) // 16 * 16
-    parity = lax.axis_index("row") % 2
+    total_rows = (chunk_rows + 2 + 7) // 8 * 8
 
     def shape(dims, dtype=BF16):
         return jax.ShapeDtypeStruct(dims, dtype)
 
     diag_own = diag_inverse[:, 0]
     diag_par = swap(diag_own, "row", 1)
-    own, par = [], []
+    own, par = [], [None] * (NLEV - 1)
     for level in range(NLEV - 1):
         tile = lower_blocks[level, 0, :, :, 0]
         mask = block_mask[level, 0, :, 0, :].astype(BF16)
         masked = (tile * mask[:, None, :, None]).reshape(cols * B, rows * B)
         own.append(masked)
-        par.append(swap(masked, "row", 1))
 
     sending = call(
         functools.partial(pack_body, rows, cols, chunk_rows, total_rows),
@@ -274,6 +289,12 @@
     )
     upper = None
     for level in range(1, NLEV):
+        if level == 1:
+            own[0], _ = lax.optimization_barrier((own[0], solved[0]))
+            par[0] = swap(own[0], "row", 1)
+        if level < NLEV - 1:
+            own[level], _ = lax.optimization_barrier((own[level], solved[-1]))
+            par[level] = swap(own[level], "row", 1)
         pieces = [solved[-1]] + [swap(solved[-1], "row", 2 * m) for m in range(1, groups)]
         sums = call(
             functools.partial(down_body, groups=groups, cols=cols),
@@ -286,17 +307,17 @@
         last = level == NLEV - 1
         result = call(
             functools.partial(residual_body, level=level),
-            shape(block),
+            [shape(block), shape((half, B))] if last else shape(block),
             (rest[level - 1], diag_own, diag_par, sums[0], *passed),
             [pltpu.VMEM(block, BF16)] * (2 if last else 1),
         )
         if last:
-            upper = result
+            upper, theirs = result
         else:
             solved.append(result)
 
-    solution = [None] * NLEV
-    solution[NLEV - 1] = upper
+    solution, others = [None] * NLEV, [None] * NLEV
+    solution[NLEV - 1], others[NLEV - 1] = upper, swap(theirs, "row", 1)
     for level in range(NLEV - 2, -1, -1):
         pieces = [upper] + [swap(upper, "col", m) for m in range(1, cols)]
         sums = call(
@@ -307,28 +328,17 @@
             flops=4 * rows * cols * B * B * half,
         )
         passed = [swap(sums[m], "row", 2 * m) for m in range(1, groups)]
-        upper = call(
+        upper, theirs = call(
             functools.partial(final_body, level=level),
-            shape(block),
+            [shape(block), shape((half, B))],
             (solved[level], diag_own, diag_par, sums[0], *passed),
             [pltpu.VMEM(block, BF16)],
         )
-        solution[level] = upper
-
-    results = []
-    for level in range(NLEV):
-        both = solution[level]
-        mine = lax.dynamic_slice_in_dim(both, parity * B, B, axis=1).T
-        theirs = lax.dynamic_slice_in_dim(both, (1 - parity) * B, B, axis=1).T
-        got = swap(theirs, "row", 1)
-        results.append(
-            jnp.where(
-                parity == 0,
-                jnp.concatenate([mine, got], axis=1),
-                jnp.concatenate([got, mine], axis=1),
-            )
-        )
-    return jnp.stack(results)[:, None]
+        solution[level], others[level] = upper, swap(theirs, "row", 1)
+
+    return call(
+        finish_body, shape((NLEV, 1, B, 2 * half)), (*solution, *others)
+    )
 
 
 def solution(mesh):

time: 129 us -> 123 us (0.953)
  Pallas kernels: 18.7 us -> 9.85 us
    pallas_call x6, Pallas kernels: 7.83 us -> 1.11 us  [fetch(): pl.pallas_call(fetch_body, out_shape=[pltpu.VMEM(own.shape, own.dtype), p...]
    all_to_all x1, waiting for transfers between devices: 3.96 us -> 6.72 us  [per_device(): lax.all_to_all(sending, ('row', 'col'), split_axis=0, concat_axis=0, tile...]
    pallas_call x15 -> x16, Pallas kernels: 10.9 us -> 8.75 us  [call(): pl.pallas_call(body, out_shape=out_shape, in_specs=in_specs, out_specs=ou...]
    ppermute x44, waiting for transfers between devices: 42.1 us -> 40.5 us  [swap(): return lax.ppermute(value, axis, [(i, i ^ distance) for i in range(count)])]
  transfers between devices with their start and end apart: 45 -> 45, of which waited for: 29 -> 32; matrix products, arithmetic and copies ran while one was open for 3% -> 5% of each run, Pallas kernels for 11% -> 4%
where the time goes in v4:
time: 123 us; the launch traced here: 122 us
  starting transfers between devices  57 us (46%)
  waiting for transfers between devices  47.2 us (38%)
  Pallas kernels  9.85 us (8%)
  local copies, waits for them, and re-layouts  5.43 us (4%)
  other arithmetic  2.65 us (2%)
    ppermute x44, starting transfers between devices, swap(): return lax.ppermute(value, axis, [(i, i ^ distance) for i in range(count)])  50 us
    ppermute x44, waiting for transfers between devices, swap(): return lax.ppermute(value, axis, [(i, i ^ distance) for i in range(count)])  40.5 us
    pallas_call x16, Pallas kernels, call(): pl.pallas_call(body, out_shape=out_shape, in_specs=in_specs, out_specs=ou...  8.75 us
    all_to_all x1, starting transfers between devices, per_device(): lax.all_to_all(sending, ('row', 'col'), split_axis=0, concat_axis=0, tile...  6.96 us
    all_to_all x1, waiting for transfers between devices, per_device(): lax.all_to_all(sending, ('row', 'col'), split_axis=0, concat_axis=0, tile...  6.72 us
    slice x1, local copies, waits for them, and re-layouts, per_device(): tile = lower_blocks[level, 0, :, :, 0]  3.07 us
  transfers between devices with their start and end apart: 45, of which 32 were waited for; matrix products, arithmetic and copies ran while one was open for 5% of the time, Pallas kernels for 4%

profile of v4, /device:TPU:0, one launch (start us, length us, event | category | flops | bytes accessed | tf_op | source)
XLA Modules:
  0.0 122.4 jit_solution(6989771061172016893)
XLA Ops:
  2.2 1.2 %shard_map.55 = bf16[32,40,128]{2,1,0:T(8,128)(2,1)} custom-call(f32[512,256]{1,0:T(8,128)S(1)} %copy-done.1, s32[1,512]{1,0:T(1,128)S(1)} %bitcast.41), custom_call_target="tpu_custom_call" | custom-call | flops 134217728 | bytes 526336 | tf_op jit(solution)/shard_map/pallas_call | solution.py:32
  3.4 7.0 %all-to-all-start = ((bf16[32,40,128]{2,1,0:T(8,128)(2,1)}), bf16[32,40,128]{2,1,0:T(8,128)(2,1)S(1)}, u32[]{:S(2)}, u32[]{:S(2)}) async-start(bf16[32,40,128]{2,1,0:T(8,128)(2,1)} %shard_map.55), calls=%async_computation | async-start | bytes 655360 | tf_op jit(solution)/shard_map/all_to_all | solution.py:275
  11.1 3.1 %fusion = (bf16[1,1,4,128,1,8,128]{6,5,4,3,2,1,0:T(8,128)(2,1)S(1)}, bf16[1,1,4,128,1,8,128]{6,5,4,3,2,1,0:T(8,128)(2,1)S(1)}, bf16[1,1,4,128,1,8,128]{6,5,4,3,2,1,0:T(8,128)(2,1)}) fusion(bf16[3,1,4,128,1,8,128]{6,5,4,3,2,1,0:T(8,128)(2,1)} %param.8), kind=kLoop, calls=%fused_computation.6 | loop fusion | bytes 6291456 | tf_op jit(solution)/shard_map/slice | solution.py:264
  14.7 6.7 %all-to-all-done.arrived_ref = bf16[32,40,128]{2,1,0:T(8,128)(2,1)S(1)} async-done(((bf16[32,40,128]{2,1,0:T(8,128)(2,1)}), bf16[32,40,128]{2,1,0:T(8,128)(2,1)S(1)}, u32[]{:S(2)}, u32[]{:S(2)}) %all-to-all-start) | async-done | bytes 327712 | tf_op jit(solution)/shard_map/all_to_all | solution.py:275
  23.8 1.5 %collective-permute-start.3 = (bf16[128,256]{1,0:T(8,128)(2,1)S(1)}, bf16[128,256]{1,0:T(8,128)(2,1)S(1)}, u32[]{:S(2)}, u32[]{:S(2)}) collective-permute-start(bf16[128,256]{1,0:T(8,128)(2,1)S(1)} %shard_map.56.after_ref.refs_0_.solved_ref), channel_id=1, source_target_pairs={{0,16},{4,20},{8,24},{12,28},{16,0},{20,4},{24,8},{28,12},{1,17},{... | collective-permute-start | bytes 196616 | tf_op jit(solution)/shard_map/ppermute | solution.py:20
  26.5 1.5 %bitcast_multiply_fusion.1.own_ref = bf16[512,1024]{1,0:T(8,128)(2,1)S(1)} fusion(bf16[64,8,8,128]{3,2,1,0:T(8,128)(2,1)S(1)} %bitcast.44, bf16[64,8,8,128]{3,2,1,0:T(8,128)(2,1)} %bitcast.46), kind=kLoop, calls=%fused_computation.1 | loop fusion | flops 524288 | bytes 3145728 | tf_op jit(solution)/shard_map/mul | solution.py:266
  31.1 1.7 %collective-permute-start.6 = (bf16[128,256]{1,0:T(8,128)(2,1)S(1)}, bf16[128,256]{1,0:T(8,128)(2,1)S(1)}, u32[]{:S(2)}, u32[]{:S(2)}) collective-permute-start(bf16[128,256]{1,0:T(8,128)(2,1)S(1)} %get-tuple-element.61), channel_id=1, source_target_pairs={{0,2},{1,3},{2,0},{3,1},{4,6},{5,7},{6,4},{7,5},{8,10},{9,11},{10,... | collective-permute-start | bytes 196616 | tf_op jit(solution)/shard_map/ppermute | solution.py:20
  32.8 2.1 %collective-permute-start.7 = (bf16[128,256]{1,0:T(8,128)(2,1)S(1)}, bf16[128,256]{1,0:T(8,128)(2,1)S(1)}, u32[]{:S(2)}, u32[]{:S(2)}) collective-permute-start(bf16[128,256]{1,0:T(8,128)(2,1)S(1)} %get-tuple-element.62), channel_id=1, source_target_pairs={{0,3},{1,2},{2,1},{3,0},{4,7},{5,6},{6,5},{7,4},{8,11},{9,10},{10,... | collective-permute-start | bytes 196616 | tf_op jit(solution)/shard_map/ppermute | solution.py:20
  36.1 2.1 %collective-permute-done.6.refs_1_ = bf16[128,256]{1,0:T(8,128)(2,1)S(1)} collective-permute-done((bf16[128,256]{1,0:T(8,128)(2,1)S(1)}, bf16[128,256]{1,0:T(8,128)(2,1)S(1)}, u32[]{:S(2)}, u32[]{:S(2)}) %collective-permute-start.6) | collective-permute-done | bytes 65568 | tf_op jit(solution)/shard_map/ppermute | solution.py:20
  39.2 1.6 %collective-permute-start.11 = (bf16[128,256]{1,0:T(8,128)(2,1)S(1)}, bf16[128,256]{1,0:T(8,128)(2,1)S(1)}, u32[]{:S(2)}, u32[]{:S(2)}) collective-permute-start(bf16[128,256]{1,0:T(8,128)(2,1)S(1)} %shard_map.60.after_ref.refs_0_.solved_ref), channel_id=1, source_target_pairs={{0,24},{4,28},{8,16},{12,20},{16,8},{20,12},{24,0},{28,4},{1,25},{... | collective-permute-start | bytes 196616 | tf_op jit(solution)/shard_map/ppermute | solution.py:20
  40.8 1.2 %collective-permute-start.10 = (bf16[128,256]{1,0:T(8,128)(2,1)S(1)}, bf16[128,256]{1,0:T(8,128)(2,1)S(1)}, u32[]{:S(2)}, u32[]{:S(2)}) collective-permute-start(bf16[128,256]{1,0:T(8,128)(2,1)S(1)} %shard_map.60.after_ref.refs_0_.solved_ref), channel_id=1, source_target_pairs={{0,16},{4,20},{8,24},{12,28},{16,0},{20,4},{24,8},{28,12},{1,17},{... | collective-permute-start | bytes 196616 | tf_op jit(solution)/shard_map/ppermute | solution.py:20
  43.0 1.8 %collective-permute-done.11.refs_3_ = bf16[128,256]{1,0:T(8,128)(2,1)S(1)} collective-permute-done((bf16[128,256]{1,0:T(8,128)(2,1)S(1)}, bf16[128,256]{1,0:T(8,128)(2,1)S(1)}, u32[]{:S(2)}, u32[]{:S(2)}) %collective-permute-start.11) | collective-permute-done | bytes 65568 | tf_op jit(solution)/shard_map/ppermute | solution.py:20
  44.7 1.3 %collective-permute-done.10.refs_2_ = bf16[128,256]{1,0:T(8,128)(2,1)S(1)} collective-permute-done((bf16[128,256]{1,0:T(8,128)(2,1)S(1)}, bf16[128,256]{1,0:T(8,128)(2,1)S(1)}, u32[]{:S(2)}, u32[]{:S(2)}) %collective-permute-start.10) | collective-permute-done | bytes 65568 | tf_op jit(solution)/shard_map/ppermute | solution.py:20
  47.2 1.3 %collective-permute-start.12 = (bf16[128,256]{1,0:T(8,128)(2,1)S(1)}, bf16[128,256]{1,0:T(8,128)(2,1)S(1)}, u32[]{:S(2)}, u32[]{:S(2)}) collective-permute-start(bf16[128,256]{1,0:T(8,128)(2,1)S(1)} %get-tuple-element.68), channel_id=1, source_target_pairs={{0,1},{1,0},{2,3},{3,2},{4,5},{5,4},{6,7},{7,6},{8,9},{9,8},{10,11... | collective-permute-start | bytes 196616 | tf_op jit(solution)/shard_map/ppermute | solution.py:20
  48.5 1.3 %collective-permute-start.13 = (bf16[128,256]{1,0:T(8,128)(2,1)S(1)}, bf16[128,256]{1,0:T(8,128)(2,1)S(1)}, u32[]{:S(2)}, u32[]{:S(2)}) collective-permute-start(bf16[128,256]{1,0:T(8,128)(2,1)S(1)} %get-tuple-element.69), channel_id=1, source_target_pairs={{0,2},{1,3},{2,0},{3,1},{4,6},{5,7},{6,4},{7,5},{8,10},{9,11},{10,... | collective-permute-start | bytes 196616 | tf_op jit(solution)/shard_map/ppermute | solution.py:20
  49.8 1.9 %collective-permute-start.14 = (bf16[128,256]{1,0:T(8,128)(2,1)S(1)}, bf16[128,256]{1,0:T(8,128)(2,1)S(1)}, u32[]{:S(2)}, u32[]{:S(2)}) collective-permute-start(bf16[128,256]{1,0:T(8,128)(2,1)S(1)} %get-tuple-element.70), channel_id=1, source_target_pairs={{0,3},{1,2},{2,1},{3,0},{4,7},{5,6},{6,5},{7,4},{8,11},{9,10},{10,... | collective-permute-start | bytes 196616 | tf_op jit(solution)/shard_map/ppermute | solution.py:20
  51.7 4.7 %collective-permute-done.13.refs_1_ = bf16[128,256]{1,0:T(8,128)(2,1)S(1)} collective-permute-done((bf16[128,256]{1,0:T(8,128)(2,1)S(1)}, bf16[128,256]{1,0:T(8,128)(2,1)S(1)}, u32[]{:S(2)}, u32[]{:S(2)}) %collective-permute-start.13) | collective-permute-done | bytes 65568 | tf_op jit(solution)/shard_map/ppermute | solution.py:20
  56.6 1.4 %collective-permute-start.18 = (bf16[128,256]{1,0:T(8,128)(2,1)S(1)}, bf16[128,256]{1,0:T(8,128)(2,1)S(1)}, u32[]{:S(2)}, u32[]{:S(2)}) collective-permute-start(bf16[128,256]{1,0:T(8,128)(2,1)S(1)} %shard_map.63.after_ref.refs_0_.solved_ref), channel_id=1, source_target_pairs={{0,24},{4,28},{8,16},{12,20},{16,8},{20,12},{24,0},{28,4},{1,25},{... | collective-permute-start | bytes 196616 | tf_op jit(solution)/shard_map/ppermute | solution.py:20
  58.0 1.5 %collective-permute-start.17 = (bf16[128,256]{1,0:T(8,128)(2,1)S(1)}, bf16[128,256]{1,0:T(8,128)(2,1)S(1)}, u32[]{:S(2)}, u32[]{:S(2)}) collective-permute-start(bf16[128,256]{1,0:T(8,128)(2,1)S(1)} %shard_map.63.after_ref.refs_0_.solved_ref), channel_id=1, source_target_pairs={{0,16},{4,20},{8,24},{12,28},{16,0},{20,4},{24,8},{28,12},{1,17},{... | collective-permute-start | bytes 196616 | tf_op jit(solution)/shard_map/ppermute | solution.py:20
  60.3 1.5 %collective-permute-done.18.refs_3_ = bf16[128,256]{1,0:T(8,128)(2,1)S(1)} collective-permute-done((bf16[128,256]{1,0:T(8,128)(2,1)S(1)}, bf16[128,256]{1,0:T(8,128)(2,1)S(1)}, u32[]{:S(2)}, u32[]{:S(2)}) %collective-permute-start.18) | collective-permute-done | bytes 65568 | tf_op jit(solution)/shard_map/ppermute | solution.py:20
  62.5 1.2 collective-permute-done.16.refs_1_
  64.6 1.3 %collective-permute-start.19 = (bf16[128,256]{1,0:T(8,128)(2,1)S(1)}, bf16[128,256]{1,0:T(8,128)(2,1)S(1)}, u32[]{:S(2)}, u32[]{:S(2)}) collective-permute-start(bf16[128,256]{1,0:T(8,128)(2,1)S(1)} %get-tuple-element.76), channel_id=1, source_target_pairs={{0,1},{1,0},{2,3},{3,2},{4,5},{5,4},{6,7},{7,6},{8,9},{9,8},{10,11... | collective-permute-start | bytes 196616 | tf_op jit(solution)/shard_map/ppermute | solution.py:20
  66.0 1.3 %collective-permute-start.20 = (bf16[128,256]{1,0:T(8,128)(2,1)S(1)}, bf16[128,256]{1,0:T(8,128)(2,1)S(1)}, u32[]{:S(2)}, u32[]{:S(2)}) collective-permute-start(bf16[128,256]{1,0:T(8,128)(2,1)S(1)} %get-tuple-element.77), channel_id=1, source_target_pairs={{0,2},{1,3},{2,0},{3,1},{4,6},{5,7},{6,4},{7,5},{8,10},{9,11},{10,... | collective-permute-start | bytes 196616 | tf_op jit(solution)/shard_map/ppermute | solution.py:20
  67.2 1.9 %collective-permute-start.21 = (bf16[128,256]{1,0:T(8,128)(2,1)S(1)}, bf16[128,256]{1,0:T(8,128)(2,1)S(1)}, u32[]{:S(2)}, u32[]{:S(2)}) collective-permute-start(bf16[128,256]{1,0:T(8,128)(2,1)S(1)} %get-tuple-element.78), channel_id=1, source_target_pairs={{0,3},{1,2},{2,1},{3,0},{4,7},{5,6},{6,5},{7,4},{8,11},{9,10},{10,... | collective-permute-start | bytes 196616 | tf_op jit(solution)/shard_map/ppermute | solution.py:20
  70.0 1.8 %collective-permute-done.20.refs_1_ = bf16[128,256]{1,0:T(8,128)(2,1)S(1)} collective-permute-done((bf16[128,256]{1,0:T(8,128)(2,1)S(1)}, bf16[128,256]{1,0:T(8,128)(2,1)S(1)}, u32[]{:S(2)}, u32[]{:S(2)}) %collective-permute-start.20) | collective-permute-done | bytes 65568 | tf_op jit(solution)/shard_map/ppermute | solution.py:20
  71.8 1.5 %collective-permute-done.21.refs_2_ = bf16[128,256]{1,0:T(8,128)(2,1)S(1)} collective-permute-done((bf16[128,256]{1,0:T(8,128)(2,1)S(1)}, bf16[128,256]{1,0:T(8,128)(2,1)S(1)}, u32[]{:S(2)}, u32[]{:S(2)}) %collective-permute-start.21) | collective-permute-done | bytes 65568 | tf_op jit(solution)/shard_map/ppermute | solution.py:20
  73.7 2.0 %collective-permute-start.24 = (bf16[128,256]{1,0:T(8,128)(2,1)S(1)}, bf16[128,256]{1,0:T(8,128)(2,1)S(1)}, u32[]{:S(2)}, u32[]{:S(2)}) collective-permute-start(bf16[128,256]{1,0:T(8,128)(2,1)S(1)} %get-tuple-element.79.after_ref.refs_0_.refs_3_), channel_id=1, source_target_pairs={{0,3},{1,2},{2,1},{3,0},{4,7},{5,6},{6,5},{7,4},{8,11},{9,10},{10,... | collective-permute-start | bytes 196616 | tf_op jit(solution)/shard_map/ppermute | solution.py:20
  75.6 2.5 %collective-permute-start.22 = (bf16[128,256]{1,0:T(8,128)(2,1)S(1)}, bf16[128,256]{1,0:T(8,128)(2,1)S(1)}, u32[]{:S(2)}, u32[]{:S(2)}) collective-permute-start(bf16[128,256]{1,0:T(8,128)(2,1)S(1)} %get-tuple-element.79.after_ref.refs_0_.refs_3_), channel_id=1, source_target_pairs={{0,1},{1,0},{2,3},{3,2},{4,5},{5,4},{6,7},{7,6},{8,9},{9,8},{10,11... | collective-permute-start | bytes 196616 | tf_op jit(solution)/shard_map/ppermute | solution.py:20
  78.3 1.5 %collective-permute-done.24.refs_3_ = bf16[128,256]{1,0:T(8,128)(2,1)S(1)} collective-permute-done((bf16[128,256]{1,0:T(8,128)(2,1)S(1)}, bf16[128,256]{1,0:T(8,128)(2,1)S(1)}, u32[]{:S(2)}, u32[]{:S(2)}) %collective-permute-start.24) | collective-permute-done | bytes 65568 | tf_op jit(solution)/shard_map/ppermute | solution.py:20
  79.8 1.4 %collective-permute-done.23.refs_2_ = bf16[128,256]{1,0:T(8,128)(2,1)S(1)} collective-permute-done((bf16[128,256]{1,0:T(8,128)(2,1)S(1)}, bf16[128,256]{1,0:T(8,128)(2,1)S(1)}, u32[]{:S(2)}, u32[]{:S(2)}) %collective-permute-start.23) | collective-permute-done | bytes 65568 | tf_op jit(solution)/shard_map/ppermute | solution.py:20
  82.5 1.3 %collective-permute-start.26 = (bf16[128,256]{1,0:T(8,128)(2,1)S(1)}, bf16[128,256]{1,0:T(8,128)(2,1)S(1)}, u32[]{:S(2)}, u32[]{:S(2)}) collective-permute-start(bf16[128,256]{1,0:T(8,128)(2,1)S(1)} %get-tuple-element.84), channel_id=1, source_target_pairs={{0,16},{4,20},{8,24},{12,28},{16,0},{20,4},{24,8},{28,12},{1,17},{... | collective-permute-start | bytes 196616 | tf_op jit(solution)/shard_map/ppermute | solution.py:20
  83.8 1.5 %collective-permute-start.27 = (bf16[128,256]{1,0:T(8,128)(2,1)S(1)}, bf16[128,256]{1,0:T(8,128)(2,1)S(1)}, u32[]{:S(2)}, u32[]{:S(2)}) collective-permute-start(bf16[128,256]{1,0:T(8,128)(2,1)S(1)} %get-tuple-element.85), channel_id=1, source_target_pairs={{0,24},{4,28},{8,16},{12,20},{16,8},{20,12},{24,0},{28,4},{1,25},{... | collective-permute-start | bytes 196616 | tf_op jit(solution)/shard_map/ppermute | solution.py:20
  86.8 2.2 %collective-permute-done.27.refs_2_ = bf16[128,256]{1,0:T(8,128)(2,1)S(1)} collective-permute-done((bf16[128,256]{1,0:T(8,128)(2,1)S(1)}, bf16[128,256]{1,0:T(8,128)(2,1)S(1)}, u32[]{:S(2)}, u32[]{:S(2)}) %collective-permute-start.27) | collective-permute-done | bytes 65568 | tf_op jit(solution)/shard_map/ppermute | solution.py:20
  89.1 2.0 %collective-permute-start.30 = (bf16[128,256]{1,0:T(8,128)(2,1)S(1)}, bf16[128,256]{1,0:T(8,128)(2,1)S(1)}, u32[]{:S(2)}, u32[]{:S(2)}) collective-permute-start(bf16[128,256]{1,0:T(8,128)(2,1)S(1)} %get-tuple-element.86.after_ref.refs_0_.refs_2_), channel_id=1, source_target_pairs={{0,3},{1,2},{2,1},{3,0},{4,7},{5,6},{6,5},{7,4},{8,11},{9,10},{10,... | collective-permute-start | bytes 196616 | tf_op jit(solution)/shard_map/ppermute | solution.py:20
  91.8 1.7 %collective-permute-start.28 = (bf16[128,256]{1,0:T(8,128)(2,1)S(1)}, bf16[128,256]{1,0:T(8,128)(2,1)S(1)}, u32[]{:S(2)}, u32[]{:S(2)}) collective-permute-start(bf16[128,256]{1,0:T(8,128)(2,1)S(1)} %get-tuple-element.86.after_ref.refs_0_.refs_2_), channel_id=1, source_target_pairs={{0,1},{1,0},{2,3},{3,2},{4,5},{5,4},{6,7},{7,6},{8,9},{9,8},{10,11... | collective-permute-start | bytes 196616 | tf_op jit(solution)/shard_map/ppermute | solution.py:20
  93.8 1.5 %collective-permute-done.30.refs_3_ = bf16[128,256]{1,0:T(8,128)(2,1)S(1)} collective-permute-done((bf16[128,256]{1,0:T(8,128)(2,1)S(1)}, bf16[128,256]{1,0:T(8,128)(2,1)S(1)}, u32[]{:S(2)}, u32[]{:S(2)}) %collective-permute-start.30) | collective-permute-done | bytes 65568 | tf_op jit(solution)/shard_map/ppermute | solution.py:20
  95.3 1.6 %collective-permute-done.29.refs_2_ = bf16[128,256]{1,0:T(8,128)(2,1)S(1)} collective-permute-done((bf16[128,256]{1,0:T(8,128)(2,1)S(1)}, bf16[128,256]{1,0:T(8,128)(2,1)S(1)}, u32[]{:S(2)}, u32[]{:S(2)}) %collective-permute-start.29) | collective-permute-done | bytes 65568 | tf_op jit(solution)/shard_map/ppermute | solution.py:20
  97.9 1.5 %collective-permute-start.32 = (bf16[128,256]{1,0:T(8,128)(2,1)S(1)}, bf16[128,256]{1,0:T(8,128)(2,1)S(1)}, u32[]{:S(2)}, u32[]{:S(2)}) collective-permute-start(bf16[128,256]{1,0:T(8,128)(2,1)S(1)} %get-tuple-element.91), channel_id=1, source_target_pairs={{0,16},{4,20},{8,24},{12,28},{16,0},{20,4},{24,8},{28,12},{1,17},{... | collective-permute-start | bytes 196616 | tf_op jit(solution)/shard_map/ppermute | solution.py:20
  99.4 1.4 %collective-permute-start.33 = (bf16[128,256]{1,0:T(8,128)(2,1)S(1)}, bf16[128,256]{1,0:T(8,128)(2,1)S(1)}, u32[]{:S(2)}, u32[]{:S(2)}) collective-permute-start(bf16[128,256]{1,0:T(8,128)(2,1)S(1)} %get-tuple-element.92), channel_id=1, source_target_pairs={{0,24},{4,28},{8,16},{12,20},{16,8},{20,12},{24,0},{28,4},{1,25},{... | collective-permute-start | bytes 196616 | tf_op jit(solution)/shard_map/ppermute | solution.py:20
  102.2 2.4 %collective-permute-done.33.refs_2_ = bf16[128,256]{1,0:T(8,128)(2,1)S(1)} collective-permute-done((bf16[128,256]{1,0:T(8,128)(2,1)S(1)}, bf16[128,256]{1,0:T(8,128)(2,1)S(1)}, u32[]{:S(2)}, u32[]{:S(2)}) %collective-permute-start.33) | collective-permute-done | bytes 65568 | tf_op jit(solution)/shard_map/ppermute | solution.py:20
  104.8 2.0 %collective-permute-start.36 = (bf16[128,256]{1,0:T(8,128)(2,1)S(1)}, bf16[128,256]{1,0:T(8,128)(2,1)S(1)}, u32[]{:S(2)}, u32[]{:S(2)}) collective-permute-start(bf16[128,256]{1,0:T(8,128)(2,1)S(1)} %get-tuple-element.93.after_ref.refs_0_.refs_1_), channel_id=1, source_target_pairs={{0,3},{1,2},{2,1},{3,0},{4,7},{5,6},{6,5},{7,4},{8,11},{9,10},{10,... | collective-permute-start | bytes 196616 | tf_op jit(solution)/shard_map/ppermute | solution.py:20
  107.4 1.9 %collective-permute-start.34 = (bf16[128,256]{1,0:T(8,128)(2,1)S(1)}, bf16[128,256]{1,0:T(8,128)(2,1)S(1)}, u32[]{:S(2)}, u32[]{:S(2)}) collective-permute-start(bf16[128,256]{1,0:T(8,128)(2,1)S(1)} %get-tuple-element.93.after_ref.refs_0_.refs_1_), channel_id=1, source_target_pairs={{0,1},{1,0},{2,3},{3,2},{4,5},{5,4},{6,7},{7,6},{8,9},{9,8},{10,11... | collective-permute-start | bytes 196616 | tf_op jit(solution)/shard_map/ppermute | solution.py:20
  109.4 1.5 %collective-permute-done.36.refs_3_ = bf16[128,256]{1,0:T(8,128)(2,1)S(1)} collective-permute-done((bf16[128,256]{1,0:T(8,128)(2,1)S(1)}, bf16[128,256]{1,0:T(8,128)(2,1)S(1)}, u32[]{:S(2)}, u32[]{:S(2)}) %collective-permute-start.36) | collective-permute-done | bytes 65568 | tf_op jit(solution)/shard_map/ppermute | solution.py:20
  110.9 1.4 %collective-permute-done.35.refs_2_ = bf16[128,256]{1,0:T(8,128)(2,1)S(1)} collective-permute-done((bf16[128,256]{1,0:T(8,128)(2,1)S(1)}, bf16[128,256]{1,0:T(8,128)(2,1)S(1)}, u32[]{:S(2)}, u32[]{:S(2)}) %collective-permute-start.35) | collective-permute-done | bytes 65568 | tf_op jit(solution)/shard_map/ppermute | solution.py:20
  113.6 1.3 %collective-permute-start.38 = (bf16[128,256]{1,0:T(8,128)(2,1)S(1)}, bf16[128,256]{1,0:T(8,128)(2,1)S(1)}, u32[]{:S(2)}, u32[]{:S(2)}) collective-permute-start(bf16[128,256]{1,0:T(8,128)(2,1)S(1)} %get-tuple-element.98), channel_id=1, source_target_pairs={{0,16},{4,20},{8,24},{12,28},{16,0},{20,4},{24,8},{28,12},{1,17},{... | collective-permute-start | bytes 196616 | tf_op jit(solution)/shard_map/ppermute | solution.py:20
  114.9 1.5 %collective-permute-start.39 = (bf16[128,256]{1,0:T(8,128)(2,1)S(1)}, bf16[128,256]{1,0:T(8,128)(2,1)S(1)}, u32[]{:S(2)}, u32[]{:S(2)}) collective-permute-start(bf16[128,256]{1,0:T(8,128)(2,1)S(1)} %get-tuple-element.99), channel_id=1, source_target_pairs={{0,24},{4,28},{8,16},{12,20},{16,8},{20,12},{24,0},{28,4},{1,25},{... | collective-permute-start | bytes 196616 | tf_op jit(solution)/shard_map/ppermute | solution.py:20
  117.9 2.2 %collective-permute-done.39.refs_2_ = bf16[128,256]{1,0:T(8,128)(2,1)S(1)} collective-permute-done((bf16[128,256]{1,0:T(8,128)(2,1)S(1)}, bf16[128,256]{1,0:T(8,128)(2,1)S(1)}, u32[]{:S(2)}, u32[]{:S(2)}) %collective-permute-start.39) | collective-permute-done | bytes 65568 | tf_op jit(solution)/shard_map/ppermute | solution.py:20
  120.4 1.2 collective-permute-done.40.refs_4_
  (81 shorter events, 29.5 us)
Async XLA Ops:
  0.0 14.6 %collective-permute-start = (bf16[4,128,128]{2,1,0:T(8,128)(2,1)}, bf16[4,128,128]{2,1,0:T(8,128)(2,1)S(1)}, u32[]{:S(2)}, u32[]{:S(2)}) collective-permute-start(bf16[4,128,128]{2,1,0:T(8,128)(2,1)} %bitcast.33), channel_id=1, source_target_pairs={{0,4},{4,0},{8,12},{12,8},{16,20},{20,16},{24,28},{28,24},{1,5},{5... | collective-permute-start | bytes 393224 | tf_op jit(solution)/shard_map/ppermute | solution.py:20
  0.5 1.0 copy-start.1
  1.5 0.7 copy-start.2
  3.4 18.0 %all-to-all-start = ((bf16[32,40,128]{2,1,0:T(8,128)(2,1)}), bf16[32,40,128]{2,1,0:T(8,128)(2,1)S(1)}, u32[]{:S(2)}, u32[]{:S(2)}) async-start(bf16[32,40,128]{2,1,0:T(8,128)(2,1)} %shard_map.55), calls=%async_computation | async-start | bytes 655360 | tf_op jit(solution)/shard_map/all_to_all | solution.py:275
  14.2 7.2 %copy-start = (bf16[4,1,128,128]{3,2,1,0:T(8,128)(2,1)S(1)}, bf16[4,1,128,128]{3,2,1,0:T(8,128)(2,1)}, u32[]{:S(2)}) copy-start(bf16[4,1,128,128]{3,2,1,0:T(8,128)(2,1)} %param.7) | copy-start | bytes 393220
  21.9 6.1 %collective-permute-start.1 = (bf16[512,1024]{1,0:T(8,128)(2,1)S(1)}, bf16[512,1024]{1,0:T(8,128)(2,1)S(1)}, u32[]{:S(2)}, u32[]{:S(2)}) collective-permute-start(bf16[512,1024]{1,0:T(8,128)(2,1)S(1)} %bitcast_multiply_fusion.2.own_ref), channel_id=1, source_target_pairs={{0,4},{4,0},{8,12},{12,8},{16,20},{20,16},{24,28},{28,24},{1,5},{5... | collective-permute-start | bytes 3145736 | tf_op jit(solution)/shard_map/ppermute | solution.py:20
  22.8 5.7 %collective-permute-start.4 = (bf16[128,256]{1,0:T(8,128)(2,1)S(1)}, bf16[128,256]{1,0:T(8,128)(2,1)S(1)}, u32[]{:S(2)}, u32[]{:S(2)}) collective-permute-start(bf16[128,256]{1,0:T(8,128)(2,1)S(1)} %shard_map.56.after_ref.refs_0_.solved_ref), channel_id=1, source_target_pairs={{0,24},{4,28},{8,16},{12,20},{16,8},{20,12},{24,0},{28,4},{1,25},{... | collective-permute-start | bytes 196616 | tf_op jit(solution)/shard_map/ppermute | solution.py:20
  23.8 5.3 %collective-permute-start.3 = (bf16[128,256]{1,0:T(8,128)(2,1)S(1)}, bf16[128,256]{1,0:T(8,128)(2,1)S(1)}, u32[]{:S(2)}, u32[]{:S(2)}) collective-permute-start(bf16[128,256]{1,0:T(8,128)(2,1)S(1)} %shard_map.56.after_ref.refs_0_.solved_ref), channel_id=1, source_target_pairs={{0,16},{4,20},{8,24},{12,28},{16,0},{20,4},{24,8},{28,12},{1,17},{... | collective-permute-start | bytes 196616 | tf_op jit(solution)/shard_map/ppermute | solution.py:20
  25.3 4.3 %collective-permute-start.2 = (bf16[128,256]{1,0:T(8,128)(2,1)S(1)}, bf16[128,256]{1,0:T(8,128)(2,1)S(1)}, u32[]{:S(2)}, u32[]{:S(2)}) collective-permute-start(bf16[128,256]{1,0:T(8,128)(2,1)S(1)} %shard_map.56.after_ref.refs_0_.solved_ref), channel_id=1, source_target_pairs={{0,8},{4,12},{8,0},{12,4},{16,24},{20,28},{24,16},{28,20},{1,9},{5... | collective-permute-start | bytes 196616 | tf_op jit(solution)/shard_map/ppermute | solution.py:20
  27.9 14.8 %collective-permute-start.8 = (bf16[512,1024]{1,0:T(8,128)(2,1)S(1)}, bf16[512,1024]{1,0:T(8,128)(2,1)S(1)}, u32[]{:S(2)}, u32[]{:S(2)}) collective-permute-start(bf16[512,1024]{1,0:T(8,128)(2,1)S(1)} %bitcast_multiply_fusion.1.own_ref), channel_id=1, source_target_pairs={{0,4},{4,0},{8,12},{12,8},{16,20},{20,16},{24,28},{28,24},{1,5},{5... | collective-permute-start | bytes 3145736 | tf_op jit(solution)/shard_map/ppermute | solution.py:20
  30.5 5.6 %collective-permute-start.5 = (bf16[128,256]{1,0:T(8,128)(2,1)S(1)}, bf16[128,256]{1,0:T(8,128)(2,1)S(1)}, u32[]{:S(2)}, u32[]{:S(2)}) collective-permute-start(bf16[128,256]{1,0:T(8,128)(2,1)S(1)} %get-tuple-element.60), channel_id=1, source_target_pairs={{0,1},{1,0},{2,3},{3,2},{4,5},{5,4},{6,7},{7,6},{8,9},{9,8},{10,11... | collective-permute-start | bytes 196616 | tf_op jit(solution)/shard_map/ppermute | solution.py:20
  31.1 7.1 %collective-permute-start.6 = (bf16[128,256]{1,0:T(8,128)(2,1)S(1)}, bf16[128,256]{1,0:T(8,128)(2,1)S(1)}, u32[]{:S(2)}, u32[]{:S(2)}) collective-permute-start(bf16[128,256]{1,0:T(8,128)(2,1)S(1)} %get-tuple-element.61), channel_id=1, source_target_pairs={{0,2},{1,3},{2,0},{3,1},{4,6},{5,7},{6,4},{7,5},{8,10},{9,11},{10,... | collective-permute-start | bytes 196616 | tf_op jit(solution)/shard_map/ppermute | solution.py:20
  32.8 6.1 %collective-permute-start.7 = (bf16[128,256]{1,0:T(8,128)(2,1)S(1)}, bf16[128,256]{1,0:T(8,128)(2,1)S(1)}, u32[]{:S(2)}, u32[]{:S(2)}) collective-permute-start(bf16[128,256]{1,0:T(8,128)(2,1)S(1)} %get-tuple-element.62), channel_id=1, source_target_pairs={{0,3},{1,2},{2,1},{3,0},{4,7},{5,6},{6,5},{7,4},{8,11},{9,10},{10,... | collective-permute-start | bytes 196616 | tf_op jit(solution)/shard_map/ppermute | solution.py:20
  39.1 21.0 %collective-permute-start.15 = (bf16[512,1024]{1,0:T(8,128)(2,1)S(1)}, bf16[512,1024]{1,0:T(8,128)(2,1)S(1)}, u32[]{:S(2)}, u32[]{:S(2)}) collective-permute-start(bf16[512,1024]{1,0:T(8,128)(2,1)S(1)} %bitcast_multiply_fusion.own_ref), channel_id=1, source_target_pairs={{0,4},{4,0},{8,12},{12,8},{16,20},{20,16},{24,28},{28,24},{1,5},{5... | collective-permute-start | bytes 3145736 | tf_op jit(solution)/shard_map/ppermute | solution.py:20
  39.2 5.5 %collective-permute-start.11 = (bf16[128,256]{1,0:T(8,128)(2,1)S(1)}, bf16[128,256]{1,0:T(8,128)(2,1)S(1)}, u32[]{:S(2)}, u32[]{:S(2)}) collective-permute-start(bf16[128,256]{1,0:T(8,128)(2,1)S(1)} %shard_map.60.after_ref.refs_0_.solved_ref), channel_id=1, source_target_pairs={{0,24},{4,28},{8,16},{12,20},{16,8},{20,12},{24,0},{28,4},{1,25},{... | collective-permute-start | bytes 196616 | tf_op jit(solution)/shard_map/ppermute | solution.py:20
  40.8 5.2 %collective-permute-start.10 = (bf16[128,256]{1,0:T(8,128)(2,1)S(1)}, bf16[128,256]{1,0:T(8,128)(2,1)S(1)}, u32[]{:S(2)}, u32[]{:S(2)}) collective-permute-start(bf16[128,256]{1,0:T(8,128)(2,1)S(1)} %shard_map.60.after_ref.refs_0_.solved_ref), channel_id=1, source_target_pairs={{0,16},{4,20},{8,24},{12,28},{16,0},{20,4},{24,8},{28,12},{1,17},{... | collective-permute-start | bytes 196616 | tf_op jit(solution)/shard_map/ppermute | solution.py:20
  42.0 4.3 %collective-permute-start.9 = (bf16[128,256]{1,0:T(8,128)(2,1)S(1)}, bf16[128,256]{1,0:T(8,128)(2,1)S(1)}, u32[]{:S(2)}, u32[]{:S(2)}) collective-permute-start(bf16[128,256]{1,0:T(8,128)(2,1)S(1)} %shard_map.60.after_ref.refs_0_.solved_ref), channel_id=1, source_target_pairs={{0,8},{4,12},{8,0},{12,4},{16,24},{20,28},{24,16},{28,20},{1,9},{5... | collective-permute-start | bytes 196616 | tf_op jit(solution)/shard_map/ppermute | solution.py:20
  47.2 4.5 %collective-permute-start.12 = (bf16[128,256]{1,0:T(8,128)(2,1)S(1)}, bf16[128,256]{1,0:T(8,128)(2,1)S(1)}, u32[]{:S(2)}, u32[]{:S(2)}) collective-permute-start(bf16[128,256]{1,0:T(8,128)(2,1)S(1)} %get-tuple-element.68), channel_id=1, source_target_pairs={{0,1},{1,0},{2,3},{3,2},{4,5},{5,4},{6,7},{7,6},{8,9},{9,8},{10,11... | collective-permute-start | bytes 196616 | tf_op jit(solution)/shard_map/ppermute | solution.py:20
  48.5 7.9 %collective-permute-start.13 = (bf16[128,256]{1,0:T(8,128)(2,1)S(1)}, bf16[128,256]{1,0:T(8,128)(2,1)S(1)}, u32[]{:S(2)}, u32[]{:S(2)}) collective-permute-start(bf16[128,256]{1,0:T(8,128)(2,1)S(1)} %get-tuple-element.69), channel_id=1, source_target_pairs={{0,2},{1,3},{2,0},{3,1},{4,6},{5,7},{6,4},{7,5},{8,10},{9,11},{10,... | collective-permute-start | bytes 196616 | tf_op jit(solution)/shard_map/ppermute | solution.py:20
  49.8 6.6 %collective-permute-start.14 = (bf16[128,256]{1,0:T(8,128)(2,1)S(1)}, bf16[128,256]{1,0:T(8,128)(2,1)S(1)}, u32[]{:S(2)}, u32[]{:S(2)}) collective-permute-start(bf16[128,256]{1,0:T(8,128)(2,1)S(1)} %get-tuple-element.70), channel_id=1, source_target_pairs={{0,3},{1,2},{2,1},{3,0},{4,7},{5,6},{6,5},{7,4},{8,11},{9,10},{10,... | collective-permute-start | bytes 196616 | tf_op jit(solution)/shard_map/ppermute | solution.py:20
  56.6 5.3 %collective-permute-start.18 = (bf16[128,256]{1,0:T(8,128)(2,1)S(1)}, bf16[128,256]{1,0:T(8,128)(2,1)S(1)}, u32[]{:S(2)}, u32[]{:S(2)}) collective-permute-start(bf16[128,256]{1,0:T(8,128)(2,1)S(1)} %shard_map.63.after_ref.refs_0_.solved_ref), channel_id=1, source_target_pairs={{0,24},{4,28},{8,16},{12,20},{16,8},{20,12},{24,0},{28,4},{1,25},{... | collective-permute-start | bytes 196616 | tf_op jit(solution)/shard_map/ppermute | solution.py:20
  58.0 4.6 %collective-permute-start.17 = (bf16[128,256]{1,0:T(8,128)(2,1)S(1)}, bf16[128,256]{1,0:T(8,128)(2,1)S(1)}, u32[]{:S(2)}, u32[]{:S(2)}) collective-permute-start(bf16[128,256]{1,0:T(8,128)(2,1)S(1)} %shard_map.63.after_ref.refs_0_.solved_ref), channel_id=1, source_target_pairs={{0,16},{4,20},{8,24},{12,28},{16,0},{20,4},{24,8},{28,12},{1,17},{... | collective-permute-start | bytes 196616 | tf_op jit(solution)/shard_map/ppermute | solution.py:20
  59.4 4.3 %collective-permute-start.16 = (bf16[128,256]{1,0:T(8,128)(2,1)S(1)}, bf16[128,256]{1,0:T(8,128)(2,1)S(1)}, u32[]{:S(2)}, u32[]{:S(2)}) collective-permute-start(bf16[128,256]{1,0:T(8,128)(2,1)S(1)} %shard_map.63.after_ref.refs_0_.solved_ref), channel_id=1, source_target_pairs={{0,8},{4,12},{8,0},{12,4},{16,24},{20,28},{24,16},{28,20},{1,9},{5... | collective-permute-start | bytes 196616 | tf_op jit(solution)/shard_map/ppermute | solution.py:20
  64.6 5.4 %collective-permute-start.19 = (bf16[128,256]{1,0:T(8,128)(2,1)S(1)}, bf16[128,256]{1,0:T(8,128)(2,1)S(1)}, u32[]{:S(2)}, u32[]{:S(2)}) collective-permute-start(bf16[128,256]{1,0:T(8,128)(2,1)S(1)} %get-tuple-element.76), channel_id=1, source_target_pairs={{0,1},{1,0},{2,3},{3,2},{4,5},{5,4},{6,7},{7,6},{8,9},{9,8},{10,11... | collective-permute-start | bytes 196616 | tf_op jit(solution)/shard_map/ppermute | solution.py:20
  66.0 5.9 %collective-permute-start.20 = (bf16[128,256]{1,0:T(8,128)(2,1)S(1)}, bf16[128,256]{1,0:T(8,128)(2,1)S(1)}, u32[]{:S(2)}, u32[]{:S(2)}) collective-permute-start(bf16[128,256]{1,0:T(8,128)(2,1)S(1)} %get-tuple-element.77), channel_id=1, source_target_pairs={{0,2},{1,3},{2,0},{3,1},{4,6},{5,7},{6,4},{7,5},{8,10},{9,11},{10,... | collective-permute-start | bytes 196616 | tf_op jit(solution)/shard_map/ppermute | solution.py:20
  67.2 6.1 %collective-permute-start.21 = (bf16[128,256]{1,0:T(8,128)(2,1)S(1)}, bf16[128,256]{1,0:T(8,128)(2,1)S(1)}, u32[]{:S(2)}, u32[]{:S(2)}) collective-permute-start(bf16[128,256]{1,0:T(8,128)(2,1)S(1)} %get-tuple-element.78), channel_id=1, source_target_pairs={{0,3},{1,2},{2,1},{3,0},{4,7},{5,6},{6,5},{7,4},{8,11},{9,10},{10,... | collective-permute-start | bytes 196616 | tf_op jit(solution)/shard_map/ppermute | solution.py:20
  73.7 6.1 %collective-permute-start.24 = (bf16[128,256]{1,0:T(8,128)(2,1)S(1)}, bf16[128,256]{1,0:T(8,128)(2,1)S(1)}, u32[]{:S(2)}, u32[]{:S(2)}) collective-permute-start(bf16[128,256]{1,0:T(8,128)(2,1)S(1)} %get-tuple-element.79.after_ref.refs_0_.refs_3_), channel_id=1, source_target_pairs={{0,3},{1,2},{2,1},{3,0},{4,7},{5,6},{6,5},{7,4},{8,11},{9,10},{10,... | collective-permute-start | bytes 196616 | tf_op jit(solution)/shard_map/ppermute | solution.py:20
  75.6 5.6 %collective-permute-start.23 = (bf16[128,256]{1,0:T(8,128)(2,1)S(1)}, bf16[128,256]{1,0:T(8,128)(2,1)S(1)}, u32[]{:S(2)}, u32[]{:S(2)}) collective-permute-start(bf16[128,256]{1,0:T(8,128)(2,1)S(1)} %get-tuple-element.79.after_ref.refs_0_.refs_3_), channel_id=1, source_target_pairs={{0,2},{1,3},{2,0},{3,1},{4,6},{5,7},{6,4},{7,5},{8,10},{9,11},{10,... | collective-permute-start | bytes 196616 | tf_op jit(solution)/shard_map/ppermute | solution.py:20
  75.6 5.6 %collective-permute-start.22 = (bf16[128,256]{1,0:T(8,128)(2,1)S(1)}, bf16[128,256]{1,0:T(8,128)(2,1)S(1)}, u32[]{:S(2)}, u32[]{:S(2)}) collective-permute-start(bf16[128,256]{1,0:T(8,128)(2,1)S(1)} %get-tuple-element.79.after_ref.refs_0_.refs_3_), channel_id=1, source_target_pairs={{0,1},{1,0},{2,3},{3,2},{4,5},{5,4},{6,7},{7,6},{8,9},{9,8},{10,11... | collective-permute-start | bytes 196616 | tf_op jit(solution)/shard_map/ppermute | solution.py:20
  81.7 4.3 %collective-permute-start.25 = (bf16[128,256]{1,0:T(8,128)(2,1)S(1)}, bf16[128,256]{1,0:T(8,128)(2,1)S(1)}, u32[]{:S(2)}, u32[]{:S(2)}) collective-permute-start(bf16[128,256]{1,0:T(8,128)(2,1)S(1)} %get-tuple-element.83), channel_id=1, source_target_pairs={{0,8},{4,12},{8,0},{12,4},{16,24},{20,28},{24,16},{28,20},{1,9},{5... | collective-permute-start | bytes 196616 | tf_op jit(solution)/shard_map/ppermute | solution.py:20
  82.5 4.3 %collective-permute-start.26 = (bf16[128,256]{1,0:T(8,128)(2,1)S(1)}, bf16[128,256]{1,0:T(8,128)(2,1)S(1)}, u32[]{:S(2)}, u32[]{:S(2)}) collective-permute-start(bf16[128,256]{1,0:T(8,128)(2,1)S(1)} %get-tuple-element.84), channel_id=1, source_target_pairs={{0,16},{4,20},{8,24},{12,28},{16,0},{20,4},{24,8},{28,12},{1,17},{... | collective-permute-start | bytes 196616 | tf_op jit(solution)/shard_map/ppermute | solution.py:20
  83.8 5.2 %collective-permute-start.27 = (bf16[128,256]{1,0:T(8,128)(2,1)S(1)}, bf16[128,256]{1,0:T(8,128)(2,1)S(1)}, u32[]{:S(2)}, u32[]{:S(2)}) collective-permute-start(bf16[128,256]{1,0:T(8,128)(2,1)S(1)} %get-tuple-element.85), channel_id=1, source_target_pairs={{0,24},{4,28},{8,16},{12,20},{16,8},{20,12},{24,0},{28,4},{1,25},{... | collective-permute-start | bytes 196616 | tf_op jit(solution)/shard_map/ppermute | solution.py:20
  89.1 6.1 %collective-permute-start.30 = (bf16[128,256]{1,0:T(8,128)(2,1)S(1)}, bf16[128,256]{1,0:T(8,128)(2,1)S(1)}, u32[]{:S(2)}, u32[]{:S(2)}) collective-permute-start(bf16[128,256]{1,0:T(8,128)(2,1)S(1)} %get-tuple-element.86.after_ref.refs_0_.refs_2_), channel_id=1, source_target_pairs={{0,3},{1,2},{2,1},{3,0},{4,7},{5,6},{6,5},{7,4},{8,11},{9,10},{10,... | collective-permute-start | bytes 196616 | tf_op jit(solution)/shard_map/ppermute | solution.py:20
  91.1 5.7 %collective-permute-start.29 = (bf16[128,256]{1,0:T(8,128)(2,1)S(1)}, bf16[128,256]{1,0:T(8,128)(2,1)S(1)}, u32[]{:S(2)}, u32[]{:S(2)}) collective-permute-start(bf16[128,256]{1,0:T(8,128)(2,1)S(1)} %get-tuple-element.86.after_ref.refs_0_.refs_2_), channel_id=1, source_target_pairs={{0,2},{1,3},{2,0},{3,1},{4,6},{5,7},{6,4},{7,5},{8,10},{9,11},{10,... | collective-permute-start | bytes 196616 | tf_op jit(solution)/shard_map/ppermute | solution.py:20
  91.8 5.0 %collective-permute-start.28 = (bf16[128,256]{1,0:T(8,128)(2,1)S(1)}, bf16[128,256]{1,0:T(8,128)(2,1)S(1)}, u32[]{:S(2)}, u32[]{:S(2)}) collective-permute-start(bf16[128,256]{1,0:T(8,128)(2,1)S(1)} %get-tuple-element.86.after_ref.refs_0_.refs_2_), channel_id=1, source_target_pairs={{0,1},{1,0},{2,3},{3,2},{4,5},{5,4},{6,7},{7,6},{8,9},{9,8},{10,11... | collective-permute-start | bytes 196616 | tf_op jit(solution)/shard_map/ppermute | solution.py:20
  97.3 4.3 %collective-permute-start.31 = (bf16[128,256]{1,0:T(8,128)(2,1)S(1)}, bf16[128,256]{1,0:T(8,128)(2,1)S(1)}, u32[]{:S(2)}, u32[]{:S(2)}) collective-permute-start(bf16[128,256]{1,0:T(8,128)(2,1)S(1)} %get-tuple-element.90), channel_id=1, source_target_pairs={{0,8},{4,12},{8,0},{12,4},{16,24},{20,28},{24,16},{28,20},{1,9},{5... | collective-permute-start | bytes 196616 | tf_op jit(solution)/shard_map/ppermute | solution.py:20
  97.9 4.3 %collective-permute-start.32 = (bf16[128,256]{1,0:T(8,128)(2,1)S(1)}, bf16[128,256]{1,0:T(8,128)(2,1)S(1)}, u32[]{:S(2)}, u32[]{:S(2)}) collective-permute-start(bf16[128,256]{1,0:T(8,128)(2,1)S(1)} %get-tuple-element.91), channel_id=1, source_target_pairs={{0,16},{4,20},{8,24},{12,28},{16,0},{20,4},{24,8},{28,12},{1,17},{... | collective-permute-start | bytes 196616 | tf_op jit(solution)/shard_map/ppermute | solution.py:20
  99.4 5.2 %collective-permute-start.33 = (bf16[128,256]{1,0:T(8,128)(2,1)S(1)}, bf16[128,256]{1,0:T(8,128)(2,1)S(1)}, u32[]{:S(2)}, u32[]{:S(2)}) collective-permute-start(bf16[128,256]{1,0:T(8,128)(2,1)S(1)} %get-tuple-element.92), channel_id=1, source_target_pairs={{0,24},{4,28},{8,16},{12,20},{16,8},{20,12},{24,0},{28,4},{1,25},{... | collective-permute-start | bytes 196616 | tf_op jit(solution)/shard_map/ppermute | solution.py:20
  104.8 6.1 %collective-permute-start.36 = (bf16[128,256]{1,0:T(8,128)(2,1)S(1)}, bf16[128,256]{1,0:T(8,128)(2,1)S(1)}, u32[]{:S(2)}, u32[]{:S(2)}) collective-permute-start(bf16[128,256]{1,0:T(8,128)(2,1)S(1)} %get-tuple-element.93.after_ref.refs_0_.refs_1_), channel_id=1, source_target_pairs={{0,3},{1,2},{2,1},{3,0},{4,7},{5,6},{6,5},{7,4},{8,11},{9,10},{10,... | collective-permute-start | bytes 196616 | tf_op jit(solution)/shard_map/ppermute | solution.py:20
  106.8 5.6 %collective-permute-start.35 = (bf16[128,256]{1,0:T(8,128)(2,1)S(1)}, bf16[128,256]{1,0:T(8,128)(2,1)S(1)}, u32[]{:S(2)}, u32[]{:S(2)}) collective-permute-start(bf16[128,256]{1,0:T(8,128)(2,1)S(1)} %get-tuple-element.93.after_ref.refs_0_.refs_1_), channel_id=1, source_target_pairs={{0,2},{1,3},{2,0},{3,1},{4,6},{5,7},{6,4},{7,5},{8,10},{9,11},{10,... | collective-permute-start | bytes 196616 | tf_op jit(solution)/shard_map/ppermute | solution.py:20
  107.4 5.0 %collective-permute-start.34 = (bf16[128,256]{1,0:T(8,128)(2,1)S(1)}, bf16[128,256]{1,0:T(8,128)(2,1)S(1)}, u32[]{:S(2)}, u32[]{:S(2)}) collective-permute-start(bf16[128,256]{1,0:T(8,128)(2,1)S(1)} %get-tuple-element.93.after_ref.refs_0_.refs_1_), channel_id=1, source_target_pairs={{0,1},{1,0},{2,3},{3,2},{4,5},{5,4},{6,7},{7,6},{8,9},{9,8},{10,11... | collective-permute-start | bytes 196616 | tf_op jit(solution)/shard_map/ppermute | solution.py:20
  112.9 4.3 %collective-permute-start.37 = (bf16[128,256]{1,0:T(8,128)(2,1)S(1)}, bf16[128,256]{1,0:T(8,128)(2,1)S(1)}, u32[]{:S(2)}, u32[]{:S(2)}) collective-permute-start(bf16[128,256]{1,0:T(8,128)(2,1)S(1)} %get-tuple-element.97), channel_id=1, source_target_pairs={{0,8},{4,12},{8,0},{12,4},{16,24},{20,28},{24,16},{28,20},{1,9},{5... | collective-permute-start | bytes 196616 | tf_op jit(solution)/shard_map/ppermute | solution.py:20
  113.6 4.3 %collective-permute-start.38 = (bf16[128,256]{1,0:T(8,128)(2,1)S(1)}, bf16[128,256]{1,0:T(8,128)(2,1)S(1)}, u32[]{:S(2)}, u32[]{:S(2)}) collective-permute-start(bf16[128,256]{1,0:T(8,128)(2,1)S(1)} %get-tuple-element.98), channel_id=1, source_target_pairs={{0,16},{4,20},{8,24},{12,28},{16,0},{20,4},{24,8},{28,12},{1,17},{... | collective-permute-start | bytes 196616 | tf_op jit(solution)/shard_map/ppermute | solution.py:20
  114.9 5.2 %collective-permute-start.39 = (bf16[128,256]{1,0:T(8,128)(2,1)S(1)}, bf16[128,256]{1,0:T(8,128)(2,1)S(1)}, u32[]{:S(2)}, u32[]{:S(2)}) collective-permute-start(bf16[128,256]{1,0:T(8,128)(2,1)S(1)} %get-tuple-element.99), channel_id=1, source_target_pairs={{0,24},{4,28},{8,16},{12,20},{16,8},{20,12},{24,0},{28,4},{1,25},{... | collective-permute-start | bytes 196616 | tf_op jit(solution)/shard_map/ppermute | solution.py:20
  116.4 4.0 %collective-permute-start.43 = (bf16[128,128]{1,0:T(8,128)(2,1)S(1)}, bf16[128,128]{1,0:T(8,128)(2,1)S(1)}, u32[]{:S(2)}, u32[]{:S(2)}) collective-permute-start(bf16[128,128]{1,0:T(8,128)(2,1)S(1)} %get-tuple-element.104), channel_id=1, source_target_pairs={{0,4},{4,0},{8,12},{12,8},{16,20},{20,16},{24,28},{28,24},{1,5},{5... | collective-permute-start | bytes 98312 | tf_op jit(solution)/shard_map/ppermute | solution.py:20
  116.4 4.0 %collective-permute-start.42 = (bf16[128,128]{1,0:T(8,128)(2,1)S(1)}, bf16[128,128]{1,0:T(8,128)(2,1)S(1)}, u32[]{:S(2)}, u32[]{:S(2)}) collective-permute-start(bf16[128,128]{1,0:T(8,128)(2,1)S(1)} %get-tuple-element.103), channel_id=1, source_target_pairs={{0,4},{4,0},{8,12},{12,8},{16,20},{20,16},{24,28},{28,24},{1,5},{5... | collective-permute-start | bytes 98312 | tf_op jit(solution)/shard_map/ppermute | solution.py:20
  117.2 3.2 %collective-permute-start.41 = (bf16[128,128]{1,0:T(8,128)(2,1)S(1)}, bf16[128,128]{1,0:T(8,128)(2,1)S(1)}, u32[]{:S(2)}, u32[]{:S(2)}) collective-permute-start(bf16[128,128]{1,0:T(8,128)(2,1)S(1)} %get-tuple-element.102), channel_id=1, source_target_pairs={{0,4},{4,0},{8,12},{12,8},{16,20},{20,16},{24,28},{28,24},{1,5},{5... | collective-permute-start | bytes 98312 | tf_op jit(solution)/shard_map/ppermute | solution.py:20
  120.3 1.3 %collective-permute-start.40 = (bf16[128,128]{1,0:T(8,128)(2,1)S(1)}, bf16[128,128]{1,0:T(8,128)(2,1)S(1)}, u32[]{:S(2)}, u32[]{:S(2)}) collective-permute-start(bf16[128,128]{1,0:T(8,128)(2,1)S(1)} %get-tuple-element.101), channel_id=1, source_target_pairs={{0,4},{4,0},{8,12},{12,8},{16,20},{20,16},{24,28},{28,24},{1,5},{5... | collective-permute-start | bytes 98312 | tf_op jit(solution)/shard_map/ppermute | solution.py:20

commit v5 on v4

--- a/solution.py
+++ b/solution.py
@@ -20,7 +20,11 @@
     return lax.ppermute(value, axis, [(i, i ^ distance) for i in range(count)])
 
 
-def call(body, out_shape, args, scratch=(), flops=0, space=pltpu.VMEM):
+def z_order(count):
+    return [count - 1, *range(1, count - 1)]
+
+
+def call(body, out_shape, args, scratch=(), flops=0, space=pltpu.VMEM, limit=VMEM_BYTES):
     moved = sum(a.size * a.dtype.itemsize for a in args)
     in_specs = [pl.BlockSpec(memory_space=space) for _ in args]
     several = isinstance(out_shape, (list, tuple))
@@ -35,7 +39,7 @@
         in_specs=in_specs,
         out_specs=out_specs,
         scratch_shapes=list(scratch),
-        compiler_params=pltpu.CompilerParams(vmem_limit_bytes=VMEM_BYTES),
+        compiler_params=pltpu.CompilerParams(vmem_limit_bytes=limit),
         cost_estimate=pl.CostEstimate(flops=flops, bytes_accessed=moved, transcendentals=0),
     )(*args)
 
@@ -44,13 +48,16 @@
     return pl.ds(pl.multiple_of(start * step, step), size)
 
 
-def fetch_body(own_ref, par_ref, after_ref, own_out, par_out, sems):
-    half = own_ref.shape[0] // 2
+def fetch_body(own_ref, par_ref, after_ref, out_ref, sems):
+    parity = lax.axis_index("row") % 2
     copies = []
-    for k, (source, target) in enumerate(((own_ref, own_out), (par_ref, par_out))):
-        for h in range(2):
-            at = pl.ds(h * half, half)
-            copies.append(pltpu.make_async_copy(source.at[at], target.at[at], sems.at[2 * k + h]))
+    for i in range(own_ref.shape[0] // B):
+        source = pl.ds(i * B, B)
+        for k, (ref, rr) in enumerate(((own_ref, parity), (par_ref, 1 - parity))):
+            target = aligned(2 * i + rr, B, B)
+            copies.append(
+                pltpu.make_async_copy(ref.at[source], out_ref.at[target], sems.at[2 * i + k])
+            )
     for copy in copies:
         copy.start()
     for copy in copies:
@@ -60,10 +67,10 @@
 def fetch(own, par, after):
     return pl.pallas_call(
         fetch_body,
-        out_shape=[pltpu.VMEM(own.shape, own.dtype), pltpu.VMEM(par.shape, par.dtype)],
+        out_shape=pltpu.VMEM((2 * own.shape[0], own.shape[1]), own.dtype),
         in_specs=[pl.BlockSpec(memory_space=pl.ANY)] * 3,
-        out_specs=[pl.BlockSpec(memory_space=pltpu.VMEM)] * 2,
-        scratch_shapes=[pltpu.SemaphoreType.DMA((4,))],
+        out_specs=pl.BlockSpec(memory_space=pltpu.VMEM),
+        scratch_shapes=[pltpu.SemaphoreType.DMA((2 * own.shape[0] // B,))],
         compiler_params=pltpu.CompilerParams(vmem_limit_bytes=VMEM_BYTES),
         cost_estimate=pl.CostEstimate(
             flops=0, bytes_accessed=4 * own.size * own.dtype.itemsize, transcendentals=0
@@ -72,8 +79,13 @@
 
 
 def pack_body(
-    rows, cols, chunk_rows, total_rows, rhs_ref, dest_ref, out_ref
+    rows, cols, chunk_rows, total_rows, rhs_hbm, dest_hbm, out_ref, rhs_ref, dest_ref, sems
 ):
+    dest_copy = pltpu.make_async_copy(dest_hbm, dest_ref, sems.at[0])
+    rhs_copy = pltpu.make_async_copy(rhs_hbm, rhs_ref, sems.at[1])
+    dest_copy.start()
+    rhs_copy.start()
+    dest_copy.wait()
     local_rows = rhs_ref.shape[0]
     supernodes = rows * cols
     pairs = supernodes // 2
@@ -114,6 +126,7 @@
         (((1,), (1,)), ((), ())),
         preferred_element_type=F32,
     )
+    rhs_copy.wait()
     sorted_rows = jnp.dot(
         jnp.where(chosen, 1.0, 0.0).astype(BF16),
         rhs_ref[...].astype(BF16),
@@ -175,19 +188,27 @@
         out[...] = placed[:, k * 2 * B : (k + 1) * 2 * B]
 
 
-def down_body(own_ref, par_ref, *refs, groups, cols):
-    pieces, outs = refs[:groups], refs[groups : groups + cols]
-    gathered, product = refs[groups + cols :]
-    row, col = lax.axis_index("row"), lax.axis_index("col")
-    parity, group = row % 2, row // 2
+def gather_pieces(pieces, position, gathered):
     for m, piece in enumerate(pieces):
-        gathered[:, aligned(group ^ m, 2 * B, 2 * B)] = piece[...]
-    product[parity] = times_t(gathered[...], own_ref[...])
-    product[1 - parity] = times_t(gathered[...], par_ref[...])
-    for m, out in enumerate(outs):
-        at = aligned(col ^ m, B, B)
-        for rr in range(2):
-            out[:, rr * B : (rr + 1) * B] = product[rr, :, at].astype(out.dtype)
+        gathered[:, aligned(position ^ m, 2 * B, 2 * B)] = piece[...]
+
+
+def down_body(tile_ref, *refs, groups, distances):
+    pieces, outs, gathered = refs[:groups], refs[groups:-1], refs[-1]
+    col = lax.axis_index("col")
+    gather_pieces(pieces, lax.axis_index("row") // 2, gathered)
+    for m, out in zip(distances, outs):
+        at = aligned(col ^ m, 2 * B, 2 * B)
+        out[...] = times_t(gathered[...], tile_ref[at, :]).astype(out.dtype)
+
+
+def up_body(tile_ref, *refs, cols, distances):
+    pieces, outs, gathered = refs[:cols], refs[cols:-1], refs[-1]
+    group = lax.axis_index("row") // 2
+    gather_pieces(pieces, lax.axis_index("col"), gathered)
+    for m, out in zip(distances, outs):
+        at = aligned(group ^ m, 2 * B, 2 * B)
+        out[...] = times(gathered[...], tile_ref[:, at]).astype(out.dtype)
 
 
 def split_off(block_ref, theirs_ref):
@@ -219,21 +240,6 @@
         split_off(outs, theirs)
 
 
-def up_body(own_ref, par_ref, *refs, groups, cols):
-    pieces, outs = refs[:cols], refs[cols : cols + groups]
-    gathered, product = refs[cols + groups :]
-    row, col = lax.axis_index("row"), lax.axis_index("col")
-    parity, group = row % 2, row // 2
-    for m, piece in enumerate(pieces):
-        for rr in range(2):
-            gathered[rr, :, aligned(col ^ m, B, B)] = piece[:, rr * B : (rr + 1) * B]
-    product[...] = times(gathered[parity], own_ref[...]) + times(
-        gathered[1 - parity], par_ref[...]
-    )
-    for m, out in enumerate(outs):
-        out[...] = product[:, aligned(group ^ m, 2 * B, 2 * B)].astype(out.dtype)
-
-
 def final_body(solved_ref, own_ref, par_ref, kept_ref, *refs, level):
     arrived, outs, theirs, residual = refs[:-3], *refs[-3:]
     back = kept_ref[...]
@@ -270,6 +276,13 @@
         functools.partial(pack_body, rows, cols, chunk_rows, total_rows),
         shape((supernodes, total_rows, half)),
         (rhs_rows, dest_row.reshape(1, local_rows)),
+        [
+            pltpu.VMEM(rhs_rows.shape, F32),
+            pltpu.VMEM((1, local_rows), jnp.int32),
+            pltpu.SemaphoreType.DMA((2,)),
+        ],
+        space=pl.ANY,
+        limit=60 * 1024 * 1024,
         flops=2 * local_rows * local_rows * 2 * half,
     )
     arrived = lax.all_to_all(sending, ("row", "col"), split_axis=0, concat_axis=0, tiled=True)
@@ -296,14 +309,20 @@
             own[level], _ = lax.optimization_barrier((own[level], solved[-1]))
             par[level] = swap(own[level], "row", 1)
         pieces = [solved[-1]] + [swap(solved[-1], "row", 2 * m) for m in range(1, groups)]
-        sums = call(
-            functools.partial(down_body, groups=groups, cols=cols),
-            [shape(block, F32 if m == 0 else BF16) for m in range(cols)],
-            (*fetch(own[level - 1], par[level - 1], solved[-1]), *pieces),
-            [pltpu.VMEM((half, rows * B), BF16), pltpu.VMEM((2, half, cols * B), F32)],
-            flops=4 * rows * cols * B * B * half,
-        )
-        passed = [swap(sums[m], "col", m) for m in range(1, cols)]
+        tiles = fetch(own[level - 1], par[level - 1], solved[-1])
+        far = list(range(1, cols))
+        sums = [
+            call(
+                functools.partial(down_body, groups=groups, distances=distances),
+                [shape(block, F32 if m == 0 else BF16) for m in distances],
+                (tiles, *pieces),
+                [pltpu.VMEM((half, rows * B), BF16)],
+                flops=4 * rows * B * B * half * len(distances),
+            )
+            for distances in (far, [0])
+        ]
+        sums = [*sums[1], *sums[0]]
+        passed = [swap(sums[m], "col", m) for m in z_order(cols)]
         last = level == NLEV - 1
         result = call(
             functools.partial(residual_body, level=level),
@@ -319,15 +338,22 @@
     solution, others = [None] * NLEV, [None] * NLEV
     solution[NLEV - 1], others[NLEV - 1] = upper, swap(theirs, "row", 1)
     for level in range(NLEV - 2, -1, -1):
-        pieces = [upper] + [swap(upper, "col", m) for m in range(1, cols)]
-        sums = call(
-            functools.partial(up_body, groups=groups, cols=cols),
-            [shape(block, F32 if m == 0 else BF16) for m in range(groups)],
-            (*fetch(own[level], par[level], upper), *pieces),
-            [pltpu.VMEM((2, half, cols * B), BF16), pltpu.VMEM((half, rows * B), F32)],
-            flops=4 * rows * cols * B * B * half,
-        )
-        passed = [swap(sums[m], "row", 2 * m) for m in range(1, groups)]
+        sent = {m: swap(upper, "col", m) for m in reversed(z_order(cols))}
+        pieces = [upper] + [sent[m] for m in range(1, cols)]
+        tiles = fetch(own[level], par[level], upper)
+        far = list(range(1, groups))
+        sums = [
+            call(
+                functools.partial(up_body, cols=cols, distances=distances),
+                [shape(block, F32 if m == 0 else BF16) for m in distances],
+                (tiles, *pieces),
+                [pltpu.VMEM((half, 2 * cols * B), BF16)],
+                flops=4 * cols * B * B * half * len(distances),
+            )
+            for distances in (far, [0])
+        ]
+        sums = [*sums[1], *sums[0]]
+        passed = [swap(sums[m], "row", 2 * m) for m in range(groups - 1, 0, -1)]
         upper, theirs = call(
             functools.partial(final_body, level=level),
             [shape(block), shape((half, B))],

time: 123 us -> 118 us (0.959)
  waiting for transfers between devices: 47.2 us -> 43.1 us
  Pallas kernels: 9.85 us -> 12 us
  local copies, waits for them, and re-layouts: 5.43 us -> 3.72 us
  other arithmetic: 2.65 us -> 1.42 us
    ppermute x44, waiting for transfers between devices: 40.5 us -> 36.4 us  [swap(): return lax.ppermute(value, axis, [(i, i ^ distance) for i in range(count)])]
    pallas_call x16 -> x22, Pallas kernels: 8.75 us -> 10.5 us  [call(): pl.pallas_call(body, out_shape=out_shape, in_specs=in_specs, out_specs=ou...]
    unnamed x8 -> x6, local copies, waits for them, and re-layouts: 1.73 us -> 0.02 us
  transfers between devices with their start and end apart: 45 -> 45, of which waited for: 32 -> 37; matrix products, arithmetic and copies ran while one was open for 5% -> 4% of each run, Pallas kernels for 4% -> 7%
where the time goes in v5:
time: 118 us
  starting transfers between devices  57 us (48%)
  waiting for transfers between devices  43.1 us (37%)
  Pallas kernels  12 us (10%)
  local copies, waits for them, and re-layouts  3.72 us (3%)
  other arithmetic  1.42 us (1%)
    ppermute x44, starting transfers between devices, swap(): return lax.ppermute(value, axis, [(i, i ^ distance) for i in range(count)])  50 us
    ppermute x44, waiting for transfers between devices, swap(): return lax.ppermute(value, axis, [(i, i ^ distance) for i in range(count)])  36.4 us
    pallas_call x22, Pallas kernels, call(): pl.pallas_call(body, out_shape=out_shape, in_specs=in_specs, out_specs=ou...  10.5 us
    all_to_all x1, starting transfers between devices, per_device(): lax.all_to_all(sending, ('row', 'col'), split_axis=0, concat_axis=0, tile...  6.97 us
    all_to_all x1, waiting for transfers between devices, per_device(): lax.all_to_all(sending, ('row', 'col'), split_axis=0, concat_axis=0, tile...  6.71 us
    slice x1, local copies, waits for them, and re-layouts, per_device(): tile = lower_blocks[level, 0, :, :, 0]  3.09 us
  transfers between devices with their start and end apart: 45, of which 37 were waited for; matrix products, arithmetic and copies ran while one was open for 4% of the time, Pallas kernels for 7%

profile of v5, /device:TPU:0, one launch (start us, length us, event | category | flops | bytes accessed | tf_op | source)
XLA Modules:
  0.0 117.6 jit_solution(3689805518688263402)
XLA Ops:
  0.5 2.3 %shard_map.55 = bf16[32,40,128]{2,1,0:T(8,128)(2,1)} custom-call(f32[512,256]{1,0:T(8,128)} %rhs_hbm.1, s32[1,512]{1,0:T(1,128)} %bitcast.48), custom_call_target="tpu_custom_call" | custom-call | flops 134217728 | bytes 526336 | tf_op jit(solution)/shard_map/pallas_call | solution.py:36
  2.8 7.0 %all-to-all-start = ((bf16[32,40,128]{2,1,0:T(8,128)(2,1)}), bf16[32,40,128]{2,1,0:T(8,128)(2,1)S(1)}, u32[]{:S(2)}, u32[]{:S(2)}) async-start(bf16[32,40,128]{2,1,0:T(8,128)(2,1)} %shard_map.55), calls=%async_computation | async-start | bytes 655360 | tf_op jit(solution)/shard_map/all_to_all | solution.py:288
  10.5 3.1 %fusion = (bf16[1,1,4,128,1,8,128]{6,5,4,3,2,1,0:T(8,128)(2,1)S(1)}, bf16[1,1,4,128,1,8,128]{6,5,4,3,2,1,0:T(8,128)(2,1)S(1)}, bf16[1,1,4,128,1,8,128]{6,5,4,3,2,1,0:T(8,128)(2,1)}) fusion(bf16[3,1,4,128,1,8,128]{6,5,4,3,2,1,0:T(8,128)(2,1)} %param.8), kind=kLoop, calls=%fused_computation.6 | loop fusion | bytes 6291456 | tf_op jit(solution)/shard_map/slice | solution.py:270
  14.0 6.7 %all-to-all-done.arrived_ref = bf16[32,40,128]{2,1,0:T(8,128)(2,1)S(1)} async-done(((bf16[32,40,128]{2,1,0:T(8,128)(2,1)}), bf16[32,40,128]{2,1,0:T(8,128)(2,1)S(1)}, u32[]{:S(2)}, u32[]{:S(2)}) %all-to-all-start) | async-done | bytes 327712 | tf_op jit(solution)/shard_map/all_to_all | solution.py:288
  22.1 1.0 collective-permute-start.4
  23.2 1.5 %collective-permute-start.3 = (bf16[128,256]{1,0:T(8,128)(2,1)S(1)}, bf16[128,256]{1,0:T(8,128)(2,1)S(1)}, u32[]{:S(2)}, u32[]{:S(2)}) collective-permute-start(bf16[128,256]{1,0:T(8,128)(2,1)S(1)} %shard_map.56.after_ref.refs_0_.solved_ref), channel_id=1, source_target_pairs={{0,16},{4,20},{8,24},{12,28},{16,0},{20,4},{24,8},{28,12},{1,17},{... | collective-permute-start | bytes 196616 | tf_op jit(solution)/shard_map/ppermute | solution.py:20
  26.4 1.3 %collective-permute-done.4.refs_3_ = bf16[128,256]{1,0:T(8,128)(2,1)S(1)} collective-permute-done((bf16[128,256]{1,0:T(8,128)(2,1)S(1)}, bf16[128,256]{1,0:T(8,128)(2,1)S(1)}, u32[]{:S(2)}, u32[]{:S(2)}) %collective-permute-start.4) | collective-permute-done | bytes 65568 | tf_op jit(solution)/shard_map/ppermute | solution.py:20
  29.6 1.8 %collective-permute-start.5 = (bf16[128,256]{1,0:T(8,128)(2,1)S(1)}, bf16[128,256]{1,0:T(8,128)(2,1)S(1)}, u32[]{:S(2)}, u32[]{:S(2)}) collective-permute-start(bf16[128,256]{1,0:T(8,128)(2,1)S(1)} %get-tuple-element.39), channel_id=1, source_target_pairs={{0,3},{1,2},{2,1},{3,0},{4,7},{5,6},{6,5},{7,4},{8,11},{9,10},{10,... | collective-permute-start | bytes 196616 | tf_op jit(solution)/shard_map/ppermute | solution.py:20
  31.3 2.7 %collective-permute-start.7 = (bf16[128,256]{1,0:T(8,128)(2,1)S(1)}, bf16[128,256]{1,0:T(8,128)(2,1)S(1)}, u32[]{:S(2)}, u32[]{:S(2)}) collective-permute-start(bf16[128,256]{1,0:T(8,128)(2,1)S(1)} %get-tuple-element.41), channel_id=1, source_target_pairs={{0,2},{1,3},{2,0},{3,1},{4,6},{5,7},{6,4},{7,5},{8,10},{9,11},{10,... | collective-permute-start | bytes 196616 | tf_op jit(solution)/shard_map/ppermute | solution.py:20
  36.1 1.4 %collective-permute-done.6.refs_1_ = bf16[128,256]{1,0:T(8,128)(2,1)S(1)} collective-permute-done((bf16[128,256]{1,0:T(8,128)(2,1)S(1)}, bf16[128,256]{1,0:T(8,128)(2,1)S(1)}, u32[]{:S(2)}, u32[]{:S(2)}) %collective-permute-start.6) | collective-permute-done | bytes 65568 | tf_op jit(solution)/shard_map/ppermute | solution.py:20
  38.9 2.3 %collective-permute-start.10 = (bf16[128,256]{1,0:T(8,128)(2,1)S(1)}, bf16[128,256]{1,0:T(8,128)(2,1)S(1)}, u32[]{:S(2)}, u32[]{:S(2)}) collective-permute-start(bf16[128,256]{1,0:T(8,128)(2,1)S(1)} %shard_map.61.after_ref.refs_0_.solved_ref), channel_id=1, source_target_pairs={{0,16},{4,20},{8,24},{12,28},{16,0},{20,4},{24,8},{28,12},{1,17},{... | collective-permute-start | bytes 196616 | tf_op jit(solution)/shard_map/ppermute | solution.py:20
  42.2 2.0 %collective-permute-done.11.refs_3_ = bf16[128,256]{1,0:T(8,128)(2,1)S(1)} collective-permute-done((bf16[128,256]{1,0:T(8,128)(2,1)S(1)}, bf16[128,256]{1,0:T(8,128)(2,1)S(1)}, u32[]{:S(2)}, u32[]{:S(2)}) %collective-permute-start.11) | collective-permute-done | bytes 65568 | tf_op jit(solution)/shard_map/ppermute | solution.py:20
  46.2 1.2 %collective-permute-start.12 = (bf16[128,256]{1,0:T(8,128)(2,1)S(1)}, bf16[128,256]{1,0:T(8,128)(2,1)S(1)}, u32[]{:S(2)}, u32[]{:S(2)}) collective-permute-start(bf16[128,256]{1,0:T(8,128)(2,1)S(1)} %get-tuple-element.44), channel_id=1, source_target_pairs={{0,3},{1,2},{2,1},{3,0},{4,7},{5,6},{6,5},{7,4},{8,11},{9,10},{10,... | collective-permute-start | bytes 196616 | tf_op jit(solution)/shard_map/ppermute | solution.py:20
  47.6 3.1 %collective-permute-start.14 = (bf16[128,256]{1,0:T(8,128)(2,1)S(1)}, bf16[128,256]{1,0:T(8,128)(2,1)S(1)}, u32[]{:S(2)}, u32[]{:S(2)}) collective-permute-start(bf16[128,256]{1,0:T(8,128)(2,1)S(1)} %get-tuple-element.46), channel_id=1, source_target_pairs={{0,2},{1,3},{2,0},{3,1},{4,6},{5,7},{6,4},{7,5},{8,10},{9,11},{10,... | collective-permute-start | bytes 196616 | tf_op jit(solution)/shard_map/ppermute | solution.py:20
  51.0 2.1 %collective-permute-done.12.refs_0_ = bf16[128,256]{1,0:T(8,128)(2,1)S(1)} collective-permute-done((bf16[128,256]{1,0:T(8,128)(2,1)S(1)}, bf16[128,256]{1,0:T(8,128)(2,1)S(1)}, u32[]{:S(2)}, u32[]{:S(2)}) %collective-permute-start.12) | collective-permute-done | bytes 65568 | tf_op jit(solution)/shard_map/ppermute | solution.py:20
  53.9 1.4 %collective-permute-start.18 = (bf16[128,256]{1,0:T(8,128)(2,1)S(1)}, bf16[128,256]{1,0:T(8,128)(2,1)S(1)}, u32[]{:S(2)}, u32[]{:S(2)}) collective-permute-start(bf16[128,256]{1,0:T(8,128)(2,1)S(1)} %shard_map.65.after_ref.refs_0_.solved_ref), channel_id=1, source_target_pairs={{0,24},{4,28},{8,16},{12,20},{16,8},{20,12},{24,0},{28,4},{1,25},{... | collective-permute-start | bytes 196616 | tf_op jit(solution)/shard_map/ppermute | solution.py:20
  55.3 1.5 %collective-permute-start.17 = (bf16[128,256]{1,0:T(8,128)(2,1)S(1)}, bf16[128,256]{1,0:T(8,128)(2,1)S(1)}, u32[]{:S(2)}, u32[]{:S(2)}) collective-permute-start(bf16[128,256]{1,0:T(8,128)(2,1)S(1)} %shard_map.65.after_ref.refs_0_.solved_ref), channel_id=1, source_target_pairs={{0,16},{4,20},{8,24},{12,28},{16,0},{20,4},{24,8},{28,12},{1,17},{... | collective-permute-start | bytes 196616 | tf_op jit(solution)/shard_map/ppermute | solution.py:20
  57.7 2.0 %collective-permute-done.18.refs_3_ = bf16[128,256]{1,0:T(8,128)(2,1)S(1)} collective-permute-done((bf16[128,256]{1,0:T(8,128)(2,1)S(1)}, bf16[128,256]{1,0:T(8,128)(2,1)S(1)}, u32[]{:S(2)}, u32[]{:S(2)}) %collective-permute-start.18) | collective-permute-done | bytes 65568 | tf_op jit(solution)/shard_map/ppermute | solution.py:20
  60.0 1.0 collective-permute-done.16.refs_1_
  61.7 2.0 %collective-permute-start.19 = (bf16[128,256]{1,0:T(8,128)(2,1)S(1)}, bf16[128,256]{1,0:T(8,128)(2,1)S(1)}, u32[]{:S(2)}, u32[]{:S(2)}) collective-permute-start(bf16[128,256]{1,0:T(8,128)(2,1)S(1)} %get-tuple-element.49), channel_id=1, source_target_pairs={{0,3},{1,2},{2,1},{3,0},{4,7},{5,6},{6,5},{7,4},{8,11},{9,10},{10,... | collective-permute-start | bytes 196616 | tf_op jit(solution)/shard_map/ppermute | solution.py:20
  64.0 2.1 %collective-permute-start.21 = (bf16[128,256]{1,0:T(8,128)(2,1)S(1)}, bf16[128,256]{1,0:T(8,128)(2,1)S(1)}, u32[]{:S(2)}, u32[]{:S(2)}) collective-permute-start(bf16[128,256]{1,0:T(8,128)(2,1)S(1)} %get-tuple-element.51), channel_id=1, source_target_pairs={{0,2},{1,3},{2,0},{3,1},{4,6},{5,7},{6,4},{7,5},{8,10},{9,11},{10,... | collective-permute-start | bytes 196616 | tf_op jit(solution)/shard_map/ppermute | solution.py:20
  66.5 1.4 %collective-permute-done.19.refs_0_ = bf16[128,256]{1,0:T(8,128)(2,1)S(1)} collective-permute-done((bf16[128,256]{1,0:T(8,128)(2,1)S(1)}, bf16[128,256]{1,0:T(8,128)(2,1)S(1)}, u32[]{:S(2)}, u32[]{:S(2)}) %collective-permute-start.19) | collective-permute-done | bytes 65568 | tf_op jit(solution)/shard_map/ppermute | solution.py:20
  68.5 1.0 collective-permute-done.21.refs_2_
  69.9 1.7 %collective-permute-start.24 = (bf16[128,256]{1,0:T(8,128)(2,1)S(1)}, bf16[128,256]{1,0:T(8,128)(2,1)S(1)}, u32[]{:S(2)}, u32[]{:S(2)}) collective-permute-start(bf16[128,256]{1,0:T(8,128)(2,1)S(1)} %get-tuple-element.52.after_ref.refs_0_.refs_3_), channel_id=1, source_target_pairs={{0,3},{1,2},{2,1},{3,0},{4,7},{5,6},{6,5},{7,4},{8,11},{9,10},{10,... | collective-permute-start | bytes 196616 | tf_op jit(solution)/shard_map/ppermute | solution.py:20
  71.6 1.6 %collective-permute-start.23 = (bf16[128,256]{1,0:T(8,128)(2,1)S(1)}, bf16[128,256]{1,0:T(8,128)(2,1)S(1)}, u32[]{:S(2)}, u32[]{:S(2)}) collective-permute-start(bf16[128,256]{1,0:T(8,128)(2,1)S(1)} %get-tuple-element.52.after_ref.refs_0_.refs_3_), channel_id=1, source_target_pairs={{0,2},{1,3},{2,0},{3,1},{4,6},{5,7},{6,4},{7,5},{8,10},{9,11},{10,... | collective-permute-start | bytes 196616 | tf_op jit(solution)/shard_map/ppermute | solution.py:20
  73.2 1.1 collective-permute-start.22
  74.6 1.5 %collective-permute-done.24.refs_3_ = bf16[128,256]{1,0:T(8,128)(2,1)S(1)} collective-permute-done((bf16[128,256]{1,0:T(8,128)(2,1)S(1)}, bf16[128,256]{1,0:T(8,128)(2,1)S(1)}, u32[]{:S(2)}, u32[]{:S(2)}) %collective-permute-start.24) | collective-permute-done | bytes 65568 | tf_op jit(solution)/shard_map/ppermute | solution.py:20
  76.1 1.5 %collective-permute-done.23.refs_2_ = bf16[128,256]{1,0:T(8,128)(2,1)S(1)} collective-permute-done((bf16[128,256]{1,0:T(8,128)(2,1)S(1)}, bf16[128,256]{1,0:T(8,128)(2,1)S(1)}, u32[]{:S(2)}, u32[]{:S(2)}) %collective-permute-start.23) | collective-permute-done | bytes 65568 | tf_op jit(solution)/shard_map/ppermute | solution.py:20
  78.2 1.7 %collective-permute-start.25 = (bf16[128,256]{1,0:T(8,128)(2,1)S(1)}, bf16[128,256]{1,0:T(8,128)(2,1)S(1)}, u32[]{:S(2)}, u32[]{:S(2)}) collective-permute-start(bf16[128,256]{1,0:T(8,128)(2,1)S(1)} %get-tuple-element.53), channel_id=1, source_target_pairs={{0,24},{4,28},{8,16},{12,20},{16,8},{20,12},{24,0},{28,4},{1,25},{... | collective-permute-start | bytes 196616 | tf_op jit(solution)/shard_map/ppermute | solution.py:20
  79.9 1.0 collective-permute-start.26
  82.0 1.4 %collective-permute-done.25.refs_0_ = bf16[128,256]{1,0:T(8,128)(2,1)S(1)} collective-permute-done((bf16[128,256]{1,0:T(8,128)(2,1)S(1)}, bf16[128,256]{1,0:T(8,128)(2,1)S(1)}, u32[]{:S(2)}, u32[]{:S(2)}) %collective-permute-start.25) | collective-permute-done | bytes 65568 | tf_op jit(solution)/shard_map/ppermute | solution.py:20
  84.2 1.0 collective-permute-done.27.refs_2_
  85.4 1.7 %collective-permute-start.30 = (bf16[128,256]{1,0:T(8,128)(2,1)S(1)}, bf16[128,256]{1,0:T(8,128)(2,1)S(1)}, u32[]{:S(2)}, u32[]{:S(2)}) collective-permute-start(bf16[128,256]{1,0:T(8,128)(2,1)S(1)} %get-tuple-element.56.after_ref.refs_0_.refs_2_), channel_id=1, source_target_pairs={{0,3},{1,2},{2,1},{3,0},{4,7},{5,6},{6,5},{7,4},{8,11},{9,10},{10,... | collective-permute-start | bytes 196616 | tf_op jit(solution)/shard_map/ppermute | solution.py:20
  87.5 2.3 %collective-permute-start.28 = (bf16[128,256]{1,0:T(8,128)(2,1)S(1)}, bf16[128,256]{1,0:T(8,128)(2,1)S(1)}, u32[]{:S(2)}, u32[]{:S(2)}) collective-permute-start(bf16[128,256]{1,0:T(8,128)(2,1)S(1)} %get-tuple-element.56.after_ref.refs_0_.refs_2_), channel_id=1, source_target_pairs={{0,1},{1,0},{2,3},{3,2},{4,5},{5,4},{6,7},{7,6},{8,9},{9,8},{10,11... | collective-permute-start | bytes 196616 | tf_op jit(solution)/shard_map/ppermute | solution.py:20
  90.1 1.4 %collective-permute-done.30.refs_3_ = bf16[128,256]{1,0:T(8,128)(2,1)S(1)} collective-permute-done((bf16[128,256]{1,0:T(8,128)(2,1)S(1)}, bf16[128,256]{1,0:T(8,128)(2,1)S(1)}, u32[]{:S(2)}, u32[]{:S(2)}) %collective-permute-start.30) | collective-permute-done | bytes 65568 | tf_op jit(solution)/shard_map/ppermute | solution.py:20
  91.5 1.4 %collective-permute-done.29.refs_2_ = bf16[128,256]{1,0:T(8,128)(2,1)S(1)} collective-permute-done((bf16[128,256]{1,0:T(8,128)(2,1)S(1)}, bf16[128,256]{1,0:T(8,128)(2,1)S(1)}, u32[]{:S(2)}, u32[]{:S(2)}) %collective-permute-start.29) | collective-permute-done | bytes 65568 | tf_op jit(solution)/shard_map/ppermute | solution.py:20
  94.0 1.7 %collective-permute-start.32 = (bf16[128,256]{1,0:T(8,128)(2,1)S(1)}, bf16[128,256]{1,0:T(8,128)(2,1)S(1)}, u32[]{:S(2)}, u32[]{:S(2)}) collective-permute-start(bf16[128,256]{1,0:T(8,128)(2,1)S(1)} %get-tuple-element.58), channel_id=1, source_target_pairs={{0,16},{4,20},{8,24},{12,28},{16,0},{20,4},{24,8},{28,12},{1,17},{... | collective-permute-start | bytes 196616 | tf_op jit(solution)/shard_map/ppermute | solution.py:20
  95.7 1.2 %collective-permute-start.33 = (bf16[128,256]{1,0:T(8,128)(2,1)S(1)}, bf16[128,256]{1,0:T(8,128)(2,1)S(1)}, u32[]{:S(2)}, u32[]{:S(2)}) collective-permute-start(bf16[128,256]{1,0:T(8,128)(2,1)S(1)} %get-tuple-element.59), channel_id=1, source_target_pairs={{0,8},{4,12},{8,0},{12,4},{16,24},{20,28},{24,16},{28,20},{1,9},{5... | collective-permute-start | bytes 196616 | tf_op jit(solution)/shard_map/ppermute | solution.py:20
  97.2 1.5 %collective-permute-done.31.refs_0_ = bf16[128,256]{1,0:T(8,128)(2,1)S(1)} collective-permute-done((bf16[128,256]{1,0:T(8,128)(2,1)S(1)}, bf16[128,256]{1,0:T(8,128)(2,1)S(1)}, u32[]{:S(2)}, u32[]{:S(2)}) %collective-permute-start.31) | collective-permute-done | bytes 65568 | tf_op jit(solution)/shard_map/ppermute | solution.py:20
  99.0 1.0 collective-permute-done.33.refs_2_
  100.2 1.9 %collective-permute-start.36 = (bf16[128,256]{1,0:T(8,128)(2,1)S(1)}, bf16[128,256]{1,0:T(8,128)(2,1)S(1)}, u32[]{:S(2)}, u32[]{:S(2)}) collective-permute-start(bf16[128,256]{1,0:T(8,128)(2,1)S(1)} %get-tuple-element.60.after_ref.refs_0_.refs_1_), channel_id=1, source_target_pairs={{0,3},{1,2},{2,1},{3,0},{4,7},{5,6},{6,5},{7,4},{8,11},{9,10},{10,... | collective-permute-start | bytes 196616 | tf_op jit(solution)/shard_map/ppermute | solution.py:20
  103.0 1.6 %collective-permute-start.34 = (bf16[128,256]{1,0:T(8,128)(2,1)S(1)}, bf16[128,256]{1,0:T(8,128)(2,1)S(1)}, u32[]{:S(2)}, u32[]{:S(2)}) collective-permute-start(bf16[128,256]{1,0:T(8,128)(2,1)S(1)} %get-tuple-element.60.after_ref.refs_0_.refs_1_), channel_id=1, source_target_pairs={{0,1},{1,0},{2,3},{3,2},{4,5},{5,4},{6,7},{7,6},{8,9},{9,8},{10,11... | collective-permute-start | bytes 196616 | tf_op jit(solution)/shard_map/ppermute | solution.py:20
  104.9 1.4 %collective-permute-done.36.refs_3_ = bf16[128,256]{1,0:T(8,128)(2,1)S(1)} collective-permute-done((bf16[128,256]{1,0:T(8,128)(2,1)S(1)}, bf16[128,256]{1,0:T(8,128)(2,1)S(1)}, u32[]{:S(2)}, u32[]{:S(2)}) %collective-permute-start.36) | collective-permute-done | bytes 65568 | tf_op jit(solution)/shard_map/ppermute | solution.py:20
  106.3 1.5 %collective-permute-done.35.refs_2_ = bf16[128,256]{1,0:T(8,128)(2,1)S(1)} collective-permute-done((bf16[128,256]{1,0:T(8,128)(2,1)S(1)}, bf16[128,256]{1,0:T(8,128)(2,1)S(1)}, u32[]{:S(2)}, u32[]{:S(2)}) %collective-permute-start.35) | collective-permute-done | bytes 65568 | tf_op jit(solution)/shard_map/ppermute | solution.py:20
  108.4 1.6 %collective-permute-start.37 = (bf16[128,256]{1,0:T(8,128)(2,1)S(1)}, bf16[128,256]{1,0:T(8,128)(2,1)S(1)}, u32[]{:S(2)}, u32[]{:S(2)}) collective-permute-start(bf16[128,256]{1,0:T(8,128)(2,1)S(1)} %get-tuple-element.61), channel_id=1, source_target_pairs={{0,24},{4,28},{8,16},{12,20},{16,8},{20,12},{24,0},{28,4},{1,25},{... | collective-permute-start | bytes 196616 | tf_op jit(solution)/shard_map/ppermute | solution.py:20
  110.0 1.0 collective-permute-start.38
  111.0 1.0 collective-permute-start.39
  115.6 1.2 collective-permute-done.40.refs_4_
  (85 shorter events, 29.2 us)
Async XLA Ops:
  0.0 14.0 %collective-permute-start = (bf16[4,128,128]{2,1,0:T(8,128)(2,1)}, bf16[4,128,128]{2,1,0:T(8,128)(2,1)S(1)}, u32[]{:S(2)}, u32[]{:S(2)}) collective-permute-start(bf16[4,128,128]{2,1,0:T(8,128)(2,1)} %bitcast.33), channel_id=1, source_target_pairs={{0,4},{4,0},{8,12},{12,8},{16,20},{20,16},{24,28},{28,24},{1,5},{5... | collective-permute-start | bytes 393224 | tf_op jit(solution)/shard_map/ppermute | solution.py:20
  2.8 18.0 %all-to-all-start = ((bf16[32,40,128]{2,1,0:T(8,128)(2,1)}), bf16[32,40,128]{2,1,0:T(8,128)(2,1)S(1)}, u32[]{:S(2)}, u32[]{:S(2)}) async-start(bf16[32,40,128]{2,1,0:T(8,128)(2,1)} %shard_map.55), calls=%async_computation | async-start | bytes 655360 | tf_op jit(solution)/shard_map/all_to_all | solution.py:288
  13.5 7.2 %copy-start = (bf16[4,1,128,128]{3,2,1,0:T(8,128)(2,1)S(1)}, bf16[4,1,128,128]{3,2,1,0:T(8,128)(2,1)}, u32[]{:S(2)}) copy-start(bf16[4,1,128,128]{3,2,1,0:T(8,128)(2,1)} %param.7) | copy-start | bytes 393220
  20.7 5.1 %copy-start.1 = (bf16[1,1,4,128,1,8,128]{6,5,4,3,2,1,0:T(8,128)(2,1)S(1)}, bf16[1,1,4,128,1,8,128]{6,5,4,3,2,1,0:T(8,128)(2,1)}, u32[]{:S(2)}) copy-start(bf16[1,1,4,128,1,8,128]{6,5,4,3,2,1,0:T(8,128)(2,1)} %get-tuple-element.71) | copy-start | bytes 3145732
  21.2 4.9 %collective-permute-start.1 = (bf16[512,1024]{1,0:T(8,128)(2,1)S(1)}, bf16[512,1024]{1,0:T(8,128)(2,1)S(1)}, u32[]{:S(2)}, u32[]{:S(2)}) collective-permute-start(bf16[512,1024]{1,0:T(8,128)(2,1)S(1)} %bitcast_multiply_fusion.2.own_ref), channel_id=1, source_target_pairs={{0,4},{4,0},{8,12},{12,8},{16,20},{20,16},{24,28},{28,24},{1,5},{5... | collective-permute-start | bytes 3145736 | tf_op jit(solution)/shard_map/ppermute | solution.py:20
  22.1 5.7 %collective-permute-start.4 = (bf16[128,256]{1,0:T(8,128)(2,1)S(1)}, bf16[128,256]{1,0:T(8,128)(2,1)S(1)}, u32[]{:S(2)}, u32[]{:S(2)}) collective-permute-start(bf16[128,256]{1,0:T(8,128)(2,1)S(1)} %shard_map.56.after_ref.refs_0_.solved_ref), channel_id=1, source_target_pairs={{0,24},{4,28},{8,16},{12,20},{16,8},{20,12},{24,0},{28,4},{1,25},{... | collective-permute-start | bytes 196616 | tf_op jit(solution)/shard_map/ppermute | solution.py:20
  23.2 5.3 %collective-permute-start.3 = (bf16[128,256]{1,0:T(8,128)(2,1)S(1)}, bf16[128,256]{1,0:T(8,128)(2,1)S(1)}, u32[]{:S(2)}, u32[]{:S(2)}) collective-permute-start(bf16[128,256]{1,0:T(8,128)(2,1)S(1)} %shard_map.56.after_ref.refs_0_.solved_ref), channel_id=1, source_target_pairs={{0,16},{4,20},{8,24},{12,28},{16,0},{20,4},{24,8},{28,12},{1,17},{... | collective-permute-start | bytes 196616 | tf_op jit(solution)/shard_map/ppermute | solution.py:20
  24.6 4.3 %collective-permute-start.2 = (bf16[128,256]{1,0:T(8,128)(2,1)S(1)}, bf16[128,256]{1,0:T(8,128)(2,1)S(1)}, u32[]{:S(2)}, u32[]{:S(2)}) collective-permute-start(bf16[128,256]{1,0:T(8,128)(2,1)S(1)} %shard_map.56.after_ref.refs_0_.solved_ref), channel_id=1, source_target_pairs={{0,8},{4,12},{8,0},{12,4},{16,24},{20,28},{24,16},{28,20},{1,9},{5... | collective-permute-start | bytes 196616 | tf_op jit(solution)/shard_map/ppermute | solution.py:20
  26.1 15.9 %collective-permute-start.8 = (bf16[512,1024]{1,0:T(8,128)(2,1)S(1)}, bf16[512,1024]{1,0:T(8,128)(2,1)S(1)}, u32[]{:S(2)}, u32[]{:S(2)}) collective-permute-start(bf16[512,1024]{1,0:T(8,128)(2,1)S(1)} %bitcast_multiply_fusion.1.own_ref), channel_id=1, source_target_pairs={{0,4},{4,0},{8,12},{12,8},{16,20},{20,16},{24,28},{28,24},{1,5},{5... | collective-permute-start | bytes 3145736 | tf_op jit(solution)/shard_map/ppermute | solution.py:20
  29.6 6.6 %collective-permute-start.5 = (bf16[128,256]{1,0:T(8,128)(2,1)S(1)}, bf16[128,256]{1,0:T(8,128)(2,1)S(1)}, u32[]{:S(2)}, u32[]{:S(2)}) collective-permute-start(bf16[128,256]{1,0:T(8,128)(2,1)S(1)} %get-tuple-element.39), channel_id=1, source_target_pairs={{0,3},{1,2},{2,1},{3,0},{4,7},{5,6},{6,5},{7,4},{8,11},{9,10},{10,... | collective-permute-start | bytes 196616 | tf_op jit(solution)/shard_map/ppermute | solution.py:20
  31.3 6.2 %collective-permute-start.6 = (bf16[128,256]{1,0:T(8,128)(2,1)S(1)}, bf16[128,256]{1,0:T(8,128)(2,1)S(1)}, u32[]{:S(2)}, u32[]{:S(2)}) collective-permute-start(bf16[128,256]{1,0:T(8,128)(2,1)S(1)} %get-tuple-element.40), channel_id=1, source_target_pairs={{0,1},{1,0},{2,3},{3,2},{4,5},{5,4},{6,7},{7,6},{8,9},{9,8},{10,11... | collective-permute-start | bytes 196616 | tf_op jit(solution)/shard_map/ppermute | solution.py:20
  31.3 6.8 %collective-permute-start.7 = (bf16[128,256]{1,0:T(8,128)(2,1)S(1)}, bf16[128,256]{1,0:T(8,128)(2,1)S(1)}, u32[]{:S(2)}, u32[]{:S(2)}) collective-permute-start(bf16[128,256]{1,0:T(8,128)(2,1)S(1)} %get-tuple-element.41), channel_id=1, source_target_pairs={{0,2},{1,3},{2,0},{3,1},{4,6},{5,7},{6,4},{7,5},{8,10},{9,11},{10,... | collective-permute-start | bytes 196616 | tf_op jit(solution)/shard_map/ppermute | solution.py:20
  38.3 19.1 %collective-permute-start.15 = (bf16[512,1024]{1,0:T(8,128)(2,1)S(1)}, bf16[512,1024]{1,0:T(8,128)(2,1)S(1)}, u32[]{:S(2)}, u32[]{:S(2)}) collective-permute-start(bf16[512,1024]{1,0:T(8,128)(2,1)S(1)} %bitcast_multiply_fusion.own_ref), channel_id=1, source_target_pairs={{0,4},{4,0},{8,12},{12,8},{16,20},{20,16},{24,28},{28,24},{1,5},{5... | collective-permute-start | bytes 3145736 | tf_op jit(solution)/shard_map/ppermute | solution.py:20
  38.4 5.8 %collective-permute-start.11 = (bf16[128,256]{1,0:T(8,128)(2,1)S(1)}, bf16[128,256]{1,0:T(8,128)(2,1)S(1)}, u32[]{:S(2)}, u32[]{:S(2)}) collective-permute-start(bf16[128,256]{1,0:T(8,128)(2,1)S(1)} %shard_map.61.after_ref.refs_0_.solved_ref), channel_id=1, source_target_pairs={{0,24},{4,28},{8,16},{12,20},{16,8},{20,12},{24,0},{28,4},{1,25},{... | collective-permute-start | bytes 196616 | tf_op jit(solution)/shard_map/ppermute | solution.py:20
  38.9 6.2 %collective-permute-start.10 = (bf16[128,256]{1,0:T(8,128)(2,1)S(1)}, bf16[128,256]{1,0:T(8,128)(2,1)S(1)}, u32[]{:S(2)}, u32[]{:S(2)}) collective-permute-start(bf16[128,256]{1,0:T(8,128)(2,1)S(1)} %shard_map.61.after_ref.refs_0_.solved_ref), channel_id=1, source_target_pairs={{0,16},{4,20},{8,24},{12,28},{16,0},{20,4},{24,8},{28,12},{1,17},{... | collective-permute-start | bytes 196616 | tf_op jit(solution)/shard_map/ppermute | solution.py:20
  41.3 4.3 %collective-permute-start.9 = (bf16[128,256]{1,0:T(8,128)(2,1)S(1)}, bf16[128,256]{1,0:T(8,128)(2,1)S(1)}, u32[]{:S(2)}, u32[]{:S(2)}) collective-permute-start(bf16[128,256]{1,0:T(8,128)(2,1)S(1)} %shard_map.61.after_ref.refs_0_.solved_ref), channel_id=1, source_target_pairs={{0,8},{4,12},{8,0},{12,4},{16,24},{20,28},{24,16},{28,20},{1,9},{5... | collective-permute-start | bytes 196616 | tf_op jit(solution)/shard_map/ppermute | solution.py:20
  46.2 6.9 %collective-permute-start.12 = (bf16[128,256]{1,0:T(8,128)(2,1)S(1)}, bf16[128,256]{1,0:T(8,128)(2,1)S(1)}, u32[]{:S(2)}, u32[]{:S(2)}) collective-permute-start(bf16[128,256]{1,0:T(8,128)(2,1)S(1)} %get-tuple-element.44), channel_id=1, source_target_pairs={{0,3},{1,2},{2,1},{3,0},{4,7},{5,6},{6,5},{7,4},{8,11},{9,10},{10,... | collective-permute-start | bytes 196616 | tf_op jit(solution)/shard_map/ppermute | solution.py:20
  47.4 5.8 %collective-permute-start.13 = (bf16[128,256]{1,0:T(8,128)(2,1)S(1)}, bf16[128,256]{1,0:T(8,128)(2,1)S(1)}, u32[]{:S(2)}, u32[]{:S(2)}) collective-permute-start(bf16[128,256]{1,0:T(8,128)(2,1)S(1)} %get-tuple-element.45), channel_id=1, source_target_pairs={{0,1},{1,0},{2,3},{3,2},{4,5},{5,4},{6,7},{7,6},{8,9},{9,8},{10,11... | collective-permute-start | bytes 196616 | tf_op jit(solution)/shard_map/ppermute | solution.py:20
  47.6 6.2 %collective-permute-start.14 = (bf16[128,256]{1,0:T(8,128)(2,1)S(1)}, bf16[128,256]{1,0:T(8,128)(2,1)S(1)}, u32[]{:S(2)}, u32[]{:S(2)}) collective-permute-start(bf16[128,256]{1,0:T(8,128)(2,1)S(1)} %get-tuple-element.46), channel_id=1, source_target_pairs={{0,2},{1,3},{2,0},{3,1},{4,6},{5,7},{6,4},{7,5},{8,10},{9,11},{10,... | collective-permute-start | bytes 196616 | tf_op jit(solution)/shard_map/ppermute | solution.py:20
  53.9 5.8 %collective-permute-start.18 = (bf16[128,256]{1,0:T(8,128)(2,1)S(1)}, bf16[128,256]{1,0:T(8,128)(2,1)S(1)}, u32[]{:S(2)}, u32[]{:S(2)}) collective-permute-start(bf16[128,256]{1,0:T(8,128)(2,1)S(1)} %shard_map.65.after_ref.refs_0_.solved_ref), channel_id=1, source_target_pairs={{0,24},{4,28},{8,16},{12,20},{16,8},{20,12},{24,0},{28,4},{1,25},{... | collective-permute-start | bytes 196616 | tf_op jit(solution)/shard_map/ppermute | solution.py:20
  55.3 4.8 %collective-permute-start.17 = (bf16[128,256]{1,0:T(8,128)(2,1)S(1)}, bf16[128,256]{1,0:T(8,128)(2,1)S(1)}, u32[]{:S(2)}, u32[]{:S(2)}) collective-permute-start(bf16[128,256]{1,0:T(8,128)(2,1)S(1)} %shard_map.65.after_ref.refs_0_.solved_ref), channel_id=1, source_target_pairs={{0,16},{4,20},{8,24},{12,28},{16,0},{20,4},{24,8},{28,12},{1,17},{... | collective-permute-start | bytes 196616 | tf_op jit(solution)/shard_map/ppermute | solution.py:20
  56.8 4.3 %collective-permute-start.16 = (bf16[128,256]{1,0:T(8,128)(2,1)S(1)}, bf16[128,256]{1,0:T(8,128)(2,1)S(1)}, u32[]{:S(2)}, u32[]{:S(2)}) collective-permute-start(bf16[128,256]{1,0:T(8,128)(2,1)S(1)} %shard_map.65.after_ref.refs_0_.solved_ref), channel_id=1, source_target_pairs={{0,8},{4,12},{8,0},{12,4},{16,24},{20,28},{24,16},{28,20},{1,9},{5... | collective-permute-start | bytes 196616 | tf_op jit(solution)/shard_map/ppermute | solution.py:20
  61.7 6.2 %collective-permute-start.19 = (bf16[128,256]{1,0:T(8,128)(2,1)S(1)}, bf16[128,256]{1,0:T(8,128)(2,1)S(1)}, u32[]{:S(2)}, u32[]{:S(2)}) collective-permute-start(bf16[128,256]{1,0:T(8,128)(2,1)S(1)} %get-tuple-element.49), channel_id=1, source_target_pairs={{0,3},{1,2},{2,1},{3,0},{4,7},{5,6},{6,5},{7,4},{8,11},{9,10},{10,... | collective-permute-start | bytes 196616 | tf_op jit(solution)/shard_map/ppermute | solution.py:20
  63.7 4.8 %collective-permute-start.20 = (bf16[128,256]{1,0:T(8,128)(2,1)S(1)}, bf16[128,256]{1,0:T(8,128)(2,1)S(1)}, u32[]{:S(2)}, u32[]{:S(2)}) collective-permute-start(bf16[128,256]{1,0:T(8,128)(2,1)S(1)} %get-tuple-element.50), channel_id=1, source_target_pairs={{0,1},{1,0},{2,3},{3,2},{4,5},{5,4},{6,7},{7,6},{8,9},{9,8},{10,11... | collective-permute-start | bytes 196616 | tf_op jit(solution)/shard_map/ppermute | solution.py:20
  64.0 5.5 %collective-permute-start.21 = (bf16[128,256]{1,0:T(8,128)(2,1)S(1)}, bf16[128,256]{1,0:T(8,128)(2,1)S(1)}, u32[]{:S(2)}, u32[]{:S(2)}) collective-permute-start(bf16[128,256]{1,0:T(8,128)(2,1)S(1)} %get-tuple-element.51), channel_id=1, source_target_pairs={{0,2},{1,3},{2,0},{3,1},{4,6},{5,7},{6,4},{7,5},{8,10},{9,11},{10,... | collective-permute-start | bytes 196616 | tf_op jit(solution)/shard_map/ppermute | solution.py:20
  69.9 6.2 %collective-permute-start.24 = (bf16[128,256]{1,0:T(8,128)(2,1)S(1)}, bf16[128,256]{1,0:T(8,128)(2,1)S(1)}, u32[]{:S(2)}, u32[]{:S(2)}) collective-permute-start(bf16[128,256]{1,0:T(8,128)(2,1)S(1)} %get-tuple-element.52.after_ref.refs_0_.refs_3_), channel_id=1, source_target_pairs={{0,3},{1,2},{2,1},{3,0},{4,7},{5,6},{6,5},{7,4},{8,11},{9,10},{10,... | collective-permute-start | bytes 196616 | tf_op jit(solution)/shard_map/ppermute | solution.py:20
  71.6 6.1 %collective-permute-start.23 = (bf16[128,256]{1,0:T(8,128)(2,1)S(1)}, bf16[128,256]{1,0:T(8,128)(2,1)S(1)}, u32[]{:S(2)}, u32[]{:S(2)}) collective-permute-start(bf16[128,256]{1,0:T(8,128)(2,1)S(1)} %get-tuple-element.52.after_ref.refs_0_.refs_3_), channel_id=1, source_target_pairs={{0,2},{1,3},{2,0},{3,1},{4,6},{5,7},{6,4},{7,5},{8,10},{9,11},{10,... | collective-permute-start | bytes 196616 | tf_op jit(solution)/shard_map/ppermute | solution.py:20
  73.2 4.6 %collective-permute-start.22 = (bf16[128,256]{1,0:T(8,128)(2,1)S(1)}, bf16[128,256]{1,0:T(8,128)(2,1)S(1)}, u32[]{:S(2)}, u32[]{:S(2)}) collective-permute-start(bf16[128,256]{1,0:T(8,128)(2,1)S(1)} %get-tuple-element.52.after_ref.refs_0_.refs_3_), channel_id=1, source_target_pairs={{0,1},{1,0},{2,3},{3,2},{4,5},{5,4},{6,7},{7,6},{8,9},{9,8},{10,11... | collective-permute-start | bytes 196616 | tf_op jit(solution)/shard_map/ppermute | solution.py:20
  78.2 5.2 %collective-permute-start.25 = (bf16[128,256]{1,0:T(8,128)(2,1)S(1)}, bf16[128,256]{1,0:T(8,128)(2,1)S(1)}, u32[]{:S(2)}, u32[]{:S(2)}) collective-permute-start(bf16[128,256]{1,0:T(8,128)(2,1)S(1)} %get-tuple-element.53), channel_id=1, source_target_pairs={{0,24},{4,28},{8,16},{12,20},{16,8},{20,12},{24,0},{28,4},{1,25},{... | collective-permute-start | bytes 196616 | tf_op jit(solution)/shard_map/ppermute | solution.py:20
  79.9 4.3 %collective-permute-start.26 = (bf16[128,256]{1,0:T(8,128)(2,1)S(1)}, bf16[128,256]{1,0:T(8,128)(2,1)S(1)}, u32[]{:S(2)}, u32[]{:S(2)}) collective-permute-start(bf16[128,256]{1,0:T(8,128)(2,1)S(1)} %get-tuple-element.54), channel_id=1, source_target_pairs={{0,16},{4,20},{8,24},{12,28},{16,0},{20,4},{24,8},{28,12},{1,17},{... | collective-permute-start | bytes 196616 | tf_op jit(solution)/shard_map/ppermute | solution.py:20
  80.9 4.3 %collective-permute-start.27 = (bf16[128,256]{1,0:T(8,128)(2,1)S(1)}, bf16[128,256]{1,0:T(8,128)(2,1)S(1)}, u32[]{:S(2)}, u32[]{:S(2)}) collective-permute-start(bf16[128,256]{1,0:T(8,128)(2,1)S(1)} %get-tuple-element.55), channel_id=1, source_target_pairs={{0,8},{4,12},{8,0},{12,4},{16,24},{20,28},{24,16},{28,20},{1,9},{5... | collective-permute-start | bytes 196616 | tf_op jit(solution)/shard_map/ppermute | solution.py:20
  85.4 6.1 %collective-permute-start.30 = (bf16[128,256]{1,0:T(8,128)(2,1)S(1)}, bf16[128,256]{1,0:T(8,128)(2,1)S(1)}, u32[]{:S(2)}, u32[]{:S(2)}) collective-permute-start(bf16[128,256]{1,0:T(8,128)(2,1)S(1)} %get-tuple-element.56.after_ref.refs_0_.refs_2_), channel_id=1, source_target_pairs={{0,3},{1,2},{2,1},{3,0},{4,7},{5,6},{6,5},{7,4},{8,11},{9,10},{10,... | collective-permute-start | bytes 196616 | tf_op jit(solution)/shard_map/ppermute | solution.py:20
  87.1 5.8 %collective-permute-start.29 = (bf16[128,256]{1,0:T(8,128)(2,1)S(1)}, bf16[128,256]{1,0:T(8,128)(2,1)S(1)}, u32[]{:S(2)}, u32[]{:S(2)}) collective-permute-start(bf16[128,256]{1,0:T(8,128)(2,1)S(1)} %get-tuple-element.56.after_ref.refs_0_.refs_2_), channel_id=1, source_target_pairs={{0,2},{1,3},{2,0},{3,1},{4,6},{5,7},{6,4},{7,5},{8,10},{9,11},{10,... | collective-permute-start | bytes 196616 | tf_op jit(solution)/shard_map/ppermute | solution.py:20
  87.5 5.4 %collective-permute-start.28 = (bf16[128,256]{1,0:T(8,128)(2,1)S(1)}, bf16[128,256]{1,0:T(8,128)(2,1)S(1)}, u32[]{:S(2)}, u32[]{:S(2)}) collective-permute-start(bf16[128,256]{1,0:T(8,128)(2,1)S(1)} %get-tuple-element.56.after_ref.refs_0_.refs_2_), channel_id=1, source_target_pairs={{0,1},{1,0},{2,3},{3,2},{4,5},{5,4},{6,7},{7,6},{8,9},{9,8},{10,11... | collective-permute-start | bytes 196616 | tf_op jit(solution)/shard_map/ppermute | solution.py:20
  93.3 5.3 %collective-permute-start.31 = (bf16[128,256]{1,0:T(8,128)(2,1)S(1)}, bf16[128,256]{1,0:T(8,128)(2,1)S(1)}, u32[]{:S(2)}, u32[]{:S(2)}) collective-permute-start(bf16[128,256]{1,0:T(8,128)(2,1)S(1)} %get-tuple-element.57), channel_id=1, source_target_pairs={{0,24},{4,28},{8,16},{12,20},{16,8},{20,12},{24,0},{28,4},{1,25},{... | collective-permute-start | bytes 196616 | tf_op jit(solution)/shard_map/ppermute | solution.py:20
  94.0 5.0 %collective-permute-start.32 = (bf16[128,256]{1,0:T(8,128)(2,1)S(1)}, bf16[128,256]{1,0:T(8,128)(2,1)S(1)}, u32[]{:S(2)}, u32[]{:S(2)}) collective-permute-start(bf16[128,256]{1,0:T(8,128)(2,1)S(1)} %get-tuple-element.58), channel_id=1, source_target_pairs={{0,16},{4,20},{8,24},{12,28},{16,0},{20,4},{24,8},{28,12},{1,17},{... | collective-permute-start | bytes 196616 | tf_op jit(solution)/shard_map/ppermute | solution.py:20
  95.7 4.3 %collective-permute-start.33 = (bf16[128,256]{1,0:T(8,128)(2,1)S(1)}, bf16[128,256]{1,0:T(8,128)(2,1)S(1)}, u32[]{:S(2)}, u32[]{:S(2)}) collective-permute-start(bf16[128,256]{1,0:T(8,128)(2,1)S(1)} %get-tuple-element.59), channel_id=1, source_target_pairs={{0,8},{4,12},{8,0},{12,4},{16,24},{20,28},{24,16},{28,20},{1,9},{5... | collective-permute-start | bytes 196616 | tf_op jit(solution)/shard_map/ppermute | solution.py:20
  100.2 6.1 %collective-permute-start.36 = (bf16[128,256]{1,0:T(8,128)(2,1)S(1)}, bf16[128,256]{1,0:T(8,128)(2,1)S(1)}, u32[]{:S(2)}, u32[]{:S(2)}) collective-permute-start(bf16[128,256]{1,0:T(8,128)(2,1)S(1)} %get-tuple-element.60.after_ref.refs_0_.refs_1_), channel_id=1, source_target_pairs={{0,3},{1,2},{2,1},{3,0},{4,7},{5,6},{6,5},{7,4},{8,11},{9,10},{10,... | collective-permute-start | bytes 196616 | tf_op jit(solution)/shard_map/ppermute | solution.py:20
  102.1 5.7 %collective-permute-start.35 = (bf16[128,256]{1,0:T(8,128)(2,1)S(1)}, bf16[128,256]{1,0:T(8,128)(2,1)S(1)}, u32[]{:S(2)}, u32[]{:S(2)}) collective-permute-start(bf16[128,256]{1,0:T(8,128)(2,1)S(1)} %get-tuple-element.60.after_ref.refs_0_.refs_1_), channel_id=1, source_target_pairs={{0,2},{1,3},{2,0},{3,1},{4,6},{5,7},{6,4},{7,5},{8,10},{9,11},{10,... | collective-permute-start | bytes 196616 | tf_op jit(solution)/shard_map/ppermute | solution.py:20
  103.0 5.0 %collective-permute-start.34 = (bf16[128,256]{1,0:T(8,128)(2,1)S(1)}, bf16[128,256]{1,0:T(8,128)(2,1)S(1)}, u32[]{:S(2)}, u32[]{:S(2)}) collective-permute-start(bf16[128,256]{1,0:T(8,128)(2,1)S(1)} %get-tuple-element.60.after_ref.refs_0_.refs_1_), channel_id=1, source_target_pairs={{0,1},{1,0},{2,3},{3,2},{4,5},{5,4},{6,7},{7,6},{8,9},{9,8},{10,11... | collective-permute-start | bytes 196616 | tf_op jit(solution)/shard_map/ppermute | solution.py:20
  108.4 5.2 %collective-permute-start.37 = (bf16[128,256]{1,0:T(8,128)(2,1)S(1)}, bf16[128,256]{1,0:T(8,128)(2,1)S(1)}, u32[]{:S(2)}, u32[]{:S(2)}) collective-permute-start(bf16[128,256]{1,0:T(8,128)(2,1)S(1)} %get-tuple-element.61), channel_id=1, source_target_pairs={{0,24},{4,28},{8,16},{12,20},{16,8},{20,12},{24,0},{28,4},{1,25},{... | collective-permute-start | bytes 196616 | tf_op jit(solution)/shard_map/ppermute | solution.py:20
  110.0 4.3 %collective-permute-start.38 = (bf16[128,256]{1,0:T(8,128)(2,1)S(1)}, bf16[128,256]{1,0:T(8,128)(2,1)S(1)}, u32[]{:S(2)}, u32[]{:S(2)}) collective-permute-start(bf16[128,256]{1,0:T(8,128)(2,1)S(1)} %get-tuple-element.62), channel_id=1, source_target_pairs={{0,16},{4,20},{8,24},{12,28},{16,0},{20,4},{24,8},{28,12},{1,17},{... | collective-permute-start | bytes 196616 | tf_op jit(solution)/shard_map/ppermute | solution.py:20
  111.0 4.3 %collective-permute-start.39 = (bf16[128,256]{1,0:T(8,128)(2,1)S(1)}, bf16[128,256]{1,0:T(8,128)(2,1)S(1)}, u32[]{:S(2)}, u32[]{:S(2)}) collective-permute-start(bf16[128,256]{1,0:T(8,128)(2,1)S(1)} %get-tuple-element.63), channel_id=1, source_target_pairs={{0,8},{4,12},{8,0},{12,4},{16,24},{20,28},{24,16},{28,20},{1,9},{5... | collective-permute-start | bytes 196616 | tf_op jit(solution)/shard_map/ppermute | solution.py:20
  112.0 3.5 %collective-permute-start.43 = (bf16[128,128]{1,0:T(8,128)(2,1)S(1)}, bf16[128,128]{1,0:T(8,128)(2,1)S(1)}, u32[]{:S(2)}, u32[]{:S(2)}) collective-permute-start(bf16[128,128]{1,0:T(8,128)(2,1)S(1)} %get-tuple-element.68), channel_id=1, source_target_pairs={{0,4},{4,0},{8,12},{12,8},{16,20},{20,16},{24,28},{28,24},{1,5},{5... | collective-permute-start | bytes 98312 | tf_op jit(solution)/shard_map/ppermute | solution.py:20
  112.0 3.6 %collective-permute-start.42 = (bf16[128,128]{1,0:T(8,128)(2,1)S(1)}, bf16[128,128]{1,0:T(8,128)(2,1)S(1)}, u32[]{:S(2)}, u32[]{:S(2)}) collective-permute-start(bf16[128,128]{1,0:T(8,128)(2,1)S(1)} %get-tuple-element.67), channel_id=1, source_target_pairs={{0,4},{4,0},{8,12},{12,8},{16,20},{20,16},{24,28},{28,24},{1,5},{5... | collective-permute-start | bytes 98312 | tf_op jit(solution)/shard_map/ppermute | solution.py:20
  113.7 1.9 %collective-permute-start.41 = (bf16[128,128]{1,0:T(8,128)(2,1)S(1)}, bf16[128,128]{1,0:T(8,128)(2,1)S(1)}, u32[]{:S(2)}, u32[]{:S(2)}) collective-permute-start(bf16[128,128]{1,0:T(8,128)(2,1)S(1)} %get-tuple-element.66), channel_id=1, source_target_pairs={{0,4},{4,0},{8,12},{12,8},{16,20},{20,16},{24,28},{28,24},{1,5},{5... | collective-permute-start | bytes 98312 | tf_op jit(solution)/shard_map/ppermute | solution.py:20
  115.4 1.3 %collective-permute-start.40 = (bf16[128,128]{1,0:T(8,128)(2,1)S(1)}, bf16[128,128]{1,0:T(8,128)(2,1)S(1)}, u32[]{:S(2)}, u32[]{:S(2)}) collective-permute-start(bf16[128,128]{1,0:T(8,128)(2,1)S(1)} %get-tuple-element.65), channel_id=1, source_target_pairs={{0,4},{4,0},{8,12},{12,8},{16,20},{20,16},{24,28},{28,24},{1,5},{5... | collective-permute-start | bytes 98312 | tf_op jit(solution)/shard_map/ppermute | solution.py:20

commit v6 on v5

--- a/solution.py
+++ b/solution.py
@@ -10,6 +10,8 @@
 B = 128
 NLEV = 4
 LANES = 128
+ROW_ORDER = (3, 1, 2)
+COL_ORDER = (3, 1, 2)
 VMEM_BYTES = 16 * 1024 * 1024
 F32 = jnp.float32
 BF16 = jnp.bfloat16
@@ -20,8 +22,9 @@
     return lax.ppermute(value, axis, [(i, i ^ distance) for i in range(count)])
 
 
-def z_order(count):
-    return [count - 1, *range(1, count - 1)]
+def issue_order(count, first):
+    ahead = [m for m in first if m < count]
+    return ahead + [m for m in range(count - 1, 0, -1) if m not in ahead]
 
 
 def call(body, out_shape, args, scratch=(), flops=0, space=pltpu.VMEM, limit=VMEM_BYTES):
@@ -78,6 +81,27 @@
     )(own, par, after)
 
 
+def fetch_turned_body(own_ref, par_ref, after_ref, out_ref):
+    parity = lax.axis_index("row") % 2
+    for i in range(own_ref.shape[0] // B):
+        source = pl.ds(i * B, B)
+        for ref, rr in ((own_ref, parity), (par_ref, 1 - parity)):
+            out_ref[:, aligned(2 * i + rr, B, B)] = ref[source, :].T
+
+
+def fetch_turned(own, par, after):
+    return pl.pallas_call(
+        fetch_turned_body,
+        out_shape=pltpu.VMEM((own.shape[1], 2 * own.shape[0]), own.dtype),
+        in_specs=[pl.BlockSpec(memory_space=pltpu.VMEM)] * 2 + [pl.BlockSpec(memory_space=pl.ANY)],
+        out_specs=pl.BlockSpec(memory_space=pltpu.VMEM),
+        compiler_params=pltpu.CompilerParams(vmem_limit_bytes=VMEM_BYTES),
+        cost_estimate=pl.CostEstimate(
+            flops=0, bytes_accessed=4 * own.size * own.dtype.itemsize, transcendentals=0
+        ),
+    )(own, par, after)
+
+
 def pack_body(
     rows, cols, chunk_rows, total_rows, rhs_hbm, dest_hbm, out_ref, rhs_ref, dest_ref, sems
 ):
@@ -85,8 +109,13 @@
     rhs_copy = pltpu.make_async_copy(rhs_hbm, rhs_ref, sems.at[1])
     dest_copy.start()
     rhs_copy.start()
+    local_rows = rhs_ref.shape[0]
+    before = (
+        lax.broadcasted_iota(jnp.int32, (local_rows, local_rows), 0)
+        < lax.broadcasted_iota(jnp.int32, (local_rows, local_rows), 1)
+    )
+    before = jnp.where(before, 1.0, 0.0).astype(BF16)
     dest_copy.wait()
-    local_rows = rhs_ref.shape[0]
     supernodes = rows * cols
     pairs = supernodes // 2
     shards_per_line = LANES // chunk_rows
@@ -102,13 +131,7 @@
     pair_iota = lax.broadcasted_iota(jnp.int32, (pairs, local_rows), 0)
     member = pair_iota == pair
     member_f = jnp.where(member, 1.0, 0.0)
-    before = (
-        lax.broadcasted_iota(jnp.int32, (local_rows, local_rows), 0)
-        < lax.broadcasted_iota(jnp.int32, (local_rows, local_rows), 1)
-    )
-    counts = jnp.dot(
-        member_f.astype(BF16), jnp.where(before, 1.0, 0.0).astype(BF16), preferred_element_type=F32
-    )
+    counts = jnp.dot(member_f.astype(BF16), before, preferred_element_type=F32)
     rank = jnp.sum(member_f * counts, axis=0, keepdims=True).astype(jnp.int32)
     slot = pair * chunk_rows + rank
     chosen = lax.broadcasted_iota(jnp.int32, (local_rows, local_rows), 0) == slot
@@ -199,7 +222,7 @@
     gather_pieces(pieces, lax.axis_index("row") // 2, gathered)
     for m, out in zip(distances, outs):
         at = aligned(col ^ m, 2 * B, 2 * B)
-        out[...] = times_t(gathered[...], tile_ref[at, :]).astype(out.dtype)
+        out[...] = times(gathered[...], tile_ref[:, at]).astype(out.dtype)
 
 
 def up_body(tile_ref, *refs, cols, distances):
@@ -216,12 +239,21 @@
 
 
 def finish_body(*refs):
-    blocks, others, out_ref = refs[:NLEV], refs[NLEV : 2 * NLEV], refs[2 * NLEV]
+    blocks, others, out_ref = refs[:NLEV], refs[NLEV:-1], refs[-1]
     parity = lax.axis_index("row") % 2
     mine, other = aligned(parity, B, B), aligned(1 - parity, B, B)
     for level in range(NLEV):
         out_ref[level, 0, :, mine] = blocks[level][:, mine].T
-        out_ref[level, 0, :, other] = others[level][...].T
+        if level:
+            out_ref[level, 0, :, other] = others[level - 1][...].T
+
+
+def last_body(started_ref, other_ref, out_ref, turned, sem):
+    turned[...] = other_ref[...].T
+    lanes = aligned(1 - lax.axis_index("row") % 2, B, B)
+    copy = pltpu.make_async_copy(turned, out_ref.at[0, 0, :, lanes], sem)
+    copy.start()
+    copy.wait()
 
 
 def residual_body(rhs_ref, own_ref, par_ref, kept_ref, *refs, level):
@@ -308,8 +340,11 @@
         if level < NLEV - 1:
             own[level], _ = lax.optimization_barrier((own[level], solved[-1]))
             par[level] = swap(own[level], "row", 1)
-        pieces = [solved[-1]] + [swap(solved[-1], "row", 2 * m) for m in range(1, groups)]
-        tiles = fetch(own[level - 1], par[level - 1], solved[-1])
+        sent = {
+            m: swap(solved[-1], "row", 2 * m) for m in reversed(issue_order(groups, ROW_ORDER))
+        }
+        pieces = [solved[-1]] + [sent[m] for m in range(1, groups)]
+        tiles = fetch_turned(own[level - 1], par[level - 1], solved[-1])
         far = list(range(1, cols))
         sums = [
             call(
@@ -322,7 +357,7 @@
             for distances in (far, [0])
         ]
         sums = [*sums[1], *sums[0]]
-        passed = [swap(sums[m], "col", m) for m in z_order(cols)]
+        passed = [swap(sums[m], "col", m) for m in issue_order(cols, COL_ORDER)]
         last = level == NLEV - 1
         result = call(
             functools.partial(residual_body, level=level),
@@ -338,7 +373,7 @@
     solution, others = [None] * NLEV, [None] * NLEV
     solution[NLEV - 1], others[NLEV - 1] = upper, swap(theirs, "row", 1)
     for level in range(NLEV - 2, -1, -1):
-        sent = {m: swap(upper, "col", m) for m in reversed(z_order(cols))}
+        sent = {m: swap(upper, "col", m) for m in reversed(issue_order(cols, COL_ORDER))}
         pieces = [upper] + [sent[m] for m in range(1, cols)]
         tiles = fetch(own[level], par[level], upper)
         far = list(range(1, groups))
@@ -353,7 +388,7 @@
             for distances in (far, [0])
         ]
         sums = [*sums[1], *sums[0]]
-        passed = [swap(sums[m], "row", 2 * m) for m in range(groups - 1, 0, -1)]
+        passed = [swap(sums[m], "row", 2 * m) for m in issue_order(groups, ROW_ORDER)]
         upper, theirs = call(
             functools.partial(final_body, level=level),
             [shape(block), shape((half, B))],
@@ -362,9 +397,18 @@
         )
         solution[level], others[level] = upper, swap(theirs, "row", 1)
 
-    return call(
-        finish_body, shape((NLEV, 1, B, 2 * half)), (*solution, *others)
-    )
+    started = call(
+        finish_body, shape((NLEV, 1, B, 2 * half)), (*solution, *others[1:])
+    )
+    return pl.pallas_call(
+        last_body,
+        out_shape=shape((NLEV, 1, B, 2 * half)),
+        in_specs=[pl.BlockSpec(memory_space=pl.ANY), pl.BlockSpec(memory_space=pltpu.VMEM)],
+        out_specs=pl.BlockSpec(memory_space=pl.ANY),
+        scratch_shapes=[pltpu.VMEM((B, half), BF16), pltpu.SemaphoreType.DMA],
+        input_output_aliases={0: 0},
+        compiler_params=pltpu.CompilerParams(vmem_limit_bytes=VMEM_BYTES),
+    )(started, others[0])
 
 
 def solution(mesh):

time: 118 us -> 116 us (0.983)
  waiting for transfers between devices: 43.1 us -> 40.2 us
    ppermute x44, waiting for transfers between devices: 36.4 us -> 33.5 us  [swap(): return lax.ppermute(value, axis, [(i, i ^ distance) for i in range(count)])]
    pallas_call x0 -> x4, Pallas kernels: none -> 2.74 us  [the longest x3 2.04 us: fetch_turned(): pl.pallas_call(fetch_turned_body, out_shape=pltpu.VMEM((own.shape[1], 2 *...]
  transfers between devices with their start and end apart: 45 -> 45, of which waited for: 37 -> 33; matrix products, arithmetic and copies ran while one was open for 4% -> 4% of each run, Pallas kernels for 7% -> 8%
where the time goes in v6:
time: 116 us
  starting transfers between devices  57 us (49%)
  waiting for transfers between devices  40.2 us (35%)
  Pallas kernels  13.1 us (11%)
  local copies, waits for them, and re-layouts  3.72 us (3%)
  other arithmetic  1.42 us (1%)
    ppermute x44, starting transfers between devices, swap(): return lax.ppermute(value, axis, [(i, i ^ distance) for i in range(count)])  50 us
    ppermute x44, waiting for transfers between devices, swap(): return lax.ppermute(value, axis, [(i, i ^ distance) for i in range(count)])  33.5 us
    pallas_call x22, Pallas kernels, call(): pl.pallas_call(body, out_shape=out_shape, in_specs=in_specs, out_specs=ou...  9.71 us
    all_to_all x1, starting transfers between devices, per_device(): lax.all_to_all(sending, ('row', 'col'), split_axis=0, concat_axis=0, tile...  6.97 us
    all_to_all x1, waiting for transfers between devices, per_device(): lax.all_to_all(sending, ('row', 'col'), split_axis=0, concat_axis=0, tile...  6.71 us
    slice x1, local copies, waits for them, and re-layouts, per_device(): tile = lower_blocks[level, 0, :, :, 0]  3.09 us
  transfers between devices with their start and end apart: 45, of which 33 were waited for; matrix products, arithmetic and copies ran while one was open for 4% of the time, Pallas kernels for 8%

profile of v6, /device:TPU:0, one launch (start us, length us, event | category | flops | bytes accessed | tf_op | source)
XLA Modules:
  0.0 115.9 jit_solution(12256933123925979902)
XLA Ops:
  0.5 2.3 %shard_map.55 = bf16[32,40,128]{2,1,0:T(8,128)(2,1)} custom-call(f32[512,256]{1,0:T(8,128)} %rhs_hbm.1, s32[1,512]{1,0:T(1,128)} %bitcast.48), custom_call_target="tpu_custom_call" | custom-call | flops 134217728 | bytes 526336 | tf_op jit(solution)/shard_map/pallas_call | solution.py:39
  2.8 7.0 %all-to-all-start = ((bf16[32,40,128]{2,1,0:T(8,128)(2,1)}), bf16[32,40,128]{2,1,0:T(8,128)(2,1)S(1)}, u32[]{:S(2)}, u32[]{:S(2)}) async-start(bf16[32,40,128]{2,1,0:T(8,128)(2,1)} %shard_map.55), calls=%async_computation | async-start | bytes 655360 | tf_op jit(solution)/shard_map/all_to_all | solution.py:320
  10.5 3.1 %fusion = (bf16[1,1,4,128,1,8,128]{6,5,4,3,2,1,0:T(8,128)(2,1)S(1)}, bf16[1,1,4,128,1,8,128]{6,5,4,3,2,1,0:T(8,128)(2,1)S(1)}, bf16[1,1,4,128,1,8,128]{6,5,4,3,2,1,0:T(8,128)(2,1)}) fusion(bf16[3,1,4,128,1,8,128]{6,5,4,3,2,1,0:T(8,128)(2,1)} %param.8), kind=kLoop, calls=%fused_computation.6 | loop fusion | bytes 6291456 | tf_op jit(solution)/shard_map/slice | solution.py:302
  14.0 6.7 %all-to-all-done.arrived_ref = bf16[32,40,128]{2,1,0:T(8,128)(2,1)S(1)} async-done(((bf16[32,40,128]{2,1,0:T(8,128)(2,1)}), bf16[32,40,128]{2,1,0:T(8,128)(2,1)S(1)}, u32[]{:S(2)}, u32[]{:S(2)}) %all-to-all-start) | async-done | bytes 327712 | tf_op jit(solution)/shard_map/all_to_all | solution.py:320
  21.2 0.9 collective-permute-start.1
  22.1 1.0 collective-permute-start.4
  23.2 1.5 %collective-permute-start.3 = (bf16[128,256]{1,0:T(8,128)(2,1)S(1)}, bf16[128,256]{1,0:T(8,128)(2,1)S(1)}, u32[]{:S(2)}, u32[]{:S(2)}) collective-permute-start(bf16[128,256]{1,0:T(8,128)(2,1)S(1)} %shard_map.56.after_ref.refs_0_.solved_ref), channel_id=1, source_target_pairs={{0,16},{4,20},{8,24},{12,28},{16,0},{20,4},{24,8},{28,12},{1,17},{... | collective-permute-start | bytes 196616 | tf_op jit(solution)/shard_map/ppermute | solution.py:22
  24.6 1.0 collective-permute-start.2
  26.9 0.9 collective-permute-done.4.refs_3_
  29.3 1.8 %collective-permute-start.5 = (bf16[128,256]{1,0:T(8,128)(2,1)S(1)}, bf16[128,256]{1,0:T(8,128)(2,1)S(1)}, u32[]{:S(2)}, u32[]{:S(2)}) collective-permute-start(bf16[128,256]{1,0:T(8,128)(2,1)S(1)} %get-tuple-element.39), channel_id=1, source_target_pairs={{0,3},{1,2},{2,1},{3,0},{4,7},{5,6},{6,5},{7,4},{8,11},{9,10},{10,... | collective-permute-start | bytes 196616 | tf_op jit(solution)/shard_map/ppermute | solution.py:22
  31.1 2.7 %collective-permute-start.7 = (bf16[128,256]{1,0:T(8,128)(2,1)S(1)}, bf16[128,256]{1,0:T(8,128)(2,1)S(1)}, u32[]{:S(2)}, u32[]{:S(2)}) collective-permute-start(bf16[128,256]{1,0:T(8,128)(2,1)S(1)} %get-tuple-element.41), channel_id=1, source_target_pairs={{0,2},{1,3},{2,0},{3,1},{4,6},{5,7},{6,4},{7,5},{8,10},{9,11},{10,... | collective-permute-start | bytes 196616 | tf_op jit(solution)/shard_map/ppermute | solution.py:22
  35.9 1.4 %collective-permute-done.6.refs_1_ = bf16[128,256]{1,0:T(8,128)(2,1)S(1)} collective-permute-done((bf16[128,256]{1,0:T(8,128)(2,1)S(1)}, bf16[128,256]{1,0:T(8,128)(2,1)S(1)}, u32[]{:S(2)}, u32[]{:S(2)}) %collective-permute-start.6) | collective-permute-done | bytes 65568 | tf_op jit(solution)/shard_map/ppermute | solution.py:22
  38.7 2.3 %collective-permute-start.10 = (bf16[128,256]{1,0:T(8,128)(2,1)S(1)}, bf16[128,256]{1,0:T(8,128)(2,1)S(1)}, u32[]{:S(2)}, u32[]{:S(2)}) collective-permute-start(bf16[128,256]{1,0:T(8,128)(2,1)S(1)} %shard_map.61.after_ref.refs_0_.solved_ref), channel_id=1, source_target_pairs={{0,16},{4,20},{8,24},{12,28},{16,0},{20,4},{24,8},{28,12},{1,17},{... | collective-permute-start | bytes 196616 | tf_op jit(solution)/shard_map/ppermute | solution.py:22
  42.4 1.6 %collective-permute-done.11.refs_3_ = bf16[128,256]{1,0:T(8,128)(2,1)S(1)} collective-permute-done((bf16[128,256]{1,0:T(8,128)(2,1)S(1)}, bf16[128,256]{1,0:T(8,128)(2,1)S(1)}, u32[]{:S(2)}, u32[]{:S(2)}) %collective-permute-start.11) | collective-permute-done | bytes 65568 | tf_op jit(solution)/shard_map/ppermute | solution.py:22
  45.7 1.2 %collective-permute-start.12 = (bf16[128,256]{1,0:T(8,128)(2,1)S(1)}, bf16[128,256]{1,0:T(8,128)(2,1)S(1)}, u32[]{:S(2)}, u32[]{:S(2)}) collective-permute-start(bf16[128,256]{1,0:T(8,128)(2,1)S(1)} %get-tuple-element.44), channel_id=1, source_target_pairs={{0,3},{1,2},{2,1},{3,0},{4,7},{5,6},{6,5},{7,4},{8,11},{9,10},{10,... | collective-permute-start | bytes 196616 | tf_op jit(solution)/shard_map/ppermute | solution.py:22
  47.1 3.1 %collective-permute-start.14 = (bf16[128,256]{1,0:T(8,128)(2,1)S(1)}, bf16[128,256]{1,0:T(8,128)(2,1)S(1)}, u32[]{:S(2)}, u32[]{:S(2)}) collective-permute-start(bf16[128,256]{1,0:T(8,128)(2,1)S(1)} %get-tuple-element.46), channel_id=1, source_target_pairs={{0,2},{1,3},{2,0},{3,1},{4,6},{5,7},{6,4},{7,5},{8,10},{9,11},{10,... | collective-permute-start | bytes 196616 | tf_op jit(solution)/shard_map/ppermute | solution.py:22
  50.5 2.1 %collective-permute-done.12.refs_0_ = bf16[128,256]{1,0:T(8,128)(2,1)S(1)} collective-permute-done((bf16[128,256]{1,0:T(8,128)(2,1)S(1)}, bf16[128,256]{1,0:T(8,128)(2,1)S(1)}, u32[]{:S(2)}, u32[]{:S(2)}) %collective-permute-start.12) | collective-permute-done | bytes 65568 | tf_op jit(solution)/shard_map/ppermute | solution.py:22
  53.4 1.4 %collective-permute-start.18 = (bf16[128,256]{1,0:T(8,128)(2,1)S(1)}, bf16[128,256]{1,0:T(8,128)(2,1)S(1)}, u32[]{:S(2)}, u32[]{:S(2)}) collective-permute-start(bf16[128,256]{1,0:T(8,128)(2,1)S(1)} %shard_map.65.after_ref.refs_0_.solved_ref), channel_id=1, source_target_pairs={{0,24},{4,28},{8,16},{12,20},{16,8},{20,12},{24,0},{28,4},{1,25},{... | collective-permute-start | bytes 196616 | tf_op jit(solution)/shard_map/ppermute | solution.py:22
  54.8 1.5 %collective-permute-start.17 = (bf16[128,256]{1,0:T(8,128)(2,1)S(1)}, bf16[128,256]{1,0:T(8,128)(2,1)S(1)}, u32[]{:S(2)}, u32[]{:S(2)}) collective-permute-start(bf16[128,256]{1,0:T(8,128)(2,1)S(1)} %shard_map.65.after_ref.refs_0_.solved_ref), channel_id=1, source_target_pairs={{0,16},{4,20},{8,24},{12,28},{16,0},{20,4},{24,8},{28,12},{1,17},{... | collective-permute-start | bytes 196616 | tf_op jit(solution)/shard_map/ppermute | solution.py:22
  57.7 1.5 %collective-permute-done.18.refs_3_ = bf16[128,256]{1,0:T(8,128)(2,1)S(1)} collective-permute-done((bf16[128,256]{1,0:T(8,128)(2,1)S(1)}, bf16[128,256]{1,0:T(8,128)(2,1)S(1)}, u32[]{:S(2)}, u32[]{:S(2)}) %collective-permute-start.18) | collective-permute-done | bytes 65568 | tf_op jit(solution)/shard_map/ppermute | solution.py:22
  59.6 1.0 collective-permute-done.16.refs_1_
  61.0 2.0 %collective-permute-start.19 = (bf16[128,256]{1,0:T(8,128)(2,1)S(1)}, bf16[128,256]{1,0:T(8,128)(2,1)S(1)}, u32[]{:S(2)}, u32[]{:S(2)}) collective-permute-start(bf16[128,256]{1,0:T(8,128)(2,1)S(1)} %get-tuple-element.49), channel_id=1, source_target_pairs={{0,3},{1,2},{2,1},{3,0},{4,7},{5,6},{6,5},{7,4},{8,11},{9,10},{10,... | collective-permute-start | bytes 196616 | tf_op jit(solution)/shard_map/ppermute | solution.py:22
  63.3 2.1 %collective-permute-start.21 = (bf16[128,256]{1,0:T(8,128)(2,1)S(1)}, bf16[128,256]{1,0:T(8,128)(2,1)S(1)}, u32[]{:S(2)}, u32[]{:S(2)}) collective-permute-start(bf16[128,256]{1,0:T(8,128)(2,1)S(1)} %get-tuple-element.51), channel_id=1, source_target_pairs={{0,2},{1,3},{2,0},{3,1},{4,6},{5,7},{6,4},{7,5},{8,10},{9,11},{10,... | collective-permute-start | bytes 196616 | tf_op jit(solution)/shard_map/ppermute | solution.py:22
  65.7 1.5 %collective-permute-done.19.refs_0_ = bf16[128,256]{1,0:T(8,128)(2,1)S(1)} collective-permute-done((bf16[128,256]{1,0:T(8,128)(2,1)S(1)}, bf16[128,256]{1,0:T(8,128)(2,1)S(1)}, u32[]{:S(2)}, u32[]{:S(2)}) %collective-permute-start.19) | collective-permute-done | bytes 65568 | tf_op jit(solution)/shard_map/ppermute | solution.py:22
  67.9 1.1 collective-permute-done.21.refs_2_
  69.3 1.6 %collective-permute-start.24 = (bf16[128,256]{1,0:T(8,128)(2,1)S(1)}, bf16[128,256]{1,0:T(8,128)(2,1)S(1)}, u32[]{:S(2)}, u32[]{:S(2)}) collective-permute-start(bf16[128,256]{1,0:T(8,128)(2,1)S(1)} %get-tuple-element.52.after_ref.refs_0_.refs_3_), channel_id=1, source_target_pairs={{0,3},{1,2},{2,1},{3,0},{4,7},{5,6},{6,5},{7,4},{8,11},{9,10},{10,... | collective-permute-start | bytes 196616 | tf_op jit(solution)/shard_map/ppermute | solution.py:22
  70.9 1.7 %collective-permute-start.23 = (bf16[128,256]{1,0:T(8,128)(2,1)S(1)}, bf16[128,256]{1,0:T(8,128)(2,1)S(1)}, u32[]{:S(2)}, u32[]{:S(2)}) collective-permute-start(bf16[128,256]{1,0:T(8,128)(2,1)S(1)} %get-tuple-element.52.after_ref.refs_0_.refs_3_), channel_id=1, source_target_pairs={{0,2},{1,3},{2,0},{3,1},{4,6},{5,7},{6,4},{7,5},{8,10},{9,11},{10,... | collective-permute-start | bytes 196616 | tf_op jit(solution)/shard_map/ppermute | solution.py:22
  72.6 1.2 %collective-permute-start.22 = (bf16[128,256]{1,0:T(8,128)(2,1)S(1)}, bf16[128,256]{1,0:T(8,128)(2,1)S(1)}, u32[]{:S(2)}, u32[]{:S(2)}) collective-permute-start(bf16[128,256]{1,0:T(8,128)(2,1)S(1)} %get-tuple-element.52.after_ref.refs_0_.refs_3_), channel_id=1, source_target_pairs={{0,1},{1,0},{2,3},{3,2},{4,5},{5,4},{6,7},{7,6},{8,9},{9,8},{10,11... | collective-permute-start | bytes 196616 | tf_op jit(solution)/shard_map/ppermute | solution.py:22
  74.0 1.5 %collective-permute-done.24.refs_3_ = bf16[128,256]{1,0:T(8,128)(2,1)S(1)} collective-permute-done((bf16[128,256]{1,0:T(8,128)(2,1)S(1)}, bf16[128,256]{1,0:T(8,128)(2,1)S(1)}, u32[]{:S(2)}, u32[]{:S(2)}) %collective-permute-start.24) | collective-permute-done | bytes 65568 | tf_op jit(solution)/shard_map/ppermute | solution.py:22
  75.5 1.5 %collective-permute-done.23.refs_2_ = bf16[128,256]{1,0:T(8,128)(2,1)S(1)} collective-permute-done((bf16[128,256]{1,0:T(8,128)(2,1)S(1)}, bf16[128,256]{1,0:T(8,128)(2,1)S(1)}, u32[]{:S(2)}, u32[]{:S(2)}) %collective-permute-start.23) | collective-permute-done | bytes 65568 | tf_op jit(solution)/shard_map/ppermute | solution.py:22
  77.4 1.9 %collective-permute-start.25 = (bf16[128,256]{1,0:T(8,128)(2,1)S(1)}, bf16[128,256]{1,0:T(8,128)(2,1)S(1)}, u32[]{:S(2)}, u32[]{:S(2)}) collective-permute-start(bf16[128,256]{1,0:T(8,128)(2,1)S(1)} %get-tuple-element.53), channel_id=1, source_target_pairs={{0,24},{4,28},{8,16},{12,20},{16,8},{20,12},{24,0},{28,4},{1,25},{... | collective-permute-start | bytes 196616 | tf_op jit(solution)/shard_map/ppermute | solution.py:22
  79.4 1.6 %collective-permute-start.27 = (bf16[128,256]{1,0:T(8,128)(2,1)S(1)}, bf16[128,256]{1,0:T(8,128)(2,1)S(1)}, u32[]{:S(2)}, u32[]{:S(2)}) collective-permute-start(bf16[128,256]{1,0:T(8,128)(2,1)S(1)} %get-tuple-element.55), channel_id=1, source_target_pairs={{0,16},{4,20},{8,24},{12,28},{16,0},{20,4},{24,8},{28,12},{1,17},{... | collective-permute-start | bytes 196616 | tf_op jit(solution)/shard_map/ppermute | solution.py:22
  81.2 1.4 %collective-permute-done.25.refs_0_ = bf16[128,256]{1,0:T(8,128)(2,1)S(1)} collective-permute-done((bf16[128,256]{1,0:T(8,128)(2,1)S(1)}, bf16[128,256]{1,0:T(8,128)(2,1)S(1)}, u32[]{:S(2)}, u32[]{:S(2)}) %collective-permute-start.25) | collective-permute-done | bytes 65568 | tf_op jit(solution)/shard_map/ppermute | solution.py:22
  82.6 1.0 collective-permute-done.26.refs_1_
  83.8 2.0 %collective-permute-start.30 = (bf16[128,256]{1,0:T(8,128)(2,1)S(1)}, bf16[128,256]{1,0:T(8,128)(2,1)S(1)}, u32[]{:S(2)}, u32[]{:S(2)}) collective-permute-start(bf16[128,256]{1,0:T(8,128)(2,1)S(1)} %get-tuple-element.56.after_ref.refs_0_.refs_2_), channel_id=1, source_target_pairs={{0,3},{1,2},{2,1},{3,0},{4,7},{5,6},{6,5},{7,4},{8,11},{9,10},{10,... | collective-permute-start | bytes 196616 | tf_op jit(solution)/shard_map/ppermute | solution.py:22
  86.2 2.1 %collective-permute-start.28 = (bf16[128,256]{1,0:T(8,128)(2,1)S(1)}, bf16[128,256]{1,0:T(8,128)(2,1)S(1)}, u32[]{:S(2)}, u32[]{:S(2)}) collective-permute-start(bf16[128,256]{1,0:T(8,128)(2,1)S(1)} %get-tuple-element.56.after_ref.refs_0_.refs_2_), channel_id=1, source_target_pairs={{0,1},{1,0},{2,3},{3,2},{4,5},{5,4},{6,7},{7,6},{8,9},{9,8},{10,11... | collective-permute-start | bytes 196616 | tf_op jit(solution)/shard_map/ppermute | solution.py:22
  88.5 1.4 %collective-permute-done.30.refs_3_ = bf16[128,256]{1,0:T(8,128)(2,1)S(1)} collective-permute-done((bf16[128,256]{1,0:T(8,128)(2,1)S(1)}, bf16[128,256]{1,0:T(8,128)(2,1)S(1)}, u32[]{:S(2)}, u32[]{:S(2)}) %collective-permute-start.30) | collective-permute-done | bytes 65568 | tf_op jit(solution)/shard_map/ppermute | solution.py:22
  90.0 1.4 %collective-permute-done.29.refs_2_ = bf16[128,256]{1,0:T(8,128)(2,1)S(1)} collective-permute-done((bf16[128,256]{1,0:T(8,128)(2,1)S(1)}, bf16[128,256]{1,0:T(8,128)(2,1)S(1)}, u32[]{:S(2)}, u32[]{:S(2)}) %collective-permute-start.29) | collective-permute-done | bytes 65568 | tf_op jit(solution)/shard_map/ppermute | solution.py:22
  91.8 2.4 %collective-permute-start.31 = (bf16[128,256]{1,0:T(8,128)(2,1)S(1)}, bf16[128,256]{1,0:T(8,128)(2,1)S(1)}, u32[]{:S(2)}, u32[]{:S(2)}) collective-permute-start(bf16[128,256]{1,0:T(8,128)(2,1)S(1)} %get-tuple-element.57), channel_id=1, source_target_pairs={{0,24},{4,28},{8,16},{12,20},{16,8},{20,12},{24,0},{28,4},{1,25},{... | collective-permute-start | bytes 196616 | tf_op jit(solution)/shard_map/ppermute | solution.py:22
  95.7 1.4 %collective-permute-done.31.refs_0_ = bf16[128,256]{1,0:T(8,128)(2,1)S(1)} collective-permute-done((bf16[128,256]{1,0:T(8,128)(2,1)S(1)}, bf16[128,256]{1,0:T(8,128)(2,1)S(1)}, u32[]{:S(2)}, u32[]{:S(2)}) %collective-permute-start.31) | collective-permute-done | bytes 65568 | tf_op jit(solution)/shard_map/ppermute | solution.py:22
  97.0 1.4 %collective-permute-done.32.refs_1_ = bf16[128,256]{1,0:T(8,128)(2,1)S(1)} collective-permute-done((bf16[128,256]{1,0:T(8,128)(2,1)S(1)}, bf16[128,256]{1,0:T(8,128)(2,1)S(1)}, u32[]{:S(2)}, u32[]{:S(2)}) %collective-permute-start.32) | collective-permute-done | bytes 65568 | tf_op jit(solution)/shard_map/ppermute | solution.py:22
  99.4 2.1 %collective-permute-start.36 = (bf16[128,256]{1,0:T(8,128)(2,1)S(1)}, bf16[128,256]{1,0:T(8,128)(2,1)S(1)}, u32[]{:S(2)}, u32[]{:S(2)}) collective-permute-start(bf16[128,256]{1,0:T(8,128)(2,1)S(1)} %get-tuple-element.60.after_ref.refs_0_.refs_1_), channel_id=1, source_target_pairs={{0,3},{1,2},{2,1},{3,0},{4,7},{5,6},{6,5},{7,4},{8,11},{9,10},{10,... | collective-permute-start | bytes 196616 | tf_op jit(solution)/shard_map/ppermute | solution.py:22
  102.1 1.7 %collective-permute-start.34 = (bf16[128,256]{1,0:T(8,128)(2,1)S(1)}, bf16[128,256]{1,0:T(8,128)(2,1)S(1)}, u32[]{:S(2)}, u32[]{:S(2)}) collective-permute-start(bf16[128,256]{1,0:T(8,128)(2,1)S(1)} %get-tuple-element.60.after_ref.refs_0_.refs_1_), channel_id=1, source_target_pairs={{0,1},{1,0},{2,3},{3,2},{4,5},{5,4},{6,7},{7,6},{8,9},{9,8},{10,11... | collective-permute-start | bytes 196616 | tf_op jit(solution)/shard_map/ppermute | solution.py:22
  104.1 1.4 %collective-permute-done.36.refs_3_ = bf16[128,256]{1,0:T(8,128)(2,1)S(1)} collective-permute-done((bf16[128,256]{1,0:T(8,128)(2,1)S(1)}, bf16[128,256]{1,0:T(8,128)(2,1)S(1)}, u32[]{:S(2)}, u32[]{:S(2)}) %collective-permute-start.36) | collective-permute-done | bytes 65568 | tf_op jit(solution)/shard_map/ppermute | solution.py:22
  105.5 1.6 %collective-permute-done.35.refs_2_ = bf16[128,256]{1,0:T(8,128)(2,1)S(1)} collective-permute-done((bf16[128,256]{1,0:T(8,128)(2,1)S(1)}, bf16[128,256]{1,0:T(8,128)(2,1)S(1)}, u32[]{:S(2)}, u32[]{:S(2)}) %collective-permute-start.35) | collective-permute-done | bytes 65568 | tf_op jit(solution)/shard_map/ppermute | solution.py:22
  107.5 1.9 %collective-permute-start.37 = (bf16[128,256]{1,0:T(8,128)(2,1)S(1)}, bf16[128,256]{1,0:T(8,128)(2,1)S(1)}, u32[]{:S(2)}, u32[]{:S(2)}) collective-permute-start(bf16[128,256]{1,0:T(8,128)(2,1)S(1)} %get-tuple-element.61), channel_id=1, source_target_pairs={{0,24},{4,28},{8,16},{12,20},{16,8},{20,12},{24,0},{28,4},{1,25},{... | collective-permute-start | bytes 196616 | tf_op jit(solution)/shard_map/ppermute | solution.py:22
  109.5 1.6 %collective-permute-start.39 = (bf16[128,256]{1,0:T(8,128)(2,1)S(1)}, bf16[128,256]{1,0:T(8,128)(2,1)S(1)}, u32[]{:S(2)}, u32[]{:S(2)}) collective-permute-start(bf16[128,256]{1,0:T(8,128)(2,1)S(1)} %get-tuple-element.63), channel_id=1, source_target_pairs={{0,16},{4,20},{8,24},{12,28},{16,0},{20,4},{24,8},{28,12},{1,17},{... | collective-permute-start | bytes 196616 | tf_op jit(solution)/shard_map/ppermute | solution.py:22
  112.8 0.9 collective-permute-done.38.refs_1_
  (86 shorter events, 26.1 us)
Async XLA Ops:
  0.0 14.0 %collective-permute-start = (bf16[4,128,128]{2,1,0:T(8,128)(2,1)}, bf16[4,128,128]{2,1,0:T(8,128)(2,1)S(1)}, u32[]{:S(2)}, u32[]{:S(2)}) collective-permute-start(bf16[4,128,128]{2,1,0:T(8,128)(2,1)} %bitcast.33), channel_id=1, source_target_pairs={{0,4},{4,0},{8,12},{12,8},{16,20},{20,16},{24,28},{28,24},{1,5},{5... | collective-permute-start | bytes 393224 | tf_op jit(solution)/shard_map/ppermute | solution.py:22
  2.8 18.0 %all-to-all-start = ((bf16[32,40,128]{2,1,0:T(8,128)(2,1)}), bf16[32,40,128]{2,1,0:T(8,128)(2,1)S(1)}, u32[]{:S(2)}, u32[]{:S(2)}) async-start(bf16[32,40,128]{2,1,0:T(8,128)(2,1)} %shard_map.55), calls=%async_computation | async-start | bytes 655360 | tf_op jit(solution)/shard_map/all_to_all | solution.py:320
  13.5 7.2 %copy-start = (bf16[4,1,128,128]{3,2,1,0:T(8,128)(2,1)S(1)}, bf16[4,1,128,128]{3,2,1,0:T(8,128)(2,1)}, u32[]{:S(2)}) copy-start(bf16[4,1,128,128]{3,2,1,0:T(8,128)(2,1)} %param.7) | copy-start | bytes 393220
  20.7 5.1 %copy-start.1 = (bf16[1,1,4,128,1,8,128]{6,5,4,3,2,1,0:T(8,128)(2,1)S(1)}, bf16[1,1,4,128,1,8,128]{6,5,4,3,2,1,0:T(8,128)(2,1)}, u32[]{:S(2)}) copy-start(bf16[1,1,4,128,1,8,128]{6,5,4,3,2,1,0:T(8,128)(2,1)} %get-tuple-element.71) | copy-start | bytes 3145732
  21.2 4.9 %collective-permute-start.1 = (bf16[512,1024]{1,0:T(8,128)(2,1)S(1)}, bf16[512,1024]{1,0:T(8,128)(2,1)S(1)}, u32[]{:S(2)}, u32[]{:S(2)}) collective-permute-start(bf16[512,1024]{1,0:T(8,128)(2,1)S(1)} %bitcast_multiply_fusion.2.own_ref), channel_id=1, source_target_pairs={{0,4},{4,0},{8,12},{12,8},{16,20},{20,16},{24,28},{28,24},{1,5},{5... | collective-permute-start | bytes 3145736 | tf_op jit(solution)/shard_map/ppermute | solution.py:22
  22.1 5.7 %collective-permute-start.4 = (bf16[128,256]{1,0:T(8,128)(2,1)S(1)}, bf16[128,256]{1,0:T(8,128)(2,1)S(1)}, u32[]{:S(2)}, u32[]{:S(2)}) collective-permute-start(bf16[128,256]{1,0:T(8,128)(2,1)S(1)} %shard_map.56.after_ref.refs_0_.solved_ref), channel_id=1, source_target_pairs={{0,24},{4,28},{8,16},{12,20},{16,8},{20,12},{24,0},{28,4},{1,25},{... | collective-permute-start | bytes 196616 | tf_op jit(solution)/shard_map/ppermute | solution.py:22
  23.2 5.3 %collective-permute-start.3 = (bf16[128,256]{1,0:T(8,128)(2,1)S(1)}, bf16[128,256]{1,0:T(8,128)(2,1)S(1)}, u32[]{:S(2)}, u32[]{:S(2)}) collective-permute-start(bf16[128,256]{1,0:T(8,128)(2,1)S(1)} %shard_map.56.after_ref.refs_0_.solved_ref), channel_id=1, source_target_pairs={{0,16},{4,20},{8,24},{12,28},{16,0},{20,4},{24,8},{28,12},{1,17},{... | collective-permute-start | bytes 196616 | tf_op jit(solution)/shard_map/ppermute | solution.py:22
  24.6 4.3 %collective-permute-start.2 = (bf16[128,256]{1,0:T(8,128)(2,1)S(1)}, bf16[128,256]{1,0:T(8,128)(2,1)S(1)}, u32[]{:S(2)}, u32[]{:S(2)}) collective-permute-start(bf16[128,256]{1,0:T(8,128)(2,1)S(1)} %shard_map.56.after_ref.refs_0_.solved_ref), channel_id=1, source_target_pairs={{0,8},{4,12},{8,0},{12,4},{16,24},{20,28},{24,16},{28,20},{1,9},{5... | collective-permute-start | bytes 196616 | tf_op jit(solution)/shard_map/ppermute | solution.py:22
  26.1 15.6 %collective-permute-start.8 = (bf16[512,1024]{1,0:T(8,128)(2,1)S(1)}, bf16[512,1024]{1,0:T(8,128)(2,1)S(1)}, u32[]{:S(2)}, u32[]{:S(2)}) collective-permute-start(bf16[512,1024]{1,0:T(8,128)(2,1)S(1)} %bitcast_multiply_fusion.1.own_ref), channel_id=1, source_target_pairs={{0,4},{4,0},{8,12},{12,8},{16,20},{20,16},{24,28},{28,24},{1,5},{5... | collective-permute-start | bytes 3145736 | tf_op jit(solution)/shard_map/ppermute | solution.py:22
  29.3 6.5 %collective-permute-start.5 = (bf16[128,256]{1,0:T(8,128)(2,1)S(1)}, bf16[128,256]{1,0:T(8,128)(2,1)S(1)}, u32[]{:S(2)}, u32[]{:S(2)}) collective-permute-start(bf16[128,256]{1,0:T(8,128)(2,1)S(1)} %get-tuple-element.39), channel_id=1, source_target_pairs={{0,3},{1,2},{2,1},{3,0},{4,7},{5,6},{6,5},{7,4},{8,11},{9,10},{10,... | collective-permute-start | bytes 196616 | tf_op jit(solution)/shard_map/ppermute | solution.py:22
  31.1 6.2 %collective-permute-start.6 = (bf16[128,256]{1,0:T(8,128)(2,1)S(1)}, bf16[128,256]{1,0:T(8,128)(2,1)S(1)}, u32[]{:S(2)}, u32[]{:S(2)}) collective-permute-start(bf16[128,256]{1,0:T(8,128)(2,1)S(1)} %get-tuple-element.40), channel_id=1, source_target_pairs={{0,1},{1,0},{2,3},{3,2},{4,5},{5,4},{6,7},{7,6},{8,9},{9,8},{10,11... | collective-permute-start | bytes 196616 | tf_op jit(solution)/shard_map/ppermute | solution.py:22
  31.1 6.8 %collective-permute-start.7 = (bf16[128,256]{1,0:T(8,128)(2,1)S(1)}, bf16[128,256]{1,0:T(8,128)(2,1)S(1)}, u32[]{:S(2)}, u32[]{:S(2)}) collective-permute-start(bf16[128,256]{1,0:T(8,128)(2,1)S(1)} %get-tuple-element.41), channel_id=1, source_target_pairs={{0,2},{1,3},{2,0},{3,1},{4,6},{5,7},{6,4},{7,5},{8,10},{9,11},{10,... | collective-permute-start | bytes 196616 | tf_op jit(solution)/shard_map/ppermute | solution.py:22
  38.1 18.9 %collective-permute-start.15 = (bf16[512,1024]{1,0:T(8,128)(2,1)S(1)}, bf16[512,1024]{1,0:T(8,128)(2,1)S(1)}, u32[]{:S(2)}, u32[]{:S(2)}) collective-permute-start(bf16[512,1024]{1,0:T(8,128)(2,1)S(1)} %bitcast_multiply_fusion.own_ref), channel_id=1, source_target_pairs={{0,4},{4,0},{8,12},{12,8},{16,20},{20,16},{24,28},{28,24},{1,5},{5... | collective-permute-start | bytes 3145736 | tf_op jit(solution)/shard_map/ppermute | solution.py:22
  38.1 5.9 %collective-permute-start.11 = (bf16[128,256]{1,0:T(8,128)(2,1)S(1)}, bf16[128,256]{1,0:T(8,128)(2,1)S(1)}, u32[]{:S(2)}, u32[]{:S(2)}) collective-permute-start(bf16[128,256]{1,0:T(8,128)(2,1)S(1)} %shard_map.61.after_ref.refs_0_.solved_ref), channel_id=1, source_target_pairs={{0,24},{4,28},{8,16},{12,20},{16,8},{20,12},{24,0},{28,4},{1,25},{... | collective-permute-start | bytes 196616 | tf_op jit(solution)/shard_map/ppermute | solution.py:22
  38.7 6.2 %collective-permute-start.10 = (bf16[128,256]{1,0:T(8,128)(2,1)S(1)}, bf16[128,256]{1,0:T(8,128)(2,1)S(1)}, u32[]{:S(2)}, u32[]{:S(2)}) collective-permute-start(bf16[128,256]{1,0:T(8,128)(2,1)S(1)} %shard_map.61.after_ref.refs_0_.solved_ref), channel_id=1, source_target_pairs={{0,16},{4,20},{8,24},{12,28},{16,0},{20,4},{24,8},{28,12},{1,17},{... | collective-permute-start | bytes 196616 | tf_op jit(solution)/shard_map/ppermute | solution.py:22
  41.0 4.3 %collective-permute-start.9 = (bf16[128,256]{1,0:T(8,128)(2,1)S(1)}, bf16[128,256]{1,0:T(8,128)(2,1)S(1)}, u32[]{:S(2)}, u32[]{:S(2)}) collective-permute-start(bf16[128,256]{1,0:T(8,128)(2,1)S(1)} %shard_map.61.after_ref.refs_0_.solved_ref), channel_id=1, source_target_pairs={{0,8},{4,12},{8,0},{12,4},{16,24},{20,28},{24,16},{28,20},{1,9},{5... | collective-permute-start | bytes 196616 | tf_op jit(solution)/shard_map/ppermute | solution.py:22
  45.7 6.9 %collective-permute-start.12 = (bf16[128,256]{1,0:T(8,128)(2,1)S(1)}, bf16[128,256]{1,0:T(8,128)(2,1)S(1)}, u32[]{:S(2)}, u32[]{:S(2)}) collective-permute-start(bf16[128,256]{1,0:T(8,128)(2,1)S(1)} %get-tuple-element.44), channel_id=1, source_target_pairs={{0,3},{1,2},{2,1},{3,0},{4,7},{5,6},{6,5},{7,4},{8,11},{9,10},{10,... | collective-permute-start | bytes 196616 | tf_op jit(solution)/shard_map/ppermute | solution.py:22
  47.0 5.8 %collective-permute-start.13 = (bf16[128,256]{1,0:T(8,128)(2,1)S(1)}, bf16[128,256]{1,0:T(8,128)(2,1)S(1)}, u32[]{:S(2)}, u32[]{:S(2)}) collective-permute-start(bf16[128,256]{1,0:T(8,128)(2,1)S(1)} %get-tuple-element.45), channel_id=1, source_target_pairs={{0,1},{1,0},{2,3},{3,2},{4,5},{5,4},{6,7},{7,6},{8,9},{9,8},{10,11... | collective-permute-start | bytes 196616 | tf_op jit(solution)/shard_map/ppermute | solution.py:22
  47.1 6.2 %collective-permute-start.14 = (bf16[128,256]{1,0:T(8,128)(2,1)S(1)}, bf16[128,256]{1,0:T(8,128)(2,1)S(1)}, u32[]{:S(2)}, u32[]{:S(2)}) collective-permute-start(bf16[128,256]{1,0:T(8,128)(2,1)S(1)} %get-tuple-element.46), channel_id=1, source_target_pairs={{0,2},{1,3},{2,0},{3,1},{4,6},{5,7},{6,4},{7,5},{8,10},{9,11},{10,... | collective-permute-start | bytes 196616 | tf_op jit(solution)/shard_map/ppermute | solution.py:22
  53.4 5.8 %collective-permute-start.18 = (bf16[128,256]{1,0:T(8,128)(2,1)S(1)}, bf16[128,256]{1,0:T(8,128)(2,1)S(1)}, u32[]{:S(2)}, u32[]{:S(2)}) collective-permute-start(bf16[128,256]{1,0:T(8,128)(2,1)S(1)} %shard_map.65.after_ref.refs_0_.solved_ref), channel_id=1, source_target_pairs={{0,24},{4,28},{8,16},{12,20},{16,8},{20,12},{24,0},{28,4},{1,25},{... | collective-permute-start | bytes 196616 | tf_op jit(solution)/shard_map/ppermute | solution.py:22
  54.8 4.8 %collective-permute-start.17 = (bf16[128,256]{1,0:T(8,128)(2,1)S(1)}, bf16[128,256]{1,0:T(8,128)(2,1)S(1)}, u32[]{:S(2)}, u32[]{:S(2)}) collective-permute-start(bf16[128,256]{1,0:T(8,128)(2,1)S(1)} %shard_map.65.after_ref.refs_0_.solved_ref), channel_id=1, source_target_pairs={{0,16},{4,20},{8,24},{12,28},{16,0},{20,4},{24,8},{28,12},{1,17},{... | collective-permute-start | bytes 196616 | tf_op jit(solution)/shard_map/ppermute | solution.py:22
  56.3 4.3 %collective-permute-start.16 = (bf16[128,256]{1,0:T(8,128)(2,1)S(1)}, bf16[128,256]{1,0:T(8,128)(2,1)S(1)}, u32[]{:S(2)}, u32[]{:S(2)}) collective-permute-start(bf16[128,256]{1,0:T(8,128)(2,1)S(1)} %shard_map.65.after_ref.refs_0_.solved_ref), channel_id=1, source_target_pairs={{0,8},{4,12},{8,0},{12,4},{16,24},{20,28},{24,16},{28,20},{1,9},{5... | collective-permute-start | bytes 196616 | tf_op jit(solution)/shard_map/ppermute | solution.py:22
  61.0 6.2 %collective-permute-start.19 = (bf16[128,256]{1,0:T(8,128)(2,1)S(1)}, bf16[128,256]{1,0:T(8,128)(2,1)S(1)}, u32[]{:S(2)}, u32[]{:S(2)}) collective-permute-start(bf16[128,256]{1,0:T(8,128)(2,1)S(1)} %get-tuple-element.49), channel_id=1, source_target_pairs={{0,3},{1,2},{2,1},{3,0},{4,7},{5,6},{6,5},{7,4},{8,11},{9,10},{10,... | collective-permute-start | bytes 196616 | tf_op jit(solution)/shard_map/ppermute | solution.py:22
  63.0 4.9 %collective-permute-start.20 = (bf16[128,256]{1,0:T(8,128)(2,1)S(1)}, bf16[128,256]{1,0:T(8,128)(2,1)S(1)}, u32[]{:S(2)}, u32[]{:S(2)}) collective-permute-start(bf16[128,256]{1,0:T(8,128)(2,1)S(1)} %get-tuple-element.50), channel_id=1, source_target_pairs={{0,1},{1,0},{2,3},{3,2},{4,5},{5,4},{6,7},{7,6},{8,9},{9,8},{10,11... | collective-permute-start | bytes 196616 | tf_op jit(solution)/shard_map/ppermute | solution.py:22
  63.3 5.6 %collective-permute-start.21 = (bf16[128,256]{1,0:T(8,128)(2,1)S(1)}, bf16[128,256]{1,0:T(8,128)(2,1)S(1)}, u32[]{:S(2)}, u32[]{:S(2)}) collective-permute-start(bf16[128,256]{1,0:T(8,128)(2,1)S(1)} %get-tuple-element.51), channel_id=1, source_target_pairs={{0,2},{1,3},{2,0},{3,1},{4,6},{5,7},{6,4},{7,5},{8,10},{9,11},{10,... | collective-permute-start | bytes 196616 | tf_op jit(solution)/shard_map/ppermute | solution.py:22
  69.3 6.2 %collective-permute-start.24 = (bf16[128,256]{1,0:T(8,128)(2,1)S(1)}, bf16[128,256]{1,0:T(8,128)(2,1)S(1)}, u32[]{:S(2)}, u32[]{:S(2)}) collective-permute-start(bf16[128,256]{1,0:T(8,128)(2,1)S(1)} %get-tuple-element.52.after_ref.refs_0_.refs_3_), channel_id=1, source_target_pairs={{0,3},{1,2},{2,1},{3,0},{4,7},{5,6},{6,5},{7,4},{8,11},{9,10},{10,... | collective-permute-start | bytes 196616 | tf_op jit(solution)/shard_map/ppermute | solution.py:22
  70.9 6.1 %collective-permute-start.23 = (bf16[128,256]{1,0:T(8,128)(2,1)S(1)}, bf16[128,256]{1,0:T(8,128)(2,1)S(1)}, u32[]{:S(2)}, u32[]{:S(2)}) collective-permute-start(bf16[128,256]{1,0:T(8,128)(2,1)S(1)} %get-tuple-element.52.after_ref.refs_0_.refs_3_), channel_id=1, source_target_pairs={{0,2},{1,3},{2,0},{3,1},{4,6},{5,7},{6,4},{7,5},{8,10},{9,11},{10,... | collective-permute-start | bytes 196616 | tf_op jit(solution)/shard_map/ppermute | solution.py:22
  72.6 4.4 %collective-permute-start.22 = (bf16[128,256]{1,0:T(8,128)(2,1)S(1)}, bf16[128,256]{1,0:T(8,128)(2,1)S(1)}, u32[]{:S(2)}, u32[]{:S(2)}) collective-permute-start(bf16[128,256]{1,0:T(8,128)(2,1)S(1)} %get-tuple-element.52.after_ref.refs_0_.refs_3_), channel_id=1, source_target_pairs={{0,1},{1,0},{2,3},{3,2},{4,5},{5,4},{6,7},{7,6},{8,9},{9,8},{10,11... | collective-permute-start | bytes 196616 | tf_op jit(solution)/shard_map/ppermute | solution.py:22
  77.4 5.2 %collective-permute-start.25 = (bf16[128,256]{1,0:T(8,128)(2,1)S(1)}, bf16[128,256]{1,0:T(8,128)(2,1)S(1)}, u32[]{:S(2)}, u32[]{:S(2)}) collective-permute-start(bf16[128,256]{1,0:T(8,128)(2,1)S(1)} %get-tuple-element.53), channel_id=1, source_target_pairs={{0,24},{4,28},{8,16},{12,20},{16,8},{20,12},{24,0},{28,4},{1,25},{... | collective-permute-start | bytes 196616 | tf_op jit(solution)/shard_map/ppermute | solution.py:22
  79.4 4.3 %collective-permute-start.26 = (bf16[128,256]{1,0:T(8,128)(2,1)S(1)}, bf16[128,256]{1,0:T(8,128)(2,1)S(1)}, u32[]{:S(2)}, u32[]{:S(2)}) collective-permute-start(bf16[128,256]{1,0:T(8,128)(2,1)S(1)} %get-tuple-element.54), channel_id=1, source_target_pairs={{0,8},{4,12},{8,0},{12,4},{16,24},{20,28},{24,16},{28,20},{1,9},{5... | collective-permute-start | bytes 196616 | tf_op jit(solution)/shard_map/ppermute | solution.py:22
  79.4 4.3 %collective-permute-start.27 = (bf16[128,256]{1,0:T(8,128)(2,1)S(1)}, bf16[128,256]{1,0:T(8,128)(2,1)S(1)}, u32[]{:S(2)}, u32[]{:S(2)}) collective-permute-start(bf16[128,256]{1,0:T(8,128)(2,1)S(1)} %get-tuple-element.55), channel_id=1, source_target_pairs={{0,16},{4,20},{8,24},{12,28},{16,0},{20,4},{24,8},{28,12},{1,17},{... | collective-permute-start | bytes 196616 | tf_op jit(solution)/shard_map/ppermute | solution.py:22
  83.8 6.1 %collective-permute-start.30 = (bf16[128,256]{1,0:T(8,128)(2,1)S(1)}, bf16[128,256]{1,0:T(8,128)(2,1)S(1)}, u32[]{:S(2)}, u32[]{:S(2)}) collective-permute-start(bf16[128,256]{1,0:T(8,128)(2,1)S(1)} %get-tuple-element.56.after_ref.refs_0_.refs_2_), channel_id=1, source_target_pairs={{0,3},{1,2},{2,1},{3,0},{4,7},{5,6},{6,5},{7,4},{8,11},{9,10},{10,... | collective-permute-start | bytes 196616 | tf_op jit(solution)/shard_map/ppermute | solution.py:22
  85.8 5.5 %collective-permute-start.29 = (bf16[128,256]{1,0:T(8,128)(2,1)S(1)}, bf16[128,256]{1,0:T(8,128)(2,1)S(1)}, u32[]{:S(2)}, u32[]{:S(2)}) collective-permute-start(bf16[128,256]{1,0:T(8,128)(2,1)S(1)} %get-tuple-element.56.after_ref.refs_0_.refs_2_), channel_id=1, source_target_pairs={{0,2},{1,3},{2,0},{3,1},{4,6},{5,7},{6,4},{7,5},{8,10},{9,11},{10,... | collective-permute-start | bytes 196616 | tf_op jit(solution)/shard_map/ppermute | solution.py:22
  86.2 5.1 %collective-permute-start.28 = (bf16[128,256]{1,0:T(8,128)(2,1)S(1)}, bf16[128,256]{1,0:T(8,128)(2,1)S(1)}, u32[]{:S(2)}, u32[]{:S(2)}) collective-permute-start(bf16[128,256]{1,0:T(8,128)(2,1)S(1)} %get-tuple-element.56.after_ref.refs_0_.refs_2_), channel_id=1, source_target_pairs={{0,1},{1,0},{2,3},{3,2},{4,5},{5,4},{6,7},{7,6},{8,9},{9,8},{10,11... | collective-permute-start | bytes 196616 | tf_op jit(solution)/shard_map/ppermute | solution.py:22
  91.8 5.2 %collective-permute-start.31 = (bf16[128,256]{1,0:T(8,128)(2,1)S(1)}, bf16[128,256]{1,0:T(8,128)(2,1)S(1)}, u32[]{:S(2)}, u32[]{:S(2)}) collective-permute-start(bf16[128,256]{1,0:T(8,128)(2,1)S(1)} %get-tuple-element.57), channel_id=1, source_target_pairs={{0,24},{4,28},{8,16},{12,20},{16,8},{20,12},{24,0},{28,4},{1,25},{... | collective-permute-start | bytes 196616 | tf_op jit(solution)/shard_map/ppermute | solution.py:22
  94.2 4.3 %collective-permute-start.32 = (bf16[128,256]{1,0:T(8,128)(2,1)S(1)}, bf16[128,256]{1,0:T(8,128)(2,1)S(1)}, u32[]{:S(2)}, u32[]{:S(2)}) collective-permute-start(bf16[128,256]{1,0:T(8,128)(2,1)S(1)} %get-tuple-element.58), channel_id=1, source_target_pairs={{0,8},{4,12},{8,0},{12,4},{16,24},{20,28},{24,16},{28,20},{1,9},{5... | collective-permute-start | bytes 196616 | tf_op jit(solution)/shard_map/ppermute | solution.py:22
  94.9 4.3 %collective-permute-start.33 = (bf16[128,256]{1,0:T(8,128)(2,1)S(1)}, bf16[128,256]{1,0:T(8,128)(2,1)S(1)}, u32[]{:S(2)}, u32[]{:S(2)}) collective-permute-start(bf16[128,256]{1,0:T(8,128)(2,1)S(1)} %get-tuple-element.59), channel_id=1, source_target_pairs={{0,16},{4,20},{8,24},{12,28},{16,0},{20,4},{24,8},{28,12},{1,17},{... | collective-permute-start | bytes 196616 | tf_op jit(solution)/shard_map/ppermute | solution.py:22
  99.4 6.1 %collective-permute-start.36 = (bf16[128,256]{1,0:T(8,128)(2,1)S(1)}, bf16[128,256]{1,0:T(8,128)(2,1)S(1)}, u32[]{:S(2)}, u32[]{:S(2)}) collective-permute-start(bf16[128,256]{1,0:T(8,128)(2,1)S(1)} %get-tuple-element.60.after_ref.refs_0_.refs_1_), channel_id=1, source_target_pairs={{0,3},{1,2},{2,1},{3,0},{4,7},{5,6},{6,5},{7,4},{8,11},{9,10},{10,... | collective-permute-start | bytes 196616 | tf_op jit(solution)/shard_map/ppermute | solution.py:22
  101.5 5.6 %collective-permute-start.35 = (bf16[128,256]{1,0:T(8,128)(2,1)S(1)}, bf16[128,256]{1,0:T(8,128)(2,1)S(1)}, u32[]{:S(2)}, u32[]{:S(2)}) collective-permute-start(bf16[128,256]{1,0:T(8,128)(2,1)S(1)} %get-tuple-element.60.after_ref.refs_0_.refs_1_), channel_id=1, source_target_pairs={{0,2},{1,3},{2,0},{3,1},{4,6},{5,7},{6,4},{7,5},{8,10},{9,11},{10,... | collective-permute-start | bytes 196616 | tf_op jit(solution)/shard_map/ppermute | solution.py:22
  102.1 5.0 %collective-permute-start.34 = (bf16[128,256]{1,0:T(8,128)(2,1)S(1)}, bf16[128,256]{1,0:T(8,128)(2,1)S(1)}, u32[]{:S(2)}, u32[]{:S(2)}) collective-permute-start(bf16[128,256]{1,0:T(8,128)(2,1)S(1)} %get-tuple-element.60.after_ref.refs_0_.refs_1_), channel_id=1, source_target_pairs={{0,1},{1,0},{2,3},{3,2},{4,5},{5,4},{6,7},{7,6},{8,9},{9,8},{10,11... | collective-permute-start | bytes 196616 | tf_op jit(solution)/shard_map/ppermute | solution.py:22
  107.5 5.2 %collective-permute-start.37 = (bf16[128,256]{1,0:T(8,128)(2,1)S(1)}, bf16[128,256]{1,0:T(8,128)(2,1)S(1)}, u32[]{:S(2)}, u32[]{:S(2)}) collective-permute-start(bf16[128,256]{1,0:T(8,128)(2,1)S(1)} %get-tuple-element.61), channel_id=1, source_target_pairs={{0,24},{4,28},{8,16},{12,20},{16,8},{20,12},{24,0},{28,4},{1,25},{... | collective-permute-start | bytes 196616 | tf_op jit(solution)/shard_map/ppermute | solution.py:22
  109.4 4.3 %collective-permute-start.38 = (bf16[128,256]{1,0:T(8,128)(2,1)S(1)}, bf16[128,256]{1,0:T(8,128)(2,1)S(1)}, u32[]{:S(2)}, u32[]{:S(2)}) collective-permute-start(bf16[128,256]{1,0:T(8,128)(2,1)S(1)} %get-tuple-element.62), channel_id=1, source_target_pairs={{0,8},{4,12},{8,0},{12,4},{16,24},{20,28},{24,16},{28,20},{1,9},{5... | collective-permute-start | bytes 196616 | tf_op jit(solution)/shard_map/ppermute | solution.py:22
  109.5 4.3 %collective-permute-start.39 = (bf16[128,256]{1,0:T(8,128)(2,1)S(1)}, bf16[128,256]{1,0:T(8,128)(2,1)S(1)}, u32[]{:S(2)}, u32[]{:S(2)}) collective-permute-start(bf16[128,256]{1,0:T(8,128)(2,1)S(1)} %get-tuple-element.63), channel_id=1, source_target_pairs={{0,16},{4,20},{8,24},{12,28},{16,0},{20,4},{24,8},{28,12},{1,17},{... | collective-permute-start | bytes 196616 | tf_op jit(solution)/shard_map/ppermute | solution.py:22
  111.1 2.9 %collective-permute-start.42 = (bf16[128,128]{1,0:T(8,128)(2,1)S(1)}, bf16[128,128]{1,0:T(8,128)(2,1)S(1)}, u32[]{:S(2)}, u32[]{:S(2)}) collective-permute-start(bf16[128,128]{1,0:T(8,128)(2,1)S(1)} %get-tuple-element.67), channel_id=1, source_target_pairs={{0,4},{4,0},{8,12},{12,8},{16,20},{20,16},{24,28},{28,24},{1,5},{5... | collective-permute-start | bytes 98312 | tf_op jit(solution)/shard_map/ppermute | solution.py:22
  111.1 2.9 %collective-permute-start.41 = (bf16[128,128]{1,0:T(8,128)(2,1)S(1)}, bf16[128,128]{1,0:T(8,128)(2,1)S(1)}, u32[]{:S(2)}, u32[]{:S(2)}) collective-permute-start(bf16[128,128]{1,0:T(8,128)(2,1)S(1)} %get-tuple-element.66), channel_id=1, source_target_pairs={{0,4},{4,0},{8,12},{12,8},{16,20},{20,16},{24,28},{28,24},{1,5},{5... | collective-permute-start | bytes 98312 | tf_op jit(solution)/shard_map/ppermute | solution.py:22
  112.8 1.3 %collective-permute-start.40 = (bf16[128,128]{1,0:T(8,128)(2,1)S(1)}, bf16[128,128]{1,0:T(8,128)(2,1)S(1)}, u32[]{:S(2)}, u32[]{:S(2)}) collective-permute-start(bf16[128,128]{1,0:T(8,128)(2,1)S(1)} %get-tuple-element.65), channel_id=1, source_target_pairs={{0,4},{4,0},{8,12},{12,8},{16,20},{20,16},{24,28},{28,24},{1,5},{5... | collective-permute-start | bytes 98312 | tf_op jit(solution)/shard_map/ppermute | solution.py:22
  113.9 1.3 %collective-permute-start.43 = (bf16[128,128]{1,0:T(8,128)(2,1)S(1)}, bf16[128,128]{1,0:T(8,128)(2,1)S(1)}, u32[]{:S(2)}, u32[]{:S(2)}) collective-permute-start(bf16[128,128]{1,0:T(8,128)(2,1)S(1)} %get-tuple-element.68), channel_id=1, source_target_pairs={{0,4},{4,0},{8,12},{12,8},{16,20},{20,16},{24,28},{28,24},{1,5},{5... | collective-permute-start | bytes 98312 | tf_op jit(solution)/shard_map/ppermute | solution.py:22

commit v7 on v6

--- a/solution.py
+++ b/solution.py
@@ -173,7 +173,7 @@
     for first in range(0, shards, shards_per_line):
         ending = jnp.zeros((8, LANES), F32)
         for s in range(first, first + shards_per_line):
-            ending = ending + arrived_ref[s, chunk_rows:, :].astype(F32)[:8]
+            ending = ending + arrived_ref[s].astype(F32)[chunk_rows : chunk_rows + 8]
         where_to = (ending[0:1] * B + ending[1:2]).astype(jnp.int32)
         hots.append(jnp.where(place == where_to, 1.0, 0.0).astype(BF16))
     hot = jnp.concatenate(hots, axis=1)

time: 116 us -> 116 us (level)
  transfers between devices with their start and end apart: 45 -> 45, of which waited for: 33 -> 37; matrix products, arithmetic and copies ran while one was open for 4% -> 4% of each run, Pallas kernels for 8% -> 8%
where the time goes in v7:
time: 116 us
  starting transfers between devices  57 us (49%)
  waiting for transfers between devices  40.3 us (35%)
  Pallas kernels  13.1 us (11%)
  local copies, waits for them, and re-layouts  3.72 us (3%)
  other arithmetic  1.42 us (1%)
    ppermute x44, starting transfers between devices, swap(): return lax.ppermute(value, axis, [(i, i ^ distance) for i in range(count)])  50 us
    ppermute x44, waiting for transfers between devices, swap(): return lax.ppermute(value, axis, [(i, i ^ distance) for i in range(count)])  33.6 us
    pallas_call x22, Pallas kernels, call(): pl.pallas_call(body, out_shape=out_shape, in_specs=in_specs, out_specs=ou...  9.71 us
    all_to_all x1, starting transfers between devices, per_device(): lax.all_to_all(sending, ('row', 'col'), split_axis=0, concat_axis=0, tile...  6.97 us
    all_to_all x1, waiting for transfers between devices, per_device(): lax.all_to_all(sending, ('row', 'col'), split_axis=0, concat_axis=0, tile...  6.71 us
    slice x1, local copies, waits for them, and re-layouts, per_device(): tile = lower_blocks[level, 0, :, :, 0]  3.09 us
  transfers between devices with their start and end apart: 45, of which 37 were waited for; matrix products, arithmetic and copies ran while one was open for 4% of the time, Pallas kernels for 8%

profile of v7, /device:TPU:0, one launch (start us, length us, event | category | flops | bytes accessed | tf_op | source)
XLA Modules:
  0.0 115.9 jit_solution(3696867046835327596)
XLA Ops:
  0.5 2.3 %shard_map.55 = bf16[32,40,128]{2,1,0:T(8,128)(2,1)} custom-call(f32[512,256]{1,0:T(8,128)} %rhs_hbm.1, s32[1,512]{1,0:T(1,128)} %bitcast.48), custom_call_target="tpu_custom_call" | custom-call | flops 134217728 | bytes 526336 | tf_op jit(solution)/shard_map/pallas_call | solution.py:39
  2.8 7.0 %all-to-all-start = ((bf16[32,40,128]{2,1,0:T(8,128)(2,1)}), bf16[32,40,128]{2,1,0:T(8,128)(2,1)S(1)}, u32[]{:S(2)}, u32[]{:S(2)}) async-start(bf16[32,40,128]{2,1,0:T(8,128)(2,1)} %shard_map.55), calls=%async_computation | async-start | bytes 655360 | tf_op jit(solution)/shard_map/all_to_all | solution.py:320
  10.5 3.1 %fusion = (bf16[1,1,4,128,1,8,128]{6,5,4,3,2,1,0:T(8,128)(2,1)S(1)}, bf16[1,1,4,128,1,8,128]{6,5,4,3,2,1,0:T(8,128)(2,1)S(1)}, bf16[1,1,4,128,1,8,128]{6,5,4,3,2,1,0:T(8,128)(2,1)}) fusion(bf16[3,1,4,128,1,8,128]{6,5,4,3,2,1,0:T(8,128)(2,1)} %param.8), kind=kLoop, calls=%fused_computation.6 | loop fusion | bytes 6291456 | tf_op jit(solution)/shard_map/slice | solution.py:302
  14.0 6.7 %all-to-all-done.arrived_ref = bf16[32,40,128]{2,1,0:T(8,128)(2,1)S(1)} async-done(((bf16[32,40,128]{2,1,0:T(8,128)(2,1)}), bf16[32,40,128]{2,1,0:T(8,128)(2,1)S(1)}, u32[]{:S(2)}, u32[]{:S(2)}) %all-to-all-start) | async-done | bytes 327712 | tf_op jit(solution)/shard_map/all_to_all | solution.py:320
  21.2 0.9 collective-permute-start.1
  22.1 1.1 collective-permute-start.4
  23.2 1.5 %collective-permute-start.3 = (bf16[128,256]{1,0:T(8,128)(2,1)S(1)}, bf16[128,256]{1,0:T(8,128)(2,1)S(1)}, u32[]{:S(2)}, u32[]{:S(2)}) collective-permute-start(bf16[128,256]{1,0:T(8,128)(2,1)S(1)} %shard_map.56.after_ref.refs_0_.solved_ref), channel_id=1, source_target_pairs={{0,16},{4,20},{8,24},{12,28},{16,0},{20,4},{24,8},{28,12},{1,17},{... | collective-permute-start | bytes 196616 | tf_op jit(solution)/shard_map/ppermute | solution.py:22
  24.6 1.0 collective-permute-start.2
  26.8 0.9 collective-permute-done.4.refs_3_
  29.3 1.8 %collective-permute-start.5 = (bf16[128,256]{1,0:T(8,128)(2,1)S(1)}, bf16[128,256]{1,0:T(8,128)(2,1)S(1)}, u32[]{:S(2)}, u32[]{:S(2)}) collective-permute-start(bf16[128,256]{1,0:T(8,128)(2,1)S(1)} %get-tuple-element.39), channel_id=1, source_target_pairs={{0,3},{1,2},{2,1},{3,0},{4,7},{5,6},{6,5},{7,4},{8,11},{9,10},{10,... | collective-permute-start | bytes 196616 | tf_op jit(solution)/shard_map/ppermute | solution.py:22
  31.1 2.7 %collective-permute-start.7 = (bf16[128,256]{1,0:T(8,128)(2,1)S(1)}, bf16[128,256]{1,0:T(8,128)(2,1)S(1)}, u32[]{:S(2)}, u32[]{:S(2)}) collective-permute-start(bf16[128,256]{1,0:T(8,128)(2,1)S(1)} %get-tuple-element.41), channel_id=1, source_target_pairs={{0,2},{1,3},{2,0},{3,1},{4,6},{5,7},{6,4},{7,5},{8,10},{9,11},{10,... | collective-permute-start | bytes 196616 | tf_op jit(solution)/shard_map/ppermute | solution.py:22
  35.9 1.4 %collective-permute-done.6.refs_1_ = bf16[128,256]{1,0:T(8,128)(2,1)S(1)} collective-permute-done((bf16[128,256]{1,0:T(8,128)(2,1)S(1)}, bf16[128,256]{1,0:T(8,128)(2,1)S(1)}, u32[]{:S(2)}, u32[]{:S(2)}) %collective-permute-start.6) | collective-permute-done | bytes 65568 | tf_op jit(solution)/shard_map/ppermute | solution.py:22
  38.7 2.3 %collective-permute-start.10 = (bf16[128,256]{1,0:T(8,128)(2,1)S(1)}, bf16[128,256]{1,0:T(8,128)(2,1)S(1)}, u32[]{:S(2)}, u32[]{:S(2)}) collective-permute-start(bf16[128,256]{1,0:T(8,128)(2,1)S(1)} %shard_map.61.after_ref.refs_0_.solved_ref), channel_id=1, source_target_pairs={{0,16},{4,20},{8,24},{12,28},{16,0},{20,4},{24,8},{28,12},{1,17},{... | collective-permute-start | bytes 196616 | tf_op jit(solution)/shard_map/ppermute | solution.py:22
  42.4 1.6 %collective-permute-done.11.refs_3_ = bf16[128,256]{1,0:T(8,128)(2,1)S(1)} collective-permute-done((bf16[128,256]{1,0:T(8,128)(2,1)S(1)}, bf16[128,256]{1,0:T(8,128)(2,1)S(1)}, u32[]{:S(2)}, u32[]{:S(2)}) %collective-permute-start.11) | collective-permute-done | bytes 65568 | tf_op jit(solution)/shard_map/ppermute | solution.py:22
  45.7 1.2 %collective-permute-start.12 = (bf16[128,256]{1,0:T(8,128)(2,1)S(1)}, bf16[128,256]{1,0:T(8,128)(2,1)S(1)}, u32[]{:S(2)}, u32[]{:S(2)}) collective-permute-start(bf16[128,256]{1,0:T(8,128)(2,1)S(1)} %get-tuple-element.44), channel_id=1, source_target_pairs={{0,3},{1,2},{2,1},{3,0},{4,7},{5,6},{6,5},{7,4},{8,11},{9,10},{10,... | collective-permute-start | bytes 196616 | tf_op jit(solution)/shard_map/ppermute | solution.py:22
  47.1 3.1 %collective-permute-start.14 = (bf16[128,256]{1,0:T(8,128)(2,1)S(1)}, bf16[128,256]{1,0:T(8,128)(2,1)S(1)}, u32[]{:S(2)}, u32[]{:S(2)}) collective-permute-start(bf16[128,256]{1,0:T(8,128)(2,1)S(1)} %get-tuple-element.46), channel_id=1, source_target_pairs={{0,2},{1,3},{2,0},{3,1},{4,6},{5,7},{6,4},{7,5},{8,10},{9,11},{10,... | collective-permute-start | bytes 196616 | tf_op jit(solution)/shard_map/ppermute | solution.py:22
  50.5 2.1 %collective-permute-done.12.refs_0_ = bf16[128,256]{1,0:T(8,128)(2,1)S(1)} collective-permute-done((bf16[128,256]{1,0:T(8,128)(2,1)S(1)}, bf16[128,256]{1,0:T(8,128)(2,1)S(1)}, u32[]{:S(2)}, u32[]{:S(2)}) %collective-permute-start.12) | collective-permute-done | bytes 65568 | tf_op jit(solution)/shard_map/ppermute | solution.py:22
  53.4 1.4 %collective-permute-start.18 = (bf16[128,256]{1,0:T(8,128)(2,1)S(1)}, bf16[128,256]{1,0:T(8,128)(2,1)S(1)}, u32[]{:S(2)}, u32[]{:S(2)}) collective-permute-start(bf16[128,256]{1,0:T(8,128)(2,1)S(1)} %shard_map.65.after_ref.refs_0_.solved_ref), channel_id=1, source_target_pairs={{0,24},{4,28},{8,16},{12,20},{16,8},{20,12},{24,0},{28,4},{1,25},{... | collective-permute-start | bytes 196616 | tf_op jit(solution)/shard_map/ppermute | solution.py:22
  54.8 1.5 %collective-permute-start.17 = (bf16[128,256]{1,0:T(8,128)(2,1)S(1)}, bf16[128,256]{1,0:T(8,128)(2,1)S(1)}, u32[]{:S(2)}, u32[]{:S(2)}) collective-permute-start(bf16[128,256]{1,0:T(8,128)(2,1)S(1)} %shard_map.65.after_ref.refs_0_.solved_ref), channel_id=1, source_target_pairs={{0,16},{4,20},{8,24},{12,28},{16,0},{20,4},{24,8},{28,12},{1,17},{... | collective-permute-start | bytes 196616 | tf_op jit(solution)/shard_map/ppermute | solution.py:22
  57.7 1.3 %collective-permute-done.18.refs_3_ = bf16[128,256]{1,0:T(8,128)(2,1)S(1)} collective-permute-done((bf16[128,256]{1,0:T(8,128)(2,1)S(1)}, bf16[128,256]{1,0:T(8,128)(2,1)S(1)}, u32[]{:S(2)}, u32[]{:S(2)}) %collective-permute-start.18) | collective-permute-done | bytes 65568 | tf_op jit(solution)/shard_map/ppermute | solution.py:22
  59.5 1.0 collective-permute-done.16.refs_1_
  61.0 2.0 %collective-permute-start.19 = (bf16[128,256]{1,0:T(8,128)(2,1)S(1)}, bf16[128,256]{1,0:T(8,128)(2,1)S(1)}, u32[]{:S(2)}, u32[]{:S(2)}) collective-permute-start(bf16[128,256]{1,0:T(8,128)(2,1)S(1)} %get-tuple-element.49), channel_id=1, source_target_pairs={{0,3},{1,2},{2,1},{3,0},{4,7},{5,6},{6,5},{7,4},{8,11},{9,10},{10,... | collective-permute-start | bytes 196616 | tf_op jit(solution)/shard_map/ppermute | solution.py:22
  63.3 2.1 %collective-permute-start.21 = (bf16[128,256]{1,0:T(8,128)(2,1)S(1)}, bf16[128,256]{1,0:T(8,128)(2,1)S(1)}, u32[]{:S(2)}, u32[]{:S(2)}) collective-permute-start(bf16[128,256]{1,0:T(8,128)(2,1)S(1)} %get-tuple-element.51), channel_id=1, source_target_pairs={{0,2},{1,3},{2,0},{3,1},{4,6},{5,7},{6,4},{7,5},{8,10},{9,11},{10,... | collective-permute-start | bytes 196616 | tf_op jit(solution)/shard_map/ppermute | solution.py:22
  65.7 1.5 %collective-permute-done.19.refs_0_ = bf16[128,256]{1,0:T(8,128)(2,1)S(1)} collective-permute-done((bf16[128,256]{1,0:T(8,128)(2,1)S(1)}, bf16[128,256]{1,0:T(8,128)(2,1)S(1)}, u32[]{:S(2)}, u32[]{:S(2)}) %collective-permute-start.19) | collective-permute-done | bytes 65568 | tf_op jit(solution)/shard_map/ppermute | solution.py:22
  67.8 1.1 collective-permute-done.21.refs_2_
  69.3 1.6 %collective-permute-start.24 = (bf16[128,256]{1,0:T(8,128)(2,1)S(1)}, bf16[128,256]{1,0:T(8,128)(2,1)S(1)}, u32[]{:S(2)}, u32[]{:S(2)}) collective-permute-start(bf16[128,256]{1,0:T(8,128)(2,1)S(1)} %get-tuple-element.52.after_ref.refs_0_.refs_3_), channel_id=1, source_target_pairs={{0,3},{1,2},{2,1},{3,0},{4,7},{5,6},{6,5},{7,4},{8,11},{9,10},{10,... | collective-permute-start | bytes 196616 | tf_op jit(solution)/shard_map/ppermute | solution.py:22
  70.9 1.7 %collective-permute-start.23 = (bf16[128,256]{1,0:T(8,128)(2,1)S(1)}, bf16[128,256]{1,0:T(8,128)(2,1)S(1)}, u32[]{:S(2)}, u32[]{:S(2)}) collective-permute-start(bf16[128,256]{1,0:T(8,128)(2,1)S(1)} %get-tuple-element.52.after_ref.refs_0_.refs_3_), channel_id=1, source_target_pairs={{0,2},{1,3},{2,0},{3,1},{4,6},{5,7},{6,4},{7,5},{8,10},{9,11},{10,... | collective-permute-start | bytes 196616 | tf_op jit(solution)/shard_map/ppermute | solution.py:22
  72.6 1.1 collective-permute-start.22
  74.0 1.5 %collective-permute-done.24.refs_3_ = bf16[128,256]{1,0:T(8,128)(2,1)S(1)} collective-permute-done((bf16[128,256]{1,0:T(8,128)(2,1)S(1)}, bf16[128,256]{1,0:T(8,128)(2,1)S(1)}, u32[]{:S(2)}, u32[]{:S(2)}) %collective-permute-start.24) | collective-permute-done | bytes 65568 | tf_op jit(solution)/shard_map/ppermute | solution.py:22
  75.5 1.5 %collective-permute-done.23.refs_2_ = bf16[128,256]{1,0:T(8,128)(2,1)S(1)} collective-permute-done((bf16[128,256]{1,0:T(8,128)(2,1)S(1)}, bf16[128,256]{1,0:T(8,128)(2,1)S(1)}, u32[]{:S(2)}, u32[]{:S(2)}) %collective-permute-start.23) | collective-permute-done | bytes 65568 | tf_op jit(solution)/shard_map/ppermute | solution.py:22
  77.6 1.8 %collective-permute-start.25 = (bf16[128,256]{1,0:T(8,128)(2,1)S(1)}, bf16[128,256]{1,0:T(8,128)(2,1)S(1)}, u32[]{:S(2)}, u32[]{:S(2)}) collective-permute-start(bf16[128,256]{1,0:T(8,128)(2,1)S(1)} %get-tuple-element.53), channel_id=1, source_target_pairs={{0,24},{4,28},{8,16},{12,20},{16,8},{20,12},{24,0},{28,4},{1,25},{... | collective-permute-start | bytes 196616 | tf_op jit(solution)/shard_map/ppermute | solution.py:22
  79.4 1.7 %collective-permute-start.27 = (bf16[128,256]{1,0:T(8,128)(2,1)S(1)}, bf16[128,256]{1,0:T(8,128)(2,1)S(1)}, u32[]{:S(2)}, u32[]{:S(2)}) collective-permute-start(bf16[128,256]{1,0:T(8,128)(2,1)S(1)} %get-tuple-element.55), channel_id=1, source_target_pairs={{0,16},{4,20},{8,24},{12,28},{16,0},{20,4},{24,8},{28,12},{1,17},{... | collective-permute-start | bytes 196616 | tf_op jit(solution)/shard_map/ppermute | solution.py:22
  81.4 1.4 %collective-permute-done.25.refs_0_ = bf16[128,256]{1,0:T(8,128)(2,1)S(1)} collective-permute-done((bf16[128,256]{1,0:T(8,128)(2,1)S(1)}, bf16[128,256]{1,0:T(8,128)(2,1)S(1)}, u32[]{:S(2)}, u32[]{:S(2)}) %collective-permute-start.25) | collective-permute-done | bytes 65568 | tf_op jit(solution)/shard_map/ppermute | solution.py:22
  83.9 2.0 %collective-permute-start.30 = (bf16[128,256]{1,0:T(8,128)(2,1)S(1)}, bf16[128,256]{1,0:T(8,128)(2,1)S(1)}, u32[]{:S(2)}, u32[]{:S(2)}) collective-permute-start(bf16[128,256]{1,0:T(8,128)(2,1)S(1)} %get-tuple-element.56.after_ref.refs_0_.refs_2_), channel_id=1, source_target_pairs={{0,3},{1,2},{2,1},{3,0},{4,7},{5,6},{6,5},{7,4},{8,11},{9,10},{10,... | collective-permute-start | bytes 196616 | tf_op jit(solution)/shard_map/ppermute | solution.py:22
  86.2 2.1 %collective-permute-start.28 = (bf16[128,256]{1,0:T(8,128)(2,1)S(1)}, bf16[128,256]{1,0:T(8,128)(2,1)S(1)}, u32[]{:S(2)}, u32[]{:S(2)}) collective-permute-start(bf16[128,256]{1,0:T(8,128)(2,1)S(1)} %get-tuple-element.56.after_ref.refs_0_.refs_2_), channel_id=1, source_target_pairs={{0,1},{1,0},{2,3},{3,2},{4,5},{5,4},{6,7},{7,6},{8,9},{9,8},{10,11... | collective-permute-start | bytes 196616 | tf_op jit(solution)/shard_map/ppermute | solution.py:22
  88.6 1.4 %collective-permute-done.30.refs_3_ = bf16[128,256]{1,0:T(8,128)(2,1)S(1)} collective-permute-done((bf16[128,256]{1,0:T(8,128)(2,1)S(1)}, bf16[128,256]{1,0:T(8,128)(2,1)S(1)}, u32[]{:S(2)}, u32[]{:S(2)}) %collective-permute-start.30) | collective-permute-done | bytes 65568 | tf_op jit(solution)/shard_map/ppermute | solution.py:22
  90.0 1.4 %collective-permute-done.29.refs_2_ = bf16[128,256]{1,0:T(8,128)(2,1)S(1)} collective-permute-done((bf16[128,256]{1,0:T(8,128)(2,1)S(1)}, bf16[128,256]{1,0:T(8,128)(2,1)S(1)}, u32[]{:S(2)}, u32[]{:S(2)}) %collective-permute-start.29) | collective-permute-done | bytes 65568 | tf_op jit(solution)/shard_map/ppermute | solution.py:22
  91.8 2.4 %collective-permute-start.31 = (bf16[128,256]{1,0:T(8,128)(2,1)S(1)}, bf16[128,256]{1,0:T(8,128)(2,1)S(1)}, u32[]{:S(2)}, u32[]{:S(2)}) collective-permute-start(bf16[128,256]{1,0:T(8,128)(2,1)S(1)} %get-tuple-element.57), channel_id=1, source_target_pairs={{0,24},{4,28},{8,16},{12,20},{16,8},{20,12},{24,0},{28,4},{1,25},{... | collective-permute-start | bytes 196616 | tf_op jit(solution)/shard_map/ppermute | solution.py:22
  94.2 0.9 collective-permute-start.32
  95.7 1.4 %collective-permute-done.31.refs_0_ = bf16[128,256]{1,0:T(8,128)(2,1)S(1)} collective-permute-done((bf16[128,256]{1,0:T(8,128)(2,1)S(1)}, bf16[128,256]{1,0:T(8,128)(2,1)S(1)}, u32[]{:S(2)}, u32[]{:S(2)}) %collective-permute-start.31) | collective-permute-done | bytes 65568 | tf_op jit(solution)/shard_map/ppermute | solution.py:22
  97.1 1.4 %collective-permute-done.32.refs_1_ = bf16[128,256]{1,0:T(8,128)(2,1)S(1)} collective-permute-done((bf16[128,256]{1,0:T(8,128)(2,1)S(1)}, bf16[128,256]{1,0:T(8,128)(2,1)S(1)}, u32[]{:S(2)}, u32[]{:S(2)}) %collective-permute-start.32) | collective-permute-done | bytes 65568 | tf_op jit(solution)/shard_map/ppermute | solution.py:22
  99.5 2.0 %collective-permute-start.36 = (bf16[128,256]{1,0:T(8,128)(2,1)S(1)}, bf16[128,256]{1,0:T(8,128)(2,1)S(1)}, u32[]{:S(2)}, u32[]{:S(2)}) collective-permute-start(bf16[128,256]{1,0:T(8,128)(2,1)S(1)} %get-tuple-element.60.after_ref.refs_0_.refs_1_), channel_id=1, source_target_pairs={{0,3},{1,2},{2,1},{3,0},{4,7},{5,6},{6,5},{7,4},{8,11},{9,10},{10,... | collective-permute-start | bytes 196616 | tf_op jit(solution)/shard_map/ppermute | solution.py:22
  102.3 1.7 %collective-permute-start.34 = (bf16[128,256]{1,0:T(8,128)(2,1)S(1)}, bf16[128,256]{1,0:T(8,128)(2,1)S(1)}, u32[]{:S(2)}, u32[]{:S(2)}) collective-permute-start(bf16[128,256]{1,0:T(8,128)(2,1)S(1)} %get-tuple-element.60.after_ref.refs_0_.refs_1_), channel_id=1, source_target_pairs={{0,1},{1,0},{2,3},{3,2},{4,5},{5,4},{6,7},{7,6},{8,9},{9,8},{10,11... | collective-permute-start | bytes 196616 | tf_op jit(solution)/shard_map/ppermute | solution.py:22
  104.2 1.4 %collective-permute-done.36.refs_3_ = bf16[128,256]{1,0:T(8,128)(2,1)S(1)} collective-permute-done((bf16[128,256]{1,0:T(8,128)(2,1)S(1)}, bf16[128,256]{1,0:T(8,128)(2,1)S(1)}, u32[]{:S(2)}, u32[]{:S(2)}) %collective-permute-start.36) | collective-permute-done | bytes 65568 | tf_op jit(solution)/shard_map/ppermute | solution.py:22
  105.7 1.5 %collective-permute-done.35.refs_2_ = bf16[128,256]{1,0:T(8,128)(2,1)S(1)} collective-permute-done((bf16[128,256]{1,0:T(8,128)(2,1)S(1)}, bf16[128,256]{1,0:T(8,128)(2,1)S(1)}, u32[]{:S(2)}, u32[]{:S(2)}) %collective-permute-start.35) | collective-permute-done | bytes 65568 | tf_op jit(solution)/shard_map/ppermute | solution.py:22
  107.7 1.8 %collective-permute-start.37 = (bf16[128,256]{1,0:T(8,128)(2,1)S(1)}, bf16[128,256]{1,0:T(8,128)(2,1)S(1)}, u32[]{:S(2)}, u32[]{:S(2)}) collective-permute-start(bf16[128,256]{1,0:T(8,128)(2,1)S(1)} %get-tuple-element.61), channel_id=1, source_target_pairs={{0,24},{4,28},{8,16},{12,20},{16,8},{20,12},{24,0},{28,4},{1,25},{... | collective-permute-start | bytes 196616 | tf_op jit(solution)/shard_map/ppermute | solution.py:22
  109.5 1.7 %collective-permute-start.39 = (bf16[128,256]{1,0:T(8,128)(2,1)S(1)}, bf16[128,256]{1,0:T(8,128)(2,1)S(1)}, u32[]{:S(2)}, u32[]{:S(2)}) collective-permute-start(bf16[128,256]{1,0:T(8,128)(2,1)S(1)} %get-tuple-element.63), channel_id=1, source_target_pairs={{0,16},{4,20},{8,24},{12,28},{16,0},{20,4},{24,8},{28,12},{1,17},{... | collective-permute-start | bytes 196616 | tf_op jit(solution)/shard_map/ppermute | solution.py:22
  112.0 0.9 collective-permute-done.37.refs_0_
  (86 shorter events, 26.5 us)
Async XLA Ops:
  0.0 14.0 %collective-permute-start = (bf16[4,128,128]{2,1,0:T(8,128)(2,1)}, bf16[4,128,128]{2,1,0:T(8,128)(2,1)S(1)}, u32[]{:S(2)}, u32[]{:S(2)}) collective-permute-start(bf16[4,128,128]{2,1,0:T(8,128)(2,1)} %bitcast.33), channel_id=1, source_target_pairs={{0,4},{4,0},{8,12},{12,8},{16,20},{20,16},{24,28},{28,24},{1,5},{5... | collective-permute-start | bytes 393224 | tf_op jit(solution)/shard_map/ppermute | solution.py:22
  2.8 18.0 %all-to-all-start = ((bf16[32,40,128]{2,1,0:T(8,128)(2,1)}), bf16[32,40,128]{2,1,0:T(8,128)(2,1)S(1)}, u32[]{:S(2)}, u32[]{:S(2)}) async-start(bf16[32,40,128]{2,1,0:T(8,128)(2,1)} %shard_map.55), calls=%async_computation | async-start | bytes 655360 | tf_op jit(solution)/shard_map/all_to_all | solution.py:320
  13.5 7.2 %copy-start = (bf16[4,1,128,128]{3,2,1,0:T(8,128)(2,1)S(1)}, bf16[4,1,128,128]{3,2,1,0:T(8,128)(2,1)}, u32[]{:S(2)}) copy-start(bf16[4,1,128,128]{3,2,1,0:T(8,128)(2,1)} %param.7) | copy-start | bytes 393220
  20.7 5.1 %copy-start.1 = (bf16[1,1,4,128,1,8,128]{6,5,4,3,2,1,0:T(8,128)(2,1)S(1)}, bf16[1,1,4,128,1,8,128]{6,5,4,3,2,1,0:T(8,128)(2,1)}, u32[]{:S(2)}) copy-start(bf16[1,1,4,128,1,8,128]{6,5,4,3,2,1,0:T(8,128)(2,1)} %get-tuple-element.71) | copy-start | bytes 3145732
  21.2 4.9 %collective-permute-start.1 = (bf16[512,1024]{1,0:T(8,128)(2,1)S(1)}, bf16[512,1024]{1,0:T(8,128)(2,1)S(1)}, u32[]{:S(2)}, u32[]{:S(2)}) collective-permute-start(bf16[512,1024]{1,0:T(8,128)(2,1)S(1)} %bitcast_multiply_fusion.2.own_ref), channel_id=1, source_target_pairs={{0,4},{4,0},{8,12},{12,8},{16,20},{20,16},{24,28},{28,24},{1,5},{5... | collective-permute-start | bytes 3145736 | tf_op jit(solution)/shard_map/ppermute | solution.py:22
  22.1 5.7 %collective-permute-start.4 = (bf16[128,256]{1,0:T(8,128)(2,1)S(1)}, bf16[128,256]{1,0:T(8,128)(2,1)S(1)}, u32[]{:S(2)}, u32[]{:S(2)}) collective-permute-start(bf16[128,256]{1,0:T(8,128)(2,1)S(1)} %shard_map.56.after_ref.refs_0_.solved_ref), channel_id=1, source_target_pairs={{0,24},{4,28},{8,16},{12,20},{16,8},{20,12},{24,0},{28,4},{1,25},{... | collective-permute-start | bytes 196616 | tf_op jit(solution)/shard_map/ppermute | solution.py:22
  23.2 5.3 %collective-permute-start.3 = (bf16[128,256]{1,0:T(8,128)(2,1)S(1)}, bf16[128,256]{1,0:T(8,128)(2,1)S(1)}, u32[]{:S(2)}, u32[]{:S(2)}) collective-permute-start(bf16[128,256]{1,0:T(8,128)(2,1)S(1)} %shard_map.56.after_ref.refs_0_.solved_ref), channel_id=1, source_target_pairs={{0,16},{4,20},{8,24},{12,28},{16,0},{20,4},{24,8},{28,12},{1,17},{... | collective-permute-start | bytes 196616 | tf_op jit(solution)/shard_map/ppermute | solution.py:22
  24.6 4.3 %collective-permute-start.2 = (bf16[128,256]{1,0:T(8,128)(2,1)S(1)}, bf16[128,256]{1,0:T(8,128)(2,1)S(1)}, u32[]{:S(2)}, u32[]{:S(2)}) collective-permute-start(bf16[128,256]{1,0:T(8,128)(2,1)S(1)} %shard_map.56.after_ref.refs_0_.solved_ref), channel_id=1, source_target_pairs={{0,8},{4,12},{8,0},{12,4},{16,24},{20,28},{24,16},{28,20},{1,9},{5... | collective-permute-start | bytes 196616 | tf_op jit(solution)/shard_map/ppermute | solution.py:22
  26.1 15.6 %collective-permute-start.8 = (bf16[512,1024]{1,0:T(8,128)(2,1)S(1)}, bf16[512,1024]{1,0:T(8,128)(2,1)S(1)}, u32[]{:S(2)}, u32[]{:S(2)}) collective-permute-start(bf16[512,1024]{1,0:T(8,128)(2,1)S(1)} %bitcast_multiply_fusion.1.own_ref), channel_id=1, source_target_pairs={{0,4},{4,0},{8,12},{12,8},{16,20},{20,16},{24,28},{28,24},{1,5},{5... | collective-permute-start | bytes 3145736 | tf_op jit(solution)/shard_map/ppermute | solution.py:22
  29.3 6.6 %collective-permute-start.5 = (bf16[128,256]{1,0:T(8,128)(2,1)S(1)}, bf16[128,256]{1,0:T(8,128)(2,1)S(1)}, u32[]{:S(2)}, u32[]{:S(2)}) collective-permute-start(bf16[128,256]{1,0:T(8,128)(2,1)S(1)} %get-tuple-element.39), channel_id=1, source_target_pairs={{0,3},{1,2},{2,1},{3,0},{4,7},{5,6},{6,5},{7,4},{8,11},{9,10},{10,... | collective-permute-start | bytes 196616 | tf_op jit(solution)/shard_map/ppermute | solution.py:22
  31.1 6.2 %collective-permute-start.6 = (bf16[128,256]{1,0:T(8,128)(2,1)S(1)}, bf16[128,256]{1,0:T(8,128)(2,1)S(1)}, u32[]{:S(2)}, u32[]{:S(2)}) collective-permute-start(bf16[128,256]{1,0:T(8,128)(2,1)S(1)} %get-tuple-element.40), channel_id=1, source_target_pairs={{0,1},{1,0},{2,3},{3,2},{4,5},{5,4},{6,7},{7,6},{8,9},{9,8},{10,11... | collective-permute-start | bytes 196616 | tf_op jit(solution)/shard_map/ppermute | solution.py:22
  31.1 6.8 %collective-permute-start.7 = (bf16[128,256]{1,0:T(8,128)(2,1)S(1)}, bf16[128,256]{1,0:T(8,128)(2,1)S(1)}, u32[]{:S(2)}, u32[]{:S(2)}) collective-permute-start(bf16[128,256]{1,0:T(8,128)(2,1)S(1)} %get-tuple-element.41), channel_id=1, source_target_pairs={{0,2},{1,3},{2,0},{3,1},{4,6},{5,7},{6,4},{7,5},{8,10},{9,11},{10,... | collective-permute-start | bytes 196616 | tf_op jit(solution)/shard_map/ppermute | solution.py:22
  38.1 18.9 %collective-permute-start.15 = (bf16[512,1024]{1,0:T(8,128)(2,1)S(1)}, bf16[512,1024]{1,0:T(8,128)(2,1)S(1)}, u32[]{:S(2)}, u32[]{:S(2)}) collective-permute-start(bf16[512,1024]{1,0:T(8,128)(2,1)S(1)} %bitcast_multiply_fusion.own_ref), channel_id=1, source_target_pairs={{0,4},{4,0},{8,12},{12,8},{16,20},{20,16},{24,28},{28,24},{1,5},{5... | collective-permute-start | bytes 3145736 | tf_op jit(solution)/shard_map/ppermute | solution.py:22
  38.1 5.9 %collective-permute-start.11 = (bf16[128,256]{1,0:T(8,128)(2,1)S(1)}, bf16[128,256]{1,0:T(8,128)(2,1)S(1)}, u32[]{:S(2)}, u32[]{:S(2)}) collective-permute-start(bf16[128,256]{1,0:T(8,128)(2,1)S(1)} %shard_map.61.after_ref.refs_0_.solved_ref), channel_id=1, source_target_pairs={{0,24},{4,28},{8,16},{12,20},{16,8},{20,12},{24,0},{28,4},{1,25},{... | collective-permute-start | bytes 196616 | tf_op jit(solution)/shard_map/ppermute | solution.py:22
  38.7 6.2 %collective-permute-start.10 = (bf16[128,256]{1,0:T(8,128)(2,1)S(1)}, bf16[128,256]{1,0:T(8,128)(2,1)S(1)}, u32[]{:S(2)}, u32[]{:S(2)}) collective-permute-start(bf16[128,256]{1,0:T(8,128)(2,1)S(1)} %shard_map.61.after_ref.refs_0_.solved_ref), channel_id=1, source_target_pairs={{0,16},{4,20},{8,24},{12,28},{16,0},{20,4},{24,8},{28,12},{1,17},{... | collective-permute-start | bytes 196616 | tf_op jit(solution)/shard_map/ppermute | solution.py:22
  41.0 4.3 %collective-permute-start.9 = (bf16[128,256]{1,0:T(8,128)(2,1)S(1)}, bf16[128,256]{1,0:T(8,128)(2,1)S(1)}, u32[]{:S(2)}, u32[]{:S(2)}) collective-permute-start(bf16[128,256]{1,0:T(8,128)(2,1)S(1)} %shard_map.61.after_ref.refs_0_.solved_ref), channel_id=1, source_target_pairs={{0,8},{4,12},{8,0},{12,4},{16,24},{20,28},{24,16},{28,20},{1,9},{5... | collective-permute-start | bytes 196616 | tf_op jit(solution)/shard_map/ppermute | solution.py:22
  45.7 6.9 %collective-permute-start.12 = (bf16[128,256]{1,0:T(8,128)(2,1)S(1)}, bf16[128,256]{1,0:T(8,128)(2,1)S(1)}, u32[]{:S(2)}, u32[]{:S(2)}) collective-permute-start(bf16[128,256]{1,0:T(8,128)(2,1)S(1)} %get-tuple-element.44), channel_id=1, source_target_pairs={{0,3},{1,2},{2,1},{3,0},{4,7},{5,6},{6,5},{7,4},{8,11},{9,10},{10,... | collective-permute-start | bytes 196616 | tf_op jit(solution)/shard_map/ppermute | solution.py:22
  47.0 5.8 %collective-permute-start.13 = (bf16[128,256]{1,0:T(8,128)(2,1)S(1)}, bf16[128,256]{1,0:T(8,128)(2,1)S(1)}, u32[]{:S(2)}, u32[]{:S(2)}) collective-permute-start(bf16[128,256]{1,0:T(8,128)(2,1)S(1)} %get-tuple-element.45), channel_id=1, source_target_pairs={{0,1},{1,0},{2,3},{3,2},{4,5},{5,4},{6,7},{7,6},{8,9},{9,8},{10,11... | collective-permute-start | bytes 196616 | tf_op jit(solution)/shard_map/ppermute | solution.py:22
  47.1 6.2 %collective-permute-start.14 = (bf16[128,256]{1,0:T(8,128)(2,1)S(1)}, bf16[128,256]{1,0:T(8,128)(2,1)S(1)}, u32[]{:S(2)}, u32[]{:S(2)}) collective-permute-start(bf16[128,256]{1,0:T(8,128)(2,1)S(1)} %get-tuple-element.46), channel_id=1, source_target_pairs={{0,2},{1,3},{2,0},{3,1},{4,6},{5,7},{6,4},{7,5},{8,10},{9,11},{10,... | collective-permute-start | bytes 196616 | tf_op jit(solution)/shard_map/ppermute | solution.py:22
  53.4 5.6 %collective-permute-start.18 = (bf16[128,256]{1,0:T(8,128)(2,1)S(1)}, bf16[128,256]{1,0:T(8,128)(2,1)S(1)}, u32[]{:S(2)}, u32[]{:S(2)}) collective-permute-start(bf16[128,256]{1,0:T(8,128)(2,1)S(1)} %shard_map.65.after_ref.refs_0_.solved_ref), channel_id=1, source_target_pairs={{0,24},{4,28},{8,16},{12,20},{16,8},{20,12},{24,0},{28,4},{1,25},{... | collective-permute-start | bytes 196616 | tf_op jit(solution)/shard_map/ppermute | solution.py:22
  54.8 4.7 %collective-permute-start.17 = (bf16[128,256]{1,0:T(8,128)(2,1)S(1)}, bf16[128,256]{1,0:T(8,128)(2,1)S(1)}, u32[]{:S(2)}, u32[]{:S(2)}) collective-permute-start(bf16[128,256]{1,0:T(8,128)(2,1)S(1)} %shard_map.65.after_ref.refs_0_.solved_ref), channel_id=1, source_target_pairs={{0,16},{4,20},{8,24},{12,28},{16,0},{20,4},{24,8},{28,12},{1,17},{... | collective-permute-start | bytes 196616 | tf_op jit(solution)/shard_map/ppermute | solution.py:22
  56.3 4.3 %collective-permute-start.16 = (bf16[128,256]{1,0:T(8,128)(2,1)S(1)}, bf16[128,256]{1,0:T(8,128)(2,1)S(1)}, u32[]{:S(2)}, u32[]{:S(2)}) collective-permute-start(bf16[128,256]{1,0:T(8,128)(2,1)S(1)} %shard_map.65.after_ref.refs_0_.solved_ref), channel_id=1, source_target_pairs={{0,8},{4,12},{8,0},{12,4},{16,24},{20,28},{24,16},{28,20},{1,9},{5... | collective-permute-start | bytes 196616 | tf_op jit(solution)/shard_map/ppermute | solution.py:22
  61.0 6.2 %collective-permute-start.19 = (bf16[128,256]{1,0:T(8,128)(2,1)S(1)}, bf16[128,256]{1,0:T(8,128)(2,1)S(1)}, u32[]{:S(2)}, u32[]{:S(2)}) collective-permute-start(bf16[128,256]{1,0:T(8,128)(2,1)S(1)} %get-tuple-element.49), channel_id=1, source_target_pairs={{0,3},{1,2},{2,1},{3,0},{4,7},{5,6},{6,5},{7,4},{8,11},{9,10},{10,... | collective-permute-start | bytes 196616 | tf_op jit(solution)/shard_map/ppermute | solution.py:22
  63.0 4.9 %collective-permute-start.20 = (bf16[128,256]{1,0:T(8,128)(2,1)S(1)}, bf16[128,256]{1,0:T(8,128)(2,1)S(1)}, u32[]{:S(2)}, u32[]{:S(2)}) collective-permute-start(bf16[128,256]{1,0:T(8,128)(2,1)S(1)} %get-tuple-element.50), channel_id=1, source_target_pairs={{0,1},{1,0},{2,3},{3,2},{4,5},{5,4},{6,7},{7,6},{8,9},{9,8},{10,11... | collective-permute-start | bytes 196616 | tf_op jit(solution)/shard_map/ppermute | solution.py:22
  63.3 5.6 %collective-permute-start.21 = (bf16[128,256]{1,0:T(8,128)(2,1)S(1)}, bf16[128,256]{1,0:T(8,128)(2,1)S(1)}, u32[]{:S(2)}, u32[]{:S(2)}) collective-permute-start(bf16[128,256]{1,0:T(8,128)(2,1)S(1)} %get-tuple-element.51), channel_id=1, source_target_pairs={{0,2},{1,3},{2,0},{3,1},{4,6},{5,7},{6,4},{7,5},{8,10},{9,11},{10,... | collective-permute-start | bytes 196616 | tf_op jit(solution)/shard_map/ppermute | solution.py:22
  69.3 6.2 %collective-permute-start.24 = (bf16[128,256]{1,0:T(8,128)(2,1)S(1)}, bf16[128,256]{1,0:T(8,128)(2,1)S(1)}, u32[]{:S(2)}, u32[]{:S(2)}) collective-permute-start(bf16[128,256]{1,0:T(8,128)(2,1)S(1)} %get-tuple-element.52.after_ref.refs_0_.refs_3_), channel_id=1, source_target_pairs={{0,3},{1,2},{2,1},{3,0},{4,7},{5,6},{6,5},{7,4},{8,11},{9,10},{10,... | collective-permute-start | bytes 196616 | tf_op jit(solution)/shard_map/ppermute | solution.py:22
  70.9 6.2 %collective-permute-start.23 = (bf16[128,256]{1,0:T(8,128)(2,1)S(1)}, bf16[128,256]{1,0:T(8,128)(2,1)S(1)}, u32[]{:S(2)}, u32[]{:S(2)}) collective-permute-start(bf16[128,256]{1,0:T(8,128)(2,1)S(1)} %get-tuple-element.52.after_ref.refs_0_.refs_3_), channel_id=1, source_target_pairs={{0,2},{1,3},{2,0},{3,1},{4,6},{5,7},{6,4},{7,5},{8,10},{9,11},{10,... | collective-permute-start | bytes 196616 | tf_op jit(solution)/shard_map/ppermute | solution.py:22
  72.6 4.6 %collective-permute-start.22 = (bf16[128,256]{1,0:T(8,128)(2,1)S(1)}, bf16[128,256]{1,0:T(8,128)(2,1)S(1)}, u32[]{:S(2)}, u32[]{:S(2)}) collective-permute-start(bf16[128,256]{1,0:T(8,128)(2,1)S(1)} %get-tuple-element.52.after_ref.refs_0_.refs_3_), channel_id=1, source_target_pairs={{0,1},{1,0},{2,3},{3,2},{4,5},{5,4},{6,7},{7,6},{8,9},{9,8},{10,11... | collective-permute-start | bytes 196616 | tf_op jit(solution)/shard_map/ppermute | solution.py:22
  77.6 5.2 %collective-permute-start.25 = (bf16[128,256]{1,0:T(8,128)(2,1)S(1)}, bf16[128,256]{1,0:T(8,128)(2,1)S(1)}, u32[]{:S(2)}, u32[]{:S(2)}) collective-permute-start(bf16[128,256]{1,0:T(8,128)(2,1)S(1)} %get-tuple-element.53), channel_id=1, source_target_pairs={{0,24},{4,28},{8,16},{12,20},{16,8},{20,12},{24,0},{28,4},{1,25},{... | collective-permute-start | bytes 196616 | tf_op jit(solution)/shard_map/ppermute | solution.py:22
  79.4 4.3 %collective-permute-start.26 = (bf16[128,256]{1,0:T(8,128)(2,1)S(1)}, bf16[128,256]{1,0:T(8,128)(2,1)S(1)}, u32[]{:S(2)}, u32[]{:S(2)}) collective-permute-start(bf16[128,256]{1,0:T(8,128)(2,1)S(1)} %get-tuple-element.54), channel_id=1, source_target_pairs={{0,8},{4,12},{8,0},{12,4},{16,24},{20,28},{24,16},{28,20},{1,9},{5... | collective-permute-start | bytes 196616 | tf_op jit(solution)/shard_map/ppermute | solution.py:22
  79.4 4.3 %collective-permute-start.27 = (bf16[128,256]{1,0:T(8,128)(2,1)S(1)}, bf16[128,256]{1,0:T(8,128)(2,1)S(1)}, u32[]{:S(2)}, u32[]{:S(2)}) collective-permute-start(bf16[128,256]{1,0:T(8,128)(2,1)S(1)} %get-tuple-element.55), channel_id=1, source_target_pairs={{0,16},{4,20},{8,24},{12,28},{16,0},{20,4},{24,8},{28,12},{1,17},{... | collective-permute-start | bytes 196616 | tf_op jit(solution)/shard_map/ppermute | solution.py:22
  83.9 6.1 %collective-permute-start.30 = (bf16[128,256]{1,0:T(8,128)(2,1)S(1)}, bf16[128,256]{1,0:T(8,128)(2,1)S(1)}, u32[]{:S(2)}, u32[]{:S(2)}) collective-permute-start(bf16[128,256]{1,0:T(8,128)(2,1)S(1)} %get-tuple-element.56.after_ref.refs_0_.refs_2_), channel_id=1, source_target_pairs={{0,3},{1,2},{2,1},{3,0},{4,7},{5,6},{6,5},{7,4},{8,11},{9,10},{10,... | collective-permute-start | bytes 196616 | tf_op jit(solution)/shard_map/ppermute | solution.py:22
  85.9 5.5 %collective-permute-start.29 = (bf16[128,256]{1,0:T(8,128)(2,1)S(1)}, bf16[128,256]{1,0:T(8,128)(2,1)S(1)}, u32[]{:S(2)}, u32[]{:S(2)}) collective-permute-start(bf16[128,256]{1,0:T(8,128)(2,1)S(1)} %get-tuple-element.56.after_ref.refs_0_.refs_2_), channel_id=1, source_target_pairs={{0,2},{1,3},{2,0},{3,1},{4,6},{5,7},{6,4},{7,5},{8,10},{9,11},{10,... | collective-permute-start | bytes 196616 | tf_op jit(solution)/shard_map/ppermute | solution.py:22
  86.2 5.2 %collective-permute-start.28 = (bf16[128,256]{1,0:T(8,128)(2,1)S(1)}, bf16[128,256]{1,0:T(8,128)(2,1)S(1)}, u32[]{:S(2)}, u32[]{:S(2)}) collective-permute-start(bf16[128,256]{1,0:T(8,128)(2,1)S(1)} %get-tuple-element.56.after_ref.refs_0_.refs_2_), channel_id=1, source_target_pairs={{0,1},{1,0},{2,3},{3,2},{4,5},{5,4},{6,7},{7,6},{8,9},{9,8},{10,11... | collective-permute-start | bytes 196616 | tf_op jit(solution)/shard_map/ppermute | solution.py:22
  91.8 5.2 %collective-permute-start.31 = (bf16[128,256]{1,0:T(8,128)(2,1)S(1)}, bf16[128,256]{1,0:T(8,128)(2,1)S(1)}, u32[]{:S(2)}, u32[]{:S(2)}) collective-permute-start(bf16[128,256]{1,0:T(8,128)(2,1)S(1)} %get-tuple-element.57), channel_id=1, source_target_pairs={{0,24},{4,28},{8,16},{12,20},{16,8},{20,12},{24,0},{28,4},{1,25},{... | collective-permute-start | bytes 196616 | tf_op jit(solution)/shard_map/ppermute | solution.py:22
  94.2 4.3 %collective-permute-start.32 = (bf16[128,256]{1,0:T(8,128)(2,1)S(1)}, bf16[128,256]{1,0:T(8,128)(2,1)S(1)}, u32[]{:S(2)}, u32[]{:S(2)}) collective-permute-start(bf16[128,256]{1,0:T(8,128)(2,1)S(1)} %get-tuple-element.58), channel_id=1, source_target_pairs={{0,8},{4,12},{8,0},{12,4},{16,24},{20,28},{24,16},{28,20},{1,9},{5... | collective-permute-start | bytes 196616 | tf_op jit(solution)/shard_map/ppermute | solution.py:22
  95.1 4.3 %collective-permute-start.33 = (bf16[128,256]{1,0:T(8,128)(2,1)S(1)}, bf16[128,256]{1,0:T(8,128)(2,1)S(1)}, u32[]{:S(2)}, u32[]{:S(2)}) collective-permute-start(bf16[128,256]{1,0:T(8,128)(2,1)S(1)} %get-tuple-element.59), channel_id=1, source_target_pairs={{0,16},{4,20},{8,24},{12,28},{16,0},{20,4},{24,8},{28,12},{1,17},{... | collective-permute-start | bytes 196616 | tf_op jit(solution)/shard_map/ppermute | solution.py:22
  99.5 6.1 %collective-permute-start.36 = (bf16[128,256]{1,0:T(8,128)(2,1)S(1)}, bf16[128,256]{1,0:T(8,128)(2,1)S(1)}, u32[]{:S(2)}, u32[]{:S(2)}) collective-permute-start(bf16[128,256]{1,0:T(8,128)(2,1)S(1)} %get-tuple-element.60.after_ref.refs_0_.refs_1_), channel_id=1, source_target_pairs={{0,3},{1,2},{2,1},{3,0},{4,7},{5,6},{6,5},{7,4},{8,11},{9,10},{10,... | collective-permute-start | bytes 196616 | tf_op jit(solution)/shard_map/ppermute | solution.py:22
  101.5 5.7 %collective-permute-start.35 = (bf16[128,256]{1,0:T(8,128)(2,1)S(1)}, bf16[128,256]{1,0:T(8,128)(2,1)S(1)}, u32[]{:S(2)}, u32[]{:S(2)}) collective-permute-start(bf16[128,256]{1,0:T(8,128)(2,1)S(1)} %get-tuple-element.60.after_ref.refs_0_.refs_1_), channel_id=1, source_target_pairs={{0,2},{1,3},{2,0},{3,1},{4,6},{5,7},{6,4},{7,5},{8,10},{9,11},{10,... | collective-permute-start | bytes 196616 | tf_op jit(solution)/shard_map/ppermute | solution.py:22
  102.3 5.0 %collective-permute-start.34 = (bf16[128,256]{1,0:T(8,128)(2,1)S(1)}, bf16[128,256]{1,0:T(8,128)(2,1)S(1)}, u32[]{:S(2)}, u32[]{:S(2)}) collective-permute-start(bf16[128,256]{1,0:T(8,128)(2,1)S(1)} %get-tuple-element.60.after_ref.refs_0_.refs_1_), channel_id=1, source_target_pairs={{0,1},{1,0},{2,3},{3,2},{4,5},{5,4},{6,7},{7,6},{8,9},{9,8},{10,11... | collective-permute-start | bytes 196616 | tf_op jit(solution)/shard_map/ppermute | solution.py:22
  107.7 5.2 %collective-permute-start.37 = (bf16[128,256]{1,0:T(8,128)(2,1)S(1)}, bf16[128,256]{1,0:T(8,128)(2,1)S(1)}, u32[]{:S(2)}, u32[]{:S(2)}) collective-permute-start(bf16[128,256]{1,0:T(8,128)(2,1)S(1)} %get-tuple-element.61), channel_id=1, source_target_pairs={{0,24},{4,28},{8,16},{12,20},{16,8},{20,12},{24,0},{28,4},{1,25},{... | collective-permute-start | bytes 196616 | tf_op jit(solution)/shard_map/ppermute | solution.py:22
  109.4 4.3 %collective-permute-start.38 = (bf16[128,256]{1,0:T(8,128)(2,1)S(1)}, bf16[128,256]{1,0:T(8,128)(2,1)S(1)}, u32[]{:S(2)}, u32[]{:S(2)}) collective-permute-start(bf16[128,256]{1,0:T(8,128)(2,1)S(1)} %get-tuple-element.62), channel_id=1, source_target_pairs={{0,8},{4,12},{8,0},{12,4},{16,24},{20,28},{24,16},{28,20},{1,9},{5... | collective-permute-start | bytes 196616 | tf_op jit(solution)/shard_map/ppermute | solution.py:22
  109.5 4.3 %collective-permute-start.39 = (bf16[128,256]{1,0:T(8,128)(2,1)S(1)}, bf16[128,256]{1,0:T(8,128)(2,1)S(1)}, u32[]{:S(2)}, u32[]{:S(2)}) collective-permute-start(bf16[128,256]{1,0:T(8,128)(2,1)S(1)} %get-tuple-element.63), channel_id=1, source_target_pairs={{0,16},{4,20},{8,24},{12,28},{16,0},{20,4},{24,8},{28,12},{1,17},{... | collective-permute-start | bytes 196616 | tf_op jit(solution)/shard_map/ppermute | solution.py:22
  111.2 2.8 %collective-permute-start.42 = (bf16[128,128]{1,0:T(8,128)(2,1)S(1)}, bf16[128,128]{1,0:T(8,128)(2,1)S(1)}, u32[]{:S(2)}, u32[]{:S(2)}) collective-permute-start(bf16[128,128]{1,0:T(8,128)(2,1)S(1)} %get-tuple-element.67), channel_id=1, source_target_pairs={{0,4},{4,0},{8,12},{12,8},{16,20},{20,16},{24,28},{28,24},{1,5},{5... | collective-permute-start | bytes 98312 | tf_op jit(solution)/shard_map/ppermute | solution.py:22
  111.2 2.8 %collective-permute-start.41 = (bf16[128,128]{1,0:T(8,128)(2,1)S(1)}, bf16[128,128]{1,0:T(8,128)(2,1)S(1)}, u32[]{:S(2)}, u32[]{:S(2)}) collective-permute-start(bf16[128,128]{1,0:T(8,128)(2,1)S(1)} %get-tuple-element.66), channel_id=1, source_target_pairs={{0,4},{4,0},{8,12},{12,8},{16,20},{20,16},{24,28},{28,24},{1,5},{5... | collective-permute-start | bytes 98312 | tf_op jit(solution)/shard_map/ppermute | solution.py:22
  112.9 1.2 %collective-permute-start.40 = (bf16[128,128]{1,0:T(8,128)(2,1)S(1)}, bf16[128,128]{1,0:T(8,128)(2,1)S(1)}, u32[]{:S(2)}, u32[]{:S(2)}) collective-permute-start(bf16[128,128]{1,0:T(8,128)(2,1)S(1)} %get-tuple-element.65), channel_id=1, source_target_pairs={{0,4},{4,0},{8,12},{12,8},{16,20},{20,16},{24,28},{28,24},{1,5},{5... | collective-permute-start | bytes 98312 | tf_op jit(solution)/shard_map/ppermute | solution.py:22
  113.9 1.3 %collective-permute-start.43 = (bf16[128,128]{1,0:T(8,128)(2,1)S(1)}, bf16[128,128]{1,0:T(8,128)(2,1)S(1)}, u32[]{:S(2)}, u32[]{:S(2)}) collective-permute-start(bf16[128,128]{1,0:T(8,128)(2,1)S(1)} %get-tuple-element.68), channel_id=1, source_target_pairs={{0,4},{4,0},{8,12},{12,8},{16,20},{20,16},{24,28},{28,24},{1,5},{5... | collective-permute-start | bytes 98312 | tf_op jit(solution)/shard_map/ppermute | solution.py:22

commit v8 on v7

--- a/solution.py
+++ b/solution.py
@@ -239,13 +239,13 @@
 
 
 def finish_body(*refs):
-    blocks, others, out_ref = refs[:NLEV], refs[NLEV:-1], refs[-1]
+    blocks, others, out_ref = refs[:NLEV], refs[NLEV], refs[-1]
     parity = lax.axis_index("row") % 2
     mine, other = aligned(parity, B, B), aligned(1 - parity, B, B)
     for level in range(NLEV):
         out_ref[level, 0, :, mine] = blocks[level][:, mine].T
         if level:
-            out_ref[level, 0, :, other] = others[level - 1][...].T
+            out_ref[level, 0, :, other] = others[:, (level - 1) * B : level * B].T
 
 
 def last_body(started_ref, other_ref, out_ref, turned, sem):
@@ -370,8 +370,8 @@
         else:
             solved.append(result)
 
-    solution, others = [None] * NLEV, [None] * NLEV
-    solution[NLEV - 1], others[NLEV - 1] = upper, swap(theirs, "row", 1)
+    solution, leaving = [None] * NLEV, [None] * NLEV
+    solution[NLEV - 1], leaving[NLEV - 1] = upper, theirs
     for level in range(NLEV - 2, -1, -1):
         sent = {m: swap(upper, "col", m) for m in reversed(issue_order(cols, COL_ORDER))}
         pieces = [upper] + [sent[m] for m in range(1, cols)]
@@ -395,11 +395,11 @@
             (solved[level], diag_own, diag_par, sums[0], *passed),
             [pltpu.VMEM(block, BF16)],
         )
-        solution[level], others[level] = upper, swap(theirs, "row", 1)
-
-    started = call(
-        finish_body, shape((NLEV, 1, B, 2 * half)), (*solution, *others[1:])
-    )
+        solution[level], leaving[level] = upper, theirs
+
+    others = swap(jnp.concatenate(leaving[1:], axis=1), "row", 1)
+    first_other = swap(leaving[0], "row", 1)
+    started = call(finish_body, shape((NLEV, 1, B, 2 * half)), (*solution, others))
     return pl.pallas_call(
         last_body,
         out_shape=shape((NLEV, 1, B, 2 * half)),
@@ -408,7 +408,7 @@
         scratch_shapes=[pltpu.VMEM((B, half), BF16), pltpu.SemaphoreType.DMA],
         input_output_aliases={0: 0},
         compiler_params=pltpu.CompilerParams(vmem_limit_bytes=VMEM_BYTES),
-    )(started, others[0])
+    )(started, first_other)
 
 
 def solution(mesh):

time: 116 us -> 116 us (level)
    ppermute x44 -> x42, starting transfers between devices: 50 us -> 49.6 us  [swap(): return lax.ppermute(value, axis, [(i, i ^ distance) for i in range(count)])]
    ppermute x44 -> x42, waiting for transfers between devices: 33.6 us -> 34 us  [swap(): return lax.ppermute(value, axis, [(i, i ^ distance) for i in range(count)])]
  transfers between devices with their start and end apart: 45 -> 43, of which waited for: 37 -> 33; matrix products, arithmetic and copies ran while one was open for 4% -> 4% of each run, Pallas kernels for 8% -> 9%
where the time goes in v8:
time: 116 us
  starting transfers between devices  56.6 us (49%)
  waiting for transfers between devices  40.7 us (35%)
  Pallas kernels  13.2 us (11%)
  local copies, waits for them, and re-layouts  3.72 us (3%)
  other arithmetic  1.44 us (1%)
    ppermute x42, starting transfers between devices, swap(): return lax.ppermute(value, axis, [(i, i ^ distance) for i in range(count)])  49.6 us
    ppermute x42, waiting for transfers between devices, swap(): return lax.ppermute(value, axis, [(i, i ^ distance) for i in range(count)])  34 us
    pallas_call x22, Pallas kernels, call(): pl.pallas_call(body, out_shape=out_shape, in_specs=in_specs, out_specs=ou...  9.71 us
    all_to_all x1, starting transfers between devices, per_device(): lax.all_to_all(sending, ('row', 'col'), split_axis=0, concat_axis=0, tile...  6.97 us
    all_to_all x1, waiting for transfers between devices, per_device(): lax.all_to_all(sending, ('row', 'col'), split_axis=0, concat_axis=0, tile...  6.71 us
    slice x1, local copies, waits for them, and re-layouts, per_device(): tile = lower_blocks[level, 0, :, :, 0]  3.08 us
  transfers between devices with their start and end apart: 43, of which 33 were waited for; matrix products, arithmetic and copies ran while one was open for 4% of the time, Pallas kernels for 9%

profile of v8, /device:TPU:0, one launch (start us, length us, event | category | flops | bytes accessed | tf_op | source)
XLA Modules:
  0.0 115.9 jit_solution(14038686617609800076)
XLA Ops:
  0.5 2.3 %shard_map.55 = bf16[32,40,128]{2,1,0:T(8,128)(2,1)} custom-call(f32[512,256]{1,0:T(8,128)} %rhs_hbm.1, s32[1,512]{1,0:T(1,128)} %bitcast.48), custom_call_target="tpu_custom_call" | custom-call | flops 134217728 | bytes 526336 | tf_op jit(solution)/shard_map/pallas_call | solution.py:39
  2.7 7.0 %all-to-all-start = ((bf16[32,40,128]{2,1,0:T(8,128)(2,1)}), bf16[32,40,128]{2,1,0:T(8,128)(2,1)S(1)}, u32[]{:S(2)}, u32[]{:S(2)}) async-start(bf16[32,40,128]{2,1,0:T(8,128)(2,1)} %shard_map.55), calls=%async_computation | async-start | bytes 655360 | tf_op jit(solution)/shard_map/all_to_all | solution.py:320
  10.4 3.1 %fusion = (bf16[1,1,4,128,1,8,128]{6,5,4,3,2,1,0:T(8,128)(2,1)S(1)}, bf16[1,1,4,128,1,8,128]{6,5,4,3,2,1,0:T(8,128)(2,1)S(1)}, bf16[1,1,4,128,1,8,128]{6,5,4,3,2,1,0:T(8,128)(2,1)}) fusion(bf16[3,1,4,128,1,8,128]{6,5,4,3,2,1,0:T(8,128)(2,1)} %param.8), kind=kLoop, calls=%fused_computation.7 | loop fusion | bytes 6291456 | tf_op jit(solution)/shard_map/slice | solution.py:302
  14.0 6.7 %all-to-all-done.arrived_ref = bf16[32,40,128]{2,1,0:T(8,128)(2,1)S(1)} async-done(((bf16[32,40,128]{2,1,0:T(8,128)(2,1)}), bf16[32,40,128]{2,1,0:T(8,128)(2,1)S(1)}, u32[]{:S(2)}, u32[]{:S(2)}) %all-to-all-start) | async-done | bytes 327712 | tf_op jit(solution)/shard_map/all_to_all | solution.py:320
  22.1 1.1 collective-permute-start.4
  23.2 1.5 %collective-permute-start.3 = (bf16[128,256]{1,0:T(8,128)(2,1)S(1)}, bf16[128,256]{1,0:T(8,128)(2,1)S(1)}, u32[]{:S(2)}, u32[]{:S(2)}) collective-permute-start(bf16[128,256]{1,0:T(8,128)(2,1)S(1)} %shard_map.56.after_ref.refs_0_.solved_ref), channel_id=1, source_target_pairs={{0,16},{4,20},{8,24},{12,28},{16,0},{20,4},{24,8},{28,12},{1,17},{... | collective-permute-start | bytes 196616 | tf_op jit(solution)/shard_map/ppermute | solution.py:22
  24.6 1.0 collective-permute-start.2
  26.8 0.9 collective-permute-done.4.refs_3_
  29.3 1.8 %collective-permute-start.5 = (bf16[128,256]{1,0:T(8,128)(2,1)S(1)}, bf16[128,256]{1,0:T(8,128)(2,1)S(1)}, u32[]{:S(2)}, u32[]{:S(2)}) collective-permute-start(bf16[128,256]{1,0:T(8,128)(2,1)S(1)} %get-tuple-element.39), channel_id=1, source_target_pairs={{0,3},{1,2},{2,1},{3,0},{4,7},{5,6},{6,5},{7,4},{8,11},{9,10},{10,... | collective-permute-start | bytes 196616 | tf_op jit(solution)/shard_map/ppermute | solution.py:22
  31.1 2.7 %collective-permute-start.7 = (bf16[128,256]{1,0:T(8,128)(2,1)S(1)}, bf16[128,256]{1,0:T(8,128)(2,1)S(1)}, u32[]{:S(2)}, u32[]{:S(2)}) collective-permute-start(bf16[128,256]{1,0:T(8,128)(2,1)S(1)} %get-tuple-element.41), channel_id=1, source_target_pairs={{0,2},{1,3},{2,0},{3,1},{4,6},{5,7},{6,4},{7,5},{8,10},{9,11},{10,... | collective-permute-start | bytes 196616 | tf_op jit(solution)/shard_map/ppermute | solution.py:22
  35.9 1.4 %collective-permute-done.6.refs_1_ = bf16[128,256]{1,0:T(8,128)(2,1)S(1)} collective-permute-done((bf16[128,256]{1,0:T(8,128)(2,1)S(1)}, bf16[128,256]{1,0:T(8,128)(2,1)S(1)}, u32[]{:S(2)}, u32[]{:S(2)}) %collective-permute-start.6) | collective-permute-done | bytes 65568 | tf_op jit(solution)/shard_map/ppermute | solution.py:22
  38.7 2.3 %collective-permute-start.10 = (bf16[128,256]{1,0:T(8,128)(2,1)S(1)}, bf16[128,256]{1,0:T(8,128)(2,1)S(1)}, u32[]{:S(2)}, u32[]{:S(2)}) collective-permute-start(bf16[128,256]{1,0:T(8,128)(2,1)S(1)} %shard_map.61.after_ref.refs_0_.solved_ref), channel_id=1, source_target_pairs={{0,16},{4,20},{8,24},{12,28},{16,0},{20,4},{24,8},{28,12},{1,17},{... | collective-permute-start | bytes 196616 | tf_op jit(solution)/shard_map/ppermute | solution.py:22
  42.4 1.6 %collective-permute-done.11.refs_3_ = bf16[128,256]{1,0:T(8,128)(2,1)S(1)} collective-permute-done((bf16[128,256]{1,0:T(8,128)(2,1)S(1)}, bf16[128,256]{1,0:T(8,128)(2,1)S(1)}, u32[]{:S(2)}, u32[]{:S(2)}) %collective-permute-start.11) | collective-permute-done | bytes 65568 | tf_op jit(solution)/shard_map/ppermute | solution.py:22
  45.7 1.2 %collective-permute-start.12 = (bf16[128,256]{1,0:T(8,128)(2,1)S(1)}, bf16[128,256]{1,0:T(8,128)(2,1)S(1)}, u32[]{:S(2)}, u32[]{:S(2)}) collective-permute-start(bf16[128,256]{1,0:T(8,128)(2,1)S(1)} %get-tuple-element.44), channel_id=1, source_target_pairs={{0,3},{1,2},{2,1},{3,0},{4,7},{5,6},{6,5},{7,4},{8,11},{9,10},{10,... | collective-permute-start | bytes 196616 | tf_op jit(solution)/shard_map/ppermute | solution.py:22
  47.1 3.1 %collective-permute-start.14 = (bf16[128,256]{1,0:T(8,128)(2,1)S(1)}, bf16[128,256]{1,0:T(8,128)(2,1)S(1)}, u32[]{:S(2)}, u32[]{:S(2)}) collective-permute-start(bf16[128,256]{1,0:T(8,128)(2,1)S(1)} %get-tuple-element.46), channel_id=1, source_target_pairs={{0,2},{1,3},{2,0},{3,1},{4,6},{5,7},{6,4},{7,5},{8,10},{9,11},{10,... | collective-permute-start | bytes 196616 | tf_op jit(solution)/shard_map/ppermute | solution.py:22
  50.5 2.1 %collective-permute-done.12.refs_0_ = bf16[128,256]{1,0:T(8,128)(2,1)S(1)} collective-permute-done((bf16[128,256]{1,0:T(8,128)(2,1)S(1)}, bf16[128,256]{1,0:T(8,128)(2,1)S(1)}, u32[]{:S(2)}, u32[]{:S(2)}) %collective-permute-start.12) | collective-permute-done | bytes 65568 | tf_op jit(solution)/shard_map/ppermute | solution.py:22
  53.4 1.4 %collective-permute-start.18 = (bf16[128,256]{1,0:T(8,128)(2,1)S(1)}, bf16[128,256]{1,0:T(8,128)(2,1)S(1)}, u32[]{:S(2)}, u32[]{:S(2)}) collective-permute-start(bf16[128,256]{1,0:T(8,128)(2,1)S(1)} %shard_map.65.after_ref.refs_0_.solved_ref), channel_id=1, source_target_pairs={{0,24},{4,28},{8,16},{12,20},{16,8},{20,12},{24,0},{28,4},{1,25},{... | collective-permute-start | bytes 196616 | tf_op jit(solution)/shard_map/ppermute | solution.py:22
  54.8 1.5 %collective-permute-start.17 = (bf16[128,256]{1,0:T(8,128)(2,1)S(1)}, bf16[128,256]{1,0:T(8,128)(2,1)S(1)}, u32[]{:S(2)}, u32[]{:S(2)}) collective-permute-start(bf16[128,256]{1,0:T(8,128)(2,1)S(1)} %shard_map.65.after_ref.refs_0_.solved_ref), channel_id=1, source_target_pairs={{0,16},{4,20},{8,24},{12,28},{16,0},{20,4},{24,8},{28,12},{1,17},{... | collective-permute-start | bytes 196616 | tf_op jit(solution)/shard_map/ppermute | solution.py:22
  57.7 1.5 %collective-permute-done.18.refs_3_ = bf16[128,256]{1,0:T(8,128)(2,1)S(1)} collective-permute-done((bf16[128,256]{1,0:T(8,128)(2,1)S(1)}, bf16[128,256]{1,0:T(8,128)(2,1)S(1)}, u32[]{:S(2)}, u32[]{:S(2)}) %collective-permute-start.18) | collective-permute-done | bytes 65568 | tf_op jit(solution)/shard_map/ppermute | solution.py:22
  59.6 1.0 collective-permute-done.16.refs_1_
  61.0 2.0 %collective-permute-start.19 = (bf16[128,256]{1,0:T(8,128)(2,1)S(1)}, bf16[128,256]{1,0:T(8,128)(2,1)S(1)}, u32[]{:S(2)}, u32[]{:S(2)}) collective-permute-start(bf16[128,256]{1,0:T(8,128)(2,1)S(1)} %get-tuple-element.49), channel_id=1, source_target_pairs={{0,3},{1,2},{2,1},{3,0},{4,7},{5,6},{6,5},{7,4},{8,11},{9,10},{10,... | collective-permute-start | bytes 196616 | tf_op jit(solution)/shard_map/ppermute | solution.py:22
  63.3 2.1 %collective-permute-start.21 = (bf16[128,256]{1,0:T(8,128)(2,1)S(1)}, bf16[128,256]{1,0:T(8,128)(2,1)S(1)}, u32[]{:S(2)}, u32[]{:S(2)}) collective-permute-start(bf16[128,256]{1,0:T(8,128)(2,1)S(1)} %get-tuple-element.51), channel_id=1, source_target_pairs={{0,2},{1,3},{2,0},{3,1},{4,6},{5,7},{6,4},{7,5},{8,10},{9,11},{10,... | collective-permute-start | bytes 196616 | tf_op jit(solution)/shard_map/ppermute | solution.py:22
  65.7 1.5 %collective-permute-done.19.refs_0_ = bf16[128,256]{1,0:T(8,128)(2,1)S(1)} collective-permute-done((bf16[128,256]{1,0:T(8,128)(2,1)S(1)}, bf16[128,256]{1,0:T(8,128)(2,1)S(1)}, u32[]{:S(2)}, u32[]{:S(2)}) %collective-permute-start.19) | collective-permute-done | bytes 65568 | tf_op jit(solution)/shard_map/ppermute | solution.py:22
  67.8 1.1 collective-permute-done.21.refs_2_
  69.3 1.6 %collective-permute-start.24 = (bf16[128,256]{1,0:T(8,128)(2,1)S(1)}, bf16[128,256]{1,0:T(8,128)(2,1)S(1)}, u32[]{:S(2)}, u32[]{:S(2)}) collective-permute-start(bf16[128,256]{1,0:T(8,128)(2,1)S(1)} %get-tuple-element.52.after_ref.refs_0_.refs_3_), channel_id=1, source_target_pairs={{0,3},{1,2},{2,1},{3,0},{4,7},{5,6},{6,5},{7,4},{8,11},{9,10},{10,... | collective-permute-start | bytes 196616 | tf_op jit(solution)/shard_map/ppermute | solution.py:22
  70.9 1.7 %collective-permute-start.23 = (bf16[128,256]{1,0:T(8,128)(2,1)S(1)}, bf16[128,256]{1,0:T(8,128)(2,1)S(1)}, u32[]{:S(2)}, u32[]{:S(2)}) collective-permute-start(bf16[128,256]{1,0:T(8,128)(2,1)S(1)} %get-tuple-element.52.after_ref.refs_0_.refs_3_), channel_id=1, source_target_pairs={{0,2},{1,3},{2,0},{3,1},{4,6},{5,7},{6,4},{7,5},{8,10},{9,11},{10,... | collective-permute-start | bytes 196616 | tf_op jit(solution)/shard_map/ppermute | solution.py:22
  72.6 1.2 %collective-permute-start.22 = (bf16[128,256]{1,0:T(8,128)(2,1)S(1)}, bf16[128,256]{1,0:T(8,128)(2,1)S(1)}, u32[]{:S(2)}, u32[]{:S(2)}) collective-permute-start(bf16[128,256]{1,0:T(8,128)(2,1)S(1)} %get-tuple-element.52.after_ref.refs_0_.refs_3_), channel_id=1, source_target_pairs={{0,1},{1,0},{2,3},{3,2},{4,5},{5,4},{6,7},{7,6},{8,9},{9,8},{10,11... | collective-permute-start | bytes 196616 | tf_op jit(solution)/shard_map/ppermute | solution.py:22
  74.0 1.5 %collective-permute-done.24.refs_3_ = bf16[128,256]{1,0:T(8,128)(2,1)S(1)} collective-permute-done((bf16[128,256]{1,0:T(8,128)(2,1)S(1)}, bf16[128,256]{1,0:T(8,128)(2,1)S(1)}, u32[]{:S(2)}, u32[]{:S(2)}) %collective-permute-start.24) | collective-permute-done | bytes 65568 | tf_op jit(solution)/shard_map/ppermute | solution.py:22
  75.5 1.5 %collective-permute-done.23.refs_2_ = bf16[128,256]{1,0:T(8,128)(2,1)S(1)} collective-permute-done((bf16[128,256]{1,0:T(8,128)(2,1)S(1)}, bf16[128,256]{1,0:T(8,128)(2,1)S(1)}, u32[]{:S(2)}, u32[]{:S(2)}) %collective-permute-start.23) | collective-permute-done | bytes 65568 | tf_op jit(solution)/shard_map/ppermute | solution.py:22
  77.4 2.0 %collective-permute-start.25 = (bf16[128,256]{1,0:T(8,128)(2,1)S(1)}, bf16[128,256]{1,0:T(8,128)(2,1)S(1)}, u32[]{:S(2)}, u32[]{:S(2)}) collective-permute-start(bf16[128,256]{1,0:T(8,128)(2,1)S(1)} %get-tuple-element.53), channel_id=1, source_target_pairs={{0,24},{4,28},{8,16},{12,20},{16,8},{20,12},{24,0},{28,4},{1,25},{... | collective-permute-start | bytes 196616 | tf_op jit(solution)/shard_map/ppermute | solution.py:22
  79.4 1.6 %collective-permute-start.27 = (bf16[128,256]{1,0:T(8,128)(2,1)S(1)}, bf16[128,256]{1,0:T(8,128)(2,1)S(1)}, u32[]{:S(2)}, u32[]{:S(2)}) collective-permute-start(bf16[128,256]{1,0:T(8,128)(2,1)S(1)} %get-tuple-element.55), channel_id=1, source_target_pairs={{0,16},{4,20},{8,24},{12,28},{16,0},{20,4},{24,8},{28,12},{1,17},{... | collective-permute-start | bytes 196616 | tf_op jit(solution)/shard_map/ppermute | solution.py:22
  81.2 1.4 %collective-permute-done.25.refs_0_ = bf16[128,256]{1,0:T(8,128)(2,1)S(1)} collective-permute-done((bf16[128,256]{1,0:T(8,128)(2,1)S(1)}, bf16[128,256]{1,0:T(8,128)(2,1)S(1)}, u32[]{:S(2)}, u32[]{:S(2)}) %collective-permute-start.25) | collective-permute-done | bytes 65568 | tf_op jit(solution)/shard_map/ppermute | solution.py:22
  82.6 1.0 collective-permute-done.26.refs_1_
  83.8 2.0 %collective-permute-start.30 = (bf16[128,256]{1,0:T(8,128)(2,1)S(1)}, bf16[128,256]{1,0:T(8,128)(2,1)S(1)}, u32[]{:S(2)}, u32[]{:S(2)}) collective-permute-start(bf16[128,256]{1,0:T(8,128)(2,1)S(1)} %get-tuple-element.56.after_ref.refs_0_.refs_2_), channel_id=1, source_target_pairs={{0,3},{1,2},{2,1},{3,0},{4,7},{5,6},{6,5},{7,4},{8,11},{9,10},{10,... | collective-permute-start | bytes 196616 | tf_op jit(solution)/shard_map/ppermute | solution.py:22
  86.2 2.1 %collective-permute-start.28 = (bf16[128,256]{1,0:T(8,128)(2,1)S(1)}, bf16[128,256]{1,0:T(8,128)(2,1)S(1)}, u32[]{:S(2)}, u32[]{:S(2)}) collective-permute-start(bf16[128,256]{1,0:T(8,128)(2,1)S(1)} %get-tuple-element.56.after_ref.refs_0_.refs_2_), channel_id=1, source_target_pairs={{0,1},{1,0},{2,3},{3,2},{4,5},{5,4},{6,7},{7,6},{8,9},{9,8},{10,11... | collective-permute-start | bytes 196616 | tf_op jit(solution)/shard_map/ppermute | solution.py:22
  88.5 1.4 %collective-permute-done.30.refs_3_ = bf16[128,256]{1,0:T(8,128)(2,1)S(1)} collective-permute-done((bf16[128,256]{1,0:T(8,128)(2,1)S(1)}, bf16[128,256]{1,0:T(8,128)(2,1)S(1)}, u32[]{:S(2)}, u32[]{:S(2)}) %collective-permute-start.30) | collective-permute-done | bytes 65568 | tf_op jit(solution)/shard_map/ppermute | solution.py:22
  90.0 1.4 %collective-permute-done.29.refs_2_ = bf16[128,256]{1,0:T(8,128)(2,1)S(1)} collective-permute-done((bf16[128,256]{1,0:T(8,128)(2,1)S(1)}, bf16[128,256]{1,0:T(8,128)(2,1)S(1)}, u32[]{:S(2)}, u32[]{:S(2)}) %collective-permute-start.29) | collective-permute-done | bytes 65568 | tf_op jit(solution)/shard_map/ppermute | solution.py:22
  91.8 2.4 %collective-permute-start.31 = (bf16[128,256]{1,0:T(8,128)(2,1)S(1)}, bf16[128,256]{1,0:T(8,128)(2,1)S(1)}, u32[]{:S(2)}, u32[]{:S(2)}) collective-permute-start(bf16[128,256]{1,0:T(8,128)(2,1)S(1)} %get-tuple-element.57), channel_id=1, source_target_pairs={{0,24},{4,28},{8,16},{12,20},{16,8},{20,12},{24,0},{28,4},{1,25},{... | collective-permute-start | bytes 196616 | tf_op jit(solution)/shard_map/ppermute | solution.py:22
  95.6 1.4 %collective-permute-done.31.refs_0_ = bf16[128,256]{1,0:T(8,128)(2,1)S(1)} collective-permute-done((bf16[128,256]{1,0:T(8,128)(2,1)S(1)}, bf16[128,256]{1,0:T(8,128)(2,1)S(1)}, u32[]{:S(2)}, u32[]{:S(2)}) %collective-permute-start.31) | collective-permute-done | bytes 65568 | tf_op jit(solution)/shard_map/ppermute | solution.py:22
  97.0 1.4 %collective-permute-done.32.refs_1_ = bf16[128,256]{1,0:T(8,128)(2,1)S(1)} collective-permute-done((bf16[128,256]{1,0:T(8,128)(2,1)S(1)}, bf16[128,256]{1,0:T(8,128)(2,1)S(1)}, u32[]{:S(2)}, u32[]{:S(2)}) %collective-permute-start.32) | collective-permute-done | bytes 65568 | tf_op jit(solution)/shard_map/ppermute | solution.py:22
  99.4 2.1 %collective-permute-start.36 = (bf16[128,256]{1,0:T(8,128)(2,1)S(1)}, bf16[128,256]{1,0:T(8,128)(2,1)S(1)}, u32[]{:S(2)}, u32[]{:S(2)}) collective-permute-start(bf16[128,256]{1,0:T(8,128)(2,1)S(1)} %get-tuple-element.60.after_ref.refs_0_.refs_1_), channel_id=1, source_target_pairs={{0,3},{1,2},{2,1},{3,0},{4,7},{5,6},{6,5},{7,4},{8,11},{9,10},{10,... | collective-permute-start | bytes 196616 | tf_op jit(solution)/shard_map/ppermute | solution.py:22
  102.1 1.7 %collective-permute-start.34 = (bf16[128,256]{1,0:T(8,128)(2,1)S(1)}, bf16[128,256]{1,0:T(8,128)(2,1)S(1)}, u32[]{:S(2)}, u32[]{:S(2)}) collective-permute-start(bf16[128,256]{1,0:T(8,128)(2,1)S(1)} %get-tuple-element.60.after_ref.refs_0_.refs_1_), channel_id=1, source_target_pairs={{0,1},{1,0},{2,3},{3,2},{4,5},{5,4},{6,7},{7,6},{8,9},{9,8},{10,11... | collective-permute-start | bytes 196616 | tf_op jit(solution)/shard_map/ppermute | solution.py:22
  104.2 1.3 %collective-permute-done.36.refs_3_ = bf16[128,256]{1,0:T(8,128)(2,1)S(1)} collective-permute-done((bf16[128,256]{1,0:T(8,128)(2,1)S(1)}, bf16[128,256]{1,0:T(8,128)(2,1)S(1)}, u32[]{:S(2)}, u32[]{:S(2)}) %collective-permute-start.36) | collective-permute-done | bytes 65568 | tf_op jit(solution)/shard_map/ppermute | solution.py:22
  105.5 1.6 %collective-permute-done.35.refs_2_ = bf16[128,256]{1,0:T(8,128)(2,1)S(1)} collective-permute-done((bf16[128,256]{1,0:T(8,128)(2,1)S(1)}, bf16[128,256]{1,0:T(8,128)(2,1)S(1)}, u32[]{:S(2)}, u32[]{:S(2)}) %collective-permute-start.35) | collective-permute-done | bytes 65568 | tf_op jit(solution)/shard_map/ppermute | solution.py:22
  107.5 1.9 %collective-permute-start.37 = (bf16[128,256]{1,0:T(8,128)(2,1)S(1)}, bf16[128,256]{1,0:T(8,128)(2,1)S(1)}, u32[]{:S(2)}, u32[]{:S(2)}) collective-permute-start(bf16[128,256]{1,0:T(8,128)(2,1)S(1)} %get-tuple-element.61), channel_id=1, source_target_pairs={{0,24},{4,28},{8,16},{12,20},{16,8},{20,12},{24,0},{28,4},{1,25},{... | collective-permute-start | bytes 196616 | tf_op jit(solution)/shard_map/ppermute | solution.py:22
  109.5 1.6 %collective-permute-start.39 = (bf16[128,256]{1,0:T(8,128)(2,1)S(1)}, bf16[128,256]{1,0:T(8,128)(2,1)S(1)}, u32[]{:S(2)}, u32[]{:S(2)}) collective-permute-start(bf16[128,256]{1,0:T(8,128)(2,1)S(1)} %get-tuple-element.63), channel_id=1, source_target_pairs={{0,16},{4,20},{8,24},{12,28},{16,0},{20,4},{24,8},{28,12},{1,17},{... | collective-permute-start | bytes 196616 | tf_op jit(solution)/shard_map/ppermute | solution.py:22
  111.4 1.4 %collective-permute-done.37.refs_0_ = bf16[128,256]{1,0:T(8,128)(2,1)S(1)} collective-permute-done((bf16[128,256]{1,0:T(8,128)(2,1)S(1)}, bf16[128,256]{1,0:T(8,128)(2,1)S(1)}, u32[]{:S(2)}, u32[]{:S(2)}) %collective-permute-start.37) | collective-permute-done | bytes 65568 | tf_op jit(solution)/shard_map/ppermute | solution.py:22
  112.8 0.9 collective-permute-done.38.refs_1_
  (83 shorter events, 25.7 us)
Async XLA Ops:
  0.0 14.0 %collective-permute-start = (bf16[4,128,128]{2,1,0:T(8,128)(2,1)}, bf16[4,128,128]{2,1,0:T(8,128)(2,1)S(1)}, u32[]{:S(2)}, u32[]{:S(2)}) collective-permute-start(bf16[4,128,128]{2,1,0:T(8,128)(2,1)} %bitcast.33), channel_id=1, source_target_pairs={{0,4},{4,0},{8,12},{12,8},{16,20},{20,16},{24,28},{28,24},{1,5},{5... | collective-permute-start | bytes 393224 | tf_op jit(solution)/shard_map/ppermute | solution.py:22
  2.7 18.0 %all-to-all-start = ((bf16[32,40,128]{2,1,0:T(8,128)(2,1)}), bf16[32,40,128]{2,1,0:T(8,128)(2,1)S(1)}, u32[]{:S(2)}, u32[]{:S(2)}) async-start(bf16[32,40,128]{2,1,0:T(8,128)(2,1)} %shard_map.55), calls=%async_computation | async-start | bytes 655360 | tf_op jit(solution)/shard_map/all_to_all | solution.py:320
  13.5 7.2 %copy-start = (bf16[4,1,128,128]{3,2,1,0:T(8,128)(2,1)S(1)}, bf16[4,1,128,128]{3,2,1,0:T(8,128)(2,1)}, u32[]{:S(2)}) copy-start(bf16[4,1,128,128]{3,2,1,0:T(8,128)(2,1)} %param.7) | copy-start | bytes 393220
  20.7 5.1 %copy-start.1 = (bf16[1,1,4,128,1,8,128]{6,5,4,3,2,1,0:T(8,128)(2,1)S(1)}, bf16[1,1,4,128,1,8,128]{6,5,4,3,2,1,0:T(8,128)(2,1)}, u32[]{:S(2)}) copy-start(bf16[1,1,4,128,1,8,128]{6,5,4,3,2,1,0:T(8,128)(2,1)} %get-tuple-element.71) | copy-start | bytes 3145732
  21.2 4.9 %collective-permute-start.1 = (bf16[512,1024]{1,0:T(8,128)(2,1)S(1)}, bf16[512,1024]{1,0:T(8,128)(2,1)S(1)}, u32[]{:S(2)}, u32[]{:S(2)}) collective-permute-start(bf16[512,1024]{1,0:T(8,128)(2,1)S(1)} %bitcast_multiply_fusion.2.own_ref), channel_id=1, source_target_pairs={{0,4},{4,0},{8,12},{12,8},{16,20},{20,16},{24,28},{28,24},{1,5},{5... | collective-permute-start | bytes 3145736 | tf_op jit(solution)/shard_map/ppermute | solution.py:22
  22.1 5.6 %collective-permute-start.4 = (bf16[128,256]{1,0:T(8,128)(2,1)S(1)}, bf16[128,256]{1,0:T(8,128)(2,1)S(1)}, u32[]{:S(2)}, u32[]{:S(2)}) collective-permute-start(bf16[128,256]{1,0:T(8,128)(2,1)S(1)} %shard_map.56.after_ref.refs_0_.solved_ref), channel_id=1, source_target_pairs={{0,24},{4,28},{8,16},{12,20},{16,8},{20,12},{24,0},{28,4},{1,25},{... | collective-permute-start | bytes 196616 | tf_op jit(solution)/shard_map/ppermute | solution.py:22
  23.2 5.3 %collective-permute-start.3 = (bf16[128,256]{1,0:T(8,128)(2,1)S(1)}, bf16[128,256]{1,0:T(8,128)(2,1)S(1)}, u32[]{:S(2)}, u32[]{:S(2)}) collective-permute-start(bf16[128,256]{1,0:T(8,128)(2,1)S(1)} %shard_map.56.after_ref.refs_0_.solved_ref), channel_id=1, source_target_pairs={{0,16},{4,20},{8,24},{12,28},{16,0},{20,4},{24,8},{28,12},{1,17},{... | collective-permute-start | bytes 196616 | tf_op jit(solution)/shard_map/ppermute | solution.py:22
  24.6 4.3 %collective-permute-start.2 = (bf16[128,256]{1,0:T(8,128)(2,1)S(1)}, bf16[128,256]{1,0:T(8,128)(2,1)S(1)}, u32[]{:S(2)}, u32[]{:S(2)}) collective-permute-start(bf16[128,256]{1,0:T(8,128)(2,1)S(1)} %shard_map.56.after_ref.refs_0_.solved_ref), channel_id=1, source_target_pairs={{0,8},{4,12},{8,0},{12,4},{16,24},{20,28},{24,16},{28,20},{1,9},{5... | collective-permute-start | bytes 196616 | tf_op jit(solution)/shard_map/ppermute | solution.py:22
  26.1 15.6 %collective-permute-start.8 = (bf16[512,1024]{1,0:T(8,128)(2,1)S(1)}, bf16[512,1024]{1,0:T(8,128)(2,1)S(1)}, u32[]{:S(2)}, u32[]{:S(2)}) collective-permute-start(bf16[512,1024]{1,0:T(8,128)(2,1)S(1)} %bitcast_multiply_fusion.1.own_ref), channel_id=1, source_target_pairs={{0,4},{4,0},{8,12},{12,8},{16,20},{20,16},{24,28},{28,24},{1,5},{5... | collective-permute-start | bytes 3145736 | tf_op jit(solution)/shard_map/ppermute | solution.py:22
  29.3 6.5 %collective-permute-start.5 = (bf16[128,256]{1,0:T(8,128)(2,1)S(1)}, bf16[128,256]{1,0:T(8,128)(2,1)S(1)}, u32[]{:S(2)}, u32[]{:S(2)}) collective-permute-start(bf16[128,256]{1,0:T(8,128)(2,1)S(1)} %get-tuple-element.39), channel_id=1, source_target_pairs={{0,3},{1,2},{2,1},{3,0},{4,7},{5,6},{6,5},{7,4},{8,11},{9,10},{10,... | collective-permute-start | bytes 196616 | tf_op jit(solution)/shard_map/ppermute | solution.py:22
  31.1 6.2 %collective-permute-start.6 = (bf16[128,256]{1,0:T(8,128)(2,1)S(1)}, bf16[128,256]{1,0:T(8,128)(2,1)S(1)}, u32[]{:S(2)}, u32[]{:S(2)}) collective-permute-start(bf16[128,256]{1,0:T(8,128)(2,1)S(1)} %get-tuple-element.40), channel_id=1, source_target_pairs={{0,1},{1,0},{2,3},{3,2},{4,5},{5,4},{6,7},{7,6},{8,9},{9,8},{10,11... | collective-permute-start | bytes 196616 | tf_op jit(solution)/shard_map/ppermute | solution.py:22
  31.1 6.8 %collective-permute-start.7 = (bf16[128,256]{1,0:T(8,128)(2,1)S(1)}, bf16[128,256]{1,0:T(8,128)(2,1)S(1)}, u32[]{:S(2)}, u32[]{:S(2)}) collective-permute-start(bf16[128,256]{1,0:T(8,128)(2,1)S(1)} %get-tuple-element.41), channel_id=1, source_target_pairs={{0,2},{1,3},{2,0},{3,1},{4,6},{5,7},{6,4},{7,5},{8,10},{9,11},{10,... | collective-permute-start | bytes 196616 | tf_op jit(solution)/shard_map/ppermute | solution.py:22
  38.0 18.9 %collective-permute-start.15 = (bf16[512,1024]{1,0:T(8,128)(2,1)S(1)}, bf16[512,1024]{1,0:T(8,128)(2,1)S(1)}, u32[]{:S(2)}, u32[]{:S(2)}) collective-permute-start(bf16[512,1024]{1,0:T(8,128)(2,1)S(1)} %bitcast_multiply_fusion.own_ref), channel_id=1, source_target_pairs={{0,4},{4,0},{8,12},{12,8},{16,20},{20,16},{24,28},{28,24},{1,5},{5... | collective-permute-start | bytes 3145736 | tf_op jit(solution)/shard_map/ppermute | solution.py:22
  38.1 5.9 %collective-permute-start.11 = (bf16[128,256]{1,0:T(8,128)(2,1)S(1)}, bf16[128,256]{1,0:T(8,128)(2,1)S(1)}, u32[]{:S(2)}, u32[]{:S(2)}) collective-permute-start(bf16[128,256]{1,0:T(8,128)(2,1)S(1)} %shard_map.61.after_ref.refs_0_.solved_ref), channel_id=1, source_target_pairs={{0,24},{4,28},{8,16},{12,20},{16,8},{20,12},{24,0},{28,4},{1,25},{... | collective-permute-start | bytes 196616 | tf_op jit(solution)/shard_map/ppermute | solution.py:22
  38.7 6.2 %collective-permute-start.10 = (bf16[128,256]{1,0:T(8,128)(2,1)S(1)}, bf16[128,256]{1,0:T(8,128)(2,1)S(1)}, u32[]{:S(2)}, u32[]{:S(2)}) collective-permute-start(bf16[128,256]{1,0:T(8,128)(2,1)S(1)} %shard_map.61.after_ref.refs_0_.solved_ref), channel_id=1, source_target_pairs={{0,16},{4,20},{8,24},{12,28},{16,0},{20,4},{24,8},{28,12},{1,17},{... | collective-permute-start | bytes 196616 | tf_op jit(solution)/shard_map/ppermute | solution.py:22
  41.0 4.3 %collective-permute-start.9 = (bf16[128,256]{1,0:T(8,128)(2,1)S(1)}, bf16[128,256]{1,0:T(8,128)(2,1)S(1)}, u32[]{:S(2)}, u32[]{:S(2)}) collective-permute-start(bf16[128,256]{1,0:T(8,128)(2,1)S(1)} %shard_map.61.after_ref.refs_0_.solved_ref), channel_id=1, source_target_pairs={{0,8},{4,12},{8,0},{12,4},{16,24},{20,28},{24,16},{28,20},{1,9},{5... | collective-permute-start | bytes 196616 | tf_op jit(solution)/shard_map/ppermute | solution.py:22
  45.7 6.9 %collective-permute-start.12 = (bf16[128,256]{1,0:T(8,128)(2,1)S(1)}, bf16[128,256]{1,0:T(8,128)(2,1)S(1)}, u32[]{:S(2)}, u32[]{:S(2)}) collective-permute-start(bf16[128,256]{1,0:T(8,128)(2,1)S(1)} %get-tuple-element.44), channel_id=1, source_target_pairs={{0,3},{1,2},{2,1},{3,0},{4,7},{5,6},{6,5},{7,4},{8,11},{9,10},{10,... | collective-permute-start | bytes 196616 | tf_op jit(solution)/shard_map/ppermute | solution.py:22
  47.0 5.8 %collective-permute-start.13 = (bf16[128,256]{1,0:T(8,128)(2,1)S(1)}, bf16[128,256]{1,0:T(8,128)(2,1)S(1)}, u32[]{:S(2)}, u32[]{:S(2)}) collective-permute-start(bf16[128,256]{1,0:T(8,128)(2,1)S(1)} %get-tuple-element.45), channel_id=1, source_target_pairs={{0,1},{1,0},{2,3},{3,2},{4,5},{5,4},{6,7},{7,6},{8,9},{9,8},{10,11... | collective-permute-start | bytes 196616 | tf_op jit(solution)/shard_map/ppermute | solution.py:22
  47.1 6.2 %collective-permute-start.14 = (bf16[128,256]{1,0:T(8,128)(2,1)S(1)}, bf16[128,256]{1,0:T(8,128)(2,1)S(1)}, u32[]{:S(2)}, u32[]{:S(2)}) collective-permute-start(bf16[128,256]{1,0:T(8,128)(2,1)S(1)} %get-tuple-element.46), channel_id=1, source_target_pairs={{0,2},{1,3},{2,0},{3,1},{4,6},{5,7},{6,4},{7,5},{8,10},{9,11},{10,... | collective-permute-start | bytes 196616 | tf_op jit(solution)/shard_map/ppermute | solution.py:22
  53.4 5.8 %collective-permute-start.18 = (bf16[128,256]{1,0:T(8,128)(2,1)S(1)}, bf16[128,256]{1,0:T(8,128)(2,1)S(1)}, u32[]{:S(2)}, u32[]{:S(2)}) collective-permute-start(bf16[128,256]{1,0:T(8,128)(2,1)S(1)} %shard_map.65.after_ref.refs_0_.solved_ref), channel_id=1, source_target_pairs={{0,24},{4,28},{8,16},{12,20},{16,8},{20,12},{24,0},{28,4},{1,25},{... | collective-permute-start | bytes 196616 | tf_op jit(solution)/shard_map/ppermute | solution.py:22
  54.8 4.8 %collective-permute-start.17 = (bf16[128,256]{1,0:T(8,128)(2,1)S(1)}, bf16[128,256]{1,0:T(8,128)(2,1)S(1)}, u32[]{:S(2)}, u32[]{:S(2)}) collective-permute-start(bf16[128,256]{1,0:T(8,128)(2,1)S(1)} %shard_map.65.after_ref.refs_0_.solved_ref), channel_id=1, source_target_pairs={{0,16},{4,20},{8,24},{12,28},{16,0},{20,4},{24,8},{28,12},{1,17},{... | collective-permute-start | bytes 196616 | tf_op jit(solution)/shard_map/ppermute | solution.py:22
  56.3 4.3 %collective-permute-start.16 = (bf16[128,256]{1,0:T(8,128)(2,1)S(1)}, bf16[128,256]{1,0:T(8,128)(2,1)S(1)}, u32[]{:S(2)}, u32[]{:S(2)}) collective-permute-start(bf16[128,256]{1,0:T(8,128)(2,1)S(1)} %shard_map.65.after_ref.refs_0_.solved_ref), channel_id=1, source_target_pairs={{0,8},{4,12},{8,0},{12,4},{16,24},{20,28},{24,16},{28,20},{1,9},{5... | collective-permute-start | bytes 196616 | tf_op jit(solution)/shard_map/ppermute | solution.py:22
  61.0 6.2 %collective-permute-start.19 = (bf16[128,256]{1,0:T(8,128)(2,1)S(1)}, bf16[128,256]{1,0:T(8,128)(2,1)S(1)}, u32[]{:S(2)}, u32[]{:S(2)}) collective-permute-start(bf16[128,256]{1,0:T(8,128)(2,1)S(1)} %get-tuple-element.49), channel_id=1, source_target_pairs={{0,3},{1,2},{2,1},{3,0},{4,7},{5,6},{6,5},{7,4},{8,11},{9,10},{10,... | collective-permute-start | bytes 196616 | tf_op jit(solution)/shard_map/ppermute | solution.py:22
  63.0 4.9 %collective-permute-start.20 = (bf16[128,256]{1,0:T(8,128)(2,1)S(1)}, bf16[128,256]{1,0:T(8,128)(2,1)S(1)}, u32[]{:S(2)}, u32[]{:S(2)}) collective-permute-start(bf16[128,256]{1,0:T(8,128)(2,1)S(1)} %get-tuple-element.50), channel_id=1, source_target_pairs={{0,1},{1,0},{2,3},{3,2},{4,5},{5,4},{6,7},{7,6},{8,9},{9,8},{10,11... | collective-permute-start | bytes 196616 | tf_op jit(solution)/shard_map/ppermute | solution.py:22
  63.3 5.6 %collective-permute-start.21 = (bf16[128,256]{1,0:T(8,128)(2,1)S(1)}, bf16[128,256]{1,0:T(8,128)(2,1)S(1)}, u32[]{:S(2)}, u32[]{:S(2)}) collective-permute-start(bf16[128,256]{1,0:T(8,128)(2,1)S(1)} %get-tuple-element.51), channel_id=1, source_target_pairs={{0,2},{1,3},{2,0},{3,1},{4,6},{5,7},{6,4},{7,5},{8,10},{9,11},{10,... | collective-permute-start | bytes 196616 | tf_op jit(solution)/shard_map/ppermute | solution.py:22
  69.3 6.2 %collective-permute-start.24 = (bf16[128,256]{1,0:T(8,128)(2,1)S(1)}, bf16[128,256]{1,0:T(8,128)(2,1)S(1)}, u32[]{:S(2)}, u32[]{:S(2)}) collective-permute-start(bf16[128,256]{1,0:T(8,128)(2,1)S(1)} %get-tuple-element.52.after_ref.refs_0_.refs_3_), channel_id=1, source_target_pairs={{0,3},{1,2},{2,1},{3,0},{4,7},{5,6},{6,5},{7,4},{8,11},{9,10},{10,... | collective-permute-start | bytes 196616 | tf_op jit(solution)/shard_map/ppermute | solution.py:22
  70.9 6.1 %collective-permute-start.23 = (bf16[128,256]{1,0:T(8,128)(2,1)S(1)}, bf16[128,256]{1,0:T(8,128)(2,1)S(1)}, u32[]{:S(2)}, u32[]{:S(2)}) collective-permute-start(bf16[128,256]{1,0:T(8,128)(2,1)S(1)} %get-tuple-element.52.after_ref.refs_0_.refs_3_), channel_id=1, source_target_pairs={{0,2},{1,3},{2,0},{3,1},{4,6},{5,7},{6,4},{7,5},{8,10},{9,11},{10,... | collective-permute-start | bytes 196616 | tf_op jit(solution)/shard_map/ppermute | solution.py:22
  72.6 4.4 %collective-permute-start.22 = (bf16[128,256]{1,0:T(8,128)(2,1)S(1)}, bf16[128,256]{1,0:T(8,128)(2,1)S(1)}, u32[]{:S(2)}, u32[]{:S(2)}) collective-permute-start(bf16[128,256]{1,0:T(8,128)(2,1)S(1)} %get-tuple-element.52.after_ref.refs_0_.refs_3_), channel_id=1, source_target_pairs={{0,1},{1,0},{2,3},{3,2},{4,5},{5,4},{6,7},{7,6},{8,9},{9,8},{10,11... | collective-permute-start | bytes 196616 | tf_op jit(solution)/shard_map/ppermute | solution.py:22
  77.4 5.2 %collective-permute-start.25 = (bf16[128,256]{1,0:T(8,128)(2,1)S(1)}, bf16[128,256]{1,0:T(8,128)(2,1)S(1)}, u32[]{:S(2)}, u32[]{:S(2)}) collective-permute-start(bf16[128,256]{1,0:T(8,128)(2,1)S(1)} %get-tuple-element.53), channel_id=1, source_target_pairs={{0,24},{4,28},{8,16},{12,20},{16,8},{20,12},{24,0},{28,4},{1,25},{... | collective-permute-start | bytes 196616 | tf_op jit(solution)/shard_map/ppermute | solution.py:22
  79.4 4.3 %collective-permute-start.26 = (bf16[128,256]{1,0:T(8,128)(2,1)S(1)}, bf16[128,256]{1,0:T(8,128)(2,1)S(1)}, u32[]{:S(2)}, u32[]{:S(2)}) collective-permute-start(bf16[128,256]{1,0:T(8,128)(2,1)S(1)} %get-tuple-element.54), channel_id=1, source_target_pairs={{0,8},{4,12},{8,0},{12,4},{16,24},{20,28},{24,16},{28,20},{1,9},{5... | collective-permute-start | bytes 196616 | tf_op jit(solution)/shard_map/ppermute | solution.py:22
  79.4 4.3 %collective-permute-start.27 = (bf16[128,256]{1,0:T(8,128)(2,1)S(1)}, bf16[128,256]{1,0:T(8,128)(2,1)S(1)}, u32[]{:S(2)}, u32[]{:S(2)}) collective-permute-start(bf16[128,256]{1,0:T(8,128)(2,1)S(1)} %get-tuple-element.55), channel_id=1, source_target_pairs={{0,16},{4,20},{8,24},{12,28},{16,0},{20,4},{24,8},{28,12},{1,17},{... | collective-permute-start | bytes 196616 | tf_op jit(solution)/shard_map/ppermute | solution.py:22
  83.8 6.1 %collective-permute-start.30 = (bf16[128,256]{1,0:T(8,128)(2,1)S(1)}, bf16[128,256]{1,0:T(8,128)(2,1)S(1)}, u32[]{:S(2)}, u32[]{:S(2)}) collective-permute-start(bf16[128,256]{1,0:T(8,128)(2,1)S(1)} %get-tuple-element.56.after_ref.refs_0_.refs_2_), channel_id=1, source_target_pairs={{0,3},{1,2},{2,1},{3,0},{4,7},{5,6},{6,5},{7,4},{8,11},{9,10},{10,... | collective-permute-start | bytes 196616 | tf_op jit(solution)/shard_map/ppermute | solution.py:22
  85.8 5.5 %collective-permute-start.29 = (bf16[128,256]{1,0:T(8,128)(2,1)S(1)}, bf16[128,256]{1,0:T(8,128)(2,1)S(1)}, u32[]{:S(2)}, u32[]{:S(2)}) collective-permute-start(bf16[128,256]{1,0:T(8,128)(2,1)S(1)} %get-tuple-element.56.after_ref.refs_0_.refs_2_), channel_id=1, source_target_pairs={{0,2},{1,3},{2,0},{3,1},{4,6},{5,7},{6,4},{7,5},{8,10},{9,11},{10,... | collective-permute-start | bytes 196616 | tf_op jit(solution)/shard_map/ppermute | solution.py:22
  86.2 5.1 %collective-permute-start.28 = (bf16[128,256]{1,0:T(8,128)(2,1)S(1)}, bf16[128,256]{1,0:T(8,128)(2,1)S(1)}, u32[]{:S(2)}, u32[]{:S(2)}) collective-permute-start(bf16[128,256]{1,0:T(8,128)(2,1)S(1)} %get-tuple-element.56.after_ref.refs_0_.refs_2_), channel_id=1, source_target_pairs={{0,1},{1,0},{2,3},{3,2},{4,5},{5,4},{6,7},{7,6},{8,9},{9,8},{10,11... | collective-permute-start | bytes 196616 | tf_op jit(solution)/shard_map/ppermute | solution.py:22
  91.8 5.2 %collective-permute-start.31 = (bf16[128,256]{1,0:T(8,128)(2,1)S(1)}, bf16[128,256]{1,0:T(8,128)(2,1)S(1)}, u32[]{:S(2)}, u32[]{:S(2)}) collective-permute-start(bf16[128,256]{1,0:T(8,128)(2,1)S(1)} %get-tuple-element.57), channel_id=1, source_target_pairs={{0,24},{4,28},{8,16},{12,20},{16,8},{20,12},{24,0},{28,4},{1,25},{... | collective-permute-start | bytes 196616 | tf_op jit(solution)/shard_map/ppermute | solution.py:22
  94.2 4.3 %collective-permute-start.32 = (bf16[128,256]{1,0:T(8,128)(2,1)S(1)}, bf16[128,256]{1,0:T(8,128)(2,1)S(1)}, u32[]{:S(2)}, u32[]{:S(2)}) collective-permute-start(bf16[128,256]{1,0:T(8,128)(2,1)S(1)} %get-tuple-element.58), channel_id=1, source_target_pairs={{0,8},{4,12},{8,0},{12,4},{16,24},{20,28},{24,16},{28,20},{1,9},{5... | collective-permute-start | bytes 196616 | tf_op jit(solution)/shard_map/ppermute | solution.py:22
  94.9 4.3 %collective-permute-start.33 = (bf16[128,256]{1,0:T(8,128)(2,1)S(1)}, bf16[128,256]{1,0:T(8,128)(2,1)S(1)}, u32[]{:S(2)}, u32[]{:S(2)}) collective-permute-start(bf16[128,256]{1,0:T(8,128)(2,1)S(1)} %get-tuple-element.59), channel_id=1, source_target_pairs={{0,16},{4,20},{8,24},{12,28},{16,0},{20,4},{24,8},{28,12},{1,17},{... | collective-permute-start | bytes 196616 | tf_op jit(solution)/shard_map/ppermute | solution.py:22
  99.4 6.1 %collective-permute-start.36 = (bf16[128,256]{1,0:T(8,128)(2,1)S(1)}, bf16[128,256]{1,0:T(8,128)(2,1)S(1)}, u32[]{:S(2)}, u32[]{:S(2)}) collective-permute-start(bf16[128,256]{1,0:T(8,128)(2,1)S(1)} %get-tuple-element.60.after_ref.refs_0_.refs_1_), channel_id=1, source_target_pairs={{0,3},{1,2},{2,1},{3,0},{4,7},{5,6},{6,5},{7,4},{8,11},{9,10},{10,... | collective-permute-start | bytes 196616 | tf_op jit(solution)/shard_map/ppermute | solution.py:22
  101.5 5.6 %collective-permute-start.35 = (bf16[128,256]{1,0:T(8,128)(2,1)S(1)}, bf16[128,256]{1,0:T(8,128)(2,1)S(1)}, u32[]{:S(2)}, u32[]{:S(2)}) collective-permute-start(bf16[128,256]{1,0:T(8,128)(2,1)S(1)} %get-tuple-element.60.after_ref.refs_0_.refs_1_), channel_id=1, source_target_pairs={{0,2},{1,3},{2,0},{3,1},{4,6},{5,7},{6,4},{7,5},{8,10},{9,11},{10,... | collective-permute-start | bytes 196616 | tf_op jit(solution)/shard_map/ppermute | solution.py:22
  102.1 5.0 %collective-permute-start.34 = (bf16[128,256]{1,0:T(8,128)(2,1)S(1)}, bf16[128,256]{1,0:T(8,128)(2,1)S(1)}, u32[]{:S(2)}, u32[]{:S(2)}) collective-permute-start(bf16[128,256]{1,0:T(8,128)(2,1)S(1)} %get-tuple-element.60.after_ref.refs_0_.refs_1_), channel_id=1, source_target_pairs={{0,1},{1,0},{2,3},{3,2},{4,5},{5,4},{6,7},{7,6},{8,9},{9,8},{10,11... | collective-permute-start | bytes 196616 | tf_op jit(solution)/shard_map/ppermute | solution.py:22
  103.8 10.2 %collective-permute-start.40 = (bf16[128,384]{1,0:T(8,128)(2,1)S(1)}, bf16[128,384]{1,0:T(8,128)(2,1)S(1)}, u32[]{:S(2)}, u32[]{:S(2)}) collective-permute-start(bf16[128,384]{1,0:T(8,128)(2,1)S(1)} %pad_maximum_fusion), channel_id=1, source_target_pairs={{0,4},{4,0},{8,12},{12,8},{16,20},{20,16},{24,28},{28,24},{1,5},{5... | collective-permute-start | bytes 294920 | tf_op jit(solution)/shard_map/ppermute | solution.py:22
  107.5 5.2 %collective-permute-start.37 = (bf16[128,256]{1,0:T(8,128)(2,1)S(1)}, bf16[128,256]{1,0:T(8,128)(2,1)S(1)}, u32[]{:S(2)}, u32[]{:S(2)}) collective-permute-start(bf16[128,256]{1,0:T(8,128)(2,1)S(1)} %get-tuple-element.61), channel_id=1, source_target_pairs={{0,24},{4,28},{8,16},{12,20},{16,8},{20,12},{24,0},{28,4},{1,25},{... | collective-permute-start | bytes 196616 | tf_op jit(solution)/shard_map/ppermute | solution.py:22
  109.4 4.3 %collective-permute-start.38 = (bf16[128,256]{1,0:T(8,128)(2,1)S(1)}, bf16[128,256]{1,0:T(8,128)(2,1)S(1)}, u32[]{:S(2)}, u32[]{:S(2)}) collective-permute-start(bf16[128,256]{1,0:T(8,128)(2,1)S(1)} %get-tuple-element.62), channel_id=1, source_target_pairs={{0,8},{4,12},{8,0},{12,4},{16,24},{20,28},{24,16},{28,20},{1,9},{5... | collective-permute-start | bytes 196616 | tf_op jit(solution)/shard_map/ppermute | solution.py:22
  109.5 4.3 %collective-permute-start.39 = (bf16[128,256]{1,0:T(8,128)(2,1)S(1)}, bf16[128,256]{1,0:T(8,128)(2,1)S(1)}, u32[]{:S(2)}, u32[]{:S(2)}) collective-permute-start(bf16[128,256]{1,0:T(8,128)(2,1)S(1)} %get-tuple-element.63), channel_id=1, source_target_pairs={{0,16},{4,20},{8,24},{12,28},{16,0},{20,4},{24,8},{28,12},{1,17},{... | collective-permute-start | bytes 196616 | tf_op jit(solution)/shard_map/ppermute | solution.py:22
  113.9 1.3 %collective-permute-start.41 = (bf16[128,128]{1,0:T(8,128)(2,1)S(1)}, bf16[128,128]{1,0:T(8,128)(2,1)S(1)}, u32[]{:S(2)}, u32[]{:S(2)}) collective-permute-start(bf16[128,128]{1,0:T(8,128)(2,1)S(1)} %get-tuple-element.68), channel_id=1, source_target_pairs={{0,4},{4,0},{8,12},{12,8},{16,20},{20,16},{24,28},{28,24},{1,5},{5... | collective-permute-start | bytes 98312 | tf_op jit(solution)/shard_map/ppermute | solution.py:22

commit v9 on v8

--- a/solution.py
+++ b/solution.py
@@ -12,6 +12,7 @@
 LANES = 128
 ROW_ORDER = (3, 1, 2)
 COL_ORDER = (3, 1, 2)
+TURN_ORDER = (2, 3, 1)
 VMEM_BYTES = 16 * 1024 * 1024
 F32 = jnp.float32
 BF16 = jnp.bfloat16
@@ -373,7 +374,7 @@
     solution, leaving = [None] * NLEV, [None] * NLEV
     solution[NLEV - 1], leaving[NLEV - 1] = upper, theirs
     for level in range(NLEV - 2, -1, -1):
-        sent = {m: swap(upper, "col", m) for m in reversed(issue_order(cols, COL_ORDER))}
+        sent = {m: swap(upper, "col", m) for m in reversed(issue_order(cols, TURN_ORDER))}
         pieces = [upper] + [sent[m] for m in range(1, cols)]
         tiles = fetch(own[level], par[level], upper)
         far = list(range(1, groups))

time: 116 us -> 116 us (level)
  no operation moved by 1% of the time
where the time goes in v9:
time: 116 us
  starting transfers between devices  56.6 us (49%)
  waiting for transfers between devices  40.7 us (35%)
  Pallas kernels  13.2 us (11%)
  local copies, waits for them, and re-layouts  3.72 us (3%)
  other arithmetic  1.44 us (1%)
    ppermute x42, starting transfers between devices, swap(): return lax.ppermute(value, axis, [(i, i ^ distance) for i in range(count)])  49.6 us
    ppermute x42, waiting for transfers between devices, swap(): return lax.ppermute(value, axis, [(i, i ^ distance) for i in range(count)])  34 us
    pallas_call x22, Pallas kernels, call(): pl.pallas_call(body, out_shape=out_shape, in_specs=in_specs, out_specs=ou...  9.71 us
    all_to_all x1, starting transfers between devices, per_device(): lax.all_to_all(sending, ('row', 'col'), split_axis=0, concat_axis=0, tile...  6.97 us
    all_to_all x1, waiting for transfers between devices, per_device(): lax.all_to_all(sending, ('row', 'col'), split_axis=0, concat_axis=0, tile...  6.71 us
    slice x1, local copies, waits for them, and re-layouts, per_device(): tile = lower_blocks[level, 0, :, :, 0]  3.08 us
  transfers between devices with their start and end apart: 43, of which 33 were waited for; matrix products, arithmetic and copies ran while one was open for 4% of the time, Pallas kernels for 9%

profile of v9, /device:TPU:0, one launch (start us, length us, event | category | flops | bytes accessed | tf_op | source)
XLA Modules:
  0.0 115.9 jit_solution(14038686617609800076)
XLA Ops:
  0.5 2.3 %shard_map.55 = bf16[32,40,128]{2,1,0:T(8,128)(2,1)} custom-call(f32[512,256]{1,0:T(8,128)} %rhs_hbm.1, s32[1,512]{1,0:T(1,128)} %bitcast.48), custom_call_target="tpu_custom_call" | custom-call | flops 134217728 | bytes 526336 | tf_op jit(solution)/shard_map/pallas_call | solution.py:40
  2.7 7.0 %all-to-all-start = ((bf16[32,40,128]{2,1,0:T(8,128)(2,1)}), bf16[32,40,128]{2,1,0:T(8,128)(2,1)S(1)}, u32[]{:S(2)}, u32[]{:S(2)}) async-start(bf16[32,40,128]{2,1,0:T(8,128)(2,1)} %shard_map.55), calls=%async_computation | async-start | bytes 655360 | tf_op jit(solution)/shard_map/all_to_all | solution.py:321
  10.4 3.1 %fusion = (bf16[1,1,4,128,1,8,128]{6,5,4,3,2,1,0:T(8,128)(2,1)S(1)}, bf16[1,1,4,128,1,8,128]{6,5,4,3,2,1,0:T(8,128)(2,1)S(1)}, bf16[1,1,4,128,1,8,128]{6,5,4,3,2,1,0:T(8,128)(2,1)}) fusion(bf16[3,1,4,128,1,8,128]{6,5,4,3,2,1,0:T(8,128)(2,1)} %param.8), kind=kLoop, calls=%fused_computation.7 | loop fusion | bytes 6291456 | tf_op jit(solution)/shard_map/slice | solution.py:303
  14.0 6.7 %all-to-all-done.arrived_ref = bf16[32,40,128]{2,1,0:T(8,128)(2,1)S(1)} async-done(((bf16[32,40,128]{2,1,0:T(8,128)(2,1)}), bf16[32,40,128]{2,1,0:T(8,128)(2,1)S(1)}, u32[]{:S(2)}, u32[]{:S(2)}) %all-to-all-start) | async-done | bytes 327712 | tf_op jit(solution)/shard_map/all_to_all | solution.py:321
  22.1 1.1 collective-permute-start.4
  23.2 1.5 %collective-permute-start.3 = (bf16[128,256]{1,0:T(8,128)(2,1)S(1)}, bf16[128,256]{1,0:T(8,128)(2,1)S(1)}, u32[]{:S(2)}, u32[]{:S(2)}) collective-permute-start(bf16[128,256]{1,0:T(8,128)(2,1)S(1)} %shard_map.56.after_ref.refs_0_.solved_ref), channel_id=1, source_target_pairs={{0,16},{4,20},{8,24},{12,28},{16,0},{20,4},{24,8},{28,12},{1,17},{... | collective-permute-start | bytes 196616 | tf_op jit(solution)/shard_map/ppermute | solution.py:23
  24.6 1.0 collective-permute-start.2
  26.8 0.9 collective-permute-done.4.refs_3_
  29.3 1.8 %collective-permute-start.5 = (bf16[128,256]{1,0:T(8,128)(2,1)S(1)}, bf16[128,256]{1,0:T(8,128)(2,1)S(1)}, u32[]{:S(2)}, u32[]{:S(2)}) collective-permute-start(bf16[128,256]{1,0:T(8,128)(2,1)S(1)} %get-tuple-element.39), channel_id=1, source_target_pairs={{0,3},{1,2},{2,1},{3,0},{4,7},{5,6},{6,5},{7,4},{8,11},{9,10},{10,... | collective-permute-start | bytes 196616 | tf_op jit(solution)/shard_map/ppermute | solution.py:23
  31.1 2.7 %collective-permute-start.7 = (bf16[128,256]{1,0:T(8,128)(2,1)S(1)}, bf16[128,256]{1,0:T(8,128)(2,1)S(1)}, u32[]{:S(2)}, u32[]{:S(2)}) collective-permute-start(bf16[128,256]{1,0:T(8,128)(2,1)S(1)} %get-tuple-element.41), channel_id=1, source_target_pairs={{0,2},{1,3},{2,0},{3,1},{4,6},{5,7},{6,4},{7,5},{8,10},{9,11},{10,... | collective-permute-start | bytes 196616 | tf_op jit(solution)/shard_map/ppermute | solution.py:23
  35.9 1.4 %collective-permute-done.6.refs_1_ = bf16[128,256]{1,0:T(8,128)(2,1)S(1)} collective-permute-done((bf16[128,256]{1,0:T(8,128)(2,1)S(1)}, bf16[128,256]{1,0:T(8,128)(2,1)S(1)}, u32[]{:S(2)}, u32[]{:S(2)}) %collective-permute-start.6) | collective-permute-done | bytes 65568 | tf_op jit(solution)/shard_map/ppermute | solution.py:23
  38.7 2.3 %collective-permute-start.10 = (bf16[128,256]{1,0:T(8,128)(2,1)S(1)}, bf16[128,256]{1,0:T(8,128)(2,1)S(1)}, u32[]{:S(2)}, u32[]{:S(2)}) collective-permute-start(bf16[128,256]{1,0:T(8,128)(2,1)S(1)} %shard_map.61.after_ref.refs_0_.solved_ref), channel_id=1, source_target_pairs={{0,16},{4,20},{8,24},{12,28},{16,0},{20,4},{24,8},{28,12},{1,17},{... | collective-permute-start | bytes 196616 | tf_op jit(solution)/shard_map/ppermute | solution.py:23
  42.4 1.6 %collective-permute-done.11.refs_3_ = bf16[128,256]{1,0:T(8,128)(2,1)S(1)} collective-permute-done((bf16[128,256]{1,0:T(8,128)(2,1)S(1)}, bf16[128,256]{1,0:T(8,128)(2,1)S(1)}, u32[]{:S(2)}, u32[]{:S(2)}) %collective-permute-start.11) | collective-permute-done | bytes 65568 | tf_op jit(solution)/shard_map/ppermute | solution.py:23
  45.7 1.2 %collective-permute-start.12 = (bf16[128,256]{1,0:T(8,128)(2,1)S(1)}, bf16[128,256]{1,0:T(8,128)(2,1)S(1)}, u32[]{:S(2)}, u32[]{:S(2)}) collective-permute-start(bf16[128,256]{1,0:T(8,128)(2,1)S(1)} %get-tuple-element.44), channel_id=1, source_target_pairs={{0,3},{1,2},{2,1},{3,0},{4,7},{5,6},{6,5},{7,4},{8,11},{9,10},{10,... | collective-permute-start | bytes 196616 | tf_op jit(solution)/shard_map/ppermute | solution.py:23
  47.1 3.1 %collective-permute-start.14 = (bf16[128,256]{1,0:T(8,128)(2,1)S(1)}, bf16[128,256]{1,0:T(8,128)(2,1)S(1)}, u32[]{:S(2)}, u32[]{:S(2)}) collective-permute-start(bf16[128,256]{1,0:T(8,128)(2,1)S(1)} %get-tuple-element.46), channel_id=1, source_target_pairs={{0,2},{1,3},{2,0},{3,1},{4,6},{5,7},{6,4},{7,5},{8,10},{9,11},{10,... | collective-permute-start | bytes 196616 | tf_op jit(solution)/shard_map/ppermute | solution.py:23
  50.5 2.1 %collective-permute-done.12.refs_0_ = bf16[128,256]{1,0:T(8,128)(2,1)S(1)} collective-permute-done((bf16[128,256]{1,0:T(8,128)(2,1)S(1)}, bf16[128,256]{1,0:T(8,128)(2,1)S(1)}, u32[]{:S(2)}, u32[]{:S(2)}) %collective-permute-start.12) | collective-permute-done | bytes 65568 | tf_op jit(solution)/shard_map/ppermute | solution.py:23
  53.4 1.4 %collective-permute-start.18 = (bf16[128,256]{1,0:T(8,128)(2,1)S(1)}, bf16[128,256]{1,0:T(8,128)(2,1)S(1)}, u32[]{:S(2)}, u32[]{:S(2)}) collective-permute-start(bf16[128,256]{1,0:T(8,128)(2,1)S(1)} %shard_map.65.after_ref.refs_0_.solved_ref), channel_id=1, source_target_pairs={{0,24},{4,28},{8,16},{12,20},{16,8},{20,12},{24,0},{28,4},{1,25},{... | collective-permute-start | bytes 196616 | tf_op jit(solution)/shard_map/ppermute | solution.py:23
  54.8 1.5 %collective-permute-start.17 = (bf16[128,256]{1,0:T(8,128)(2,1)S(1)}, bf16[128,256]{1,0:T(8,128)(2,1)S(1)}, u32[]{:S(2)}, u32[]{:S(2)}) collective-permute-start(bf16[128,256]{1,0:T(8,128)(2,1)S(1)} %shard_map.65.after_ref.refs_0_.solved_ref), channel_id=1, source_target_pairs={{0,16},{4,20},{8,24},{12,28},{16,0},{20,4},{24,8},{28,12},{1,17},{... | collective-permute-start | bytes 196616 | tf_op jit(solution)/shard_map/ppermute | solution.py:23
  57.7 1.5 %collective-permute-done.18.refs_3_ = bf16[128,256]{1,0:T(8,128)(2,1)S(1)} collective-permute-done((bf16[128,256]{1,0:T(8,128)(2,1)S(1)}, bf16[128,256]{1,0:T(8,128)(2,1)S(1)}, u32[]{:S(2)}, u32[]{:S(2)}) %collective-permute-start.18) | collective-permute-done | bytes 65568 | tf_op jit(solution)/shard_map/ppermute | solution.py:23
  59.6 1.0 collective-permute-done.16.refs_1_
  61.0 2.0 %collective-permute-start.19 = (bf16[128,256]{1,0:T(8,128)(2,1)S(1)}, bf16[128,256]{1,0:T(8,128)(2,1)S(1)}, u32[]{:S(2)}, u32[]{:S(2)}) collective-permute-start(bf16[128,256]{1,0:T(8,128)(2,1)S(1)} %get-tuple-element.49), channel_id=1, source_target_pairs={{0,3},{1,2},{2,1},{3,0},{4,7},{5,6},{6,5},{7,4},{8,11},{9,10},{10,... | collective-permute-start | bytes 196616 | tf_op jit(solution)/shard_map/ppermute | solution.py:23
  63.3 2.1 %collective-permute-start.21 = (bf16[128,256]{1,0:T(8,128)(2,1)S(1)}, bf16[128,256]{1,0:T(8,128)(2,1)S(1)}, u32[]{:S(2)}, u32[]{:S(2)}) collective-permute-start(bf16[128,256]{1,0:T(8,128)(2,1)S(1)} %get-tuple-element.51), channel_id=1, source_target_pairs={{0,2},{1,3},{2,0},{3,1},{4,6},{5,7},{6,4},{7,5},{8,10},{9,11},{10,... | collective-permute-start | bytes 196616 | tf_op jit(solution)/shard_map/ppermute | solution.py:23
  65.7 1.5 %collective-permute-done.19.refs_0_ = bf16[128,256]{1,0:T(8,128)(2,1)S(1)} collective-permute-done((bf16[128,256]{1,0:T(8,128)(2,1)S(1)}, bf16[128,256]{1,0:T(8,128)(2,1)S(1)}, u32[]{:S(2)}, u32[]{:S(2)}) %collective-permute-start.19) | collective-permute-done | bytes 65568 | tf_op jit(solution)/shard_map/ppermute | solution.py:23
  67.8 1.1 collective-permute-done.21.refs_2_
  69.3 1.6 %collective-permute-start.24 = (bf16[128,256]{1,0:T(8,128)(2,1)S(1)}, bf16[128,256]{1,0:T(8,128)(2,1)S(1)}, u32[]{:S(2)}, u32[]{:S(2)}) collective-permute-start(bf16[128,256]{1,0:T(8,128)(2,1)S(1)} %get-tuple-element.52.after_ref.refs_0_.refs_3_), channel_id=1, source_target_pairs={{0,3},{1,2},{2,1},{3,0},{4,7},{5,6},{6,5},{7,4},{8,11},{9,10},{10,... | collective-permute-start | bytes 196616 | tf_op jit(solution)/shard_map/ppermute | solution.py:23
  70.9 1.7 %collective-permute-start.23 = (bf16[128,256]{1,0:T(8,128)(2,1)S(1)}, bf16[128,256]{1,0:T(8,128)(2,1)S(1)}, u32[]{:S(2)}, u32[]{:S(2)}) collective-permute-start(bf16[128,256]{1,0:T(8,128)(2,1)S(1)} %get-tuple-element.52.after_ref.refs_0_.refs_3_), channel_id=1, source_target_pairs={{0,2},{1,3},{2,0},{3,1},{4,6},{5,7},{6,4},{7,5},{8,10},{9,11},{10,... | collective-permute-start | bytes 196616 | tf_op jit(solution)/shard_map/ppermute | solution.py:23
  72.6 1.2 %collective-permute-start.22 = (bf16[128,256]{1,0:T(8,128)(2,1)S(1)}, bf16[128,256]{1,0:T(8,128)(2,1)S(1)}, u32[]{:S(2)}, u32[]{:S(2)}) collective-permute-start(bf16[128,256]{1,0:T(8,128)(2,1)S(1)} %get-tuple-element.52.after_ref.refs_0_.refs_3_), channel_id=1, source_target_pairs={{0,1},{1,0},{2,3},{3,2},{4,5},{5,4},{6,7},{7,6},{8,9},{9,8},{10,11... | collective-permute-start | bytes 196616 | tf_op jit(solution)/shard_map/ppermute | solution.py:23
  74.0 1.5 %collective-permute-done.24.refs_3_ = bf16[128,256]{1,0:T(8,128)(2,1)S(1)} collective-permute-done((bf16[128,256]{1,0:T(8,128)(2,1)S(1)}, bf16[128,256]{1,0:T(8,128)(2,1)S(1)}, u32[]{:S(2)}, u32[]{:S(2)}) %collective-permute-start.24) | collective-permute-done | bytes 65568 | tf_op jit(solution)/shard_map/ppermute | solution.py:23
  75.5 1.5 %collective-permute-done.23.refs_2_ = bf16[128,256]{1,0:T(8,128)(2,1)S(1)} collective-permute-done((bf16[128,256]{1,0:T(8,128)(2,1)S(1)}, bf16[128,256]{1,0:T(8,128)(2,1)S(1)}, u32[]{:S(2)}, u32[]{:S(2)}) %collective-permute-start.23) | collective-permute-done | bytes 65568 | tf_op jit(solution)/shard_map/ppermute | solution.py:23
  77.4 2.0 %collective-permute-start.25 = (bf16[128,256]{1,0:T(8,128)(2,1)S(1)}, bf16[128,256]{1,0:T(8,128)(2,1)S(1)}, u32[]{:S(2)}, u32[]{:S(2)}) collective-permute-start(bf16[128,256]{1,0:T(8,128)(2,1)S(1)} %get-tuple-element.53), channel_id=1, source_target_pairs={{0,24},{4,28},{8,16},{12,20},{16,8},{20,12},{24,0},{28,4},{1,25},{... | collective-permute-start | bytes 196616 | tf_op jit(solution)/shard_map/ppermute | solution.py:23
  79.4 1.6 %collective-permute-start.27 = (bf16[128,256]{1,0:T(8,128)(2,1)S(1)}, bf16[128,256]{1,0:T(8,128)(2,1)S(1)}, u32[]{:S(2)}, u32[]{:S(2)}) collective-permute-start(bf16[128,256]{1,0:T(8,128)(2,1)S(1)} %get-tuple-element.55), channel_id=1, source_target_pairs={{0,16},{4,20},{8,24},{12,28},{16,0},{20,4},{24,8},{28,12},{1,17},{... | collective-permute-start | bytes 196616 | tf_op jit(solution)/shard_map/ppermute | solution.py:23
  81.2 1.4 %collective-permute-done.25.refs_0_ = bf16[128,256]{1,0:T(8,128)(2,1)S(1)} collective-permute-done((bf16[128,256]{1,0:T(8,128)(2,1)S(1)}, bf16[128,256]{1,0:T(8,128)(2,1)S(1)}, u32[]{:S(2)}, u32[]{:S(2)}) %collective-permute-start.25) | collective-permute-done | bytes 65568 | tf_op jit(solution)/shard_map/ppermute | solution.py:23
  82.6 1.0 collective-permute-done.26.refs_1_
  83.8 2.0 %collective-permute-start.30 = (bf16[128,256]{1,0:T(8,128)(2,1)S(1)}, bf16[128,256]{1,0:T(8,128)(2,1)S(1)}, u32[]{:S(2)}, u32[]{:S(2)}) collective-permute-start(bf16[128,256]{1,0:T(8,128)(2,1)S(1)} %get-tuple-element.56.after_ref.refs_0_.refs_2_), channel_id=1, source_target_pairs={{0,3},{1,2},{2,1},{3,0},{4,7},{5,6},{6,5},{7,4},{8,11},{9,10},{10,... | collective-permute-start | bytes 196616 | tf_op jit(solution)/shard_map/ppermute | solution.py:23
  86.2 2.1 %collective-permute-start.28 = (bf16[128,256]{1,0:T(8,128)(2,1)S(1)}, bf16[128,256]{1,0:T(8,128)(2,1)S(1)}, u32[]{:S(2)}, u32[]{:S(2)}) collective-permute-start(bf16[128,256]{1,0:T(8,128)(2,1)S(1)} %get-tuple-element.56.after_ref.refs_0_.refs_2_), channel_id=1, source_target_pairs={{0,1},{1,0},{2,3},{3,2},{4,5},{5,4},{6,7},{7,6},{8,9},{9,8},{10,11... | collective-permute-start | bytes 196616 | tf_op jit(solution)/shard_map/ppermute | solution.py:23
  88.5 1.4 %collective-permute-done.30.refs_3_ = bf16[128,256]{1,0:T(8,128)(2,1)S(1)} collective-permute-done((bf16[128,256]{1,0:T(8,128)(2,1)S(1)}, bf16[128,256]{1,0:T(8,128)(2,1)S(1)}, u32[]{:S(2)}, u32[]{:S(2)}) %collective-permute-start.30) | collective-permute-done | bytes 65568 | tf_op jit(solution)/shard_map/ppermute | solution.py:23
  90.0 1.4 %collective-permute-done.29.refs_2_ = bf16[128,256]{1,0:T(8,128)(2,1)S(1)} collective-permute-done((bf16[128,256]{1,0:T(8,128)(2,1)S(1)}, bf16[128,256]{1,0:T(8,128)(2,1)S(1)}, u32[]{:S(2)}, u32[]{:S(2)}) %collective-permute-start.29) | collective-permute-done | bytes 65568 | tf_op jit(solution)/shard_map/ppermute | solution.py:23
  91.8 2.4 %collective-permute-start.31 = (bf16[128,256]{1,0:T(8,128)(2,1)S(1)}, bf16[128,256]{1,0:T(8,128)(2,1)S(1)}, u32[]{:S(2)}, u32[]{:S(2)}) collective-permute-start(bf16[128,256]{1,0:T(8,128)(2,1)S(1)} %get-tuple-element.57), channel_id=1, source_target_pairs={{0,24},{4,28},{8,16},{12,20},{16,8},{20,12},{24,0},{28,4},{1,25},{... | collective-permute-start | bytes 196616 | tf_op jit(solution)/shard_map/ppermute | solution.py:23
  95.6 1.4 %collective-permute-done.31.refs_0_ = bf16[128,256]{1,0:T(8,128)(2,1)S(1)} collective-permute-done((bf16[128,256]{1,0:T(8,128)(2,1)S(1)}, bf16[128,256]{1,0:T(8,128)(2,1)S(1)}, u32[]{:S(2)}, u32[]{:S(2)}) %collective-permute-start.31) | collective-permute-done | bytes 65568 | tf_op jit(solution)/shard_map/ppermute | solution.py:23
  97.0 1.4 %collective-permute-done.32.refs_1_ = bf16[128,256]{1,0:T(8,128)(2,1)S(1)} collective-permute-done((bf16[128,256]{1,0:T(8,128)(2,1)S(1)}, bf16[128,256]{1,0:T(8,128)(2,1)S(1)}, u32[]{:S(2)}, u32[]{:S(2)}) %collective-permute-start.32) | collective-permute-done | bytes 65568 | tf_op jit(solution)/shard_map/ppermute | solution.py:23
  99.4 2.1 %collective-permute-start.36 = (bf16[128,256]{1,0:T(8,128)(2,1)S(1)}, bf16[128,256]{1,0:T(8,128)(2,1)S(1)}, u32[]{:S(2)}, u32[]{:S(2)}) collective-permute-start(bf16[128,256]{1,0:T(8,128)(2,1)S(1)} %get-tuple-element.60.after_ref.refs_0_.refs_1_), channel_id=1, source_target_pairs={{0,3},{1,2},{2,1},{3,0},{4,7},{5,6},{6,5},{7,4},{8,11},{9,10},{10,... | collective-permute-start | bytes 196616 | tf_op jit(solution)/shard_map/ppermute | solution.py:23
  102.1 1.7 %collective-permute-start.34 = (bf16[128,256]{1,0:T(8,128)(2,1)S(1)}, bf16[128,256]{1,0:T(8,128)(2,1)S(1)}, u32[]{:S(2)}, u32[]{:S(2)}) collective-permute-start(bf16[128,256]{1,0:T(8,128)(2,1)S(1)} %get-tuple-element.60.after_ref.refs_0_.refs_1_), channel_id=1, source_target_pairs={{0,1},{1,0},{2,3},{3,2},{4,5},{5,4},{6,7},{7,6},{8,9},{9,8},{10,11... | collective-permute-start | bytes 196616 | tf_op jit(solution)/shard_map/ppermute | solution.py:23
  104.2 1.3 %collective-permute-done.36.refs_3_ = bf16[128,256]{1,0:T(8,128)(2,1)S(1)} collective-permute-done((bf16[128,256]{1,0:T(8,128)(2,1)S(1)}, bf16[128,256]{1,0:T(8,128)(2,1)S(1)}, u32[]{:S(2)}, u32[]{:S(2)}) %collective-permute-start.36) | collective-permute-done | bytes 65568 | tf_op jit(solution)/shard_map/ppermute | solution.py:23
  105.5 1.6 %collective-permute-done.35.refs_2_ = bf16[128,256]{1,0:T(8,128)(2,1)S(1)} collective-permute-done((bf16[128,256]{1,0:T(8,128)(2,1)S(1)}, bf16[128,256]{1,0:T(8,128)(2,1)S(1)}, u32[]{:S(2)}, u32[]{:S(2)}) %collective-permute-start.35) | collective-permute-done | bytes 65568 | tf_op jit(solution)/shard_map/ppermute | solution.py:23
  107.5 1.9 %collective-permute-start.37 = (bf16[128,256]{1,0:T(8,128)(2,1)S(1)}, bf16[128,256]{1,0:T(8,128)(2,1)S(1)}, u32[]{:S(2)}, u32[]{:S(2)}) collective-permute-start(bf16[128,256]{1,0:T(8,128)(2,1)S(1)} %get-tuple-element.61), channel_id=1, source_target_pairs={{0,24},{4,28},{8,16},{12,20},{16,8},{20,12},{24,0},{28,4},{1,25},{... | collective-permute-start | bytes 196616 | tf_op jit(solution)/shard_map/ppermute | solution.py:23
  109.5 1.6 %collective-permute-start.39 = (bf16[128,256]{1,0:T(8,128)(2,1)S(1)}, bf16[128,256]{1,0:T(8,128)(2,1)S(1)}, u32[]{:S(2)}, u32[]{:S(2)}) collective-permute-start(bf16[128,256]{1,0:T(8,128)(2,1)S(1)} %get-tuple-element.63), channel_id=1, source_target_pairs={{0,16},{4,20},{8,24},{12,28},{16,0},{20,4},{24,8},{28,12},{1,17},{... | collective-permute-start | bytes 196616 | tf_op jit(solution)/shard_map/ppermute | solution.py:23
  111.4 1.4 %collective-permute-done.37.refs_0_ = bf16[128,256]{1,0:T(8,128)(2,1)S(1)} collective-permute-done((bf16[128,256]{1,0:T(8,128)(2,1)S(1)}, bf16[128,256]{1,0:T(8,128)(2,1)S(1)}, u32[]{:S(2)}, u32[]{:S(2)}) %collective-permute-start.37) | collective-permute-done | bytes 65568 | tf_op jit(solution)/shard_map/ppermute | solution.py:23
  112.8 0.9 collective-permute-done.38.refs_1_
  (83 shorter events, 25.7 us)
Async XLA Ops:
  0.0 14.0 %collective-permute-start = (bf16[4,128,128]{2,1,0:T(8,128)(2,1)}, bf16[4,128,128]{2,1,0:T(8,128)(2,1)S(1)}, u32[]{:S(2)}, u32[]{:S(2)}) collective-permute-start(bf16[4,128,128]{2,1,0:T(8,128)(2,1)} %bitcast.33), channel_id=1, source_target_pairs={{0,4},{4,0},{8,12},{12,8},{16,20},{20,16},{24,28},{28,24},{1,5},{5... | collective-permute-start | bytes 393224 | tf_op jit(solution)/shard_map/ppermute | solution.py:23
  2.7 18.0 %all-to-all-start = ((bf16[32,40,128]{2,1,0:T(8,128)(2,1)}), bf16[32,40,128]{2,1,0:T(8,128)(2,1)S(1)}, u32[]{:S(2)}, u32[]{:S(2)}) async-start(bf16[32,40,128]{2,1,0:T(8,128)(2,1)} %shard_map.55), calls=%async_computation | async-start | bytes 655360 | tf_op jit(solution)/shard_map/all_to_all | solution.py:321
  13.5 7.2 %copy-start = (bf16[4,1,128,128]{3,2,1,0:T(8,128)(2,1)S(1)}, bf16[4,1,128,128]{3,2,1,0:T(8,128)(2,1)}, u32[]{:S(2)}) copy-start(bf16[4,1,128,128]{3,2,1,0:T(8,128)(2,1)} %param.7) | copy-start | bytes 393220
  20.7 5.1 %copy-start.1 = (bf16[1,1,4,128,1,8,128]{6,5,4,3,2,1,0:T(8,128)(2,1)S(1)}, bf16[1,1,4,128,1,8,128]{6,5,4,3,2,1,0:T(8,128)(2,1)}, u32[]{:S(2)}) copy-start(bf16[1,1,4,128,1,8,128]{6,5,4,3,2,1,0:T(8,128)(2,1)} %get-tuple-element.71) | copy-start | bytes 3145732
  21.2 4.9 %collective-permute-start.1 = (bf16[512,1024]{1,0:T(8,128)(2,1)S(1)}, bf16[512,1024]{1,0:T(8,128)(2,1)S(1)}, u32[]{:S(2)}, u32[]{:S(2)}) collective-permute-start(bf16[512,1024]{1,0:T(8,128)(2,1)S(1)} %bitcast_multiply_fusion.2.own_ref), channel_id=1, source_target_pairs={{0,4},{4,0},{8,12},{12,8},{16,20},{20,16},{24,28},{28,24},{1,5},{5... | collective-permute-start | bytes 3145736 | tf_op jit(solution)/shard_map/ppermute | solution.py:23
  22.1 5.6 %collective-permute-start.4 = (bf16[128,256]{1,0:T(8,128)(2,1)S(1)}, bf16[128,256]{1,0:T(8,128)(2,1)S(1)}, u32[]{:S(2)}, u32[]{:S(2)}) collective-permute-start(bf16[128,256]{1,0:T(8,128)(2,1)S(1)} %shard_map.56.after_ref.refs_0_.solved_ref), channel_id=1, source_target_pairs={{0,24},{4,28},{8,16},{12,20},{16,8},{20,12},{24,0},{28,4},{1,25},{... | collective-permute-start | bytes 196616 | tf_op jit(solution)/shard_map/ppermute | solution.py:23
  23.2 5.3 %collective-permute-start.3 = (bf16[128,256]{1,0:T(8,128)(2,1)S(1)}, bf16[128,256]{1,0:T(8,128)(2,1)S(1)}, u32[]{:S(2)}, u32[]{:S(2)}) collective-permute-start(bf16[128,256]{1,0:T(8,128)(2,1)S(1)} %shard_map.56.after_ref.refs_0_.solved_ref), channel_id=1, source_target_pairs={{0,16},{4,20},{8,24},{12,28},{16,0},{20,4},{24,8},{28,12},{1,17},{... | collective-permute-start | bytes 196616 | tf_op jit(solution)/shard_map/ppermute | solution.py:23
  24.6 4.3 %collective-permute-start.2 = (bf16[128,256]{1,0:T(8,128)(2,1)S(1)}, bf16[128,256]{1,0:T(8,128)(2,1)S(1)}, u32[]{:S(2)}, u32[]{:S(2)}) collective-permute-start(bf16[128,256]{1,0:T(8,128)(2,1)S(1)} %shard_map.56.after_ref.refs_0_.solved_ref), channel_id=1, source_target_pairs={{0,8},{4,12},{8,0},{12,4},{16,24},{20,28},{24,16},{28,20},{1,9},{5... | collective-permute-start | bytes 196616 | tf_op jit(solution)/shard_map/ppermute | solution.py:23
  26.1 15.6 %collective-permute-start.8 = (bf16[512,1024]{1,0:T(8,128)(2,1)S(1)}, bf16[512,1024]{1,0:T(8,128)(2,1)S(1)}, u32[]{:S(2)}, u32[]{:S(2)}) collective-permute-start(bf16[512,1024]{1,0:T(8,128)(2,1)S(1)} %bitcast_multiply_fusion.1.own_ref), channel_id=1, source_target_pairs={{0,4},{4,0},{8,12},{12,8},{16,20},{20,16},{24,28},{28,24},{1,5},{5... | collective-permute-start | bytes 3145736 | tf_op jit(solution)/shard_map/ppermute | solution.py:23
  29.3 6.5 %collective-permute-start.5 = (bf16[128,256]{1,0:T(8,128)(2,1)S(1)}, bf16[128,256]{1,0:T(8,128)(2,1)S(1)}, u32[]{:S(2)}, u32[]{:S(2)}) collective-permute-start(bf16[128,256]{1,0:T(8,128)(2,1)S(1)} %get-tuple-element.39), channel_id=1, source_target_pairs={{0,3},{1,2},{2,1},{3,0},{4,7},{5,6},{6,5},{7,4},{8,11},{9,10},{10,... | collective-permute-start | bytes 196616 | tf_op jit(solution)/shard_map/ppermute | solution.py:23
  31.1 6.2 %collective-permute-start.6 = (bf16[128,256]{1,0:T(8,128)(2,1)S(1)}, bf16[128,256]{1,0:T(8,128)(2,1)S(1)}, u32[]{:S(2)}, u32[]{:S(2)}) collective-permute-start(bf16[128,256]{1,0:T(8,128)(2,1)S(1)} %get-tuple-element.40), channel_id=1, source_target_pairs={{0,1},{1,0},{2,3},{3,2},{4,5},{5,4},{6,7},{7,6},{8,9},{9,8},{10,11... | collective-permute-start | bytes 196616 | tf_op jit(solution)/shard_map/ppermute | solution.py:23
  31.1 6.8 %collective-permute-start.7 = (bf16[128,256]{1,0:T(8,128)(2,1)S(1)}, bf16[128,256]{1,0:T(8,128)(2,1)S(1)}, u32[]{:S(2)}, u32[]{:S(2)}) collective-permute-start(bf16[128,256]{1,0:T(8,128)(2,1)S(1)} %get-tuple-element.41), channel_id=1, source_target_pairs={{0,2},{1,3},{2,0},{3,1},{4,6},{5,7},{6,4},{7,5},{8,10},{9,11},{10,... | collective-permute-start | bytes 196616 | tf_op jit(solution)/shard_map/ppermute | solution.py:23
  38.0 18.9 %collective-permute-start.15 = (bf16[512,1024]{1,0:T(8,128)(2,1)S(1)}, bf16[512,1024]{1,0:T(8,128)(2,1)S(1)}, u32[]{:S(2)}, u32[]{:S(2)}) collective-permute-start(bf16[512,1024]{1,0:T(8,128)(2,1)S(1)} %bitcast_multiply_fusion.own_ref), channel_id=1, source_target_pairs={{0,4},{4,0},{8,12},{12,8},{16,20},{20,16},{24,28},{28,24},{1,5},{5... | collective-permute-start | bytes 3145736 | tf_op jit(solution)/shard_map/ppermute | solution.py:23
  38.1 5.9 %collective-permute-start.11 = (bf16[128,256]{1,0:T(8,128)(2,1)S(1)}, bf16[128,256]{1,0:T(8,128)(2,1)S(1)}, u32[]{:S(2)}, u32[]{:S(2)}) collective-permute-start(bf16[128,256]{1,0:T(8,128)(2,1)S(1)} %shard_map.61.after_ref.refs_0_.solved_ref), channel_id=1, source_target_pairs={{0,24},{4,28},{8,16},{12,20},{16,8},{20,12},{24,0},{28,4},{1,25},{... | collective-permute-start | bytes 196616 | tf_op jit(solution)/shard_map/ppermute | solution.py:23
  38.7 6.2 %collective-permute-start.10 = (bf16[128,256]{1,0:T(8,128)(2,1)S(1)}, bf16[128,256]{1,0:T(8,128)(2,1)S(1)}, u32[]{:S(2)}, u32[]{:S(2)}) collective-permute-start(bf16[128,256]{1,0:T(8,128)(2,1)S(1)} %shard_map.61.after_ref.refs_0_.solved_ref), channel_id=1, source_target_pairs={{0,16},{4,20},{8,24},{12,28},{16,0},{20,4},{24,8},{28,12},{1,17},{... | collective-permute-start | bytes 196616 | tf_op jit(solution)/shard_map/ppermute | solution.py:23
  41.0 4.3 %collective-permute-start.9 = (bf16[128,256]{1,0:T(8,128)(2,1)S(1)}, bf16[128,256]{1,0:T(8,128)(2,1)S(1)}, u32[]{:S(2)}, u32[]{:S(2)}) collective-permute-start(bf16[128,256]{1,0:T(8,128)(2,1)S(1)} %shard_map.61.after_ref.refs_0_.solved_ref), channel_id=1, source_target_pairs={{0,8},{4,12},{8,0},{12,4},{16,24},{20,28},{24,16},{28,20},{1,9},{5... | collective-permute-start | bytes 196616 | tf_op jit(solution)/shard_map/ppermute | solution.py:23
  45.7 6.9 %collective-permute-start.12 = (bf16[128,256]{1,0:T(8,128)(2,1)S(1)}, bf16[128,256]{1,0:T(8,128)(2,1)S(1)}, u32[]{:S(2)}, u32[]{:S(2)}) collective-permute-start(bf16[128,256]{1,0:T(8,128)(2,1)S(1)} %get-tuple-element.44), channel_id=1, source_target_pairs={{0,3},{1,2},{2,1},{3,0},{4,7},{5,6},{6,5},{7,4},{8,11},{9,10},{10,... | collective-permute-start | bytes 196616 | tf_op jit(solution)/shard_map/ppermute | solution.py:23
  47.0 5.8 %collective-permute-start.13 = (bf16[128,256]{1,0:T(8,128)(2,1)S(1)}, bf16[128,256]{1,0:T(8,128)(2,1)S(1)}, u32[]{:S(2)}, u32[]{:S(2)}) collective-permute-start(bf16[128,256]{1,0:T(8,128)(2,1)S(1)} %get-tuple-element.45), channel_id=1, source_target_pairs={{0,1},{1,0},{2,3},{3,2},{4,5},{5,4},{6,7},{7,6},{8,9},{9,8},{10,11... | collective-permute-start | bytes 196616 | tf_op jit(solution)/shard_map/ppermute | solution.py:23
  47.1 6.2 %collective-permute-start.14 = (bf16[128,256]{1,0:T(8,128)(2,1)S(1)}, bf16[128,256]{1,0:T(8,128)(2,1)S(1)}, u32[]{:S(2)}, u32[]{:S(2)}) collective-permute-start(bf16[128,256]{1,0:T(8,128)(2,1)S(1)} %get-tuple-element.46), channel_id=1, source_target_pairs={{0,2},{1,3},{2,0},{3,1},{4,6},{5,7},{6,4},{7,5},{8,10},{9,11},{10,... | collective-permute-start | bytes 196616 | tf_op jit(solution)/shard_map/ppermute | solution.py:23
  53.4 5.8 %collective-permute-start.18 = (bf16[128,256]{1,0:T(8,128)(2,1)S(1)}, bf16[128,256]{1,0:T(8,128)(2,1)S(1)}, u32[]{:S(2)}, u32[]{:S(2)}) collective-permute-start(bf16[128,256]{1,0:T(8,128)(2,1)S(1)} %shard_map.65.after_ref.refs_0_.solved_ref), channel_id=1, source_target_pairs={{0,24},{4,28},{8,16},{12,20},{16,8},{20,12},{24,0},{28,4},{1,25},{... | collective-permute-start | bytes 196616 | tf_op jit(solution)/shard_map/ppermute | solution.py:23
  54.8 4.8 %collective-permute-start.17 = (bf16[128,256]{1,0:T(8,128)(2,1)S(1)}, bf16[128,256]{1,0:T(8,128)(2,1)S(1)}, u32[]{:S(2)}, u32[]{:S(2)}) collective-permute-start(bf16[128,256]{1,0:T(8,128)(2,1)S(1)} %shard_map.65.after_ref.refs_0_.solved_ref), channel_id=1, source_target_pairs={{0,16},{4,20},{8,24},{12,28},{16,0},{20,4},{24,8},{28,12},{1,17},{... | collective-permute-start | bytes 196616 | tf_op jit(solution)/shard_map/ppermute | solution.py:23
  56.3 4.3 %collective-permute-start.16 = (bf16[128,256]{1,0:T(8,128)(2,1)S(1)}, bf16[128,256]{1,0:T(8,128)(2,1)S(1)}, u32[]{:S(2)}, u32[]{:S(2)}) collective-permute-start(bf16[128,256]{1,0:T(8,128)(2,1)S(1)} %shard_map.65.after_ref.refs_0_.solved_ref), channel_id=1, source_target_pairs={{0,8},{4,12},{8,0},{12,4},{16,24},{20,28},{24,16},{28,20},{1,9},{5... | collective-permute-start | bytes 196616 | tf_op jit(solution)/shard_map/ppermute | solution.py:23
  61.0 6.2 %collective-permute-start.19 = (bf16[128,256]{1,0:T(8,128)(2,1)S(1)}, bf16[128,256]{1,0:T(8,128)(2,1)S(1)}, u32[]{:S(2)}, u32[]{:S(2)}) collective-permute-start(bf16[128,256]{1,0:T(8,128)(2,1)S(1)} %get-tuple-element.49), channel_id=1, source_target_pairs={{0,3},{1,2},{2,1},{3,0},{4,7},{5,6},{6,5},{7,4},{8,11},{9,10},{10,... | collective-permute-start | bytes 196616 | tf_op jit(solution)/shard_map/ppermute | solution.py:23
  63.0 4.9 %collective-permute-start.20 = (bf16[128,256]{1,0:T(8,128)(2,1)S(1)}, bf16[128,256]{1,0:T(8,128)(2,1)S(1)}, u32[]{:S(2)}, u32[]{:S(2)}) collective-permute-start(bf16[128,256]{1,0:T(8,128)(2,1)S(1)} %get-tuple-element.50), channel_id=1, source_target_pairs={{0,1},{1,0},{2,3},{3,2},{4,5},{5,4},{6,7},{7,6},{8,9},{9,8},{10,11... | collective-permute-start | bytes 196616 | tf_op jit(solution)/shard_map/ppermute | solution.py:23
  63.3 5.6 %collective-permute-start.21 = (bf16[128,256]{1,0:T(8,128)(2,1)S(1)}, bf16[128,256]{1,0:T(8,128)(2,1)S(1)}, u32[]{:S(2)}, u32[]{:S(2)}) collective-permute-start(bf16[128,256]{1,0:T(8,128)(2,1)S(1)} %get-tuple-element.51), channel_id=1, source_target_pairs={{0,2},{1,3},{2,0},{3,1},{4,6},{5,7},{6,4},{7,5},{8,10},{9,11},{10,... | collective-permute-start | bytes 196616 | tf_op jit(solution)/shard_map/ppermute | solution.py:23
  69.3 6.2 %collective-permute-start.24 = (bf16[128,256]{1,0:T(8,128)(2,1)S(1)}, bf16[128,256]{1,0:T(8,128)(2,1)S(1)}, u32[]{:S(2)}, u32[]{:S(2)}) collective-permute-start(bf16[128,256]{1,0:T(8,128)(2,1)S(1)} %get-tuple-element.52.after_ref.refs_0_.refs_3_), channel_id=1, source_target_pairs={{0,3},{1,2},{2,1},{3,0},{4,7},{5,6},{6,5},{7,4},{8,11},{9,10},{10,... | collective-permute-start | bytes 196616 | tf_op jit(solution)/shard_map/ppermute | solution.py:23
  70.9 6.1 %collective-permute-start.23 = (bf16[128,256]{1,0:T(8,128)(2,1)S(1)}, bf16[128,256]{1,0:T(8,128)(2,1)S(1)}, u32[]{:S(2)}, u32[]{:S(2)}) collective-permute-start(bf16[128,256]{1,0:T(8,128)(2,1)S(1)} %get-tuple-element.52.after_ref.refs_0_.refs_3_), channel_id=1, source_target_pairs={{0,2},{1,3},{2,0},{3,1},{4,6},{5,7},{6,4},{7,5},{8,10},{9,11},{10,... | collective-permute-start | bytes 196616 | tf_op jit(solution)/shard_map/ppermute | solution.py:23
  72.6 4.4 %collective-permute-start.22 = (bf16[128,256]{1,0:T(8,128)(2,1)S(1)}, bf16[128,256]{1,0:T(8,128)(2,1)S(1)}, u32[]{:S(2)}, u32[]{:S(2)}) collective-permute-start(bf16[128,256]{1,0:T(8,128)(2,1)S(1)} %get-tuple-element.52.after_ref.refs_0_.refs_3_), channel_id=1, source_target_pairs={{0,1},{1,0},{2,3},{3,2},{4,5},{5,4},{6,7},{7,6},{8,9},{9,8},{10,11... | collective-permute-start | bytes 196616 | tf_op jit(solution)/shard_map/ppermute | solution.py:23
  77.4 5.2 %collective-permute-start.25 = (bf16[128,256]{1,0:T(8,128)(2,1)S(1)}, bf16[128,256]{1,0:T(8,128)(2,1)S(1)}, u32[]{:S(2)}, u32[]{:S(2)}) collective-permute-start(bf16[128,256]{1,0:T(8,128)(2,1)S(1)} %get-tuple-element.53), channel_id=1, source_target_pairs={{0,24},{4,28},{8,16},{12,20},{16,8},{20,12},{24,0},{28,4},{1,25},{... | collective-permute-start | bytes 196616 | tf_op jit(solution)/shard_map/ppermute | solution.py:23
  79.4 4.3 %collective-permute-start.26 = (bf16[128,256]{1,0:T(8,128)(2,1)S(1)}, bf16[128,256]{1,0:T(8,128)(2,1)S(1)}, u32[]{:S(2)}, u32[]{:S(2)}) collective-permute-start(bf16[128,256]{1,0:T(8,128)(2,1)S(1)} %get-tuple-element.54), channel_id=1, source_target_pairs={{0,8},{4,12},{8,0},{12,4},{16,24},{20,28},{24,16},{28,20},{1,9},{5... | collective-permute-start | bytes 196616 | tf_op jit(solution)/shard_map/ppermute | solution.py:23
  79.4 4.3 %collective-permute-start.27 = (bf16[128,256]{1,0:T(8,128)(2,1)S(1)}, bf16[128,256]{1,0:T(8,128)(2,1)S(1)}, u32[]{:S(2)}, u32[]{:S(2)}) collective-permute-start(bf16[128,256]{1,0:T(8,128)(2,1)S(1)} %get-tuple-element.55), channel_id=1, source_target_pairs={{0,16},{4,20},{8,24},{12,28},{16,0},{20,4},{24,8},{28,12},{1,17},{... | collective-permute-start | bytes 196616 | tf_op jit(solution)/shard_map/ppermute | solution.py:23
  83.8 6.1 %collective-permute-start.30 = (bf16[128,256]{1,0:T(8,128)(2,1)S(1)}, bf16[128,256]{1,0:T(8,128)(2,1)S(1)}, u32[]{:S(2)}, u32[]{:S(2)}) collective-permute-start(bf16[128,256]{1,0:T(8,128)(2,1)S(1)} %get-tuple-element.56.after_ref.refs_0_.refs_2_), channel_id=1, source_target_pairs={{0,3},{1,2},{2,1},{3,0},{4,7},{5,6},{6,5},{7,4},{8,11},{9,10},{10,... | collective-permute-start | bytes 196616 | tf_op jit(solution)/shard_map/ppermute | solution.py:23
  85.8 5.5 %collective-permute-start.29 = (bf16[128,256]{1,0:T(8,128)(2,1)S(1)}, bf16[128,256]{1,0:T(8,128)(2,1)S(1)}, u32[]{:S(2)}, u32[]{:S(2)}) collective-permute-start(bf16[128,256]{1,0:T(8,128)(2,1)S(1)} %get-tuple-element.56.after_ref.refs_0_.refs_2_), channel_id=1, source_target_pairs={{0,2},{1,3},{2,0},{3,1},{4,6},{5,7},{6,4},{7,5},{8,10},{9,11},{10,... | collective-permute-start | bytes 196616 | tf_op jit(solution)/shard_map/ppermute | solution.py:23
  86.2 5.1 %collective-permute-start.28 = (bf16[128,256]{1,0:T(8,128)(2,1)S(1)}, bf16[128,256]{1,0:T(8,128)(2,1)S(1)}, u32[]{:S(2)}, u32[]{:S(2)}) collective-permute-start(bf16[128,256]{1,0:T(8,128)(2,1)S(1)} %get-tuple-element.56.after_ref.refs_0_.refs_2_), channel_id=1, source_target_pairs={{0,1},{1,0},{2,3},{3,2},{4,5},{5,4},{6,7},{7,6},{8,9},{9,8},{10,11... | collective-permute-start | bytes 196616 | tf_op jit(solution)/shard_map/ppermute | solution.py:23
  91.8 5.2 %collective-permute-start.31 = (bf16[128,256]{1,0:T(8,128)(2,1)S(1)}, bf16[128,256]{1,0:T(8,128)(2,1)S(1)}, u32[]{:S(2)}, u32[]{:S(2)}) collective-permute-start(bf16[128,256]{1,0:T(8,128)(2,1)S(1)} %get-tuple-element.57), channel_id=1, source_target_pairs={{0,24},{4,28},{8,16},{12,20},{16,8},{20,12},{24,0},{28,4},{1,25},{... | collective-permute-start | bytes 196616 | tf_op jit(solution)/shard_map/ppermute | solution.py:23
  94.2 4.3 %collective-permute-start.32 = (bf16[128,256]{1,0:T(8,128)(2,1)S(1)}, bf16[128,256]{1,0:T(8,128)(2,1)S(1)}, u32[]{:S(2)}, u32[]{:S(2)}) collective-permute-start(bf16[128,256]{1,0:T(8,128)(2,1)S(1)} %get-tuple-element.58), channel_id=1, source_target_pairs={{0,8},{4,12},{8,0},{12,4},{16,24},{20,28},{24,16},{28,20},{1,9},{5... | collective-permute-start | bytes 196616 | tf_op jit(solution)/shard_map/ppermute | solution.py:23
  94.9 4.3 %collective-permute-start.33 = (bf16[128,256]{1,0:T(8,128)(2,1)S(1)}, bf16[128,256]{1,0:T(8,128)(2,1)S(1)}, u32[]{:S(2)}, u32[]{:S(2)}) collective-permute-start(bf16[128,256]{1,0:T(8,128)(2,1)S(1)} %get-tuple-element.59), channel_id=1, source_target_pairs={{0,16},{4,20},{8,24},{12,28},{16,0},{20,4},{24,8},{28,12},{1,17},{... | collective-permute-start | bytes 196616 | tf_op jit(solution)/shard_map/ppermute | solution.py:23
  99.4 6.1 %collective-permute-start.36 = (bf16[128,256]{1,0:T(8,128)(2,1)S(1)}, bf16[128,256]{1,0:T(8,128)(2,1)S(1)}, u32[]{:S(2)}, u32[]{:S(2)}) collective-permute-start(bf16[128,256]{1,0:T(8,128)(2,1)S(1)} %get-tuple-element.60.after_ref.refs_0_.refs_1_), channel_id=1, source_target_pairs={{0,3},{1,2},{2,1},{3,0},{4,7},{5,6},{6,5},{7,4},{8,11},{9,10},{10,... | collective-permute-start | bytes 196616 | tf_op jit(solution)/shard_map/ppermute | solution.py:23
  101.5 5.6 %collective-permute-start.35 = (bf16[128,256]{1,0:T(8,128)(2,1)S(1)}, bf16[128,256]{1,0:T(8,128)(2,1)S(1)}, u32[]{:S(2)}, u32[]{:S(2)}) collective-permute-start(bf16[128,256]{1,0:T(8,128)(2,1)S(1)} %get-tuple-element.60.after_ref.refs_0_.refs_1_), channel_id=1, source_target_pairs={{0,2},{1,3},{2,0},{3,1},{4,6},{5,7},{6,4},{7,5},{8,10},{9,11},{10,... | collective-permute-start | bytes 196616 | tf_op jit(solution)/shard_map/ppermute | solution.py:23
  102.1 5.0 %collective-permute-start.34 = (bf16[128,256]{1,0:T(8,128)(2,1)S(1)}, bf16[128,256]{1,0:T(8,128)(2,1)S(1)}, u32[]{:S(2)}, u32[]{:S(2)}) collective-permute-start(bf16[128,256]{1,0:T(8,128)(2,1)S(1)} %get-tuple-element.60.after_ref.refs_0_.refs_1_), channel_id=1, source_target_pairs={{0,1},{1,0},{2,3},{3,2},{4,5},{5,4},{6,7},{7,6},{8,9},{9,8},{10,11... | collective-permute-start | bytes 196616 | tf_op jit(solution)/shard_map/ppermute | solution.py:23
  103.8 10.2 %collective-permute-start.40 = (bf16[128,384]{1,0:T(8,128)(2,1)S(1)}, bf16[128,384]{1,0:T(8,128)(2,1)S(1)}, u32[]{:S(2)}, u32[]{:S(2)}) collective-permute-start(bf16[128,384]{1,0:T(8,128)(2,1)S(1)} %pad_maximum_fusion), channel_id=1, source_target_pairs={{0,4},{4,0},{8,12},{12,8},{16,20},{20,16},{24,28},{28,24},{1,5},{5... | collective-permute-start | bytes 294920 | tf_op jit(solution)/shard_map/ppermute | solution.py:23
  107.5 5.2 %collective-permute-start.37 = (bf16[128,256]{1,0:T(8,128)(2,1)S(1)}, bf16[128,256]{1,0:T(8,128)(2,1)S(1)}, u32[]{:S(2)}, u32[]{:S(2)}) collective-permute-start(bf16[128,256]{1,0:T(8,128)(2,1)S(1)} %get-tuple-element.61), channel_id=1, source_target_pairs={{0,24},{4,28},{8,16},{12,20},{16,8},{20,12},{24,0},{28,4},{1,25},{... | collective-permute-start | bytes 196616 | tf_op jit(solution)/shard_map/ppermute | solution.py:23
  109.4 4.3 %collective-permute-start.38 = (bf16[128,256]{1,0:T(8,128)(2,1)S(1)}, bf16[128,256]{1,0:T(8,128)(2,1)S(1)}, u32[]{:S(2)}, u32[]{:S(2)}) collective-permute-start(bf16[128,256]{1,0:T(8,128)(2,1)S(1)} %get-tuple-element.62), channel_id=1, source_target_pairs={{0,8},{4,12},{8,0},{12,4},{16,24},{20,28},{24,16},{28,20},{1,9},{5... | collective-permute-start | bytes 196616 | tf_op jit(solution)/shard_map/ppermute | solution.py:23
  109.5 4.3 %collective-permute-start.39 = (bf16[128,256]{1,0:T(8,128)(2,1)S(1)}, bf16[128,256]{1,0:T(8,128)(2,1)S(1)}, u32[]{:S(2)}, u32[]{:S(2)}) collective-permute-start(bf16[128,256]{1,0:T(8,128)(2,1)S(1)} %get-tuple-element.63), channel_id=1, source_target_pairs={{0,16},{4,20},{8,24},{12,28},{16,0},{20,4},{24,8},{28,12},{1,17},{... | collective-permute-start | bytes 196616 | tf_op jit(solution)/shard_map/ppermute | solution.py:23
  113.9 1.3 %collective-permute-start.41 = (bf16[128,128]{1,0:T(8,128)(2,1)S(1)}, bf16[128,128]{1,0:T(8,128)(2,1)S(1)}, u32[]{:S(2)}, u32[]{:S(2)}) collective-permute-start(bf16[128,128]{1,0:T(8,128)(2,1)S(1)} %get-tuple-element.68), channel_id=1, source_target_pairs={{0,4},{4,0},{8,12},{12,8},{16,20},{20,16},{24,28},{28,24},{1,5},{5... | collective-permute-start | bytes 98312 | tf_op jit(solution)/shard_map/ppermute | solution.py:23
